TPU v7x, 32 devices: a whole 2x2x4 slice. The times are simulated.
32 devices in a mesh: groups: 2 (over y), seq: 4 (over z), segment: 2 (over x), owner: 2 (over core).
Axes of the slice: x: 2, y: 2, z: 4, core: 2. Of those that a mesh axis runs over, the one named last changes fastest.
Arguments:
- layer_input_rows: bfloat16 [2, 512, 5376], P('segment', ('groups', 'seq')), parts along dimension 1, may hold values from -40 to 40
- encoded_query_rows: bfloat16 [2, 512, 2048], P('segment', ('groups', 'seq'), 'owner'), parts along dimension 1, may hold values from -213 to 213
- encoded_key_rows: bfloat16 [2, 512, 1024], P('segment', ('groups', 'seq'), 'owner'), parts along dimension 1, may hold values from -6 to 6
- layer_norm_gain: float32 [2, 5376], P('segment'), may hold values from 0.25 to 1.75
- base_value_matrix: bfloat16 [2, 5376, 1024], P('segment', ('seq', 'owner')), may hold values from -0.078125 to 0.078125
- adapter_down_panels: bfloat16 [2, 8, 5376, 64], P('segment', 'seq', 'owner'), may hold values from -0.078125 to 0.078125
- adapter_up_panels: bfloat16 [2, 8, 64, 1024], P('segment', 'seq', None, 'owner'), may hold values from -0.75 to 0.75
- request_token_lengths: int32 [8], P('groups'), parts along dimension 0, may hold values from 1 to 128, 256 in all
- adapter_per_request: int32 [8], P('groups'), parts along dimension 0, may hold values from 0 to 7
- rank_per_adapter: int32 [8], replicated, may hold values from 16 to 64
- slot_per_adapter: int32 [8], replicated, may hold values from 0 to 7, each once
Outputs:
- layer_output: bfloat16 [2, 512, 2048], P('segment', ('groups', 'seq'), 'owner'), parts along dimension 1
There are 2 independent parts, one for each index of `groups`. A program takes and returns all parts, laid end to end along the dimension named above; an argument that names none is the same for every part. Nothing has to cross between parts.
All inputs are finite; a program needn't handle non-finite values.
Results may differ from a plain program's by a relative error of at most 0.0065.
Values may be sent and summed in bfloat16 or wider, within the bound.
No kernel may reach another device: no remote copies, remote signals or barrier semaphores. Data moves between devices by JAX's collectives and lax.ppermute only.
A program may use at most 128 MiB of HBM per device.

v0:
```python
import jax
import jax.numpy as jnp
from jax import lax
from jax.sharding import PartitionSpec as P

WINDOW = 1024
HEADS = 16
KEY_VALUE_HEADS = 8
HEAD_SIZE = 128


query_scale = 168.0 ** (-0.5)
adapter_strength = 32.0
norm_eps = 1e-06


def broadcast(x, axis, root):
    mine = lax.axis_index(axis) == root
    return lax.psum(jnp.where(mine, x, jnp.zeros_like(x)), axis)


def from_behind(value, axis, steps):
    count = lax.axis_size(axis)
    first, last = (max(0, -steps), min(count, count - steps))
    return lax.ppermute(value, axis, [(source, source + steps) for source in range(first, last)])


def per_device(
    layer_input_rows,
    encoded_query_rows,
    encoded_key_rows,
    layer_norm_gain,
    base_value_matrix,
    adapter_down_panels,
    adapter_up_panels,
    request_token_lengths,
    adapter_per_request,
    rank_per_adapter,
    slot_per_adapter,
):
    hidden = layer_input_rows[0]
    row_count = hidden.shape[0]
    seq_now = lax.axis_index("seq")
    owner_now = lax.axis_index("owner")
    reach_count = min(WINDOW // row_count, lax.axis_size("seq") - 1)
    requests = request_token_lengths.shape[0]
    library = slot_per_adapter.shape[0]
    slots_here = adapter_down_panels.shape[1]
    rows_halved = adapter_down_panels.shape[2]
    rank_span_width = adapter_down_panels.shape[3]
    key_value_halved = adapter_up_panels.shape[3]
    group_size = HEADS // KEY_VALUE_HEADS
    request_ends = jnp.cumsum(request_token_lengths)
    position = seq_now * row_count + jnp.arange(row_count, dtype=jnp.int32)
    context = seq_now * row_count + jnp.arange(-reach_count * row_count, row_count, dtype=jnp.int32)
    request_lookup = jnp.sum((position[:, None] >= request_ends[None, :]).astype(jnp.int32), axis=1)
    request_ctx = jnp.sum((context[:, None] >= request_ends[None, :]).astype(jnp.int32), axis=1)
    live_mask = (context[None, :] <= position[:, None]) & (
        context[None, :] > position[:, None] - WINDOW
    )
    live_mask = (
        live_mask & (context[None, :] >= 0) & (request_ctx[None, :] == request_lookup[:, None])
    )
    choose = adapter_per_request[:, None] == jnp.arange(library, dtype=jnp.int32)[None, :]
    slot_of = jnp.sum(jnp.where(choose, slot_per_adapter[None, :], 0), axis=1)
    rank_lookup = jnp.sum(jnp.where(choose, rank_per_adapter[None, :], 0), axis=1)
    scale_lookup = adapter_strength / rank_lookup.astype(jnp.float32)
    in_request = request_lookup[:, None] == jnp.arange(requests, dtype=jnp.int32)[None, :]
    column_live = jnp.arange(rank_span_width, dtype=jnp.int32)[None, :] < rank_lookup[:, None]
    row_gain_weight = jnp.where(in_request, scale_lookup[None, :], jnp.float32(0.0))
    down_panel_here = adapter_down_panels[0]
    up_panel_here = adapter_up_panels[0]
    queries = encoded_query_rows[0]
    keys_own = encoded_key_rows[0]
    key_heads = keys_own.shape[1] // HEAD_SIZE
    wide_rows = hidden.astype(jnp.float32)
    normalized_rows = wide_rows * lax.rsqrt(
        jnp.mean(wide_rows * wide_rows, axis=1, keepdims=True) + norm_eps
    )
    normalized_rows = (normalized_rows * layer_norm_gain[0][None, :]).astype(jnp.bfloat16)
    normed_half = lax.dynamic_slice_in_dim(normalized_rows, owner_now * rows_halved, rows_halved, 1)
    full_value = jnp.dot(
        normalized_rows,
        lax.all_gather(base_value_matrix[0], ("seq", "owner"), axis=0, tiled=True),
        preferred_element_type=jnp.float32,
    )
    value_base_rows = lax.dynamic_slice_in_dim(
        full_value, owner_now * key_value_halved, key_value_halved, 1
    )

    def fetch_one(reduced_rows, request_index):
        owner_slot = slot_of[request_index]
        holder = owner_slot // slots_here
        local_slot = owner_slot % slots_here
        down_local = lax.dynamic_slice_in_dim(down_panel_here, local_slot, 1, 0)
        up_local = lax.dynamic_slice_in_dim(up_panel_here, local_slot, 1, 0)
        down_piece, up_piece = (
            broadcast(down_local, "seq", holder),
            broadcast(up_local, "seq", holder),
        )
        keep_mask = in_request[:, request_index][:, None] & column_live[request_index][None, :]
        matrix_product = jnp.dot(normed_half, down_piece[0], preferred_element_type=jnp.float32)
        return (reduced_rows + jnp.where(keep_mask, matrix_product, jnp.float32(0.0)), up_piece[0])

    start_low = jnp.zeros((row_count, rank_span_width), jnp.float32)
    reduced_rows, panels_up = lax.scan(fetch_one, start_low, jnp.arange(requests, dtype=jnp.int32))
    reduced_rows = lax.psum(reduced_rows, "owner").astype(jnp.bfloat16)
    raised_rows = jnp.einsum(
        "tr,qrk->qtk", reduced_rows, panels_up, preferred_element_type=jnp.float32
    )
    adapter_value = jnp.sum(row_gain_weight.T[:, :, None] * raised_rows, axis=0)
    value_output_rows = (value_base_rows + adapter_value).astype(jnp.bfloat16)
    key_parts = []
    value_parts = []
    for shift_by in range(reach_count, 0, -1):
        key_piece, value_piece = from_behind((keys_own, value_output_rows), "seq", shift_by)
        key_parts.append(key_piece)
        value_parts.append(value_piece)
    keys_all = jnp.concatenate(key_parts + [keys_own], axis=0)
    values_all = jnp.concatenate(value_parts + [value_output_rows], axis=0)
    query_view = queries.reshape(row_count, key_heads, group_size, HEAD_SIZE)
    key_view = keys_all.reshape(-1, key_heads, HEAD_SIZE)
    value_view = values_all.reshape(-1, key_heads, HEAD_SIZE)
    head_outputs = []
    for head_index in range(key_heads):
        query_head = query_view[:, head_index]
        scores = (
            jnp.einsum(
                "tcd,jd->ctj",
                query_head,
                key_view[:, head_index],
                preferred_element_type=jnp.float32,
            )
            * query_scale
        )
        scores = jnp.where(live_mask[None], scores, jnp.float32(-1e30))
        row_max = jnp.max(scores, axis=-1, keepdims=True)
        weights = jnp.exp(scores - row_max)
        row_total = jnp.sum(weights, axis=-1, keepdims=True)
        softmax_rows = (weights / row_total).astype(jnp.bfloat16)
        mixed = jnp.einsum(
            "ctj,jd->tcd",
            softmax_rows,
            value_view[:, head_index],
            preferred_element_type=jnp.float32,
        )
        head_outputs.append(mixed.astype(jnp.bfloat16).reshape(row_count, group_size * HEAD_SIZE))
    result = jnp.concatenate(head_outputs, axis=1)
    return result[None]


def solution(mesh):
    in_specs = (
        P("segment", ("groups", "seq"), None),
        P("segment", ("groups", "seq"), "owner"),
        P("segment", ("groups", "seq"), "owner"),
        P("segment", None),
        P("segment", ("seq", "owner"), None),
        P("segment", "seq", "owner", None),
        P("segment", "seq", None, "owner"),
        P("groups"),
        P("groups"),
        P(),
        P(),
    )
    out_specs = P("segment", ("groups", "seq"), "owner")
    return jax.shard_map(
        per_device, mesh=mesh, in_specs=in_specs, out_specs=out_specs, check_vma=False
    )
```

profile of v0, /device:TPU:0, one launch (start us, length us, event | category | flops | bytes accessed | tf_op | source)
XLA Modules:
  0.0 354.5 jit_solution(13641821148216391470)
XLA Ops:
  7.4 1.4 fusion.8
  8.8 0.8 reduce-window.8
  9.7 0.9 select_reduce_fusion
  10.7 1.7 copy.36
  12.8 0.5 copy-done.1
  13.4 212.2 %while.15 = (s32[]{:T(128)}, f32[64,64]{0,1:T(8,128)S(1)}, bf16[4,64,512]{2,1,0:T(8,128)(2,1)S(1)}, s32[4]{0:T(128)S(1)}, pred[64,4]{0,1:T(4,128)(4,1)S(1)}, /*i...) while((s32[]{:T(128)}, f32[64,64]{0,1:T(8,128)S(1)}, ...), condition=%wide.region_8.9_spmd.clone, body=%wide.region_5.8_spmd.clone.sunk | while | flops 22446112 | bytes 4817837 | solution.py:106
  13.4 0.6 dynamic_slice.67
  15.9 0.6 dynamic_slice.68
  19.1 0.9 select_bitcast_fusion.2
  20.0 0.6 dynamic-slice_select_fusion.2
  20.7 45.9 %all-reduce.5.cloned.1.call-done = (bf16[2688,64]{1,0:T(8,128)(2,1)}, bf16[1,64,512]{2,1,0:T(8,128)(2,1)}) async-done(((bf16[2688,64]{1,0:T(8,128)(2,1)}, bf16[1,64,512]{2,1,0:T(8,128)(2,1)}), (bf16[2688,64]{1,0:T(8,128)(2,1)}, bf16[1,64,512]{2,1,0:T(8,128)(2,1)})) %all-reduce.5.cloned.1.call-update) | async-done | bytes 409616 | tf_op jit(solution)/shard_map/while/body/eval_jaxpr/psum | solution.py:19
  66.6 0.8 constant_dynamic-update-slice_fusion.2
  67.5 1.5 fusion.74
  69.0 0.6 dynamic_slice.67
  71.6 0.6 dynamic_slice.68
  74.8 0.9 select_bitcast_fusion.2
  75.7 0.6 dynamic-slice_select_fusion.2
  76.4 42.5 %all-reduce.5.cloned.1.call-done = (bf16[2688,64]{1,0:T(8,128)(2,1)}, bf16[1,64,512]{2,1,0:T(8,128)(2,1)}) async-done(((bf16[2688,64]{1,0:T(8,128)(2,1)}, bf16[1,64,512]{2,1,0:T(8,128)(2,1)}), (bf16[2688,64]{1,0:T(8,128)(2,1)}, bf16[1,64,512]{2,1,0:T(8,128)(2,1)})) %all-reduce.5.cloned.1.call-update) | async-done | bytes 409616 | tf_op jit(solution)/shard_map/while/body/eval_jaxpr/psum | solution.py:19
  118.8 0.8 constant_dynamic-update-slice_fusion.2
  119.7 1.5 fusion.74
  121.2 0.6 dynamic_slice.67
  123.8 0.6 dynamic_slice.68
  127.0 0.9 select_bitcast_fusion.2
  127.9 0.6 dynamic-slice_select_fusion.2
  128.6 42.5 %all-reduce.5.cloned.1.call-done = (bf16[2688,64]{1,0:T(8,128)(2,1)}, bf16[1,64,512]{2,1,0:T(8,128)(2,1)}) async-done(((bf16[2688,64]{1,0:T(8,128)(2,1)}, bf16[1,64,512]{2,1,0:T(8,128)(2,1)}), (bf16[2688,64]{1,0:T(8,128)(2,1)}, bf16[1,64,512]{2,1,0:T(8,128)(2,1)})) %all-reduce.5.cloned.1.call-update) | async-done | bytes 409616 | tf_op jit(solution)/shard_map/while/body/eval_jaxpr/psum | solution.py:19
  171.1 0.8 constant_dynamic-update-slice_fusion.2
  171.9 1.5 fusion.74
  173.5 0.6 dynamic_slice.67
  176.0 0.6 dynamic_slice.68
  179.2 0.9 select_bitcast_fusion.2
  180.1 0.6 dynamic-slice_select_fusion.2
  180.8 42.5 %all-reduce.5.cloned.1.call-done = (bf16[2688,64]{1,0:T(8,128)(2,1)}, bf16[1,64,512]{2,1,0:T(8,128)(2,1)}) async-done(((bf16[2688,64]{1,0:T(8,128)(2,1)}, bf16[1,64,512]{2,1,0:T(8,128)(2,1)}), (bf16[2688,64]{1,0:T(8,128)(2,1)}, bf16[1,64,512]{2,1,0:T(8,128)(2,1)})) %all-reduce.5.cloned.1.call-update) | async-done | bytes 409616 | tf_op jit(solution)/shard_map/while/body/eval_jaxpr/psum | solution.py:19
  223.3 0.8 constant_dynamic-update-slice_fusion.2
  224.1 1.5 fusion.74
  225.7 0.5 all-gather.3.cloned.1.call-update
  226.5 3.7 %collective-permute-start.3 = (bf16[64,512]{1,0:T(8,128)(2,1)S(1)}, bf16[64,512]{1,0:T(8,128)(2,1)S(1)}, u32[]{:S(2)}, u32[]{:S(2)}) collective-permute-start(bf16[64,512]{1,0:T(8,128)(2,1)S(1)} %bitcast.212), channel_id=1, source_target_pairs={{0,12},{1,13},{2,14},{3,15},{16,28},{17,29},{18,30},{19,31}} | collective-permute-start | bytes 196616 | tf_op jit(solution)/shard_map/ppermute | solution.py:25
  230.2 1.3 collective-permute-start.4
  231.5 2.5 collective-permute-start.5
  234.1 3.4 psum.27
  240.0 90.6 %all-gather.3.cloned.1.call-done = bf16[1,5376,1024]{2,1,0:T(8,128)(2,1)} async-done(((bf16[1,672,1024]{2,1,0:T(8,128)(2,1)}), bf16[1,5376,1024]{2,1,0:T(8,128)(2,1)}) %all-gather.3.cloned.1.call-update) | async-done | bytes 11010064 | tf_op jit(solution)/shard_map/all_gather | solution.py:84
  330.6 6.1 %fusion.6 = f32[64,1024]{1,0:T(8,128)S(1)} fusion(bf16[64,5376]{1,0:T(8,128)(2,1)S(1)} %fusion.10, bf16[1,5376,1024]{2,1,0:T(8,128)(2,1)} %all-gather.3.cloned.1.call-done), kind=kOutput, calls=%fused_computation.12 | convolution fusion | flops 704643072 | bytes 11960320 | tf_op jit(solution)/shard_map/dot_general | solution.py:82
  336.8 2.3 collective-permute-start
  339.1 1.3 collective-permute-start.1
  340.4 2.5 collective-permute-start.2
  342.9 0.3 fusion.54
  343.3 1.5 collective-permute-done.2
  344.9 0.4 fusion.52
  346.7 0.7 maximum_bitcast_fusion
  (75 shorter events, 5.0 us)
Async XLA Ops:
  7.4 5.1 %copy-start.4 = (f32[1,5376]{1,0:T(1,128)S(1)}, f32[1,5376]{1,0:T(1,128)}, u32[]{:S(2)}) copy-start(f32[1,5376]{1,0:T(1,128)} %param.16) | copy-start | bytes 64516
  7.4 5.2 %copy-start = (bf16[1,64,5376]{2,1,0:T(8,128)(2,1)S(1)}, bf16[1,64,5376]{2,1,0:T(8,128)(2,1)}, u32[]{:S(2)}) copy-start(bf16[1,64,5376]{2,1,0:T(8,128)(2,1)} %param.13) | copy-start | bytes 2064388
  12.5 0.9 copy-start.1
  13.4 53.2 %all-reduce.5.cloned.1.call-start = ((), (), s32[]{:S(2)}) async-start(), calls=%async_computation.1 | async-start | bytes 1507328 | tf_op jit(solution)/shard_map/while/body/eval_jaxpr/psum | solution.py:19
  69.0 49.9 %all-reduce.5.cloned.1.call-start = ((), (), s32[]{:S(2)}) async-start(), calls=%async_computation.1 | async-start | bytes 1507328 | tf_op jit(solution)/shard_map/while/body/eval_jaxpr/psum | solution.py:19
  121.2 49.9 %all-reduce.5.cloned.1.call-start = ((), (), s32[]{:S(2)}) async-start(), calls=%async_computation.1 | async-start | bytes 1507328 | tf_op jit(solution)/shard_map/while/body/eval_jaxpr/psum | solution.py:19
  173.4 49.9 %all-reduce.5.cloned.1.call-start = ((), (), s32[]{:S(2)}) async-start(), calls=%async_computation.1 | async-start | bytes 1507328 | tf_op jit(solution)/shard_map/while/body/eval_jaxpr/psum | solution.py:19
  225.6 0.8 copy-start.3
  225.6 8.4 %copy-start.2 = (bf16[1,64,1024]{2,1,0:T(8,128)(2,1)S(1)}, bf16[1,64,1024]{2,1,0:T(8,128)(2,1)}, u32[]{:S(2)}) copy-start(bf16[1,64,1024]{2,1,0:T(8,128)(2,1)} %param.14) | copy-start | bytes 393220
  225.6 105.0 %all-gather.3.cloned.1.call-start = ((), (), s32[]{:S(2)}) async-start(), calls=%async_computation | async-start | bytes 12386304 | tf_op jit(solution)/shard_map/all_gather | solution.py:84
  226.5 11.7 %collective-permute-start.3 = (bf16[64,512]{1,0:T(8,128)(2,1)S(1)}, bf16[64,512]{1,0:T(8,128)(2,1)S(1)}, u32[]{:S(2)}, u32[]{:S(2)}) collective-permute-start(bf16[64,512]{1,0:T(8,128)(2,1)S(1)} %bitcast.212), channel_id=1, source_target_pairs={{0,12},{1,13},{2,14},{3,15},{16,28},{17,29},{18,30},{19,31}} | collective-permute-start | bytes 196616 | tf_op jit(solution)/shard_map/ppermute | solution.py:25
  230.2 8.0 %collective-permute-start.4 = (bf16[64,512]{1,0:T(8,128)(2,1)S(1)}, bf16[64,512]{1,0:T(8,128)(2,1)S(1)}, u32[]{:S(2)}, u32[]{:S(2)}) collective-permute-start(bf16[64,512]{1,0:T(8,128)(2,1)S(1)} %bitcast.213), channel_id=1, source_target_pairs={{0,8},{4,12},{1,9},{5,13},{2,10},{6,14},{3,11},{7,15},{16,24},{20,... | collective-permute-start | bytes 196616 | tf_op jit(solution)/shard_map/ppermute | solution.py:25
  231.5 6.8 %collective-permute-start.5 = (bf16[64,512]{1,0:T(8,128)(2,1)S(1)}, bf16[64,512]{1,0:T(8,128)(2,1)S(1)}, u32[]{:S(2)}, u32[]{:S(2)}) collective-permute-start(bf16[64,512]{1,0:T(8,128)(2,1)S(1)} %bitcast.214), channel_id=1, source_target_pairs={{0,4},{4,8},{8,12},{1,5},{5,9},{9,13},{2,6},{6,10},{10,14},{3,7},{... | collective-permute-start | bytes 196616 | tf_op jit(solution)/shard_map/ppermute | solution.py:25
  336.8 6.4 %collective-permute-start = (bf16[64,512]{1,0:T(8,128)(2,1)S(1)}, bf16[64,512]{1,0:T(8,128)(2,1)S(1)}, u32[]{:S(2)}, u32[]{:S(2)}) collective-permute-start(bf16[64,512]{1,0:T(8,128)(2,1)S(1)} %fusion.32), channel_id=1, source_target_pairs={{0,12},{1,13},{2,14},{3,15},{16,28},{17,29},{18,30},{19,31}} | collective-permute-start | bytes 196616 | tf_op jit(solution)/shard_map/ppermute | solution.py:25
  339.1 4.1 %collective-permute-start.1 = (bf16[64,512]{1,0:T(8,128)(2,1)S(1)}, bf16[64,512]{1,0:T(8,128)(2,1)S(1)}, u32[]{:S(2)}, u32[]{:S(2)}) collective-permute-start(bf16[64,512]{1,0:T(8,128)(2,1)S(1)} %fusion.32), channel_id=1, source_target_pairs={{0,8},{4,12},{1,9},{5,13},{2,10},{6,14},{3,11},{7,15},{16,24},{20,... | collective-permute-start | bytes 196616 | tf_op jit(solution)/shard_map/ppermute | solution.py:25
  340.4 4.4 %collective-permute-start.2 = (bf16[64,512]{1,0:T(8,128)(2,1)S(1)}, bf16[64,512]{1,0:T(8,128)(2,1)S(1)}, u32[]{:S(2)}, u32[]{:S(2)}) collective-permute-start(bf16[64,512]{1,0:T(8,128)(2,1)S(1)} %fusion.32), channel_id=1, source_target_pairs={{0,4},{4,8},{8,12},{1,5},{5,9},{9,13},{2,6},{6,10},{10,14},{3,7},{... | collective-permute-start | bytes 196616 | tf_op jit(solution)/shard_map/ppermute | solution.py:25
Sparse Core Ops, SparseCore 0:
  20.8 45.7 all-reduce.4
  76.5 42.3 all-reduce.4
  128.7 42.3 all-reduce.4
  180.9 42.3 all-reduce.4
Sparse Core Ops, SparseCore 1:
  227.8 102.8 all-gather.2
where the time goes:
time: 356 us; the launch traced here: 354 us
  waiting for transfers between devices  266 us (75%)
  loops' own time  18.5 us (5%)
  matrix products  15.6 us (4%)
  between operations  14.9 us (4%)
  starting transfers between devices  13.7 us (4%)
  local copies, waits for them, and re-layouts  11.6 us (3%)
  other arithmetic  10.8 us (3%)
    psum x4, waiting for transfers between devices, broadcast(): return lax.psum(jnp.where(mine, x, jnp.zeros_like(x)), axis)  173 us
    all_gather x1, waiting for transfers between devices, per_device(): lax.all_gather(base_value_matrix[0], ('seq', 'owner'), axis=0, tiled=True)  90.6 us
    another operation x1, loops' own time, per_device(): lax.scan(fetch_one, start_low, jnp.arange(requests, dtype=jnp.int32))  18.5 us
    ppermute x6, starting transfers between devices, from_behind(): lax.ppermute(value, axis, [(source, source + steps) for source in range(f...  13.5 us
  transfers between devices with their start and end apart: 11, of which 6 were waited for; matrix products, arithmetic and copies ran while one was open for 1% of the time, Pallas kernels for 0%

commit v1 on v0

--- a/solution.py
+++ b/solution.py
@@ -1,17 +1,423 @@
+import functools
+
 import jax
 import jax.numpy as jnp
 from jax import lax
+from jax.experimental import pallas as pl
+from jax.experimental.pallas import tpu as pltpu
 from jax.sharding import PartitionSpec as P
 
 WINDOW = 1024
 HEADS = 16
 KEY_VALUE_HEADS = 8
 HEAD_SIZE = 128
-
+LANES = 128
 
 query_scale = 168.0 ** (-0.5)
 adapter_strength = 32.0
 norm_eps = 1e-06
+
+VMEM = pl.BlockSpec(memory_space=pltpu.VMEM)
+SMEM = pl.BlockSpec(memory_space=pltpu.SMEM)
+ANY = pl.BlockSpec(memory_space=pl.ANY)
+PARAMS = pltpu.CompilerParams(vmem_limit_bytes=32 * 1024 * 1024)
+bf16 = jnp.bfloat16
+f32 = jnp.float32
+
+
+def turn(value, axis, steps):
+    count = lax.axis_size(axis)
+    return lax.ppermute(value, axis, [(i, (i + steps) % count) for i in range(count)])
+
+
+class Sizes:
+    def __init__(self, x, queries, down, up, requests):
+        self.seq = lax.axis_size("seq")
+        self.groups = lax.axis_size("groups")
+        self.rows = x.shape[0]
+        self.rows_half = self.rows // 2
+        self.width = x.shape[1]
+        self.half = down.shape[1]
+        self.side = self.seq // 2
+        self.features = self.width // self.seq
+        self.slots_here, self.rank = down.shape[0], down.shape[2]
+        self.requests = requests
+        self.heads_here = up.shape[2] // HEAD_SIZE
+        self.group_size = HEADS // KEY_VALUE_HEADS
+        self.tokens = self.rows * self.seq
+        tiles = [
+            -(-((i * self.features) % LANES + self.features) // LANES) for i in range(self.side)
+        ]
+        self.tiles = max(tiles)
+        self.span = self.tiles * LANES
+
+    def fits(self):
+        return (
+            lax.axis_size("owner") == 2
+            and self.seq % 2 == 0
+            and self.half % LANES == 0
+            and self.half * 2 == self.width
+            and self.heads_here == self.seq
+            and self.slots_here == self.groups
+            and self.features % 32 == 0
+            and self.rows % 64 == 0
+            and 2 * self.rank == LANES
+        )
+
+    def start_in_half(self, i):
+        return jnp.minimum((i * self.features) // LANES, self.half // LANES - self.tiles) * LANES
+
+    def start(self, chip):
+        return (chip // self.side) * self.half + self.start_in_half(chip % self.side)
+
+
+def request_column(sz, lengths, position):
+    found = jnp.zeros_like(position)
+    end = jnp.int32(0)
+    for r in range(sz.requests):
+        end = end + lengths[r]
+        found = found + (position >= end).astype(jnp.int32)
+    return found
+
+
+def panels_kernel(sz, down, *outs_and_sem):
+    outs, sem = outs_and_sem[:-1], outs_and_sem[-1]
+    here, group = lax.axis_index("seq"), lax.axis_index("groups")
+    copies = []
+    for m, out in enumerate(outs):
+        first = pl.multiple_of(sz.start_in_half((here + m) % sz.side), LANES)
+        copies.append(
+            pltpu.make_async_copy(down.at[group, :, pl.ds(first, sz.span)], out, sem.at[m])
+        )
+    for copy in copies:
+        copy.start()
+    for copy in copies:
+        copy.wait()
+
+
+def norm_kernel(sz, x, gain, *outs_and_scratch):
+    outs, whole = outs_and_scratch[:-1], outs_and_scratch[-1]
+    here, core = lax.axis_index("seq"), lax.axis_index("owner")
+    rows = x[pl.ds(pl.multiple_of(core * sz.rows_half, sz.rows_half), sz.rows_half), :]
+    rows = rows.astype(f32)
+    rows = rows * lax.rsqrt(jnp.mean(rows * rows, axis=1, keepdims=True) + norm_eps)
+    whole[...] = (rows * gain[...]).astype(bf16)
+    lane = lax.broadcasted_iota(jnp.int32, (sz.rows_half, sz.span), 1)
+    for k, out in enumerate(outs):
+        chip = (here + k) % sz.seq
+        first = pl.multiple_of(sz.start(chip), LANES)
+        skip = chip * sz.features - first
+        piece = whole[:, pl.ds(first, sz.span)]
+        live = (lane >= skip) & (lane < skip + sz.features)
+        out[...] = jnp.where(live, piece.astype(f32), 0.0).astype(bf16)
+
+
+def heads_kernel(sz, queries, keys, up, *outs_and_sem):
+    outs, sem = outs_and_sem[:-1], outs_and_sem[-1]
+    here = lax.axis_index("seq")
+    copies = []
+    for k, out in enumerate(outs):
+        head = (here + k) % sz.seq
+        parts = []
+        for c in range(sz.group_size):
+            first = pl.multiple_of((head * sz.group_size + c) * HEAD_SIZE, HEAD_SIZE)
+            parts.append(queries.at[:, pl.ds(first, HEAD_SIZE)])
+        first = pl.multiple_of(head * HEAD_SIZE, HEAD_SIZE)
+        parts.append(keys.at[:, pl.ds(first, HEAD_SIZE)])
+        for j in range(sz.slots_here):
+            parts.append(up.at[j, :, pl.ds(first, HEAD_SIZE)])
+        at = 0
+        for part in parts:
+            size = part.shape[0]
+            copies.append(
+                pltpu.make_async_copy(part, out.at[pl.ds(at, size)], sem.at[len(copies)])
+            )
+            at += size
+    for copy in copies:
+        copy.start()
+    for copy in copies:
+        copy.wait()
+
+
+def softmax_kernel(sz, lengths, *refs):
+    pieces, out = refs[: sz.seq], refs[sz.seq]
+    query, key = refs[sz.seq + 1 :]
+    here = lax.axis_index("seq")
+    for k, piece in enumerate(pieces):
+        chip = (here + sz.seq - k) % sz.seq
+        place = pl.ds(pl.multiple_of(chip * sz.rows, sz.rows), sz.rows)
+        for c in range(sz.group_size):
+            query[c, place, :] = piece[c * sz.rows : (c + 1) * sz.rows]
+        key[place, :] = piece[sz.group_size * sz.rows : (sz.group_size + 1) * sz.rows]
+    shape = (sz.tokens, sz.tokens)
+    mine = lax.broadcasted_iota(jnp.int32, shape, 0)
+    theirs = lax.broadcasted_iota(jnp.int32, shape, 1)
+    live = (theirs <= mine) & (theirs > mine - WINDOW)
+    live = live & (request_column(sz, lengths, mine) == request_column(sz, lengths, theirs))
+    for c in range(sz.group_size):
+        scores = lax.dot_general(
+            query[c], key[...], (((1,), (1,)), ((), ())), preferred_element_type=f32
+        )
+        scores = jnp.where(live, scores * query_scale, -1e30)
+        weights = jnp.exp(scores - jnp.max(scores, axis=1, keepdims=True))
+        out[c] = (weights / jnp.sum(weights, axis=1, keepdims=True)).astype(bf16)
+
+
+def project_kernel(sz, lengths, adapters, ranks, slots, base, base_other, *refs):
+    pieces, refs = refs[: sz.seq], refs[sz.seq :]
+    count = 2 * sz.groups * sz.side
+    panels, refs = refs[:count], refs[count:]
+    outs, (rows, matrix, picked, product, base_sem, panel_sem) = refs[: sz.seq], refs[sz.seq :]
+    here, core, group = (lax.axis_index(a) for a in ("seq", "owner", "groups"))
+    depth = base.shape[0]
+    skip = here * sz.features - sz.start(here)
+    spare = sz.span - sz.features
+    matrix[0:spare] = jnp.zeros((spare, matrix.shape[1]), bf16)
+    matrix[sz.span - spare :] = jnp.zeros((spare, matrix.shape[1]), bf16)
+    copies = []
+    for j, (ref, owner) in enumerate(((base, core), (base_other, 1 - core))):
+        first = pl.multiple_of(skip + owner * depth, 16)
+        copies.append(
+            pltpu.make_async_copy(ref, matrix.at[pl.ds(first, depth)], base_sem.at[j])
+        )
+        copies[-1].start()
+    rank_of = []
+    for r in range(sz.requests):
+        adapter = adapters[r]
+        slot = slots[adapter]
+        rank_of.append(ranks[adapter])
+        chip = slot // sz.slots_here
+        other = jnp.where(chip // sz.side == core, 0, 1)
+        away = lax.rem(slot % sz.slots_here - group + sz.groups, sz.groups)
+        m = lax.rem(here % sz.side - chip % sz.side + sz.side, sz.side)
+        index = (other * sz.groups + away) * sz.side + m
+        for p, panel in enumerate(panels):
+
+            @pl.when(index == p)
+            def _(panel=panel, r=r):
+                pltpu.make_async_copy(
+                    panel, picked.at[pl.ds(r * sz.rank, sz.rank)], panel_sem.at[r]
+                ).start()
+
+    for k, piece in enumerate(pieces):
+        chip = (here + sz.seq - k) % sz.seq
+        rows[pl.ds(pl.multiple_of(chip * sz.rows_half, sz.rows_half), sz.rows_half), :] = piece[...]
+    for r in range(sz.requests):
+        pltpu.make_async_copy(
+            panels[0], picked.at[pl.ds(r * sz.rank, sz.rank)], panel_sem.at[r]
+        ).wait()
+    low = lax.dot_general(
+        rows[...], picked[...], (((1,), (1,)), ((), ())), preferred_element_type=f32
+    )
+    count = sz.seq * sz.rows_half
+    row = lax.broadcasted_iota(jnp.int32, (count, sz.rank), 0)
+    column = lax.broadcasted_iota(jnp.int32, (count, sz.rank), 1)
+    position = (row // sz.rows_half) * sz.rows + core * sz.rows_half + row % sz.rows_half
+    request = request_column(sz, lengths, position)
+    reduced = jnp.zeros((count, sz.rank), f32)
+    for r in range(sz.requests):
+        keep = (request == r) & (column < rank_of[r])
+        reduced = reduced + jnp.where(keep, low[:, r * sz.rank : (r + 1) * sz.rank], 0.0)
+    packed = jnp.concatenate([reduced[: count // 2], reduced[count // 2 :]], axis=1).astype(bf16)
+    for copy in copies:
+        copy.wait()
+    product[...] = jnp.dot(rows[...], matrix[...], preferred_element_type=f32).astype(bf16)
+    for k, out in enumerate(outs):
+        head = (here + k) % sz.seq
+        for j in range(2):
+            first = pl.multiple_of((j * sz.heads_here + head) * HEAD_SIZE, HEAD_SIZE)
+            out[j * count : (j + 1) * count] = product[:, pl.ds(first, HEAD_SIZE)]
+        out[2 * count :] = packed
+
+
+def add_kernel(sz, *refs):
+    pieces, (kept, sent) = refs[: sz.seq], refs[sz.seq :]
+    core = lax.axis_index("owner")
+    count = sz.seq * sz.rows_half
+    for out, head in ((kept, core), (sent, 1 - core)):
+        place = pl.ds(pl.multiple_of(head * count, count), count)
+        out[:count] = sum(piece[place, :].astype(f32) for piece in pieces).astype(bf16)
+    low = sum(piece[2 * count :].astype(f32) for piece in pieces).astype(bf16)
+    kept[count:] = low
+    sent[count:] = low
+
+
+def mix_kernel(sz, lengths, adapters, ranks, slots, kept, received, softmax, *refs):
+    pieces, refs = refs[: sz.seq], refs[sz.seq :]
+    outs, (base, low, wide, raise_all, raise_picked, mixed) = refs[: sz.seq], refs[sz.seq :]
+    here, core = lax.axis_index("seq"), lax.axis_index("owner")
+    count = sz.seq * sz.rows_half
+    for ref, owner in ((kept, core), (received, 1 - core)):
+        reduced = jnp.concatenate([ref[count:, : sz.rank], ref[count:, sz.rank :]], axis=0)
+        for chip in range(sz.seq):
+            place = pl.ds(
+                pl.multiple_of(chip * sz.rows + owner * sz.rows_half, sz.rows_half), sz.rows_half
+            )
+            own = slice(chip * sz.rows_half, (chip + 1) * sz.rows_half)
+            base[place, :] = ref[own]
+            low[place, :] = reduced[own]
+    panel_first = (sz.group_size + 1) * sz.rows
+    for k, piece in enumerate(pieces):
+        size = sz.slots_here * sz.rank
+        raise_all[k * size : (k + 1) * size] = piece[panel_first : panel_first + size]
+    position = lax.broadcasted_iota(jnp.int32, (sz.tokens, sz.rank), 0)
+    request = request_column(sz, lengths, position)
+    position = lax.broadcasted_iota(jnp.int32, (sz.tokens, HEAD_SIZE), 0)
+    request_wide = request_column(sz, lengths, position)
+    rank_here = jnp.ones((sz.tokens, HEAD_SIZE), jnp.int32)
+    reduced = low[...].astype(f32)
+    for r in range(sz.requests):
+        adapter = adapters[r]
+        slot = slots[adapter]
+        rank_here = jnp.where(request_wide == r, ranks[adapter], rank_here)
+        k = lax.rem(here - slot // sz.slots_here + sz.seq, sz.seq)
+        first = (k * sz.slots_here + slot % sz.slots_here) * sz.rank
+        own = slice(r * sz.rank, (r + 1) * sz.rank)
+        raise_picked[own] = raise_all[pl.ds(pl.multiple_of(first, sz.rank), sz.rank), :]
+        wide[:, own] = jnp.where(request == r, reduced, 0.0).astype(bf16)
+    scale = adapter_strength / rank_here.astype(f32)
+    raised = jnp.dot(wide[...], raise_picked[...], preferred_element_type=f32)
+    values = (base[...].astype(f32) + scale * raised).astype(bf16)
+    for c in range(sz.group_size):
+        mixed[:, c * HEAD_SIZE : (c + 1) * HEAD_SIZE] = jnp.dot(
+            softmax[c], values, preferred_element_type=f32
+        ).astype(bf16)
+    for k, out in enumerate(outs):
+        chip = (here + k) % sz.seq
+        out[...] = mixed[pl.ds(pl.multiple_of(chip * sz.rows, sz.rows), sz.rows), :]
+
+
+def place_kernel(sz, *refs):
+    pieces, out = refs[: sz.seq], refs[sz.seq]
+    here = lax.axis_index("seq")
+    wide = sz.group_size * HEAD_SIZE
+    for k, piece in enumerate(pieces):
+        head = (here + sz.seq - k) % sz.seq
+        out[:, pl.ds(pl.multiple_of(head * wide, wide), wide)] = piece[...]
+
+
+def by_heads(sz, x, queries, keys, gain, base, down, up, lengths, adapters, ranks, slots):
+    count = sz.seq * sz.rows_half
+    around = range(1, sz.seq)
+
+    panel = jax.ShapeDtypeStruct((sz.rank, sz.span), bf16)
+    sent = pl.pallas_call(
+        functools.partial(panels_kernel, sz),
+        out_shape=[panel] * sz.side,
+        in_specs=[ANY],
+        out_specs=[ANY] * sz.side,
+        scratch_shapes=[pltpu.SemaphoreType.DMA((sz.side,))],
+        compiler_params=PARAMS,
+        name="panels_out",
+    )(jnp.swapaxes(down, 1, 2))
+    own_line = []
+    for m in range(sz.side):
+        pairs = [
+            (h * 2 + c, (c * sz.side + (h + m) % sz.side) * 2 + h // sz.side)
+            for h in range(sz.seq)
+            for c in range(2)
+        ]
+        own_line.append(lax.ppermute(sent[m], ("seq", "owner"), pairs))
+
+    rows_out = pl.pallas_call(
+        functools.partial(norm_kernel, sz),
+        out_shape=[jax.ShapeDtypeStruct((sz.rows_half, sz.span), bf16)] * sz.seq,
+        in_specs=[VMEM, VMEM],
+        out_specs=[VMEM] * sz.seq,
+        scratch_shapes=[pltpu.VMEM((sz.rows_half, sz.width), bf16)],
+        compiler_params=PARAMS,
+        name="norm_rows",
+    )(x, gain)
+    rows_in = [rows_out[0]] + [turn(rows_out[k], "seq", k) for k in around]
+    base_other = turn(base, "owner", 1)
+
+    here_panels = list(own_line)
+    for k in range(1, sz.groups):
+        here_panels += [turn(p, "groups", sz.groups - k) for p in own_line]
+    all_panels = here_panels + [turn(p, "owner", 1) for p in here_panels]
+
+    heads_rows = (sz.group_size + 1) * sz.rows + sz.slots_here * sz.rank
+    parts = sz.group_size + 1 + sz.slots_here
+    heads_out = pl.pallas_call(
+        functools.partial(heads_kernel, sz),
+        out_shape=[jax.ShapeDtypeStruct((heads_rows, HEAD_SIZE), bf16)] * sz.seq,
+        in_specs=[ANY] * 3,
+        out_specs=[ANY] * sz.seq,
+        scratch_shapes=[pltpu.SemaphoreType.DMA((parts * sz.seq,))],
+        compiler_params=PARAMS,
+        name="heads_out",
+    )(queries, keys, up)
+    heads_in = [heads_out[0]] + [turn(heads_out[k], "seq", k) for k in around]
+
+    softmax = pl.pallas_call(
+        functools.partial(softmax_kernel, sz),
+        out_shape=jax.ShapeDtypeStruct((sz.group_size, sz.tokens, sz.tokens), bf16),
+        in_specs=[SMEM] + [VMEM] * sz.seq,
+        out_specs=VMEM,
+        scratch_shapes=[
+            pltpu.VMEM((sz.group_size, sz.tokens, HEAD_SIZE), bf16),
+            pltpu.VMEM((sz.tokens, HEAD_SIZE), bf16),
+        ],
+        compiler_params=PARAMS,
+        name="softmax_rows",
+    )(lengths, *heads_in)
+
+    partial_rows = 2 * count + count // 2
+    partial_out = pl.pallas_call(
+        functools.partial(project_kernel, sz),
+        out_shape=[jax.ShapeDtypeStruct((partial_rows, HEAD_SIZE), bf16)] * sz.seq,
+        in_specs=[SMEM] * 4 + [ANY] * 2 + [VMEM] * sz.seq + [ANY] * len(all_panels),
+        out_specs=[VMEM] * sz.seq,
+        scratch_shapes=[
+            pltpu.VMEM((count, sz.span), bf16),
+            pltpu.VMEM((sz.span, base.shape[1]), bf16),
+            pltpu.VMEM((sz.requests * sz.rank, sz.span), bf16),
+            pltpu.VMEM((count, base.shape[1]), bf16),
+            pltpu.SemaphoreType.DMA((2,)),
+            pltpu.SemaphoreType.DMA((sz.requests,)),
+        ],
+        compiler_params=PARAMS,
+        name="project",
+    )(lengths, adapters, ranks, slots, base, base_other, *rows_in, *all_panels)
+    partial_in = [partial_out[0]] + [turn(partial_out[k], "seq", k) for k in around]
+
+    half_shape = jax.ShapeDtypeStruct((count + count // 2, HEAD_SIZE), bf16)
+    kept, sent = pl.pallas_call(
+        functools.partial(add_kernel, sz),
+        out_shape=[half_shape] * 2,
+        in_specs=[VMEM] * sz.seq,
+        out_specs=[VMEM] * 2,
+        compiler_params=PARAMS,
+        name="add_partials",
+    )(*partial_in)
+    received = turn(sent, "owner", 1)
+
+    wide = sz.group_size * HEAD_SIZE
+    mixed = pl.pallas_call(
+        functools.partial(mix_kernel, sz),
+        out_shape=[jax.ShapeDtypeStruct((sz.rows, wide), bf16)] * sz.seq,
+        in_specs=[SMEM] * 4 + [VMEM] * (3 + sz.seq),
+        out_specs=[VMEM] * sz.seq,
+        scratch_shapes=[
+            pltpu.VMEM((sz.tokens, HEAD_SIZE), bf16),
+            pltpu.VMEM((sz.tokens, sz.rank), bf16),
+            pltpu.VMEM((sz.tokens, sz.requests * sz.rank), bf16),
+            pltpu.VMEM((sz.seq * sz.slots_here * sz.rank, HEAD_SIZE), bf16),
+            pltpu.VMEM((sz.requests * sz.rank, HEAD_SIZE), bf16),
+            pltpu.VMEM((sz.tokens, wide), bf16),
+        ],
+        compiler_params=PARAMS,
+        name="mix_values",
+    )(lengths, adapters, ranks, slots, kept, received, softmax, *heads_in)
+    mixed_in = [mixed[0]] + [turn(mixed[k], "seq", k) for k in around]
+    return pl.pallas_call(
+        functools.partial(place_kernel, sz),
+        out_shape=jax.ShapeDtypeStruct((sz.rows, sz.seq * wide), bf16),
+        in_specs=[VMEM] * sz.seq,
+        out_specs=VMEM,
+        compiler_params=PARAMS,
+        name="place_heads",
+    )(*mixed_in)
 
 
 def broadcast(x, axis, root):
@@ -25,7 +431,7 @@
     return lax.ppermute(value, axis, [(source, source + steps) for source in range(first, last)])
 
 
-def per_device(
+def by_tokens(
     layer_input_rows,
     encoded_query_rows,
     encoded_key_rows,
@@ -149,6 +555,51 @@
     return result[None]
 
 
+def per_device(
+    layer_input_rows,
+    encoded_query_rows,
+    encoded_key_rows,
+    layer_norm_gain,
+    base_value_matrix,
+    adapter_down_panels,
+    adapter_up_panels,
+    request_token_lengths,
+    adapter_per_request,
+    rank_per_adapter,
+    slot_per_adapter,
+):
+    sz = Sizes(
+        layer_input_rows[0],
+        encoded_query_rows[0],
+        adapter_down_panels[0],
+        adapter_up_panels[0],
+        request_token_lengths.shape[0],
+    )
+    scalars = (request_token_lengths, adapter_per_request, rank_per_adapter, slot_per_adapter)
+    if not sz.fits():
+        return by_tokens(
+            layer_input_rows,
+            encoded_query_rows,
+            encoded_key_rows,
+            layer_norm_gain,
+            base_value_matrix,
+            adapter_down_panels,
+            adapter_up_panels,
+            *scalars,
+        )
+    return by_heads(
+        sz,
+        layer_input_rows[0],
+        encoded_query_rows[0],
+        encoded_key_rows[0],
+        layer_norm_gain,
+        base_value_matrix[0],
+        adapter_down_panels[0],
+        adapter_up_panels[0],
+        *scalars,
+    )[None]
+
+
 def solution(mesh):
     in_specs = (
         P("segment", ("groups", "seq"), None),

time: 356 us -> 62.5 us (0.18)
  waiting for transfers between devices: 266 us -> 17.4 us
  loops' own time: 18.5 us -> 0 us
  starting transfers between devices: 13.7 us -> 31.8 us
  matrix products: 15.6 us -> 0 us
  between operations: 14.9 us -> 0.17 us
  other arithmetic: 10.8 us -> 0 us
  Pallas kernels: 0 us -> 7.27 us
  local copies, waits for them, and re-layouts: 11.6 us -> 5.58 us
    psum x4 -> x0, waiting for transfers between devices: 173 us -> none  [broadcast(): return lax.psum(jnp.where(mine, x, jnp.zeros_like(x)), axis)]
    all_gather x1 -> x0, waiting for transfers between devices: 90.6 us -> none  [per_device(): lax.all_gather(base_value_matrix[0], ('seq', 'owner'), axis=0, tiled=True)]
    another operation x1 -> x0, loops' own time: 18.5 us -> none  [per_device(): lax.scan(fetch_one, start_low, jnp.arange(requests, dtype=jnp.int32))]
    ppermute x6 -> x22, starting transfers between devices: 13.5 us -> 31.8 us  [the longest x20 28.4 us: turn(): lax.ppermute(value, axis, [(i, (i + steps) % count) for i in range(count)])]
    ppermute x6 -> x22, waiting for transfers between devices: 1.54 us -> 17.4 us  [the longest x20 17.4 us: turn(): lax.ppermute(value, axis, [(i, (i + steps) % count) for i in range(count)])]
    dot_general x14 -> x0, matrix products: 14.3 us -> none  [the longest x1 6.14 us: per_device(): jnp.dot(normalized_rows, lax.all_gather(base_value_matrix[0], ('seq', 'ow...]
    pallas_call x0 -> x8, Pallas kernels: none -> 7.27 us  [the longest x1 3.75 us: by_heads(): pl.pallas_call(functools.partial(project_kernel, sz), out_shape=[jax.Shap...]
    dynamic_slice x9 -> x0, local copies, waits for them, and re-layouts: 4.73 us -> none  [the longest x4 2.35 us: per_device(): lax.scan(fetch_one, start_low, jnp.arange(requests, dtype=jnp.int32))]
  transfers between devices with their start and end apart: 11 -> 22, of which waited for: 6 -> 11; matrix products, arithmetic and copies ran while one was open for 1% -> 0% of each run, Pallas kernels for 0% -> 3%
where the time goes in v1:
time: 62.5 us; the launch traced here: 62.2 us
  starting transfers between devices  31.8 us (51%)
  waiting for transfers between devices  17.4 us (28%)
  Pallas kernels  7.27 us (12%)
  local copies, waits for them, and re-layouts  5.58 us (9%)
    ppermute x20, starting transfers between devices, turn(): lax.ppermute(value, axis, [(i, (i + steps) % count) for i in range(count)])  28.4 us
    ppermute x20, waiting for transfers between devices, turn(): lax.ppermute(value, axis, [(i, (i + steps) % count) for i in range(count)])  17.4 us
    unnamed x30, local copies, waits for them, and re-layouts  5.58 us
    pallas_call x1, Pallas kernels, by_heads(): pl.pallas_call(functools.partial(project_kernel, sz), out_shape=[jax.Shap...  3.75 us
    ppermute x2, starting transfers between devices, by_heads(): own_line.append(lax.ppermute(sent[m], ('seq', 'owner'), pairs))  3.42 us
  transfers between devices with their start and end apart: 22, of which 11 were waited for; matrix products, arithmetic and copies ran while one was open for 0% of the time, Pallas kernels for 3%

profile of v1, /device:TPU:0, one launch (start us, length us, event | category | flops | bytes accessed | tf_op | source)
XLA Modules:
  0.0 62.2 jit_solution(2247417914414299215)
XLA Ops:
  0.0 0.5 collective-permute-start
  0.5 1.1 %copy-done.2 = bf16[1,2,2688,64]{2,3,1,0:T(8,128)(2,1)S(1)} copy-done((bf16[1,2,2688,64]{2,3,1,0:T(8,128)(2,1)S(1)}, bf16[1,2,2688,64]{2,3,1,0:T(8,128)(2,1)}, u32[]{:S(2)}) %copy-start.2) | copy-done | bytes 688152
  1.6 0.1 panels_out.1
  1.6 0.7 %collective-permute-start.4 = (bf16[64,1408]{1,0:T(8,128)(2,1)S(1)}, bf16[64,1408]{1,0:T(8,128)(2,1)S(1)}, u32[]{:S(2)}, u32[]{:S(2)}) collective-permute-start(bf16[64,1408]{1,0:T(8,128)(2,1)S(1)} %get-tuple-element.29), channel_id=1, source_target_pairs={{0,0},{1,8},{4,4},{5,12},{8,1},{9,9},{12,5},{13,13},{2,2},{3,10},{... | collective-permute-start | bytes 540680 | tf_op jit(solution)/shard_map/ppermute | solution.py:320
  2.3 2.7 %collective-permute-start.5 = (bf16[64,1408]{1,0:T(8,128)(2,1)S(1)}, bf16[64,1408]{1,0:T(8,128)(2,1)S(1)}, u32[]{:S(2)}, u32[]{:S(2)}) collective-permute-start(bf16[64,1408]{1,0:T(8,128)(2,1)S(1)} %get-tuple-element.30), channel_id=1, source_target_pairs={{0,4},{1,12},{4,0},{5,8},{8,5},{9,13},{12,1},{13,9},{2,6},{3,14},{... | collective-permute-start | bytes 540680 | tf_op jit(solution)/shard_map/ppermute | solution.py:320
  5.1 1.1 %copy-done.1 = bf16[1,64,5376]{2,1,0:T(8,128)(2,1)S(1)} copy-done((bf16[1,64,5376]{2,1,0:T(8,128)(2,1)S(1)}, bf16[1,64,5376]{2,1,0:T(8,128)(2,1)}, u32[]{:S(2)}) %copy-start.1) | copy-done | bytes 688152
  6.2 0.7 %copy-done.6 = f32[1,5376]{1,0:T(1,128)S(1)} copy-done((f32[1,5376]{1,0:T(1,128)S(1)}, f32[1,5376]{1,0:T(1,128)}, u32[]{:S(2)}) %copy-start.6) | copy-done | bytes 21528
  6.9 0.3 norm_rows.1
  7.2 0.1 collective-permute-start.1
  7.3 1.9 %collective-permute-start.6 = (bf16[64,1408]{1,0:T(8,128)(2,1)S(1)}, bf16[64,1408]{1,0:T(8,128)(2,1)S(1)}, u32[]{:S(2)}, u32[]{:S(2)}) collective-permute-start(bf16[64,1408]{1,0:T(8,128)(2,1)S(1)} %collective-permute-done.4.refs_4_), channel_id=1, source_target_pairs={{0,16},{16,0},{1,17},{17,1},{2,18},{18,2},{3,19},{19,3},{4,20},{20... | collective-permute-start | bytes 540680 | tf_op jit(solution)/shard_map/ppermute | solution.py:30
  9.2 1.3 %collective-permute-start.7 = (bf16[64,1408]{1,0:T(8,128)(2,1)S(1)}, bf16[64,1408]{1,0:T(8,128)(2,1)S(1)}, u32[]{:S(2)}, u32[]{:S(2)}) collective-permute-start(bf16[64,1408]{1,0:T(8,128)(2,1)S(1)} %collective-permute-done.5.refs_5_), channel_id=1, source_target_pairs={{0,16},{16,0},{1,17},{17,1},{2,18},{18,2},{3,19},{19,3},{4,20},{20... | collective-permute-start | bytes 540680 | tf_op jit(solution)/shard_map/ppermute | solution.py:30
  10.5 10.9 %collective-permute-start.2 = (bf16[32,1408]{1,0:T(8,128)(2,1)S(1)}, bf16[32,1408]{1,0:T(8,128)(2,1)S(1)}, u32[]{:S(2)}, u32[]{:S(2)}) collective-permute-start(bf16[32,1408]{1,0:T(8,128)(2,1)S(1)} %get-tuple-element.27), channel_id=1, source_target_pairs={{0,8},{4,12},{8,0},{12,4},{1,9},{5,13},{9,1},{13,5},{2,10},{6,14},... | collective-permute-start | bytes 270344 | tf_op jit(solution)/shard_map/ppermute | solution.py:30
  21.4 4.6 %collective-permute-done.2.refs_2_ = bf16[32,1408]{1,0:T(8,128)(2,1)S(1)} collective-permute-done((bf16[32,1408]{1,0:T(8,128)(2,1)S(1)}, bf16[32,1408]{1,0:T(8,128)(2,1)S(1)}, u32[]{:S(2)}, u32[]{:S(2)}) %collective-permute-start.2) | collective-permute-done | bytes 90144 | tf_op jit(solution)/shard_map/ppermute | solution.py:30
  26.0 0.0 collective-permute-start.8
  26.0 0.4 collective-permute-done.3.refs_3_
  26.5 0.1 collective-permute-start.9
  26.5 0.0 collective-permute-done.6.refs_6_
  26.5 0.4 collective-permute-start.10
  27.0 0.0 collective-permute-done.7.refs_7_
  27.0 0.1 collective-permute-start.11
  27.1 0.4 collective-permute-done.8.refs_8_
  27.4 0.4 collective-permute-done.9.refs_9_
  27.9 0.3 collective-permute-done.10.refs_10_
  28.1 0.3 collective-permute-done.11.refs_11_
  28.4 0.7 %copy-done.7 = s32[4]{0:T(128)S(1)} copy-done((s32[4]{0:T(128)S(1)}, s32[4]{0:T(128)}, u32[]{:S(2)}) %copy-start.7) | copy-done | bytes 40
  29.1 0.7 %copy-done.9 = s32[4]{0:T(128)S(1)} copy-done((s32[4]{0:T(128)S(1)}, s32[4]{0:T(128)}, u32[]{:S(2)}) %copy-start.9) | copy-done | bytes 40
  29.7 0.7 %copy-done.11 = s32[8]{0:T(128)S(1)} copy-done((s32[8]{0:T(128)S(1)}, s32[8]{0:T(128)}, u32[]{:S(2)}) %copy-start.11) | copy-done | bytes 56
  30.4 0.7 %copy-done.13 = s32[8]{0:T(128)S(1)} copy-done((s32[8]{0:T(128)S(1)}, s32[8]{0:T(128)}, u32[]{:S(2)}) %copy-start.13) | copy-done | bytes 56
  31.1 3.7 %project.1 = (bf16[320,128]{1,0:T(8,128)(2,1)S(1)}, bf16[320,128]{1,0:T(8,128)(2,1)S(1)}, bf16[320,128]{1,0:T(8,128)(2,1)S(1)}, bf16[320,128]{1,0:T(8,128)(2,1)S(1)}) custom-call(s32[4]{0:T(128)S(1)} %copy-done.7, s32[4]{0:T(128)S(1)} %copy-done.9, s32[8]{0:T(128)S(1)} %copy-done.11, s32[8]{0:T(128)S(1)} %copy-done.13, bf16[672,1024]{1,0:T(8,128)(2,1)S(1)} %bitcast.10, ...), custom_call_target="tpu_custom_call" | custom-call | tf_op jit(solution)/shard_map/project/pallas_call | solution.py:366
  34.8 1.3 %collective-permute-start.12 = (bf16[320,128]{1,0:T(8,128)(2,1)S(1)}, bf16[320,128]{1,0:T(8,128)(2,1)S(1)}, u32[]{:S(2)}, u32[]{:S(2)}) collective-permute-start(bf16[320,128]{1,0:T(8,128)(2,1)S(1)} %get-tuple-element.32), channel_id=1, source_target_pairs={{0,4},{4,8},{8,12},{12,0},{1,5},{5,9},{9,13},{13,1},{2,6},{6,10},{... | collective-permute-start | bytes 245768 | tf_op jit(solution)/shard_map/ppermute | solution.py:30
  36.2 2.5 %collective-permute-start.13 = (bf16[320,128]{1,0:T(8,128)(2,1)S(1)}, bf16[320,128]{1,0:T(8,128)(2,1)S(1)}, u32[]{:S(2)}, u32[]{:S(2)}) collective-permute-start(bf16[320,128]{1,0:T(8,128)(2,1)S(1)} %get-tuple-element.33), channel_id=1, source_target_pairs={{0,8},{4,12},{8,0},{12,4},{1,9},{5,13},{9,1},{13,5},{2,10},{6,14},... | collective-permute-start | bytes 245768 | tf_op jit(solution)/shard_map/ppermute | solution.py:30
  38.7 0.5 collective-permute-start.14
  39.1 0.3 heads_out.1
  39.5 1.6 %collective-permute-start.16 = (bf16[320,128]{1,0:T(8,128)(2,1)S(1)}, bf16[320,128]{1,0:T(8,128)(2,1)S(1)}, u32[]{:S(2)}, u32[]{:S(2)}) collective-permute-start(bf16[320,128]{1,0:T(8,128)(2,1)S(1)} %get-tuple-element.38), channel_id=1, source_target_pairs={{0,4},{4,8},{8,12},{12,0},{1,5},{5,9},{9,13},{13,1},{2,6},{6,10},{... | collective-permute-start | bytes 245768 | tf_op jit(solution)/shard_map/ppermute | solution.py:30
  41.1 0.5 collective-permute-start.17
  41.5 0.5 collective-permute-done.12.refs_1_
  42.1 2.0 %collective-permute-start.18 = (bf16[320,128]{1,0:T(8,128)(2,1)S(1)}, bf16[320,128]{1,0:T(8,128)(2,1)S(1)}, u32[]{:S(2)}, u32[]{:S(2)}) collective-permute-start(bf16[320,128]{1,0:T(8,128)(2,1)S(1)} %get-tuple-element.40), channel_id=1, source_target_pairs={{0,12},{4,0},{8,4},{12,8},{1,13},{5,1},{9,5},{13,9},{2,14},{6,2},{... | collective-permute-start | bytes 245768 | tf_op jit(solution)/shard_map/ppermute | solution.py:30
  44.1 3.8 %collective-permute-done.13.refs_2_ = bf16[320,128]{1,0:T(8,128)(2,1)S(1)} collective-permute-done((bf16[320,128]{1,0:T(8,128)(2,1)S(1)}, bf16[320,128]{1,0:T(8,128)(2,1)S(1)}, u32[]{:S(2)}, u32[]{:S(2)}) %collective-permute-start.13) | collective-permute-done | bytes 81952 | tf_op jit(solution)/shard_map/ppermute | solution.py:30
  47.9 0.1 collective-permute-start.15
  48.0 4.0 %collective-permute-done.17.refs_2_ = bf16[320,128]{1,0:T(8,128)(2,1)S(1)} collective-permute-done((bf16[320,128]{1,0:T(8,128)(2,1)S(1)}, bf16[320,128]{1,0:T(8,128)(2,1)S(1)}, u32[]{:S(2)}, u32[]{:S(2)}) %collective-permute-start.17) | collective-permute-done | bytes 81952 | tf_op jit(solution)/shard_map/ppermute | solution.py:30
  52.0 1.0 %softmax_rows.1.softmax = bf16[2,256,256]{2,1,0:T(8,128)(2,1)S(1)} custom-call(s32[4]{0:T(128)S(1)} %copy-done.8, bf16[320,128]{1,0:T(8,128)(2,1)S(1)} %get-tuple-element.37.refs_0_, bf16[320,128]{1,0:T(8,128)(2,1)S(1)} %collective-permute-done.16.refs_1_, bf16[320,128]{1,0:T(8,128)(2,1)S(1)} %collective-permute-done.17.refs_2_, ...), custom_call_target="tpu_custom_call" | custom-call | tf_op jit(solution)/shard_map/softmax_rows/pallas_call | solution.py:352
  53.0 1.1 %mix_values.1 = (bf16[64,256]{1,0:T(8,128)(2,1)S(1)}, bf16[64,256]{1,0:T(8,128)(2,1)S(1)}, bf16[64,256]{1,0:T(8,128)(2,1)S(1)}, bf16[64,256]{1,0:T(8,128)(2,1)S(1)}) custom-call(s32[4]{0:T(128)S(1)} %copy-done.8, s32[4]{0:T(128)S(1)} %copy-done.10, s32[8]{0:T(128)S(1)} %copy-done.12, s32[8]{0:T(128)S(1)} %copy-done.14, ...), custom_call_target="tpu_custom_call" | custom-call | tf_op jit(solution)/shard_map/mix_values/pallas_call | solution.py:396
  54.1 2.3 %collective-permute-start.19 = (bf16[64,256]{1,0:T(8,128)(2,1)S(1)}, bf16[64,256]{1,0:T(8,128)(2,1)S(1)}, u32[]{:S(2)}, u32[]{:S(2)}) collective-permute-start(bf16[64,256]{1,0:T(8,128)(2,1)S(1)} %get-tuple-element.42), channel_id=1, source_target_pairs={{0,4},{4,8},{8,12},{12,0},{1,5},{5,9},{9,13},{13,1},{2,6},{6,10},{... | collective-permute-start | bytes 98312 | tf_op jit(solution)/shard_map/ppermute | solution.py:30
  56.4 0.9 %collective-permute-start.20 = (bf16[64,256]{1,0:T(8,128)(2,1)S(1)}, bf16[64,256]{1,0:T(8,128)(2,1)S(1)}, u32[]{:S(2)}, u32[]{:S(2)}) collective-permute-start(bf16[64,256]{1,0:T(8,128)(2,1)S(1)} %get-tuple-element.43), channel_id=1, source_target_pairs={{0,8},{4,12},{8,0},{12,4},{1,9},{5,13},{9,1},{13,5},{2,10},{6,14},... | collective-permute-start | bytes 98312 | tf_op jit(solution)/shard_map/ppermute | solution.py:30
  57.3 1.6 %collective-permute-start.21 = (bf16[64,256]{1,0:T(8,128)(2,1)S(1)}, bf16[64,256]{1,0:T(8,128)(2,1)S(1)}, u32[]{:S(2)}, u32[]{:S(2)}) collective-permute-start(bf16[64,256]{1,0:T(8,128)(2,1)S(1)} %get-tuple-element.44), channel_id=1, source_target_pairs={{0,12},{4,0},{8,4},{12,8},{1,13},{5,1},{9,5},{13,9},{2,14},{6,2},{... | collective-permute-start | bytes 98312 | tf_op jit(solution)/shard_map/ppermute | solution.py:30
  58.9 1.3 %collective-permute-done.19.refs_1_ = bf16[64,256]{1,0:T(8,128)(2,1)S(1)} collective-permute-done((bf16[64,256]{1,0:T(8,128)(2,1)S(1)}, bf16[64,256]{1,0:T(8,128)(2,1)S(1)}, u32[]{:S(2)}, u32[]{:S(2)}) %collective-permute-start.19) | collective-permute-done | bytes 32800 | tf_op jit(solution)/shard_map/ppermute | solution.py:30
  60.2 1.4 %collective-permute-done.20.refs_2_ = bf16[64,256]{1,0:T(8,128)(2,1)S(1)} collective-permute-done((bf16[64,256]{1,0:T(8,128)(2,1)S(1)}, bf16[64,256]{1,0:T(8,128)(2,1)S(1)}, u32[]{:S(2)}, u32[]{:S(2)}) %collective-permute-start.20) | collective-permute-done | bytes 32800 | tf_op jit(solution)/shard_map/ppermute | solution.py:30
  61.5 0.7 %place_heads.1 = bf16[64,1024]{1,0:T(8,128)(2,1)} custom-call(bf16[64,256]{1,0:T(8,128)(2,1)S(1)} %get-tuple-element.41.refs_0_, bf16[64,256]{1,0:T(8,128)(2,1)S(1)} %collective-permute-done.19.refs_1_, bf16[64,256]{1,0:T(8,128)(2,1)S(1)} %collective-permute-done.20.refs_2_, bf16[64,256]{1,0:T(8,128)(2,1)S(1)} %collective-permute-done.21.refs_3_), custom_call_target="tpu_custom_call" | custom-call | tf_op jit(solution)/shard_map/place_heads/pallas_call | solution.py:413
  (34 shorter events, 0.1 us)
Async XLA Ops:
  0.0 28.4 %copy-start = (bf16[1,672,1024]{2,1,0:T(8,128)(2,1)S(1)}, bf16[1,672,1024]{2,1,0:T(8,128)(2,1)}, u32[]{:S(2)}) copy-start(bf16[1,672,1024]{2,1,0:T(8,128)(2,1)} %param.15) | copy-start | bytes 4128772
  0.0 28.4 %collective-permute-start = (bf16[672,1024]{1,0:T(8,128)(2,1)}, bf16[672,1024]{1,0:T(8,128)(2,1)S(1)}, u32[]{:S(2)}, u32[]{:S(2)}) collective-permute-start(bf16[672,1024]{1,0:T(8,128)(2,1)} %bitcast.9), channel_id=1, source_target_pairs={{0,1},{1,0},{2,3},{3,2},{4,5},{5,4},{6,7},{7,6},{8,9},{9,8},{10,11... | collective-permute-start | bytes 4128776 | tf_op jit(solution)/shard_map/ppermute | solution.py:30
  0.5 1.1 %copy-start.2 = (bf16[1,2,2688,64]{2,3,1,0:T(8,128)(2,1)S(1)}, bf16[1,2,2688,64]{2,3,1,0:T(8,128)(2,1)}, u32[]{:S(2)}) copy-start(bf16[1,2,2688,64]{2,3,1,0:T(8,128)(2,1)} %param.16) | copy-start | bytes 2064388
  1.6 5.6 %collective-permute-start.4 = (bf16[64,1408]{1,0:T(8,128)(2,1)S(1)}, bf16[64,1408]{1,0:T(8,128)(2,1)S(1)}, u32[]{:S(2)}, u32[]{:S(2)}) collective-permute-start(bf16[64,1408]{1,0:T(8,128)(2,1)S(1)} %get-tuple-element.29), channel_id=1, source_target_pairs={{0,0},{1,8},{4,4},{5,12},{8,1},{9,9},{12,5},{13,13},{2,2},{3,10},{... | collective-permute-start | bytes 540680 | tf_op jit(solution)/shard_map/ppermute | solution.py:320
  2.3 6.9 %collective-permute-start.5 = (bf16[64,1408]{1,0:T(8,128)(2,1)S(1)}, bf16[64,1408]{1,0:T(8,128)(2,1)S(1)}, u32[]{:S(2)}, u32[]{:S(2)}) collective-permute-start(bf16[64,1408]{1,0:T(8,128)(2,1)S(1)} %get-tuple-element.30), channel_id=1, source_target_pairs={{0,4},{1,12},{4,0},{5,8},{8,5},{9,13},{12,1},{13,9},{2,6},{3,14},{... | collective-permute-start | bytes 540680 | tf_op jit(solution)/shard_map/ppermute | solution.py:320
  5.1 1.1 %copy-start.1 = (bf16[1,64,5376]{2,1,0:T(8,128)(2,1)S(1)}, bf16[1,64,5376]{2,1,0:T(8,128)(2,1)}, u32[]{:S(2)}) copy-start(bf16[1,64,5376]{2,1,0:T(8,128)(2,1)} %param.11) | copy-start | bytes 2064388
  6.2 0.7 %copy-start.6 = (f32[1,5376]{1,0:T(1,128)S(1)}, f32[1,5376]{1,0:T(1,128)}, u32[]{:S(2)}) copy-start(f32[1,5376]{1,0:T(1,128)} %gain.1) | copy-start | bytes 64516
  7.2 14.2 %collective-permute-start.1 = (bf16[32,1408]{1,0:T(8,128)(2,1)S(1)}, bf16[32,1408]{1,0:T(8,128)(2,1)S(1)}, u32[]{:S(2)}, u32[]{:S(2)}) collective-permute-start(bf16[32,1408]{1,0:T(8,128)(2,1)S(1)} %get-tuple-element.26), channel_id=1, source_target_pairs={{0,4},{4,8},{8,12},{12,0},{1,5},{5,9},{9,13},{13,1},{2,6},{6,10},{... | collective-permute-start | bytes 270344 | tf_op jit(solution)/shard_map/ppermute | solution.py:30
  7.3 19.3 %collective-permute-start.6 = (bf16[64,1408]{1,0:T(8,128)(2,1)S(1)}, bf16[64,1408]{1,0:T(8,128)(2,1)S(1)}, u32[]{:S(2)}, u32[]{:S(2)}) collective-permute-start(bf16[64,1408]{1,0:T(8,128)(2,1)S(1)} %collective-permute-done.4.refs_4_), channel_id=1, source_target_pairs={{0,16},{16,0},{1,17},{17,1},{2,18},{18,2},{3,19},{19,3},{4,20},{20... | collective-permute-start | bytes 540680 | tf_op jit(solution)/shard_map/ppermute | solution.py:30
  9.2 17.8 %collective-permute-start.7 = (bf16[64,1408]{1,0:T(8,128)(2,1)S(1)}, bf16[64,1408]{1,0:T(8,128)(2,1)S(1)}, u32[]{:S(2)}, u32[]{:S(2)}) collective-permute-start(bf16[64,1408]{1,0:T(8,128)(2,1)S(1)} %collective-permute-done.5.refs_5_), channel_id=1, source_target_pairs={{0,16},{16,0},{1,17},{17,1},{2,18},{18,2},{3,19},{19,3},{4,20},{20... | collective-permute-start | bytes 540680 | tf_op jit(solution)/shard_map/ppermute | solution.py:30
  10.5 15.5 %collective-permute-start.2 = (bf16[32,1408]{1,0:T(8,128)(2,1)S(1)}, bf16[32,1408]{1,0:T(8,128)(2,1)S(1)}, u32[]{:S(2)}, u32[]{:S(2)}) collective-permute-start(bf16[32,1408]{1,0:T(8,128)(2,1)S(1)} %get-tuple-element.27), channel_id=1, source_target_pairs={{0,8},{4,12},{8,0},{12,4},{1,9},{5,13},{9,1},{13,5},{2,10},{6,14},... | collective-permute-start | bytes 270344 | tf_op jit(solution)/shard_map/ppermute | solution.py:30
  21.4 5.1 %collective-permute-start.3 = (bf16[32,1408]{1,0:T(8,128)(2,1)S(1)}, bf16[32,1408]{1,0:T(8,128)(2,1)S(1)}, u32[]{:S(2)}, u32[]{:S(2)}) collective-permute-start(bf16[32,1408]{1,0:T(8,128)(2,1)S(1)} %get-tuple-element.28), channel_id=1, source_target_pairs={{0,12},{4,0},{8,4},{12,8},{1,13},{5,1},{9,5},{13,9},{2,14},{6,2},{... | collective-permute-start | bytes 270344 | tf_op jit(solution)/shard_map/ppermute | solution.py:30
  26.0 1.4 %collective-permute-start.8 = (bf16[64,1408]{1,0:T(8,128)(2,1)S(1)}, bf16[64,1408]{1,0:T(8,128)(2,1)S(1)}, u32[]{:S(2)}, u32[]{:S(2)}) collective-permute-start(bf16[64,1408]{1,0:T(8,128)(2,1)S(1)} %collective-permute-done.4.refs_4_), channel_id=1, source_target_pairs={{0,1},{1,0},{2,3},{3,2},{4,5},{5,4},{6,7},{7,6},{8,9},{9,8},{10,11... | collective-permute-start | bytes 540680 | tf_op jit(solution)/shard_map/ppermute | solution.py:30
  26.5 1.4 %collective-permute-start.9 = (bf16[64,1408]{1,0:T(8,128)(2,1)S(1)}, bf16[64,1408]{1,0:T(8,128)(2,1)S(1)}, u32[]{:S(2)}, u32[]{:S(2)}) collective-permute-start(bf16[64,1408]{1,0:T(8,128)(2,1)S(1)} %collective-permute-done.5.refs_5_), channel_id=1, source_target_pairs={{0,1},{1,0},{2,3},{3,2},{4,5},{5,4},{6,7},{7,6},{8,9},{9,8},{10,11... | collective-permute-start | bytes 540680 | tf_op jit(solution)/shard_map/ppermute | solution.py:30
  26.5 1.6 %collective-permute-start.10 = (bf16[64,1408]{1,0:T(8,128)(2,1)S(1)}, bf16[64,1408]{1,0:T(8,128)(2,1)S(1)}, u32[]{:S(2)}, u32[]{:S(2)}) collective-permute-start(bf16[64,1408]{1,0:T(8,128)(2,1)S(1)} %collective-permute-done.6.refs_6_), channel_id=1, source_target_pairs={{0,1},{1,0},{2,3},{3,2},{4,5},{5,4},{6,7},{7,6},{8,9},{9,8},{10,11... | collective-permute-start | bytes 540680 | tf_op jit(solution)/shard_map/ppermute | solution.py:30
  27.0 1.4 %collective-permute-start.11 = (bf16[64,1408]{1,0:T(8,128)(2,1)S(1)}, bf16[64,1408]{1,0:T(8,128)(2,1)S(1)}, u32[]{:S(2)}, u32[]{:S(2)}) collective-permute-start(bf16[64,1408]{1,0:T(8,128)(2,1)S(1)} %collective-permute-done.7.refs_7_), channel_id=1, source_target_pairs={{0,1},{1,0},{2,3},{3,2},{4,5},{5,4},{6,7},{7,6},{8,9},{9,8},{10,11... | collective-permute-start | bytes 540680 | tf_op jit(solution)/shard_map/ppermute | solution.py:30
  28.4 0.7 %copy-start.7 = (s32[4]{0:T(128)S(1)}, s32[4]{0:T(128)}, u32[]{:S(2)}) copy-start(s32[4]{0:T(128)} %lengths.5) | copy-start | bytes 52
  29.1 0.7 %copy-start.9 = (s32[4]{0:T(128)S(1)}, s32[4]{0:T(128)}, u32[]{:S(2)}) copy-start(s32[4]{0:T(128)} %adapters.3) | copy-start | bytes 52
  29.7 0.7 %copy-start.11 = (s32[8]{0:T(128)S(1)}, s32[8]{0:T(128)}, u32[]{:S(2)}) copy-start(s32[8]{0:T(128)} %ranks.3) | copy-start | bytes 100
  30.4 0.7 %copy-start.13 = (s32[8]{0:T(128)S(1)}, s32[8]{0:T(128)}, u32[]{:S(2)}) copy-start(s32[8]{0:T(128)} %slots.3) | copy-start | bytes 100
  31.0 8.1 %copy-start.3 = (bf16[1,64,1024]{2,1,0:T(8,128)(2,1)S(1)}, bf16[1,64,1024]{2,1,0:T(8,128)(2,1)}, u32[]{:S(2)}) copy-start(bf16[1,64,1024]{2,1,0:T(8,128)(2,1)} %param.12) | copy-start | bytes 393220
  31.0 8.1 %copy-start.4 = (bf16[1,2,64,512]{3,2,1,0:T(8,128)(2,1)S(1)}, bf16[1,2,64,512]{3,2,1,0:T(8,128)(2,1)}, u32[]{:S(2)}) copy-start(bf16[1,2,64,512]{3,2,1,0:T(8,128)(2,1)} %param.17) | copy-start | bytes 393220
  31.0 8.1 %copy-start.5 = (bf16[1,64,512]{2,1,0:T(8,128)(2,1)S(1)}, bf16[1,64,512]{2,1,0:T(8,128)(2,1)}, u32[]{:S(2)}) copy-start(bf16[1,64,512]{2,1,0:T(8,128)(2,1)} %param.13) | copy-start | bytes 196612
  31.0 20.9 %copy-start.8 = (s32[4]{0:T(128)S(1)}, s32[4]{0:T(128)}, u32[]{:S(2)}) copy-start(s32[4]{0:T(128)} %lengths.5) | copy-start | bytes 52
  31.0 21.9 %copy-start.10 = (s32[4]{0:T(128)S(1)}, s32[4]{0:T(128)}, u32[]{:S(2)}) copy-start(s32[4]{0:T(128)} %adapters.3) | copy-start | bytes 52
  31.1 21.9 %copy-start.12 = (s32[8]{0:T(128)S(1)}, s32[8]{0:T(128)}, u32[]{:S(2)}) copy-start(s32[8]{0:T(128)} %ranks.3) | copy-start | bytes 100
  31.1 21.9 %copy-start.14 = (s32[8]{0:T(128)S(1)}, s32[8]{0:T(128)}, u32[]{:S(2)}) copy-start(s32[8]{0:T(128)} %slots.3) | copy-start | bytes 100
  34.8 7.2 %collective-permute-start.12 = (bf16[320,128]{1,0:T(8,128)(2,1)S(1)}, bf16[320,128]{1,0:T(8,128)(2,1)S(1)}, u32[]{:S(2)}, u32[]{:S(2)}) collective-permute-start(bf16[320,128]{1,0:T(8,128)(2,1)S(1)} %get-tuple-element.32), channel_id=1, source_target_pairs={{0,4},{4,8},{8,12},{12,0},{1,5},{5,9},{9,13},{13,1},{2,6},{6,10},{... | collective-permute-start | bytes 245768 | tf_op jit(solution)/shard_map/ppermute | solution.py:30
  36.2 11.7 %collective-permute-start.13 = (bf16[320,128]{1,0:T(8,128)(2,1)S(1)}, bf16[320,128]{1,0:T(8,128)(2,1)S(1)}, u32[]{:S(2)}, u32[]{:S(2)}) collective-permute-start(bf16[320,128]{1,0:T(8,128)(2,1)S(1)} %get-tuple-element.33), channel_id=1, source_target_pairs={{0,8},{4,12},{8,0},{12,4},{1,9},{5,13},{9,1},{13,5},{2,10},{6,14},... | collective-permute-start | bytes 245768 | tf_op jit(solution)/shard_map/ppermute | solution.py:30
  38.7 9.2 %collective-permute-start.14 = (bf16[320,128]{1,0:T(8,128)(2,1)S(1)}, bf16[320,128]{1,0:T(8,128)(2,1)S(1)}, u32[]{:S(2)}, u32[]{:S(2)}) collective-permute-start(bf16[320,128]{1,0:T(8,128)(2,1)S(1)} %get-tuple-element.34), channel_id=1, source_target_pairs={{0,12},{4,0},{8,4},{12,8},{1,13},{5,1},{9,5},{13,9},{2,14},{6,2},{... | collective-permute-start | bytes 245768 | tf_op jit(solution)/shard_map/ppermute | solution.py:30
  39.5 8.5 %collective-permute-start.16 = (bf16[320,128]{1,0:T(8,128)(2,1)S(1)}, bf16[320,128]{1,0:T(8,128)(2,1)S(1)}, u32[]{:S(2)}, u32[]{:S(2)}) collective-permute-start(bf16[320,128]{1,0:T(8,128)(2,1)S(1)} %get-tuple-element.38), channel_id=1, source_target_pairs={{0,4},{4,8},{8,12},{12,0},{1,5},{5,9},{9,13},{13,1},{2,6},{6,10},{... | collective-permute-start | bytes 245768 | tf_op jit(solution)/shard_map/ppermute | solution.py:30
  41.1 10.9 %collective-permute-start.17 = (bf16[320,128]{1,0:T(8,128)(2,1)S(1)}, bf16[320,128]{1,0:T(8,128)(2,1)S(1)}, u32[]{:S(2)}, u32[]{:S(2)}) collective-permute-start(bf16[320,128]{1,0:T(8,128)(2,1)S(1)} %get-tuple-element.39), channel_id=1, source_target_pairs={{0,8},{4,12},{8,0},{12,4},{1,9},{5,13},{9,1},{13,5},{2,10},{6,14},... | collective-permute-start | bytes 245768 | tf_op jit(solution)/shard_map/ppermute | solution.py:30
  42.1 9.9 %collective-permute-start.18 = (bf16[320,128]{1,0:T(8,128)(2,1)S(1)}, bf16[320,128]{1,0:T(8,128)(2,1)S(1)}, u32[]{:S(2)}, u32[]{:S(2)}) collective-permute-start(bf16[320,128]{1,0:T(8,128)(2,1)S(1)} %get-tuple-element.40), channel_id=1, source_target_pairs={{0,12},{4,0},{8,4},{12,8},{1,13},{5,1},{9,5},{13,9},{2,14},{6,2},{... | collective-permute-start | bytes 245768 | tf_op jit(solution)/shard_map/ppermute | solution.py:30
  47.9 5.0 %collective-permute-start.15 = (bf16[192,128]{1,0:T(8,128)(2,1)S(1)}, bf16[192,128]{1,0:T(8,128)(2,1)S(1)}, u32[]{:S(2)}, u32[]{:S(2)}) collective-permute-start(bf16[192,128]{1,0:T(8,128)(2,1)S(1)} %get-tuple-element.36), channel_id=1, source_target_pairs={{0,1},{1,0},{2,3},{3,2},{4,5},{5,4},{6,7},{7,6},{8,9},{9,8},{10,11... | collective-permute-start | bytes 147464 | tf_op jit(solution)/shard_map/ppermute | solution.py:30
  54.1 6.1 %collective-permute-start.19 = (bf16[64,256]{1,0:T(8,128)(2,1)S(1)}, bf16[64,256]{1,0:T(8,128)(2,1)S(1)}, u32[]{:S(2)}, u32[]{:S(2)}) collective-permute-start(bf16[64,256]{1,0:T(8,128)(2,1)S(1)} %get-tuple-element.42), channel_id=1, source_target_pairs={{0,4},{4,8},{8,12},{12,0},{1,5},{5,9},{9,13},{13,1},{2,6},{6,10},{... | collective-permute-start | bytes 98312 | tf_op jit(solution)/shard_map/ppermute | solution.py:30
  56.4 5.1 %collective-permute-start.20 = (bf16[64,256]{1,0:T(8,128)(2,1)S(1)}, bf16[64,256]{1,0:T(8,128)(2,1)S(1)}, u32[]{:S(2)}, u32[]{:S(2)}) collective-permute-start(bf16[64,256]{1,0:T(8,128)(2,1)S(1)} %get-tuple-element.43), channel_id=1, source_target_pairs={{0,8},{4,12},{8,0},{12,4},{1,9},{5,13},{9,1},{13,5},{2,10},{6,14},... | collective-permute-start | bytes 98312 | tf_op jit(solution)/shard_map/ppermute | solution.py:30
  57.3 4.3 %collective-permute-start.21 = (bf16[64,256]{1,0:T(8,128)(2,1)S(1)}, bf16[64,256]{1,0:T(8,128)(2,1)S(1)}, u32[]{:S(2)}, u32[]{:S(2)}) collective-permute-start(bf16[64,256]{1,0:T(8,128)(2,1)S(1)} %get-tuple-element.44), channel_id=1, source_target_pairs={{0,12},{4,0},{8,4},{12,8},{1,13},{5,1},{9,5},{13,9},{2,14},{6,2},{... | collective-permute-start | bytes 98312 | tf_op jit(solution)/shard_map/ppermute | solution.py:30

commit v2 on v0

--- a/solution.py
+++ b/solution.py
@@ -1,17 +1,426 @@
+import functools
+
 import jax
 import jax.numpy as jnp
 from jax import lax
+from jax.experimental import pallas as pl
+from jax.experimental.pallas import tpu as pltpu
 from jax.sharding import PartitionSpec as P
 
 WINDOW = 1024
 HEADS = 16
 KEY_VALUE_HEADS = 8
 HEAD_SIZE = 128
-
+LANES = 128
 
 query_scale = 168.0 ** (-0.5)
 adapter_strength = 32.0
 norm_eps = 1e-06
+
+VMEM = pl.BlockSpec(memory_space=pltpu.VMEM)
+SMEM = pl.BlockSpec(memory_space=pltpu.SMEM)
+ANY = pl.BlockSpec(memory_space=pl.ANY)
+HBM = pl.BlockSpec(memory_space=pltpu.HBM)
+PARAMS = pltpu.CompilerParams(vmem_limit_bytes=16 * 1024 * 1024)
+FIRST = pltpu.CompilerParams(vmem_limit_bytes=60 * 1024 * 1024)
+bf16 = jnp.bfloat16
+f32 = jnp.float32
+
+
+def swap(value, axis, mask):
+    return lax.ppermute(value, axis, [(i, i ^ mask) for i in range(lax.axis_size(axis))])
+
+
+class Sizes:
+    def __init__(self, x, queries, down, up, requests):
+        self.seq = lax.axis_size("seq")
+        self.groups = lax.axis_size("groups")
+        self.rows = x.shape[0]
+        self.rows_half = self.rows // 2
+        self.width = x.shape[1]
+        self.half = down.shape[1]
+        self.side = self.seq // 2
+        self.features = self.width // self.seq
+        self.slots_here, self.rank = down.shape[0], down.shape[2]
+        self.requests = requests
+        self.heads_here = up.shape[2] // HEAD_SIZE
+        self.group_size = HEADS // KEY_VALUE_HEADS
+        self.tokens = self.rows * self.seq
+        tiles = [
+            -(-((i * self.features) % LANES + self.features) // LANES) for i in range(self.side)
+        ]
+        self.tiles = max(tiles)
+        self.span = self.tiles * LANES
+
+    def fits(self):
+        return (
+            lax.axis_size("owner") == 2
+            and self.seq & (self.seq - 1) == 0
+            and self.groups & (self.groups - 1) == 0
+            and self.half % LANES == 0
+            and self.half * 2 == self.width
+            and self.heads_here == self.seq
+            and self.slots_here == self.groups
+            and self.features % 32 == 0
+            and self.rows % 64 == 0
+            and self.rank % self.rows_half == 0
+            and self.pieces() * LANES <= self.span
+            and 2 * self.rank == LANES
+        )
+
+    def pieces(self):
+        return ((self.group_size + 1) * self.rows + self.slots_here * self.rank) // self.rows_half
+
+    def start_in_half(self, i):
+        return jnp.minimum((i * self.features) // LANES, self.half // LANES - self.tiles) * LANES
+
+    def start(self, chip):
+        return (chip // self.side) * self.half + self.start_in_half(chip % self.side)
+
+
+def request_column(sz, table, position):
+    found = jnp.zeros_like(position)
+    for r in range(sz.requests):
+        found = found + (position >= table[0, r]).astype(jnp.int32)
+    return found
+
+
+def table_kernel(sz, lengths, adapters, ranks, slots, out):
+    here, core, group = (lax.axis_index(a) for a in ("seq", "owner", "groups"))
+    end = jnp.int32(0)
+    for r in range(sz.requests):
+        end = end + lengths[r]
+        adapter = adapters[r]
+        slot = slots[adapter]
+        chip, local = slot // sz.slots_here, slot % sz.slots_here
+        other = jnp.where(chip // sz.side == core, 0, 1)
+        m = (here % sz.side) ^ (chip % sz.side)
+        out[0, r] = end
+        out[1, r] = ranks[adapter]
+        out[2, r] = (other * sz.groups + (local ^ group)) * sz.side + m
+        out[3, r] = ((here ^ chip) * sz.slots_here + local) * sz.rank
+
+
+def panels_kernel(sz, down, *outs_and_sem):
+    outs, sem = outs_and_sem[:-1], outs_and_sem[-1]
+    here, group = lax.axis_index("seq"), lax.axis_index("groups")
+    copies = []
+    for m, out in enumerate(outs):
+        first = pl.multiple_of(sz.start_in_half((here % sz.side) ^ m), LANES)
+        copies.append(
+            pltpu.make_async_copy(down.at[group, :, pl.ds(first, sz.span)], out, sem.at[m])
+        )
+    for copy in copies:
+        copy.start()
+    for copy in copies:
+        copy.wait()
+
+
+def norm_kernel(sz, x, gain, queries, keys, up, *outs_and_scratch):
+    outs, scratch = outs_and_scratch[: sz.seq], outs_and_scratch[sz.seq :]
+    taken, gains, query, key, raised, whole, sem = scratch
+    here, core = lax.axis_index("seq"), lax.axis_index("owner")
+    place = pl.ds(pl.multiple_of(core * sz.rows_half, sz.rows_half), sz.rows_half)
+    pairs = ((x.at[place], taken), (gain, gains), (queries, query), (keys, key), (up, raised))
+    copies = [pltpu.make_async_copy(a, b, sem.at[i]) for i, (a, b) in enumerate(pairs)]
+    for copy in copies:
+        copy.start()
+    for copy in copies[:2]:
+        copy.wait()
+    rows = taken[...].astype(f32)
+    rows = rows * lax.rsqrt(jnp.mean(rows * rows, axis=1, keepdims=True) + norm_eps)
+    whole[...] = (rows * gains[...]).astype(bf16)
+    lane = lax.broadcasted_iota(jnp.int32, (sz.rows_half, sz.span), 1)
+    for copy in copies[2:]:
+        copy.wait()
+    for k, out in enumerate(outs):
+        head = here ^ k
+        first = pl.multiple_of(sz.start(head), LANES)
+        skip = head * sz.features - first
+        piece = whole[:, pl.ds(first, sz.span)]
+        live = (lane >= skip) & (lane < skip + sz.features)
+        out[: sz.rows_half] = jnp.where(live, piece.astype(f32), 0.0).astype(bf16)
+        parts = []
+        for c in range(sz.group_size):
+            first = pl.multiple_of((head * sz.group_size + c) * HEAD_SIZE, HEAD_SIZE)
+            parts.append(query[:, pl.ds(first, HEAD_SIZE)])
+        first = pl.multiple_of(head * HEAD_SIZE, HEAD_SIZE)
+        parts.append(key[:, pl.ds(first, HEAD_SIZE)])
+        for j in range(sz.slots_here):
+            parts.append(raised[j, :, pl.ds(first, HEAD_SIZE)])
+        at = 0
+        for part in parts:
+            for top in range(0, part.shape[0], sz.rows_half):
+                out[sz.rows_half :, at : at + HEAD_SIZE] = part[top : top + sz.rows_half]
+                at += HEAD_SIZE
+        if at < sz.span:
+            out[sz.rows_half :, at:] = jnp.zeros((sz.rows_half, sz.span - at), bf16)
+
+
+def unpack(sz, piece, out, part, first, size):
+    for top in range(0, size, sz.rows_half):
+        lanes = slice((part + top // sz.rows_half) * HEAD_SIZE, (part + top // sz.rows_half + 1) * HEAD_SIZE)
+        place = pl.ds(pl.multiple_of(first + top, sz.rows_half), sz.rows_half)
+        out[place, :] = piece[sz.rows_half :, lanes]
+
+
+def softmax_kernel(sz, table, *refs):
+    pieces, out = refs[: sz.seq], refs[sz.seq]
+    query, key = refs[sz.seq + 1 :]
+    here = lax.axis_index("seq")
+    parts = sz.rows // sz.rows_half
+    for k, piece in enumerate(pieces):
+        first = (here ^ k) * sz.rows
+        for c in range(sz.group_size):
+            unpack(sz, piece, query.at[c], c * parts, first, sz.rows)
+        unpack(sz, piece, key, sz.group_size * parts, first, sz.rows)
+    shape = (sz.tokens, sz.tokens)
+    mine = lax.broadcasted_iota(jnp.int32, shape, 0)
+    theirs = lax.broadcasted_iota(jnp.int32, shape, 1)
+    live = (theirs <= mine) & (theirs > mine - WINDOW)
+    live = live & (request_column(sz, table, mine) == request_column(sz, table, theirs))
+    for c in range(sz.group_size):
+        scores = lax.dot_general(
+            query[c], key[...], (((1,), (1,)), ((), ())), preferred_element_type=f32
+        )
+        scores = jnp.where(live, scores * query_scale, -1e30)
+        weights = jnp.exp(scores - jnp.max(scores, axis=1, keepdims=True))
+        out[c] = (weights / jnp.sum(weights, axis=1, keepdims=True)).astype(bf16)
+
+
+def matrix_kernel(sz, base, base_other, out, sem):
+    here, core = lax.axis_index("seq"), lax.axis_index("owner")
+    depth, wide = base.shape[0], out.shape[1]
+    skip = here * sz.features - sz.start(here)
+    spare = sz.span - sz.features
+    out[0:spare] = jnp.zeros((spare, wide), bf16)
+    out[sz.span - spare :] = jnp.zeros((spare, wide), bf16)
+    columns = pl.ds(pl.multiple_of(core * wide, wide), wide)
+    copies = []
+    for j, (ref, owner) in enumerate(((base, core), (base_other, 1 - core))):
+        place = pl.ds(pl.multiple_of(skip + owner * depth, 16), depth)
+        copies.append(pltpu.make_async_copy(ref.at[:, columns], out.at[place], sem.at[j]))
+        copies[-1].start()
+    for copy in copies:
+        copy.wait()
+
+
+def gather_kernel(sz, *refs):
+    pieces, out = refs[: sz.seq], refs[sz.seq]
+    here = lax.axis_index("seq")
+    for k, piece in enumerate(pieces):
+        first = pl.multiple_of((here ^ k) * sz.rows_half, sz.rows_half)
+        out[pl.ds(first, sz.rows_half), :] = piece[: sz.rows_half]
+
+
+def project_kernel(sz, table, matrix, own, other, *refs):
+    count = 2 * sz.groups * sz.side
+    panels, refs = refs[:count], refs[count:]
+    outs, (rows, stacked, product) = refs[: sz.seq], refs[sz.seq :]
+    here, core = lax.axis_index("seq"), lax.axis_index("owner")
+    for p, panel in enumerate(panels):
+        stacked[p * sz.rank : (p + 1) * sz.rank] = panel[...]
+    for ref, owner in ((own, core), (other, 1 - core)):
+        for chip in range(sz.seq):
+            first = pl.multiple_of(chip * sz.rows + owner * sz.rows_half, sz.rows_half)
+            rows[pl.ds(first, sz.rows_half), :] = ref[
+                chip * sz.rows_half : (chip + 1) * sz.rows_half
+            ]
+    product[...] = jnp.dot(rows[...], matrix[...], preferred_element_type=f32).astype(bf16)
+    for k, out in enumerate(outs):
+        first = pl.multiple_of((here ^ k) * HEAD_SIZE, HEAD_SIZE)
+        out[: sz.tokens] = product[:, pl.ds(first, HEAD_SIZE)]
+    low = lax.dot_general(
+        rows[...], stacked[...], (((1,), (1,)), ((), ())), preferred_element_type=f32
+    )
+    shape = (sz.tokens, sz.rank)
+    request = request_column(sz, table, lax.broadcasted_iota(jnp.int32, shape, 0))
+    column = lax.broadcasted_iota(jnp.int32, shape, 1)
+    panel_here = jnp.full(shape, -1)
+    for r in range(sz.requests):
+        panel_here = jnp.where((request == r) & (column < table[1, r]), table[2, r], panel_here)
+    reduced = jnp.zeros(shape, f32)
+    for p in range(count):
+        reduced = jnp.where(panel_here == p, low[:, p * sz.rank : (p + 1) * sz.rank], reduced)
+    half = sz.tokens // 2
+    packed = jnp.concatenate([reduced[:half], reduced[half:]], axis=1).astype(bf16)
+    for out in outs:
+        out[sz.tokens :] = packed
+
+
+def mix_kernel(sz, table, softmax, *refs):
+    pieces, refs = refs[: sz.seq], refs[sz.seq :]
+    partials, refs = refs[: sz.seq], refs[sz.seq :]
+    outs, (wide, raise_all, raise_picked, mixed) = refs[: sz.seq], refs[sz.seq :]
+    here = lax.axis_index("seq")
+    parts = (sz.group_size + 1) * (sz.rows // sz.rows_half)
+    for k, piece in enumerate(pieces):
+        size = sz.slots_here * sz.rank
+        unpack(sz, piece, raise_all, parts, k * size, size)
+    position = lax.broadcasted_iota(jnp.int32, (sz.tokens, sz.rank), 0)
+    request = request_column(sz, table, position)
+    position = lax.broadcasted_iota(jnp.int32, (sz.tokens, HEAD_SIZE), 0)
+    request_wide = request_column(sz, table, position)
+    rank_here = jnp.ones((sz.tokens, HEAD_SIZE), jnp.int32)
+    low = sum(partial[sz.tokens :].astype(f32) for partial in partials)
+    low = jnp.concatenate([low[:, : sz.rank], low[:, sz.rank :]], axis=0)
+    for r in range(sz.requests):
+        rank_here = jnp.where(request_wide == r, table[1, r], rank_here)
+        own = slice(r * sz.rank, (r + 1) * sz.rank)
+        raise_picked[own] = raise_all[pl.ds(pl.multiple_of(table[3, r], sz.rank), sz.rank), :]
+        wide[:, own] = jnp.where(request == r, low, 0.0).astype(bf16)
+    scale = adapter_strength / rank_here.astype(f32)
+    raised = jnp.dot(wide[...], raise_picked[...], preferred_element_type=f32)
+    base = sum(partial[: sz.tokens].astype(f32) for partial in partials)
+    values = (base + scale * raised).astype(bf16)
+    for c in range(sz.group_size):
+        mixed[:, c * HEAD_SIZE : (c + 1) * HEAD_SIZE] = jnp.dot(
+            softmax[c], values, preferred_element_type=f32
+        ).astype(bf16)
+    for k, out in enumerate(outs):
+        chip = here ^ k
+        out[...] = mixed[pl.ds(pl.multiple_of(chip * sz.rows, sz.rows), sz.rows), :]
+
+
+def place_kernel(sz, *refs):
+    pieces, out = refs[: sz.seq], refs[sz.seq]
+    here = lax.axis_index("seq")
+    wide = sz.group_size * HEAD_SIZE
+    for k, piece in enumerate(pieces):
+        head = here ^ k
+        out[:, pl.ds(pl.multiple_of(head * wide, wide), wide)] = piece[...]
+
+
+def by_heads(sz, x, queries, keys, gain, base, down, up, lengths, adapters, ranks, slots):
+    around = range(1, sz.seq)
+    half_columns = base.shape[1] // 2
+    spread = (2 * sz.rows_half, sz.span)
+
+    def call(kernel, name, ins, outs, args, scratch=(), params=PARAMS):
+        return pl.pallas_call(
+            functools.partial(kernel, sz),
+            out_shape=[jax.ShapeDtypeStruct(shape, dtype) for shape, dtype, _ in outs],
+            in_specs=ins,
+            out_specs=[spec for _, _, spec in outs],
+            scratch_shapes=list(scratch),
+            compiler_params=params,
+            name=name,
+        )(*args)
+
+    panels_out = call(
+        panels_kernel,
+        "panels_out",
+        [HBM],
+        [((sz.rank, sz.span), bf16, VMEM)] * sz.side,
+        (jnp.swapaxes(down, 1, 2),),
+        (pltpu.SemaphoreType.DMA((sz.side,)),),
+        FIRST,
+    )
+    panels = []
+    for m in range(sz.side):
+        pairs = [
+            (h * 2 + c, (c * sz.side + ((h % sz.side) ^ m)) * 2 + h // sz.side)
+            for h in range(sz.seq)
+            for c in range(2)
+        ]
+        panels.append(lax.ppermute(panels_out[m], ("seq", "owner"), pairs))
+    x, _ = lax.optimization_barrier((x, panels_out[0]))
+    rows_out = call(
+        norm_kernel,
+        "norm_rows",
+        [HBM] * 5,
+        [(spread, bf16, VMEM)] * sz.seq,
+        (x, gain, queries, keys, up),
+        (
+            pltpu.VMEM((sz.rows_half, sz.width), bf16),
+            pltpu.VMEM((1, sz.width), f32),
+            pltpu.VMEM(queries.shape, bf16),
+            pltpu.VMEM(keys.shape, bf16),
+            pltpu.VMEM(up.shape, bf16),
+            pltpu.VMEM((sz.rows_half, sz.width), bf16),
+            pltpu.SemaphoreType.DMA((5,)),
+        ),
+        FIRST,
+    )
+    rows_in = [rows_out[0]] + [swap(rows_out[k], "seq", k) for k in around]
+
+    (table,) = call(
+        table_kernel,
+        "table",
+        [SMEM] * 4,
+        [((4, sz.requests), jnp.int32, SMEM)],
+        (lengths, adapters, ranks, slots),
+    )
+    (matrix,) = call(
+        matrix_kernel,
+        "matrix_rows",
+        [HBM, ANY],
+        [((sz.span, half_columns), bf16, VMEM)],
+        (base, swap(base, "owner", 1)),
+        (pltpu.SemaphoreType.DMA((2,)),),
+    )
+
+    panels, rows_out = lax.optimization_barrier((panels, rows_out))
+    panels = panels + [swap(p, "groups", k) for k in range(1, sz.groups) for p in panels]
+    panels = panels + [swap(p, "owner", 1) for p in panels]
+    rows_in, table, matrix, panels = lax.optimization_barrier((rows_in, table, matrix, panels))
+    (own,) = call(
+        gather_kernel,
+        "gather_rows",
+        [VMEM] * sz.seq,
+        [((sz.seq * sz.rows_half, sz.span), bf16, VMEM)],
+        rows_in,
+    )
+    other = swap(own, "owner", 1)
+    (softmax,) = call(
+        softmax_kernel,
+        "softmax_rows",
+        [SMEM] + [VMEM] * sz.seq,
+        [((sz.group_size, sz.tokens, sz.tokens), bf16, VMEM)],
+        (table, *rows_in),
+        (
+            pltpu.VMEM((sz.group_size, sz.tokens, HEAD_SIZE), bf16),
+            pltpu.VMEM((sz.tokens, HEAD_SIZE), bf16),
+        ),
+    )
+
+    partial_shape = (sz.tokens + sz.tokens // 2, HEAD_SIZE)
+    partial_out = call(
+        project_kernel,
+        "project",
+        [SMEM] + [VMEM] * (3 + len(panels)),
+        [(partial_shape, bf16, VMEM)] * sz.seq,
+        (table, matrix, own, other, *panels),
+        (
+            pltpu.VMEM((sz.tokens, sz.span), bf16),
+            pltpu.VMEM((len(panels) * sz.rank, sz.span), bf16),
+            pltpu.VMEM((sz.tokens, half_columns), bf16),
+        ),
+    )
+    partial_in = [partial_out[0]] + [swap(partial_out[k], "seq", k) for k in around]
+    wide = sz.group_size * HEAD_SIZE
+    mixed = call(
+        mix_kernel,
+        "mix_values",
+        [SMEM] + [VMEM] * (1 + 2 * sz.seq),
+        [((sz.rows, wide), bf16, VMEM)] * sz.seq,
+        (table, softmax, *rows_in, *partial_in),
+        (
+            pltpu.VMEM((sz.tokens, sz.requests * sz.rank), bf16),
+            pltpu.VMEM((sz.seq * sz.slots_here * sz.rank, HEAD_SIZE), bf16),
+            pltpu.VMEM((sz.requests * sz.rank, HEAD_SIZE), bf16),
+            pltpu.VMEM((sz.tokens, wide), bf16),
+        ),
+    )
+    mixed_in = [mixed[0]] + [swap(mixed[k], "seq", k) for k in around]
+    (result,) = call(
+        place_kernel,
+        "place_heads",
+        [VMEM] * sz.seq,
+        [((sz.rows, sz.seq * wide), bf16, VMEM)],
+        mixed_in,
+    )
+    return result
 
 
 def broadcast(x, axis, root):
@@ -25,7 +434,7 @@
     return lax.ppermute(value, axis, [(source, source + steps) for source in range(first, last)])
 
 
-def per_device(
+def by_tokens(
     layer_input_rows,
     encoded_query_rows,
     encoded_key_rows,
@@ -149,6 +558,51 @@
     return result[None]
 
 
+def per_device(
+    layer_input_rows,
+    encoded_query_rows,
+    encoded_key_rows,
+    layer_norm_gain,
+    base_value_matrix,
+    adapter_down_panels,
+    adapter_up_panels,
+    request_token_lengths,
+    adapter_per_request,
+    rank_per_adapter,
+    slot_per_adapter,
+):
+    sz = Sizes(
+        layer_input_rows[0],
+        encoded_query_rows[0],
+        adapter_down_panels[0],
+        adapter_up_panels[0],
+        request_token_lengths.shape[0],
+    )
+    scalars = (request_token_lengths, adapter_per_request, rank_per_adapter, slot_per_adapter)
+    if not sz.fits():
+        return by_tokens(
+            layer_input_rows,
+            encoded_query_rows,
+            encoded_key_rows,
+            layer_norm_gain,
+            base_value_matrix,
+            adapter_down_panels,
+            adapter_up_panels,
+            *scalars,
+        )
+    return by_heads(
+        sz,
+        layer_input_rows[0],
+        encoded_query_rows[0],
+        encoded_key_rows[0],
+        layer_norm_gain,
+        base_value_matrix[0],
+        adapter_down_panels[0],
+        adapter_up_panels[0],
+        *scalars,
+    )[None]
+
+
 def solution(mesh):
     in_specs = (
         P("segment", ("groups", "seq"), None),

time: 356 us -> 59 us (0.17)
  waiting for transfers between devices: 266 us -> 19.7 us
  loops' own time: 18.5 us -> 0 us
  matrix products: 15.6 us -> 0 us
  between operations: 14.9 us -> 0.15 us
  starting transfers between devices: 13.7 us -> 28.2 us
  local copies, waits for them, and re-layouts: 11.6 us -> 0.64 us
  other arithmetic: 10.8 us -> 0 us
  Pallas kernels: 0 us -> 10.1 us
    psum x4 -> x0, waiting for transfers between devices: 173 us -> none  [broadcast(): return lax.psum(jnp.where(mine, x, jnp.zeros_like(x)), axis)]
    all_gather x1 -> x0, waiting for transfers between devices: 90.6 us -> none  [per_device(): lax.all_gather(base_value_matrix[0], ('seq', 'owner'), axis=0, tiled=True)]
    another operation x1 -> x0, loops' own time: 18.5 us -> none  [per_device(): lax.scan(fetch_one, start_low, jnp.arange(requests, dtype=jnp.int32))]
    ppermute x6 -> x19, waiting for transfers between devices: 1.54 us -> 19.7 us  [the longest x17 19.7 us: swap(): lax.ppermute(value, axis, [(i, i ^ mask) for i in range(lax.axis_size(axi...]
    ppermute x6 -> x19, starting transfers between devices: 13.5 us -> 28.2 us  [the longest x17 23.9 us: swap(): lax.ppermute(value, axis, [(i, i ^ mask) for i in range(lax.axis_size(axi...]
    dot_general x14 -> x0, matrix products: 14.3 us -> none  [the longest x1 6.14 us: per_device(): jnp.dot(normalized_rows, lax.all_gather(base_value_matrix[0], ('seq', 'ow...]
    pallas_call x0 -> x9, Pallas kernels: none -> 10.1 us  [call(): pl.pallas_call(functools.partial(kernel, sz), out_shape=[jax.ShapeDtypeSt...]
    dynamic_slice x9 -> x0, local copies, waits for them, and re-layouts: 4.73 us -> none  [the longest x4 2.35 us: per_device(): lax.scan(fetch_one, start_low, jnp.arange(requests, dtype=jnp.int32))]
  transfers between devices with their start and end apart: 11 -> 19, of which waited for: 6 -> 6; matrix products, arithmetic and copies ran while one was open for 1% -> 0% of each run, Pallas kernels for 0% -> 11%
where the time goes in v2:
time: 59 us; the launch traced here: 58.8 us
  starting transfers between devices  28.2 us (48%)
  waiting for transfers between devices  19.7 us (33%)
  Pallas kernels  10.1 us (17%)
  local copies, waits for them, and re-layouts  0.64 us (1%)
    ppermute x17, starting transfers between devices, swap(): lax.ppermute(value, axis, [(i, i ^ mask) for i in range(lax.axis_size(axi...  23.9 us
    ppermute x17, waiting for transfers between devices, swap(): lax.ppermute(value, axis, [(i, i ^ mask) for i in range(lax.axis_size(axi...  19.7 us
    pallas_call x9, Pallas kernels, call(): pl.pallas_call(functools.partial(kernel, sz), out_shape=[jax.ShapeDtypeSt...  10.1 us
    ppermute x2, starting transfers between devices, by_heads(): panels.append(lax.ppermute(panels_out[m], ('seq', 'owner'), pairs))  4.28 us
  transfers between devices with their start and end apart: 19, of which 6 were waited for; matrix products, arithmetic and copies ran while one was open for 0% of the time, Pallas kernels for 11%

profile of v2, /device:TPU:0, one launch (start us, length us, event | category | flops | bytes accessed | tf_op | source)
XLA Modules:
  0.0 58.8 jit_solution(6688889534952181766)
XLA Ops:
  0.0 0.5 collective-permute-start.3
  0.5 1.8 %panels_out.1 = (bf16[64,1408]{1,0:T(8,128)(2,1)}, bf16[64,1408]{1,0:T(8,128)(2,1)}) custom-call(bf16[2,64,2688]{2,1,0:T(8,128)(2,1)} %bitcast.12), custom_call_target="tpu_custom_call" | custom-call | tf_op jit(solution)/shard_map/panels_out/pallas_call | solution.py:300
  2.3 1.6 %collective-permute-start.4 = (bf16[64,1408]{1,0:T(8,128)(2,1)}, bf16[64,1408]{1,0:T(8,128)(2,1)S(1)}, u32[]{:S(2)}, u32[]{:S(2)}) collective-permute-start(bf16[64,1408]{1,0:T(8,128)(2,1)} %get-tuple-element.36), channel_id=1, source_target_pairs={{0,0},{1,8},{4,4},{5,12},{8,1},{9,9},{12,5},{13,13},{2,2},{3,10},{... | collective-permute-start | bytes 540680 | tf_op jit(solution)/shard_map/ppermute | solution.py:326
  3.9 2.7 %collective-permute-start.5 = (bf16[64,1408]{1,0:T(8,128)(2,1)}, bf16[64,1408]{1,0:T(8,128)(2,1)S(1)}, u32[]{:S(2)}, u32[]{:S(2)}) collective-permute-start(bf16[64,1408]{1,0:T(8,128)(2,1)} %get-tuple-element.42), channel_id=1, source_target_pairs={{0,4},{1,12},{4,0},{5,8},{8,5},{9,13},{12,1},{13,9},{2,6},{3,14},{... | collective-permute-start | bytes 540680 | tf_op jit(solution)/shard_map/ppermute | solution.py:326
  6.6 2.2 %norm_rows.1 = (bf16[64,1408]{1,0:T(8,128)(2,1)}, bf16[64,1408]{1,0:T(8,128)(2,1)}, bf16[64,1408]{1,0:T(8,128)(2,1)}, bf16[64,1408]{1,0:T(8,128)(2,1)}) custom-call(bf16[64,5376]{1,0:T(8,128)(2,1)} %bitcast.11, f32[1,5376]{1,0:T(1,128)} %gain.1, bf16[64,1024]{1,0:T(8,128)(2,1)} %bitcast.13, bf16[64,512]{1,0:T(8,128)(2,1)} %bitcast.15, ...), custom_call_target="tpu_custom_call" | custom-call | tf_op jit(solution)/shard_map/norm_rows/pallas_call | solution.py:300
  8.8 0.1 collective-permute-start
  8.9 5.5 %collective-permute-start.1 = (bf16[64,1408]{1,0:T(8,128)(2,1)}, bf16[64,1408]{1,0:T(8,128)(2,1)S(1)}, u32[]{:S(2)}, u32[]{:S(2)}) collective-permute-start(bf16[64,1408]{1,0:T(8,128)(2,1)} %get-tuple-element.40), channel_id=1, source_target_pairs={{0,8},{4,12},{8,0},{12,4},{1,9},{5,13},{9,1},{13,5},{2,10},{6,14},... | collective-permute-start | bytes 540680 | tf_op jit(solution)/shard_map/ppermute | solution.py:31
  14.4 0.0 collective-permute-done.4.refs_0_
  14.4 0.0 collective-permute-done.5.refs_1_
  14.4 1.5 %collective-permute-start.6 = (bf16[64,1408]{1,0:T(8,128)(2,1)S(1)}, bf16[64,1408]{1,0:T(8,128)(2,1)S(1)}, u32[]{:S(2)}, u32[]{:S(2)}) collective-permute-start(bf16[64,1408]{1,0:T(8,128)(2,1)S(1)} %collective-permute-done.4.refs_0_), channel_id=1, source_target_pairs={{0,16},{16,0},{1,17},{17,1},{2,18},{18,2},{3,19},{19,3},{4,20},{20... | collective-permute-start | bytes 540680 | tf_op jit(solution)/shard_map/ppermute | solution.py:31
  15.9 0.5 collective-permute-start.7
  16.5 0.0 collective-permute-done.refs_1_
  16.5 5.6 %collective-permute-start.2 = (bf16[64,1408]{1,0:T(8,128)(2,1)}, bf16[64,1408]{1,0:T(8,128)(2,1)S(1)}, u32[]{:S(2)}, u32[]{:S(2)}) collective-permute-start(bf16[64,1408]{1,0:T(8,128)(2,1)} %get-tuple-element.41), channel_id=1, source_target_pairs={{0,12},{4,8},{8,4},{12,0},{1,13},{5,9},{9,5},{13,1},{2,14},{6,10},... | collective-permute-start | bytes 540680 | tf_op jit(solution)/shard_map/ppermute | solution.py:31
  22.1 7.7 %collective-permute-done.1.refs_2_ = bf16[64,1408]{1,0:T(8,128)(2,1)S(1)} collective-permute-done((bf16[64,1408]{1,0:T(8,128)(2,1)}, bf16[64,1408]{1,0:T(8,128)(2,1)S(1)}, u32[]{:S(2)}, u32[]{:S(2)}) %collective-permute-start.1) | collective-permute-done | bytes 180256 | tf_op jit(solution)/shard_map/ppermute | solution.py:31
  29.8 0.0 collective-permute-start.8
  29.8 0.0 collective-permute-done.6.refs_2_
  29.8 0.5 collective-permute-start.9
  30.3 0.0 collective-permute-done.7.refs_3_
  30.3 0.1 collective-permute-start.10
  30.4 0.0 collective-permute-done.3.base_other
  30.4 0.4 collective-permute-start.11
  30.8 0.0 copy-done.5
  30.8 1.3 %table.1 = s32[4,4]{1,0:T(4,128)S(1)} custom-call(s32[4]{0:T(128)S(1)} %copy-done.2, s32[4]{0:T(128)S(1)} %copy-done.3, s32[8]{0:T(128)S(1)} %copy-done.4, s32[8]{0:T(128)S(1)} %copy-done.5), custom_call_target="tpu_custom_call" | custom-call | tf_op jit(solution)/shard_map/table/pallas_call | solution.py:300
  32.1 0.2 matrix_rows.1.matrix
  32.3 0.0 collective-permute-done.2.refs_3_
  32.3 0.0 collective-permute-done.8.refs_4_
  32.4 0.0 collective-permute-done.9.refs_5_
  32.4 0.0 collective-permute-done.10.refs_6_
  32.4 0.0 collective-permute-done.11.refs_7_
  32.4 0.6 %copy-done = bf16[64,1408]{1,0:T(8,128)(2,1)S(1)} copy-done((bf16[64,1408]{1,0:T(8,128)(2,1)S(1)}, bf16[64,1408]{1,0:T(8,128)(2,1)}, u32[]{:S(2)}) %copy-start) | copy-done | bytes 180248
  33.0 0.1 collective-permute-start.12
  33.2 1.6 %collective-permute-done.12.other = bf16[128,1408]{1,0:T(8,128)(2,1)S(1)} collective-permute-done((bf16[128,1408]{1,0:T(8,128)(2,1)S(1)}, bf16[128,1408]{1,0:T(8,128)(2,1)S(1)}, u32[]{:S(2)}, u32[]{:S(2)}) %collective-permute-start.12) | collective-permute-done | bytes 360480 | tf_op jit(solution)/shard_map/ppermute | solution.py:31
  34.8 1.8 %project.1 = (bf16[384,128]{1,0:T(8,128)(2,1)S(1)}, bf16[384,128]{1,0:T(8,128)(2,1)S(1)}, bf16[384,128]{1,0:T(8,128)(2,1)S(1)}, bf16[384,128]{1,0:T(8,128)(2,1)S(1)}) custom-call(s32[4,4]{1,0:T(4,128)S(1)} %table.1, bf16[1408,512]{1,0:T(8,128)(2,1)S(1)} %matrix_rows.1.matrix, bf16[128,1408]{1,0:T(8,128)(2,1)S(1)} %gather_rows.1.own, ...), custom_call_target="tpu_custom_call" | custom-call | tf_op jit(solution)/shard_map/project/pallas_call | solution.py:300
  36.6 0.7 %collective-permute-start.13 = (bf16[384,128]{1,0:T(8,128)(2,1)S(1)}, bf16[384,128]{1,0:T(8,128)(2,1)S(1)}, u32[]{:S(2)}, u32[]{:S(2)}) collective-permute-start(bf16[384,128]{1,0:T(8,128)(2,1)S(1)} %get-tuple-element.60), channel_id=1, source_target_pairs={{0,4},{4,0},{8,12},{12,8},{1,5},{5,1},{9,13},{13,9},{2,6},{6,2},{1... | collective-permute-start | bytes 294920 | tf_op jit(solution)/shard_map/ppermute | solution.py:31
  37.3 2.7 %collective-permute-start.14 = (bf16[384,128]{1,0:T(8,128)(2,1)S(1)}, bf16[384,128]{1,0:T(8,128)(2,1)S(1)}, u32[]{:S(2)}, u32[]{:S(2)}) collective-permute-start(bf16[384,128]{1,0:T(8,128)(2,1)S(1)} %get-tuple-element.61), channel_id=1, source_target_pairs={{0,8},{4,12},{8,0},{12,4},{1,9},{5,13},{9,1},{13,5},{2,10},{6,14},... | collective-permute-start | bytes 294920 | tf_op jit(solution)/shard_map/ppermute | solution.py:31
  39.9 1.1 %collective-permute-start.15 = (bf16[384,128]{1,0:T(8,128)(2,1)S(1)}, bf16[384,128]{1,0:T(8,128)(2,1)S(1)}, u32[]{:S(2)}, u32[]{:S(2)}) collective-permute-start(bf16[384,128]{1,0:T(8,128)(2,1)S(1)} %get-tuple-element.62), channel_id=1, source_target_pairs={{0,12},{4,8},{8,4},{12,0},{1,13},{5,9},{9,5},{13,1},{2,14},{6,10},... | collective-permute-start | bytes 294920 | tf_op jit(solution)/shard_map/ppermute | solution.py:31
  41.1 1.0 %softmax_rows.1.softmax = bf16[2,256,256]{2,1,0:T(8,128)(2,1)S(1)} custom-call(s32[4,4]{1,0:T(4,128)S(1)} %table.1, bf16[64,1408]{1,0:T(8,128)(2,1)S(1)} %copy-done, bf16[64,1408]{1,0:T(8,128)(2,1)S(1)} %collective-permute-done.refs_1_, bf16[64,1408]{1,0:T(8,128)(2,1)S(1)} %collective-permute-done.1.refs_2_, bf16[64,1408]{1,0:T(8,128)(2,1)S(1)} %collective-permute-done.2.refs_3_), custom_call_target="tpu_custom_call" | custom-call | tf_op jit(solution)/shard_map/softmax_rows/pallas_call | solution.py:300
  42.1 1.0 %collective-permute-done.13.refs_5_ = bf16[384,128]{1,0:T(8,128)(2,1)S(1)} collective-permute-done((bf16[384,128]{1,0:T(8,128)(2,1)S(1)}, bf16[384,128]{1,0:T(8,128)(2,1)S(1)}, u32[]{:S(2)}, u32[]{:S(2)}) %collective-permute-start.13) | collective-permute-done | bytes 98336 | tf_op jit(solution)/shard_map/ppermute | solution.py:31
  43.1 4.9 %collective-permute-done.14.refs_6_ = bf16[384,128]{1,0:T(8,128)(2,1)S(1)} collective-permute-done((bf16[384,128]{1,0:T(8,128)(2,1)S(1)}, bf16[384,128]{1,0:T(8,128)(2,1)S(1)}, u32[]{:S(2)}, u32[]{:S(2)}) %collective-permute-start.14) | collective-permute-done | bytes 98336 | tf_op jit(solution)/shard_map/ppermute | solution.py:31
  48.0 0.0 collective-permute-done.15.refs_7_
  48.0 1.1 %mix_values.1 = (bf16[64,256]{1,0:T(8,128)(2,1)S(1)}, bf16[64,256]{1,0:T(8,128)(2,1)S(1)}, bf16[64,256]{1,0:T(8,128)(2,1)S(1)}, bf16[64,256]{1,0:T(8,128)(2,1)S(1)}) custom-call(s32[4,4]{1,0:T(4,128)S(1)} %table.1, bf16[2,256,256]{2,1,0:T(8,128)(2,1)S(1)} %softmax_rows.1.softmax, bf16[64,1408]{1,0:T(8,128)(2,1)S(1)} %copy-done, ...), custom_call_target="tpu_custom_call" | custom-call | tf_op jit(solution)/shard_map/mix_values/pallas_call | solution.py:300
  49.1 2.0 %collective-permute-start.16 = (bf16[64,256]{1,0:T(8,128)(2,1)S(1)}, bf16[64,256]{1,0:T(8,128)(2,1)S(1)}, u32[]{:S(2)}, u32[]{:S(2)}) collective-permute-start(bf16[64,256]{1,0:T(8,128)(2,1)S(1)} %get-tuple-element.64), channel_id=1, source_target_pairs={{0,4},{4,0},{8,12},{12,8},{1,5},{5,1},{9,13},{13,9},{2,6},{6,2},{1... | collective-permute-start | bytes 98312 | tf_op jit(solution)/shard_map/ppermute | solution.py:31
  51.1 1.3 %collective-permute-start.17 = (bf16[64,256]{1,0:T(8,128)(2,1)S(1)}, bf16[64,256]{1,0:T(8,128)(2,1)S(1)}, u32[]{:S(2)}, u32[]{:S(2)}) collective-permute-start(bf16[64,256]{1,0:T(8,128)(2,1)S(1)} %get-tuple-element.65), channel_id=1, source_target_pairs={{0,8},{4,12},{8,0},{12,4},{1,9},{5,13},{9,1},{13,5},{2,10},{6,14},... | collective-permute-start | bytes 98312 | tf_op jit(solution)/shard_map/ppermute | solution.py:31
  52.4 1.2 %collective-permute-start.18 = (bf16[64,256]{1,0:T(8,128)(2,1)S(1)}, bf16[64,256]{1,0:T(8,128)(2,1)S(1)}, u32[]{:S(2)}, u32[]{:S(2)}) collective-permute-start(bf16[64,256]{1,0:T(8,128)(2,1)S(1)} %get-tuple-element.66), channel_id=1, source_target_pairs={{0,12},{4,8},{8,4},{12,0},{1,13},{5,9},{9,5},{13,1},{2,14},{6,10},... | collective-permute-start | bytes 98312 | tf_op jit(solution)/shard_map/ppermute | solution.py:31
  53.6 0.0 collective-permute-done.16.refs_1_
  53.6 2.9 %collective-permute-done.17.refs_2_ = bf16[64,256]{1,0:T(8,128)(2,1)S(1)} collective-permute-done((bf16[64,256]{1,0:T(8,128)(2,1)S(1)}, bf16[64,256]{1,0:T(8,128)(2,1)S(1)}, u32[]{:S(2)}, u32[]{:S(2)}) %collective-permute-start.17) | collective-permute-done | bytes 32800 | tf_op jit(solution)/shard_map/ppermute | solution.py:31
  56.6 1.5 %collective-permute-done.18.refs_3_ = bf16[64,256]{1,0:T(8,128)(2,1)S(1)} collective-permute-done((bf16[64,256]{1,0:T(8,128)(2,1)S(1)}, bf16[64,256]{1,0:T(8,128)(2,1)S(1)}, u32[]{:S(2)}, u32[]{:S(2)}) %collective-permute-start.18) | collective-permute-done | bytes 32800 | tf_op jit(solution)/shard_map/ppermute | solution.py:31
  58.1 0.7 %place_heads.1 = bf16[64,1024]{1,0:T(8,128)(2,1)} custom-call(bf16[64,256]{1,0:T(8,128)(2,1)S(1)} %get-tuple-element.63.refs_0_, bf16[64,256]{1,0:T(8,128)(2,1)S(1)} %collective-permute-done.16.refs_1_, bf16[64,256]{1,0:T(8,128)(2,1)S(1)} %collective-permute-done.17.refs_2_, bf16[64,256]{1,0:T(8,128)(2,1)S(1)} %collective-permute-done.18.refs_3_), custom_call_target="tpu_custom_call" | custom-call | tf_op jit(solution)/shard_map/place_heads/pallas_call | solution.py:300
  (11 shorter events, 0.1 us)
Async XLA Ops:
  0.0 32.1 %copy-start.1 = (bf16[1,672,1024]{2,1,0:T(8,128)(2,1)S(1)}, bf16[1,672,1024]{2,1,0:T(8,128)(2,1)}, u32[]{:S(2)}) copy-start(bf16[1,672,1024]{2,1,0:T(8,128)(2,1)} %param.15) | copy-start | bytes 4128772
  0.0 30.8 %copy-start.2 = (s32[4]{0:T(128)S(1)}, s32[4]{0:T(128)}, u32[]{:S(2)}) copy-start(s32[4]{0:T(128)} %lengths.1) | copy-start | bytes 52
  0.0 30.8 %copy-start.3 = (s32[4]{0:T(128)S(1)}, s32[4]{0:T(128)}, u32[]{:S(2)}) copy-start(s32[4]{0:T(128)} %adapters.1) | copy-start | bytes 52
  0.0 30.8 %copy-start.4 = (s32[8]{0:T(128)S(1)}, s32[8]{0:T(128)}, u32[]{:S(2)}) copy-start(s32[8]{0:T(128)} %ranks.1) | copy-start | bytes 100
  0.0 30.8 %copy-start.5 = (s32[8]{0:T(128)S(1)}, s32[8]{0:T(128)}, u32[]{:S(2)}) copy-start(s32[8]{0:T(128)} %slots.1) | copy-start | bytes 100
  0.0 30.3 %collective-permute-start.3 = (bf16[672,1024]{1,0:T(8,128)(2,1)}, bf16[672,1024]{1,0:T(8,128)(2,1)S(1)}, u32[]{:S(2)}, u32[]{:S(2)}) collective-permute-start(bf16[672,1024]{1,0:T(8,128)(2,1)} %bitcast.9), channel_id=1, source_target_pairs={{0,1},{1,0},{2,3},{3,2},{4,5},{5,4},{6,7},{7,6},{8,9},{9,8},{10,11... | collective-permute-start | bytes 4128776 | tf_op jit(solution)/shard_map/ppermute | solution.py:31
  2.3 12.1 %collective-permute-start.4 = (bf16[64,1408]{1,0:T(8,128)(2,1)}, bf16[64,1408]{1,0:T(8,128)(2,1)S(1)}, u32[]{:S(2)}, u32[]{:S(2)}) collective-permute-start(bf16[64,1408]{1,0:T(8,128)(2,1)} %get-tuple-element.36), channel_id=1, source_target_pairs={{0,0},{1,8},{4,4},{5,12},{8,1},{9,9},{12,5},{13,13},{2,2},{3,10},{... | collective-permute-start | bytes 540680 | tf_op jit(solution)/shard_map/ppermute | solution.py:326
  3.9 10.5 %collective-permute-start.5 = (bf16[64,1408]{1,0:T(8,128)(2,1)}, bf16[64,1408]{1,0:T(8,128)(2,1)S(1)}, u32[]{:S(2)}, u32[]{:S(2)}) collective-permute-start(bf16[64,1408]{1,0:T(8,128)(2,1)} %get-tuple-element.42), channel_id=1, source_target_pairs={{0,4},{1,12},{4,0},{5,8},{8,5},{9,13},{12,1},{13,9},{2,6},{3,14},{... | collective-permute-start | bytes 540680 | tf_op jit(solution)/shard_map/ppermute | solution.py:326
  8.8 7.6 %collective-permute-start = (bf16[64,1408]{1,0:T(8,128)(2,1)}, bf16[64,1408]{1,0:T(8,128)(2,1)S(1)}, u32[]{:S(2)}, u32[]{:S(2)}) collective-permute-start(bf16[64,1408]{1,0:T(8,128)(2,1)} %get-tuple-element.39), channel_id=1, source_target_pairs={{0,4},{4,0},{8,12},{12,8},{1,5},{5,1},{9,13},{13,9},{2,6},{6,2},{1... | collective-permute-start | bytes 540680 | tf_op jit(solution)/shard_map/ppermute | solution.py:31
  8.9 20.9 %collective-permute-start.1 = (bf16[64,1408]{1,0:T(8,128)(2,1)}, bf16[64,1408]{1,0:T(8,128)(2,1)S(1)}, u32[]{:S(2)}, u32[]{:S(2)}) collective-permute-start(bf16[64,1408]{1,0:T(8,128)(2,1)} %get-tuple-element.40), channel_id=1, source_target_pairs={{0,8},{4,12},{8,0},{12,4},{1,9},{5,13},{9,1},{13,5},{2,10},{6,14},... | collective-permute-start | bytes 540680 | tf_op jit(solution)/shard_map/ppermute | solution.py:31
  14.4 15.3 %collective-permute-start.6 = (bf16[64,1408]{1,0:T(8,128)(2,1)S(1)}, bf16[64,1408]{1,0:T(8,128)(2,1)S(1)}, u32[]{:S(2)}, u32[]{:S(2)}) collective-permute-start(bf16[64,1408]{1,0:T(8,128)(2,1)S(1)} %collective-permute-done.4.refs_0_), channel_id=1, source_target_pairs={{0,16},{16,0},{1,17},{17,1},{2,18},{18,2},{3,19},{19,3},{4,20},{20... | collective-permute-start | bytes 540680 | tf_op jit(solution)/shard_map/ppermute | solution.py:31
  15.9 14.3 %collective-permute-start.7 = (bf16[64,1408]{1,0:T(8,128)(2,1)S(1)}, bf16[64,1408]{1,0:T(8,128)(2,1)S(1)}, u32[]{:S(2)}, u32[]{:S(2)}) collective-permute-start(bf16[64,1408]{1,0:T(8,128)(2,1)S(1)} %collective-permute-done.5.refs_1_), channel_id=1, source_target_pairs={{0,16},{16,0},{1,17},{17,1},{2,18},{18,2},{3,19},{19,3},{4,20},{20... | collective-permute-start | bytes 540680 | tf_op jit(solution)/shard_map/ppermute | solution.py:31
  16.5 15.9 %collective-permute-start.2 = (bf16[64,1408]{1,0:T(8,128)(2,1)}, bf16[64,1408]{1,0:T(8,128)(2,1)S(1)}, u32[]{:S(2)}, u32[]{:S(2)}) collective-permute-start(bf16[64,1408]{1,0:T(8,128)(2,1)} %get-tuple-element.41), channel_id=1, source_target_pairs={{0,12},{4,8},{8,4},{12,0},{1,13},{5,9},{9,5},{13,1},{2,14},{6,10},... | collective-permute-start | bytes 540680 | tf_op jit(solution)/shard_map/ppermute | solution.py:31
  29.8 2.6 %collective-permute-start.8 = (bf16[64,1408]{1,0:T(8,128)(2,1)S(1)}, bf16[64,1408]{1,0:T(8,128)(2,1)S(1)}, u32[]{:S(2)}, u32[]{:S(2)}) collective-permute-start(bf16[64,1408]{1,0:T(8,128)(2,1)S(1)} %collective-permute-done.4.refs_0_), channel_id=1, source_target_pairs={{0,1},{1,0},{2,3},{3,2},{4,5},{5,4},{6,7},{7,6},{8,9},{9,8},{10,11... | collective-permute-start | bytes 540680 | tf_op jit(solution)/shard_map/ppermute | solution.py:31
  29.8 2.6 %collective-permute-start.9 = (bf16[64,1408]{1,0:T(8,128)(2,1)S(1)}, bf16[64,1408]{1,0:T(8,128)(2,1)S(1)}, u32[]{:S(2)}, u32[]{:S(2)}) collective-permute-start(bf16[64,1408]{1,0:T(8,128)(2,1)S(1)} %collective-permute-done.5.refs_1_), channel_id=1, source_target_pairs={{0,1},{1,0},{2,3},{3,2},{4,5},{5,4},{6,7},{7,6},{8,9},{9,8},{10,11... | collective-permute-start | bytes 540680 | tf_op jit(solution)/shard_map/ppermute | solution.py:31
  30.3 2.1 %collective-permute-start.10 = (bf16[64,1408]{1,0:T(8,128)(2,1)S(1)}, bf16[64,1408]{1,0:T(8,128)(2,1)S(1)}, u32[]{:S(2)}, u32[]{:S(2)}) collective-permute-start(bf16[64,1408]{1,0:T(8,128)(2,1)S(1)} %collective-permute-done.6.refs_2_), channel_id=1, source_target_pairs={{0,1},{1,0},{2,3},{3,2},{4,5},{5,4},{6,7},{7,6},{8,9},{9,8},{10,11... | collective-permute-start | bytes 540680 | tf_op jit(solution)/shard_map/ppermute | solution.py:31
  30.4 2.0 %collective-permute-start.11 = (bf16[64,1408]{1,0:T(8,128)(2,1)S(1)}, bf16[64,1408]{1,0:T(8,128)(2,1)S(1)}, u32[]{:S(2)}, u32[]{:S(2)}) collective-permute-start(bf16[64,1408]{1,0:T(8,128)(2,1)S(1)} %collective-permute-done.7.refs_3_), channel_id=1, source_target_pairs={{0,1},{1,0},{2,3},{3,2},{4,5},{5,4},{6,7},{7,6},{8,9},{9,8},{10,11... | collective-permute-start | bytes 540680 | tf_op jit(solution)/shard_map/ppermute | solution.py:31
  32.1 0.9 %copy-start = (bf16[64,1408]{1,0:T(8,128)(2,1)S(1)}, bf16[64,1408]{1,0:T(8,128)(2,1)}, u32[]{:S(2)}) copy-start(bf16[64,1408]{1,0:T(8,128)(2,1)} %get-tuple-element.46.refs_0_) | copy-start | bytes 540676
  33.0 1.7 %collective-permute-start.12 = (bf16[128,1408]{1,0:T(8,128)(2,1)S(1)}, bf16[128,1408]{1,0:T(8,128)(2,1)S(1)}, u32[]{:S(2)}, u32[]{:S(2)}) collective-permute-start(bf16[128,1408]{1,0:T(8,128)(2,1)S(1)} %gather_rows.1.own), channel_id=1, source_target_pairs={{0,1},{1,0},{2,3},{3,2},{4,5},{5,4},{6,7},{7,6},{8,9},{9,8},{10,11... | collective-permute-start | bytes 1081352 | tf_op jit(solution)/shard_map/ppermute | solution.py:31
  36.6 6.5 %collective-permute-start.13 = (bf16[384,128]{1,0:T(8,128)(2,1)S(1)}, bf16[384,128]{1,0:T(8,128)(2,1)S(1)}, u32[]{:S(2)}, u32[]{:S(2)}) collective-permute-start(bf16[384,128]{1,0:T(8,128)(2,1)S(1)} %get-tuple-element.60), channel_id=1, source_target_pairs={{0,4},{4,0},{8,12},{12,8},{1,5},{5,1},{9,13},{13,9},{2,6},{6,2},{1... | collective-permute-start | bytes 294920 | tf_op jit(solution)/shard_map/ppermute | solution.py:31
  37.3 10.7 %collective-permute-start.14 = (bf16[384,128]{1,0:T(8,128)(2,1)S(1)}, bf16[384,128]{1,0:T(8,128)(2,1)S(1)}, u32[]{:S(2)}, u32[]{:S(2)}) collective-permute-start(bf16[384,128]{1,0:T(8,128)(2,1)S(1)} %get-tuple-element.61), channel_id=1, source_target_pairs={{0,8},{4,12},{8,0},{12,4},{1,9},{5,13},{9,1},{13,5},{2,10},{6,14},... | collective-permute-start | bytes 294920 | tf_op jit(solution)/shard_map/ppermute | solution.py:31
  39.9 8.0 %collective-permute-start.15 = (bf16[384,128]{1,0:T(8,128)(2,1)S(1)}, bf16[384,128]{1,0:T(8,128)(2,1)S(1)}, u32[]{:S(2)}, u32[]{:S(2)}) collective-permute-start(bf16[384,128]{1,0:T(8,128)(2,1)S(1)} %get-tuple-element.62), channel_id=1, source_target_pairs={{0,12},{4,8},{8,4},{12,0},{1,13},{5,9},{9,5},{13,1},{2,14},{6,10},... | collective-permute-start | bytes 294920 | tf_op jit(solution)/shard_map/ppermute | solution.py:31
  49.1 4.5 %collective-permute-start.16 = (bf16[64,256]{1,0:T(8,128)(2,1)S(1)}, bf16[64,256]{1,0:T(8,128)(2,1)S(1)}, u32[]{:S(2)}, u32[]{:S(2)}) collective-permute-start(bf16[64,256]{1,0:T(8,128)(2,1)S(1)} %get-tuple-element.64), channel_id=1, source_target_pairs={{0,4},{4,0},{8,12},{12,8},{1,5},{5,1},{9,13},{13,9},{2,6},{6,2},{1... | collective-permute-start | bytes 98312 | tf_op jit(solution)/shard_map/ppermute | solution.py:31
  51.1 5.5 %collective-permute-start.17 = (bf16[64,256]{1,0:T(8,128)(2,1)S(1)}, bf16[64,256]{1,0:T(8,128)(2,1)S(1)}, u32[]{:S(2)}, u32[]{:S(2)}) collective-permute-start(bf16[64,256]{1,0:T(8,128)(2,1)S(1)} %get-tuple-element.65), channel_id=1, source_target_pairs={{0,8},{4,12},{8,0},{12,4},{1,9},{5,13},{9,1},{13,5},{2,10},{6,14},... | collective-permute-start | bytes 98312 | tf_op jit(solution)/shard_map/ppermute | solution.py:31
  52.4 5.7 %collective-permute-start.18 = (bf16[64,256]{1,0:T(8,128)(2,1)S(1)}, bf16[64,256]{1,0:T(8,128)(2,1)S(1)}, u32[]{:S(2)}, u32[]{:S(2)}) collective-permute-start(bf16[64,256]{1,0:T(8,128)(2,1)S(1)} %get-tuple-element.66), channel_id=1, source_target_pairs={{0,12},{4,8},{8,4},{12,0},{1,13},{5,9},{9,5},{13,1},{2,14},{6,10},... | collective-permute-start | bytes 98312 | tf_op jit(solution)/shard_map/ppermute | solution.py:31

commit v3 on v2

--- a/solution.py
+++ b/solution.py
@@ -46,6 +46,7 @@
         self.heads_here = up.shape[2] // HEAD_SIZE
         self.group_size = HEADS // KEY_VALUE_HEADS
         self.tokens = self.rows * self.seq
+        self.order = [0, 3, 2, 1]
         tiles = [
             -(-((i * self.features) % LANES + self.features) // LANES) for i in range(self.side)
         ]
@@ -85,8 +86,10 @@
     return found
 
 
-def table_kernel(sz, lengths, adapters, ranks, slots, out):
+def table_kernel(sz, lengths, adapters, ranks, slots, piece, out, held, sem):
     here, core, group = (lax.axis_index(a) for a in ("seq", "owner", "groups"))
+    copy = pltpu.make_async_copy(piece, held, sem)
+    copy.start()
     end = jnp.int32(0)
     for r in range(sz.requests):
         end = end + lengths[r]
@@ -99,6 +102,7 @@
         out[1, r] = ranks[adapter]
         out[2, r] = (other * sz.groups + (local ^ group)) * sz.side + m
         out[3, r] = ((here ^ chip) * sz.slots_here + local) * sz.rank
+    copy.wait()
 
 
 def panels_kernel(sz, down, *outs_and_sem):
@@ -169,7 +173,7 @@
     query, key = refs[sz.seq + 1 :]
     here = lax.axis_index("seq")
     parts = sz.rows // sz.rows_half
-    for k, piece in enumerate(pieces):
+    for k, piece in zip(sz.order, pieces):
         first = (here ^ k) * sz.rows
         for c in range(sz.group_size):
             unpack(sz, piece, query.at[c], c * parts, first, sz.rows)
@@ -208,43 +212,55 @@
 def gather_kernel(sz, *refs):
     pieces, out = refs[: sz.seq], refs[sz.seq]
     here = lax.axis_index("seq")
-    for k, piece in enumerate(pieces):
+    for k, piece in zip(sz.order, pieces):
         first = pl.multiple_of((here ^ k) * sz.rows_half, sz.rows_half)
         out[pl.ds(first, sz.rows_half), :] = piece[: sz.rows_half]
 
 
-def project_kernel(sz, table, matrix, own, other, *refs):
-    count = 2 * sz.groups * sz.side
-    panels, refs = refs[:count], refs[count:]
-    outs, (rows, stacked, product) = refs[: sz.seq], refs[sz.seq :]
-    here, core = lax.axis_index("seq"), lax.axis_index("owner")
-    for p, panel in enumerate(panels):
-        stacked[p * sz.rank : (p + 1) * sz.rank] = panel[...]
-    for ref, owner in ((own, core), (other, 1 - core)):
-        for chip in range(sz.seq):
-            first = pl.multiple_of(chip * sz.rows + owner * sz.rows_half, sz.rows_half)
-            rows[pl.ds(first, sz.rows_half), :] = ref[
-                chip * sz.rows_half : (chip + 1) * sz.rows_half
-            ]
-    product[...] = jnp.dot(rows[...], matrix[...], preferred_element_type=f32).astype(bf16)
-    for k, out in enumerate(outs):
-        first = pl.multiple_of((here ^ k) * HEAD_SIZE, HEAD_SIZE)
-        out[: sz.tokens] = product[:, pl.ds(first, HEAD_SIZE)]
+def project_half(sz, table, matrix, rows, stacked, owner):
+    values = jnp.dot(rows[...], matrix[...], preferred_element_type=f32)
     low = lax.dot_general(
         rows[...], stacked[...], (((1,), (1,)), ((), ())), preferred_element_type=f32
     )
-    shape = (sz.tokens, sz.rank)
-    request = request_column(sz, table, lax.broadcasted_iota(jnp.int32, shape, 0))
+    shape = (sz.seq * sz.rows_half, sz.rank)
+    row = lax.broadcasted_iota(jnp.int32, shape, 0)
+    position = row // sz.rows_half * sz.rows + owner * sz.rows_half + row % sz.rows_half
+    request = request_column(sz, table, position)
     column = lax.broadcasted_iota(jnp.int32, shape, 1)
     panel_here = jnp.full(shape, -1)
     for r in range(sz.requests):
         panel_here = jnp.where((request == r) & (column < table[1, r]), table[2, r], panel_here)
     reduced = jnp.zeros(shape, f32)
-    for p in range(count):
+    for p in range(stacked.shape[0] // sz.rank):
         reduced = jnp.where(panel_here == p, low[:, p * sz.rank : (p + 1) * sz.rank], reduced)
+    return values.astype(bf16), reduced
+
+
+def project_own_kernel(sz, table, matrix, own, *refs):
+    panels, (stacked, values, low) = refs[:-3], refs[-3:]
+    for p, panel in enumerate(panels):
+        stacked[p * sz.rank : (p + 1) * sz.rank] = panel[...]
+    values[...], low[...] = project_half(
+        sz, table, matrix, own, stacked, lax.axis_index("owner")
+    )
+
+
+def project_other_kernel(sz, table, matrix, other, stacked, values_own, low_own, *refs):
+    outs, (product, reduced) = refs[: sz.seq], refs[sz.seq :]
+    here, core = lax.axis_index("seq"), lax.axis_index("owner")
+    values_other, low_other = project_half(sz, table, matrix, other, stacked, 1 - core)
+    pairs = ((values_own[...], low_own[...], core), (values_other, low_other, 1 - core))
+    for values, low, owner in pairs:
+        for chip in range(sz.seq):
+            first = pl.multiple_of(chip * sz.rows + owner * sz.rows_half, sz.rows_half)
+            taken = slice(chip * sz.rows_half, (chip + 1) * sz.rows_half)
+            product[pl.ds(first, sz.rows_half), :] = values[taken]
+            reduced[pl.ds(first, sz.rows_half), :] = low[taken]
     half = sz.tokens // 2
     packed = jnp.concatenate([reduced[:half], reduced[half:]], axis=1).astype(bf16)
-    for out in outs:
+    for k, out in enumerate(outs):
+        first = pl.multiple_of((here ^ k) * HEAD_SIZE, HEAD_SIZE)
+        out[: sz.tokens] = product[:, pl.ds(first, HEAD_SIZE)]
         out[sz.tokens :] = packed
 
 
@@ -254,7 +270,7 @@
     outs, (wide, raise_all, raise_picked, mixed) = refs[: sz.seq], refs[sz.seq :]
     here = lax.axis_index("seq")
     parts = (sz.group_size + 1) * (sz.rows // sz.rows_half)
-    for k, piece in enumerate(pieces):
+    for k, piece in zip(sz.order, pieces):
         size = sz.slots_here * sz.rank
         unpack(sz, piece, raise_all, parts, k * size, size)
     position = lax.broadcasted_iota(jnp.int32, (sz.tokens, sz.rank), 0)
@@ -286,7 +302,7 @@
     pieces, out = refs[: sz.seq], refs[sz.seq]
     here = lax.axis_index("seq")
     wide = sz.group_size * HEAD_SIZE
-    for k, piece in enumerate(pieces):
+    for k, piece in zip(sz.order, pieces):
         head = here ^ k
         out[:, pl.ds(pl.multiple_of(head * wide, wide), wide)] = piece[...]
 
@@ -294,6 +310,10 @@
 def by_heads(sz, x, queries, keys, gain, base, down, up, lengths, adapters, ranks, slots):
     around = range(1, sz.seq)
     half_columns = base.shape[1] // 2
+
+    def ordered(values):
+        return [values[k] for k in sz.order]
+
     spread = (2 * sz.rows_half, sz.span)
 
     def call(kernel, name, ins, outs, args, scratch=(), params=PARAMS):
@@ -314,7 +334,6 @@
         [((sz.rank, sz.span), bf16, VMEM)] * sz.side,
         (jnp.swapaxes(down, 1, 2),),
         (pltpu.SemaphoreType.DMA((sz.side,)),),
-        FIRST,
     )
     panels = []
     for m in range(sz.side):
@@ -342,14 +361,13 @@
         ),
         FIRST,
     )
-    rows_in = [rows_out[0]] + [swap(rows_out[k], "seq", k) for k in around]
-
-    (table,) = call(
+    table, held = call(
         table_kernel,
         "table",
-        [SMEM] * 4,
-        [((4, sz.requests), jnp.int32, SMEM)],
-        (lengths, adapters, ranks, slots),
+        [SMEM] * 4 + [ANY],
+        [((4, sz.requests), jnp.int32, SMEM), (spread, bf16, VMEM)],
+        (lengths, adapters, ranks, slots, rows_out[0]),
+        (pltpu.SemaphoreType.DMA,),
     )
     (matrix,) = call(
         matrix_kernel,
@@ -359,17 +377,23 @@
         (base, swap(base, "owner", 1)),
         (pltpu.SemaphoreType.DMA((2,)),),
     )
-
-    panels, rows_out = lax.optimization_barrier((panels, rows_out))
+    rows_in = [held] + [swap(rows_out[k], "seq", k) for k in around]
+
+    panels[0], table, matrix, held = lax.optimization_barrier((panels[0], table, matrix, held))
+    rows_ready = rows_out[0]
+    for m in range(sz.side):
+        panels[m], rows_ready = lax.optimization_barrier((panels[m], rows_ready))
+    rows_in[0] = held
     panels = panels + [swap(p, "groups", k) for k in range(1, sz.groups) for p in panels]
     panels = panels + [swap(p, "owner", 1) for p in panels]
-    rows_in, table, matrix, panels = lax.optimization_barrier((rows_in, table, matrix, panels))
+    rows_ordered, panels = lax.optimization_barrier(([rows_in[k] for k in [0, 1, 3, 2]], panels))
+    rows_in = [rows_ordered[[0, 1, 3, 2].index(k)] for k in range(sz.seq)]
     (own,) = call(
         gather_kernel,
         "gather_rows",
         [VMEM] * sz.seq,
         [((sz.seq * sz.rows_half, sz.span), bf16, VMEM)],
-        rows_in,
+        ordered(rows_in),
     )
     other = swap(own, "owner", 1)
     (softmax,) = call(
@@ -377,7 +401,7 @@
         "softmax_rows",
         [SMEM] + [VMEM] * sz.seq,
         [((sz.group_size, sz.tokens, sz.tokens), bf16, VMEM)],
-        (table, *rows_in),
+        (table, *ordered(rows_in)),
         (
             pltpu.VMEM((sz.group_size, sz.tokens, HEAD_SIZE), bf16),
             pltpu.VMEM((sz.tokens, HEAD_SIZE), bf16),
@@ -385,17 +409,25 @@
     )
 
     partial_shape = (sz.tokens + sz.tokens // 2, HEAD_SIZE)
+    rows_half_all = sz.seq * sz.rows_half
+    stacked, values_own, low_own = call(
+        project_own_kernel,
+        "project_own",
+        [SMEM] + [VMEM] * (2 + len(panels)),
+        [
+            ((len(panels) * sz.rank, sz.span), bf16, VMEM),
+            ((rows_half_all, half_columns), bf16, VMEM),
+            ((rows_half_all, sz.rank), f32, VMEM),
+        ],
+        (table, matrix, own, *panels),
+    )
     partial_out = call(
-        project_kernel,
-        "project",
-        [SMEM] + [VMEM] * (3 + len(panels)),
+        project_other_kernel,
+        "project_other",
+        [SMEM] + [VMEM] * 5,
         [(partial_shape, bf16, VMEM)] * sz.seq,
-        (table, matrix, own, other, *panels),
-        (
-            pltpu.VMEM((sz.tokens, sz.span), bf16),
-            pltpu.VMEM((len(panels) * sz.rank, sz.span), bf16),
-            pltpu.VMEM((sz.tokens, half_columns), bf16),
-        ),
+        (table, matrix, other, stacked, values_own, low_own),
+        (pltpu.VMEM((sz.tokens, half_columns), bf16), pltpu.VMEM((sz.tokens, sz.rank), f32)),
     )
     partial_in = [partial_out[0]] + [swap(partial_out[k], "seq", k) for k in around]
     wide = sz.group_size * HEAD_SIZE
@@ -404,7 +436,7 @@
         "mix_values",
         [SMEM] + [VMEM] * (1 + 2 * sz.seq),
         [((sz.rows, wide), bf16, VMEM)] * sz.seq,
-        (table, softmax, *rows_in, *partial_in),
+        (table, softmax, *ordered(rows_in), *ordered(partial_in)),
         (
             pltpu.VMEM((sz.tokens, sz.requests * sz.rank), bf16),
             pltpu.VMEM((sz.seq * sz.slots_here * sz.rank, HEAD_SIZE), bf16),
@@ -418,7 +450,7 @@
         "place_heads",
         [VMEM] * sz.seq,
         [((sz.rows, sz.seq * wide), bf16, VMEM)],
-        mixed_in,
+        ordered(mixed_in),
     )
     return result
 

time: 59 us -> 54.4 us (0.922)
  starting transfers between devices: 28.2 us -> 23 us
  local copies, waits for them, and re-layouts: 0.64 us -> 2.04 us
  waiting for transfers between devices: 19.7 us -> 18.9 us
    ppermute x17, starting transfers between devices: 23.9 us -> 19.6 us  [swap(): lax.ppermute(value, axis, [(i, i ^ mask) for i in range(lax.axis_size(axi...]
    unnamed x12 -> x16, local copies, waits for them, and re-layouts: 0.64 us -> 2.04 us
    ppermute x2, starting transfers between devices: 4.28 us -> 3.41 us  [by_heads(): panels.append(lax.ppermute(panels_out[m], ('seq', 'owner'), pairs))]
    ppermute x17, waiting for transfers between devices: 19.7 us -> 18.9 us  [swap(): lax.ppermute(value, axis, [(i, i ^ mask) for i in range(lax.axis_size(axi...]
    pallas_call x9 -> x10, Pallas kernels: 10.1 us -> 10 us  [call(): pl.pallas_call(functools.partial(kernel, sz), out_shape=[jax.ShapeDtypeSt...]
  transfers between devices with their start and end apart: 19 -> 19, of which waited for: 6 -> 8; matrix products, arithmetic and copies ran while one was open for 0% -> 0% of each run, Pallas kernels for 11% -> 12%
where the time goes in v3:
time: 54.4 us; the launch traced here: 54.2 us
  starting transfers between devices  23 us (42%)
  waiting for transfers between devices  18.9 us (35%)
  Pallas kernels  10 us (18%)
  local copies, waits for them, and re-layouts  2.04 us (4%)
    ppermute x17, starting transfers between devices, swap(): lax.ppermute(value, axis, [(i, i ^ mask) for i in range(lax.axis_size(axi...  19.6 us
    ppermute x17, waiting for transfers between devices, swap(): lax.ppermute(value, axis, [(i, i ^ mask) for i in range(lax.axis_size(axi...  18.9 us
    pallas_call x10, Pallas kernels, call(): pl.pallas_call(functools.partial(kernel, sz), out_shape=[jax.ShapeDtypeSt...  10 us
    ppermute x2, starting transfers between devices, by_heads(): panels.append(lax.ppermute(panels_out[m], ('seq', 'owner'), pairs))  3.41 us
    unnamed x16, local copies, waits for them, and re-layouts  2.04 us
  transfers between devices with their start and end apart: 19, of which 8 were waited for; matrix products, arithmetic and copies ran while one was open for 0% of the time, Pallas kernels for 12%

profile of v3, /device:TPU:0, one launch (start us, length us, event | category | flops | bytes accessed | tf_op | source)
XLA Modules:
  0.0 54.2 jit_solution(726570339455167466)
XLA Ops:
  0.0 0.5 collective-permute-start.1
  0.5 1.1 %copy-done.1 = bf16[1,2,2688,64]{2,3,1,0:T(8,128)(2,1)S(1)} copy-done((bf16[1,2,2688,64]{2,3,1,0:T(8,128)(2,1)S(1)}, bf16[1,2,2688,64]{2,3,1,0:T(8,128)(2,1)}, u32[]{:S(2)}) %copy-start.1) | copy-done | bytes 688152
  1.6 0.1 panels_out.1
  1.7 2.7 %collective-permute-start.5 = (bf16[64,1408]{1,0:T(8,128)(2,1)S(1)}, bf16[64,1408]{1,0:T(8,128)(2,1)S(1)}, u32[]{:S(2)}, u32[]{:S(2)}) collective-permute-start(bf16[64,1408]{1,0:T(8,128)(2,1)S(1)} %get-tuple-element.54), channel_id=1, source_target_pairs={{0,4},{1,12},{4,0},{5,8},{8,5},{9,13},{12,1},{13,9},{2,6},{3,14},{... | collective-permute-start | bytes 540680 | tf_op jit(solution)/shard_map/ppermute | solution.py:345
  4.4 0.7 %collective-permute-start = (bf16[64,1408]{1,0:T(8,128)(2,1)S(1)}, bf16[64,1408]{1,0:T(8,128)(2,1)S(1)}, u32[]{:S(2)}, u32[]{:S(2)}) collective-permute-start(bf16[64,1408]{1,0:T(8,128)(2,1)S(1)} %get-tuple-element.42), channel_id=1, source_target_pairs={{0,0},{1,8},{4,4},{5,12},{8,1},{9,9},{12,5},{13,13},{2,2},{3,10},{... | collective-permute-start | bytes 540680 | tf_op jit(solution)/shard_map/ppermute | solution.py:345
  5.1 2.2 %norm_rows.1 = (bf16[64,1408]{1,0:T(8,128)(2,1)}, bf16[64,1408]{1,0:T(8,128)(2,1)}, bf16[64,1408]{1,0:T(8,128)(2,1)}, bf16[64,1408]{1,0:T(8,128)(2,1)}) custom-call(bf16[64,5376]{1,0:T(8,128)(2,1)} %bitcast.12, f32[1,5376]{1,0:T(1,128)} %gain.1, bf16[64,1024]{1,0:T(8,128)(2,1)} %bitcast.13, bf16[64,512]{1,0:T(8,128)(2,1)} %bitcast.15, ...), custom_call_target="tpu_custom_call" | custom-call | tf_op jit(solution)/shard_map/norm_rows/pallas_call | solution.py:320
  7.3 0.1 collective-permute-start.2
  7.4 7.3 %collective-permute-start.3 = (bf16[64,1408]{1,0:T(8,128)(2,1)}, bf16[64,1408]{1,0:T(8,128)(2,1)S(1)}, u32[]{:S(2)}, u32[]{:S(2)}) collective-permute-start(bf16[64,1408]{1,0:T(8,128)(2,1)} %get-tuple-element.50), channel_id=1, source_target_pairs={{0,12},{4,8},{8,4},{12,0},{1,13},{5,9},{9,5},{13,1},{2,14},{6,10},... | collective-permute-start | bytes 540680 | tf_op jit(solution)/shard_map/ppermute | solution.py:31
  14.8 0.9 %copy-done.2 = bf16[64,1408]{1,0:T(8,128)(2,1)S(1)} copy-done((bf16[64,1408]{1,0:T(8,128)(2,1)S(1)}, bf16[64,1408]{1,0:T(8,128)(2,1)}, u32[]{:S(2)}) %copy-start.2) | copy-done | bytes 180248
  15.7 1.5 %table.1 = (s32[4,4]{1,0:T(4,128)S(1)}, bf16[64,1408]{1,0:T(8,128)(2,1)S(1)}) custom-call(s32[4]{0:T(128)S(1)} %copy-done.3, s32[4]{0:T(128)S(1)} %copy-done.4, s32[8]{0:T(128)S(1)} %copy-done.5, s32[8]{0:T(128)S(1)} %copy-done.6, bf16[64,1408]{1,0:T(8,128)(2,1)S(1)} %copy-done.2), custom_call_target="tpu_custom_call" | custom-call | tf_op jit(solution)/shard_map/table/pallas_call | solution.py:320
  17.2 0.0 collective-permute-done.5.refs_1_
  17.2 1.6 %collective-permute-start.7 = (bf16[64,1408]{1,0:T(8,128)(2,1)S(1)}, bf16[64,1408]{1,0:T(8,128)(2,1)S(1)}, u32[]{:S(2)}, u32[]{:S(2)}) collective-permute-start(bf16[64,1408]{1,0:T(8,128)(2,1)S(1)} %collective-permute-done.5.refs_1_), channel_id=1, source_target_pairs={{0,16},{16,0},{1,17},{17,1},{2,18},{18,2},{3,19},{19,3},{4,20},{20... | collective-permute-start | bytes 540680 | tf_op jit(solution)/shard_map/ppermute | solution.py:31
  18.8 0.0 collective-permute-done.1.base_other
  18.8 0.2 matrix_rows.1.matrix
  19.1 0.0 collective-permute-done.refs_0_
  19.1 0.6 %collective-permute-start.6 = (bf16[64,1408]{1,0:T(8,128)(2,1)S(1)}, bf16[64,1408]{1,0:T(8,128)(2,1)S(1)}, u32[]{:S(2)}, u32[]{:S(2)}) collective-permute-start(bf16[64,1408]{1,0:T(8,128)(2,1)S(1)} %collective-permute-done.refs_0_), channel_id=1, source_target_pairs={{0,16},{16,0},{1,17},{17,1},{2,18},{18,2},{3,19},{19,3},{4,20},{20... | collective-permute-start | bytes 540680 | tf_op jit(solution)/shard_map/ppermute | solution.py:31
  19.7 0.0 collective-permute-start.4
  19.7 0.0 collective-permute-done.2.refs_3_
  19.7 0.1 collective-permute-start.9
  19.8 4.4 %collective-permute-done.7.refs_3_ = bf16[64,1408]{1,0:T(8,128)(2,1)S(1)} collective-permute-done((bf16[64,1408]{1,0:T(8,128)(2,1)S(1)}, bf16[64,1408]{1,0:T(8,128)(2,1)S(1)}, u32[]{:S(2)}, u32[]{:S(2)}) %collective-permute-start.7) | collective-permute-done | bytes 180256 | tf_op jit(solution)/shard_map/ppermute | solution.py:31
  24.1 0.0 collective-permute-start.11
  24.1 0.0 collective-permute-done.3.refs_1_
  24.1 0.5 collective-permute-start.8
  24.7 1.4 %collective-permute-done.6.refs_2_ = bf16[64,1408]{1,0:T(8,128)(2,1)S(1)} collective-permute-done((bf16[64,1408]{1,0:T(8,128)(2,1)S(1)}, bf16[64,1408]{1,0:T(8,128)(2,1)S(1)}, u32[]{:S(2)}, u32[]{:S(2)}) %collective-permute-start.6) | collective-permute-done | bytes 180256 | tf_op jit(solution)/shard_map/ppermute | solution.py:31
  26.1 0.0 collective-permute-start.10
  26.1 5.0 %collective-permute-done.4.refs_2_ = bf16[64,1408]{1,0:T(8,128)(2,1)S(1)} collective-permute-done((bf16[64,1408]{1,0:T(8,128)(2,1)S(1)}, bf16[64,1408]{1,0:T(8,128)(2,1)S(1)}, u32[]{:S(2)}, u32[]{:S(2)}) %collective-permute-start.4) | collective-permute-done | bytes 180256 | tf_op jit(solution)/shard_map/ppermute | solution.py:31
  31.1 0.0 collective-permute-done.9.refs_5_
  31.1 0.0 collective-permute-done.11.refs_7_
  31.1 0.0 collective-permute-done.8.refs_4_
  31.1 0.0 collective-permute-done.10.refs_6_
  31.2 0.1 collective-permute-start.12
  31.2 1.5 %project_own.1 = (bf16[512,1408]{1,0:T(8,128)(2,1)S(1)}, bf16[128,512]{1,0:T(8,128)(2,1)S(1)}, f32[128,64]{1,0:T(8,128)S(1)}) custom-call(s32[4,4]{1,0:T(4,128)S(1)} %get-tuple-element.47.table, bf16[1408,512]{1,0:T(8,128)(2,1)S(1)} %matrix_rows.1.matrix, bf16[128,1408]{1,0:T(8,128)(2,1)S(1)} %gather_rows.1.own, ...), custom_call_target="tpu_custom_call" | custom-call | tf_op jit(solution)/shard_map/project_own/pallas_call | solution.py:320
  32.8 0.1 collective-permute-done.12.other
  32.9 1.6 %project_other.1 = (bf16[384,128]{1,0:T(8,128)(2,1)S(1)}, bf16[384,128]{1,0:T(8,128)(2,1)S(1)}, bf16[384,128]{1,0:T(8,128)(2,1)S(1)}, bf16[384,128]{1,0:T(8,128)(2,1)S(1)}) custom-call(s32[4,4]{1,0:T(4,128)S(1)} %get-tuple-element.47.table, bf16[1408,512]{1,0:T(8,128)(2,1)S(1)} %matrix_rows.1.matrix, bf16[128,1408]{1,0:T(8,128)(2,1)S(1)} %collective-permute-done.12.other, ...), custom_call_target="tpu_custom_call" | custom-call | tf_op jit(solution)/shard_map/project_other/pallas_call | solution.py:320
  34.5 1.9 %collective-permute-start.13 = (bf16[384,128]{1,0:T(8,128)(2,1)S(1)}, bf16[384,128]{1,0:T(8,128)(2,1)S(1)}, u32[]{:S(2)}, u32[]{:S(2)}) collective-permute-start(bf16[384,128]{1,0:T(8,128)(2,1)S(1)} %get-tuple-element.72), channel_id=1, source_target_pairs={{0,12},{4,8},{8,4},{12,0},{1,13},{5,9},{9,5},{13,1},{2,14},{6,10},... | collective-permute-start | bytes 294920 | tf_op jit(solution)/shard_map/ppermute | solution.py:31
  36.5 0.0 collective-permute-start.14
  36.5 2.5 %collective-permute-start.15 = (bf16[384,128]{1,0:T(8,128)(2,1)S(1)}, bf16[384,128]{1,0:T(8,128)(2,1)S(1)}, u32[]{:S(2)}, u32[]{:S(2)}) collective-permute-start(bf16[384,128]{1,0:T(8,128)(2,1)S(1)} %get-tuple-element.74), channel_id=1, source_target_pairs={{0,4},{4,0},{8,12},{12,8},{1,5},{5,1},{9,13},{13,9},{2,6},{6,2},{1... | collective-permute-start | bytes 294920 | tf_op jit(solution)/shard_map/ppermute | solution.py:31
  39.0 1.0 %softmax_rows.1.softmax = bf16[2,256,256]{2,1,0:T(8,128)(2,1)S(1)} custom-call(s32[4,4]{1,0:T(4,128)S(1)} %get-tuple-element.47.table, bf16[64,1408]{1,0:T(8,128)(2,1)S(1)} %get-tuple-element.55.refs_0_, bf16[64,1408]{1,0:T(8,128)(2,1)S(1)} %collective-permute-done.3.refs_1_, bf16[64,1408]{1,0:T(8,128)(2,1)S(1)} %collective-permute-done.4.refs_2_, ...), custom_call_target="tpu_custom_call" | custom-call | tf_op jit(solution)/shard_map/softmax_rows/pallas_call | solution.py:320
  40.0 2.1 %collective-permute-done.13.refs_5_ = bf16[384,128]{1,0:T(8,128)(2,1)S(1)} collective-permute-done((bf16[384,128]{1,0:T(8,128)(2,1)S(1)}, bf16[384,128]{1,0:T(8,128)(2,1)S(1)}, u32[]{:S(2)}, u32[]{:S(2)}) %collective-permute-start.13) | collective-permute-done | bytes 98336 | tf_op jit(solution)/shard_map/ppermute | solution.py:31
  42.1 3.5 %collective-permute-done.14.refs_6_ = bf16[384,128]{1,0:T(8,128)(2,1)S(1)} collective-permute-done((bf16[384,128]{1,0:T(8,128)(2,1)S(1)}, bf16[384,128]{1,0:T(8,128)(2,1)S(1)}, u32[]{:S(2)}, u32[]{:S(2)}) %collective-permute-start.14) | collective-permute-done | bytes 98336 | tf_op jit(solution)/shard_map/ppermute | solution.py:31
  45.7 0.0 collective-permute-done.15.refs_7_
  45.7 1.1 %mix_values.1 = (bf16[64,256]{1,0:T(8,128)(2,1)S(1)}, bf16[64,256]{1,0:T(8,128)(2,1)S(1)}, bf16[64,256]{1,0:T(8,128)(2,1)S(1)}, bf16[64,256]{1,0:T(8,128)(2,1)S(1)}) custom-call(s32[4,4]{1,0:T(4,128)S(1)} %get-tuple-element.47.table, bf16[2,256,256]{2,1,0:T(8,128)(2,1)S(1)} %softmax_rows.1.softmax, bf16[64,1408]{1,0:T(8,128)(2,1)S(1)} %get-tuple-element.55.refs_0_, ...), custom_call_target="tpu_custom_call" | custom-call | tf_op jit(solution)/shard_map/mix_values/pallas_call | solution.py:320
  46.8 1.9 %collective-permute-start.16 = (bf16[64,256]{1,0:T(8,128)(2,1)S(1)}, bf16[64,256]{1,0:T(8,128)(2,1)S(1)}, u32[]{:S(2)}, u32[]{:S(2)}) collective-permute-start(bf16[64,256]{1,0:T(8,128)(2,1)S(1)} %get-tuple-element.76), channel_id=1, source_target_pairs={{0,12},{4,8},{8,4},{12,0},{1,13},{5,9},{9,5},{13,1},{2,14},{6,10},... | collective-permute-start | bytes 98312 | tf_op jit(solution)/shard_map/ppermute | solution.py:31
  48.7 2.5 %collective-permute-start.18 = (bf16[64,256]{1,0:T(8,128)(2,1)S(1)}, bf16[64,256]{1,0:T(8,128)(2,1)S(1)}, u32[]{:S(2)}, u32[]{:S(2)}) collective-permute-start(bf16[64,256]{1,0:T(8,128)(2,1)S(1)} %get-tuple-element.78), channel_id=1, source_target_pairs={{0,4},{4,0},{8,12},{12,8},{1,5},{5,1},{9,13},{13,9},{2,6},{6,2},{1... | collective-permute-start | bytes 98312 | tf_op jit(solution)/shard_map/ppermute | solution.py:31
  51.2 1.4 %collective-permute-done.16.refs_1_ = bf16[64,256]{1,0:T(8,128)(2,1)S(1)} collective-permute-done((bf16[64,256]{1,0:T(8,128)(2,1)S(1)}, bf16[64,256]{1,0:T(8,128)(2,1)S(1)}, u32[]{:S(2)}, u32[]{:S(2)}) %collective-permute-start.16) | collective-permute-done | bytes 32800 | tf_op jit(solution)/shard_map/ppermute | solution.py:31
  52.7 0.9 %collective-permute-done.17.refs_2_ = bf16[64,256]{1,0:T(8,128)(2,1)S(1)} collective-permute-done((bf16[64,256]{1,0:T(8,128)(2,1)S(1)}, bf16[64,256]{1,0:T(8,128)(2,1)S(1)}, u32[]{:S(2)}, u32[]{:S(2)}) %collective-permute-start.17) | collective-permute-done | bytes 32800 | tf_op jit(solution)/shard_map/ppermute | solution.py:31
  53.5 0.0 collective-permute-done.18.refs_3_
  53.5 0.7 %place_heads.1 = bf16[64,1024]{1,0:T(8,128)(2,1)} custom-call(bf16[64,256]{1,0:T(8,128)(2,1)S(1)} %get-tuple-element.75.refs_0_, bf16[64,256]{1,0:T(8,128)(2,1)S(1)} %collective-permute-done.16.refs_1_, bf16[64,256]{1,0:T(8,128)(2,1)S(1)} %collective-permute-done.17.refs_2_, bf16[64,256]{1,0:T(8,128)(2,1)S(1)} %collective-permute-done.18.refs_3_), custom_call_target="tpu_custom_call" | custom-call | tf_op jit(solution)/shard_map/place_heads/pallas_call | solution.py:320
  (16 shorter events, 0.1 us)
Async XLA Ops:
  0.0 18.8 %copy-start = (bf16[1,672,1024]{2,1,0:T(8,128)(2,1)S(1)}, bf16[1,672,1024]{2,1,0:T(8,128)(2,1)}, u32[]{:S(2)}) copy-start(bf16[1,672,1024]{2,1,0:T(8,128)(2,1)} %param.15) | copy-start | bytes 4128772
  0.0 18.8 %collective-permute-start.1 = (bf16[672,1024]{1,0:T(8,128)(2,1)}, bf16[672,1024]{1,0:T(8,128)(2,1)S(1)}, u32[]{:S(2)}, u32[]{:S(2)}) collective-permute-start(bf16[672,1024]{1,0:T(8,128)(2,1)} %bitcast.9), channel_id=1, source_target_pairs={{0,1},{1,0},{2,3},{3,2},{4,5},{5,4},{6,7},{7,6},{8,9},{9,8},{10,11... | collective-permute-start | bytes 4128776 | tf_op jit(solution)/shard_map/ppermute | solution.py:31
  0.5 1.1 %copy-start.1 = (bf16[1,2,2688,64]{2,3,1,0:T(8,128)(2,1)S(1)}, bf16[1,2,2688,64]{2,3,1,0:T(8,128)(2,1)}, u32[]{:S(2)}) copy-start(bf16[1,2,2688,64]{2,3,1,0:T(8,128)(2,1)} %param.16) | copy-start | bytes 2064388
  1.6 13.2 %copy-start.3 = (s32[4]{0:T(128)S(1)}, s32[4]{0:T(128)}, u32[]{:S(2)}) copy-start(s32[4]{0:T(128)} %lengths.1) | copy-start | bytes 52
  1.6 13.2 %copy-start.4 = (s32[4]{0:T(128)S(1)}, s32[4]{0:T(128)}, u32[]{:S(2)}) copy-start(s32[4]{0:T(128)} %adapters.1) | copy-start | bytes 52
  1.6 13.2 %copy-start.5 = (s32[8]{0:T(128)S(1)}, s32[8]{0:T(128)}, u32[]{:S(2)}) copy-start(s32[8]{0:T(128)} %ranks.1) | copy-start | bytes 100
  1.6 13.2 %copy-start.6 = (s32[8]{0:T(128)S(1)}, s32[8]{0:T(128)}, u32[]{:S(2)}) copy-start(s32[8]{0:T(128)} %slots.1) | copy-start | bytes 100
  1.7 15.6 %collective-permute-start.5 = (bf16[64,1408]{1,0:T(8,128)(2,1)S(1)}, bf16[64,1408]{1,0:T(8,128)(2,1)S(1)}, u32[]{:S(2)}, u32[]{:S(2)}) collective-permute-start(bf16[64,1408]{1,0:T(8,128)(2,1)S(1)} %get-tuple-element.54), channel_id=1, source_target_pairs={{0,4},{1,12},{4,0},{5,8},{8,5},{9,13},{12,1},{13,9},{2,6},{3,14},{... | collective-permute-start | bytes 540680 | tf_op jit(solution)/shard_map/ppermute | solution.py:345
  4.4 14.6 %collective-permute-start = (bf16[64,1408]{1,0:T(8,128)(2,1)S(1)}, bf16[64,1408]{1,0:T(8,128)(2,1)S(1)}, u32[]{:S(2)}, u32[]{:S(2)}) collective-permute-start(bf16[64,1408]{1,0:T(8,128)(2,1)S(1)} %get-tuple-element.42), channel_id=1, source_target_pairs={{0,0},{1,8},{4,4},{5,12},{8,1},{9,9},{12,5},{13,13},{2,2},{3,10},{... | collective-permute-start | bytes 540680 | tf_op jit(solution)/shard_map/ppermute | solution.py:345
  7.3 12.3 %collective-permute-start.2 = (bf16[64,1408]{1,0:T(8,128)(2,1)}, bf16[64,1408]{1,0:T(8,128)(2,1)S(1)}, u32[]{:S(2)}, u32[]{:S(2)}) collective-permute-start(bf16[64,1408]{1,0:T(8,128)(2,1)} %get-tuple-element.49), channel_id=1, source_target_pairs={{0,4},{4,0},{8,12},{12,8},{1,5},{5,1},{9,13},{13,9},{2,6},{6,2},{1... | collective-permute-start | bytes 540680 | tf_op jit(solution)/shard_map/ppermute | solution.py:31
  7.4 16.7 %collective-permute-start.3 = (bf16[64,1408]{1,0:T(8,128)(2,1)}, bf16[64,1408]{1,0:T(8,128)(2,1)S(1)}, u32[]{:S(2)}, u32[]{:S(2)}) collective-permute-start(bf16[64,1408]{1,0:T(8,128)(2,1)} %get-tuple-element.50), channel_id=1, source_target_pairs={{0,12},{4,8},{8,4},{12,0},{1,13},{5,9},{9,5},{13,1},{2,14},{6,10},... | collective-permute-start | bytes 540680 | tf_op jit(solution)/shard_map/ppermute | solution.py:31
  14.8 0.9 %copy-start.2 = (bf16[64,1408]{1,0:T(8,128)(2,1)S(1)}, bf16[64,1408]{1,0:T(8,128)(2,1)}, u32[]{:S(2)}) copy-start(bf16[64,1408]{1,0:T(8,128)(2,1)} %get-tuple-element.44.piece) | copy-start | bytes 540676
  17.2 2.4 %copy-start.7 = (bf16[64,1408]{1,0:T(8,128)(2,1)S(1)}, bf16[64,1408]{1,0:T(8,128)(2,1)}, u32[]{:S(2)}) copy-start(bf16[64,1408]{1,0:T(8,128)(2,1)} %get-tuple-element.51) | copy-start | bytes 540676
  17.2 6.9 %collective-permute-start.7 = (bf16[64,1408]{1,0:T(8,128)(2,1)S(1)}, bf16[64,1408]{1,0:T(8,128)(2,1)S(1)}, u32[]{:S(2)}, u32[]{:S(2)}) collective-permute-start(bf16[64,1408]{1,0:T(8,128)(2,1)S(1)} %collective-permute-done.5.refs_1_), channel_id=1, source_target_pairs={{0,16},{16,0},{1,17},{17,1},{2,18},{18,2},{3,19},{19,3},{4,20},{20... | collective-permute-start | bytes 540680 | tf_op jit(solution)/shard_map/ppermute | solution.py:31
  19.1 7.0 %collective-permute-start.6 = (bf16[64,1408]{1,0:T(8,128)(2,1)S(1)}, bf16[64,1408]{1,0:T(8,128)(2,1)S(1)}, u32[]{:S(2)}, u32[]{:S(2)}) collective-permute-start(bf16[64,1408]{1,0:T(8,128)(2,1)S(1)} %collective-permute-done.refs_0_), channel_id=1, source_target_pairs={{0,16},{16,0},{1,17},{17,1},{2,18},{18,2},{3,19},{19,3},{4,20},{20... | collective-permute-start | bytes 540680 | tf_op jit(solution)/shard_map/ppermute | solution.py:31
  19.7 11.4 %collective-permute-start.4 = (bf16[64,1408]{1,0:T(8,128)(2,1)S(1)}, bf16[64,1408]{1,0:T(8,128)(2,1)S(1)}, u32[]{:S(2)}, u32[]{:S(2)}) collective-permute-start(bf16[64,1408]{1,0:T(8,128)(2,1)S(1)} %copy-done.7), channel_id=1, source_target_pairs={{0,8},{4,12},{8,0},{12,4},{1,9},{5,13},{9,1},{13,5},{2,10},{6,14},... | collective-permute-start | bytes 540680 | tf_op jit(solution)/shard_map/ppermute | solution.py:31
  19.7 11.4 %collective-permute-start.9 = (bf16[64,1408]{1,0:T(8,128)(2,1)S(1)}, bf16[64,1408]{1,0:T(8,128)(2,1)S(1)}, u32[]{:S(2)}, u32[]{:S(2)}) collective-permute-start(bf16[64,1408]{1,0:T(8,128)(2,1)S(1)} %collective-permute-done.5.refs_1_), channel_id=1, source_target_pairs={{0,1},{1,0},{2,3},{3,2},{4,5},{5,4},{6,7},{7,6},{8,9},{9,8},{10,11... | collective-permute-start | bytes 540680 | tf_op jit(solution)/shard_map/ppermute | solution.py:31
  24.1 7.0 %collective-permute-start.11 = (bf16[64,1408]{1,0:T(8,128)(2,1)S(1)}, bf16[64,1408]{1,0:T(8,128)(2,1)S(1)}, u32[]{:S(2)}, u32[]{:S(2)}) collective-permute-start(bf16[64,1408]{1,0:T(8,128)(2,1)S(1)} %collective-permute-done.7.refs_3_), channel_id=1, source_target_pairs={{0,1},{1,0},{2,3},{3,2},{4,5},{5,4},{6,7},{7,6},{8,9},{9,8},{10,11... | collective-permute-start | bytes 540680 | tf_op jit(solution)/shard_map/ppermute | solution.py:31
  24.1 7.0 %collective-permute-start.8 = (bf16[64,1408]{1,0:T(8,128)(2,1)S(1)}, bf16[64,1408]{1,0:T(8,128)(2,1)S(1)}, u32[]{:S(2)}, u32[]{:S(2)}) collective-permute-start(bf16[64,1408]{1,0:T(8,128)(2,1)S(1)} %collective-permute-done.refs_0_), channel_id=1, source_target_pairs={{0,1},{1,0},{2,3},{3,2},{4,5},{5,4},{6,7},{7,6},{8,9},{9,8},{10,11... | collective-permute-start | bytes 540680 | tf_op jit(solution)/shard_map/ppermute | solution.py:31
  26.1 5.0 %collective-permute-start.10 = (bf16[64,1408]{1,0:T(8,128)(2,1)S(1)}, bf16[64,1408]{1,0:T(8,128)(2,1)S(1)}, u32[]{:S(2)}, u32[]{:S(2)}) collective-permute-start(bf16[64,1408]{1,0:T(8,128)(2,1)S(1)} %collective-permute-done.6.refs_2_), channel_id=1, source_target_pairs={{0,1},{1,0},{2,3},{3,2},{4,5},{5,4},{6,7},{7,6},{8,9},{9,8},{10,11... | collective-permute-start | bytes 540680 | tf_op jit(solution)/shard_map/ppermute | solution.py:31
  31.2 1.7 %collective-permute-start.12 = (bf16[128,1408]{1,0:T(8,128)(2,1)S(1)}, bf16[128,1408]{1,0:T(8,128)(2,1)S(1)}, u32[]{:S(2)}, u32[]{:S(2)}) collective-permute-start(bf16[128,1408]{1,0:T(8,128)(2,1)S(1)} %gather_rows.1.own), channel_id=1, source_target_pairs={{0,1},{1,0},{2,3},{3,2},{4,5},{5,4},{6,7},{7,6},{8,9},{9,8},{10,11... | collective-permute-start | bytes 1081352 | tf_op jit(solution)/shard_map/ppermute | solution.py:31
  34.5 7.6 %collective-permute-start.13 = (bf16[384,128]{1,0:T(8,128)(2,1)S(1)}, bf16[384,128]{1,0:T(8,128)(2,1)S(1)}, u32[]{:S(2)}, u32[]{:S(2)}) collective-permute-start(bf16[384,128]{1,0:T(8,128)(2,1)S(1)} %get-tuple-element.72), channel_id=1, source_target_pairs={{0,12},{4,8},{8,4},{12,0},{1,13},{5,9},{9,5},{13,1},{2,14},{6,10},... | collective-permute-start | bytes 294920 | tf_op jit(solution)/shard_map/ppermute | solution.py:31
  36.5 9.2 %collective-permute-start.14 = (bf16[384,128]{1,0:T(8,128)(2,1)S(1)}, bf16[384,128]{1,0:T(8,128)(2,1)S(1)}, u32[]{:S(2)}, u32[]{:S(2)}) collective-permute-start(bf16[384,128]{1,0:T(8,128)(2,1)S(1)} %get-tuple-element.73), channel_id=1, source_target_pairs={{0,8},{4,12},{8,0},{12,4},{1,9},{5,13},{9,1},{13,5},{2,10},{6,14},... | collective-permute-start | bytes 294920 | tf_op jit(solution)/shard_map/ppermute | solution.py:31
  36.5 9.2 %collective-permute-start.15 = (bf16[384,128]{1,0:T(8,128)(2,1)S(1)}, bf16[384,128]{1,0:T(8,128)(2,1)S(1)}, u32[]{:S(2)}, u32[]{:S(2)}) collective-permute-start(bf16[384,128]{1,0:T(8,128)(2,1)S(1)} %get-tuple-element.74), channel_id=1, source_target_pairs={{0,4},{4,0},{8,12},{12,8},{1,5},{5,1},{9,13},{13,9},{2,6},{6,2},{1... | collective-permute-start | bytes 294920 | tf_op jit(solution)/shard_map/ppermute | solution.py:31
  46.8 5.9 %collective-permute-start.16 = (bf16[64,256]{1,0:T(8,128)(2,1)S(1)}, bf16[64,256]{1,0:T(8,128)(2,1)S(1)}, u32[]{:S(2)}, u32[]{:S(2)}) collective-permute-start(bf16[64,256]{1,0:T(8,128)(2,1)S(1)} %get-tuple-element.76), channel_id=1, source_target_pairs={{0,12},{4,8},{8,4},{12,0},{1,13},{5,9},{9,5},{13,1},{2,14},{6,10},... | collective-permute-start | bytes 98312 | tf_op jit(solution)/shard_map/ppermute | solution.py:31
  48.7 4.8 %collective-permute-start.17 = (bf16[64,256]{1,0:T(8,128)(2,1)S(1)}, bf16[64,256]{1,0:T(8,128)(2,1)S(1)}, u32[]{:S(2)}, u32[]{:S(2)}) collective-permute-start(bf16[64,256]{1,0:T(8,128)(2,1)S(1)} %get-tuple-element.77), channel_id=1, source_target_pairs={{0,8},{4,12},{8,0},{12,4},{1,9},{5,13},{9,1},{13,5},{2,10},{6,14},... | collective-permute-start | bytes 98312 | tf_op jit(solution)/shard_map/ppermute | solution.py:31
  48.7 4.8 %collective-permute-start.18 = (bf16[64,256]{1,0:T(8,128)(2,1)S(1)}, bf16[64,256]{1,0:T(8,128)(2,1)S(1)}, u32[]{:S(2)}, u32[]{:S(2)}) collective-permute-start(bf16[64,256]{1,0:T(8,128)(2,1)S(1)} %get-tuple-element.78), channel_id=1, source_target_pairs={{0,4},{4,0},{8,12},{12,8},{1,5},{5,1},{9,13},{13,9},{2,6},{6,2},{1... | collective-permute-start | bytes 98312 | tf_op jit(solution)/shard_map/ppermute | solution.py:31

commit v4 on v3

--- a/solution.py
+++ b/solution.py
@@ -43,10 +43,14 @@
         self.features = self.width // self.seq
         self.slots_here, self.rank = down.shape[0], down.shape[2]
         self.requests = requests
+        self.slot_bits = self.slots_here.bit_length() - 1
+        self.side_bits = self.side.bit_length() - 1
         self.heads_here = up.shape[2] // HEAD_SIZE
         self.group_size = HEADS // KEY_VALUE_HEADS
         self.tokens = self.rows * self.seq
         self.order = [0, 3, 2, 1]
+        self.order_sum = [0, 2, 1, 3]
+        self.order_out = [0, 2, 3, 1]
         tiles = [
             -(-((i * self.features) % LANES + self.features) // LANES) for i in range(self.side)
         ]
@@ -67,6 +71,7 @@
             and self.rank % self.rows_half == 0
             and self.pieces() * LANES <= self.span
             and 2 * self.rank == LANES
+            and self.seq * self.rows_half == LANES
         )
 
     def pieces(self):
@@ -84,6 +89,13 @@
     for r in range(sz.requests):
         found = found + (position >= table[0, r]).astype(jnp.int32)
     return found
+
+
+def token_at(sz, place):
+    count = sz.seq * sz.rows_half
+    owner = (place >= count).astype(jnp.int32)
+    place = place - owner * count
+    return place // sz.rows_half * sz.rows + owner * sz.rows_half + place % sz.rows_half
 
 
 def table_kernel(sz, lengths, adapters, ranks, slots, piece, out, held, sem):
@@ -95,24 +107,24 @@
         end = end + lengths[r]
         adapter = adapters[r]
         slot = slots[adapter]
-        chip, local = slot // sz.slots_here, slot % sz.slots_here
-        other = jnp.where(chip // sz.side == core, 0, 1)
-        m = (here % sz.side) ^ (chip % sz.side)
+        chip, local = slot >> sz.slot_bits, slot & (sz.slots_here - 1)
+        other = (chip >> sz.side_bits) ^ core
+        m = (here ^ chip) & (sz.side - 1)
         out[0, r] = end
         out[1, r] = ranks[adapter]
-        out[2, r] = (other * sz.groups + (local ^ group)) * sz.side + m
+        out[2, r] = (((other << sz.slot_bits) | (local ^ group)) << sz.side_bits) | m
         out[3, r] = ((here ^ chip) * sz.slots_here + local) * sz.rank
     copy.wait()
 
 
 def panels_kernel(sz, down, *outs_and_sem):
     outs, sem = outs_and_sem[:-1], outs_and_sem[-1]
-    here, group = lax.axis_index("seq"), lax.axis_index("groups")
+    here = lax.axis_index("seq")
     copies = []
     for m, out in enumerate(outs):
         first = pl.multiple_of(sz.start_in_half((here % sz.side) ^ m), LANES)
         copies.append(
-            pltpu.make_async_copy(down.at[group, :, pl.ds(first, sz.span)], out, sem.at[m])
+            pltpu.make_async_copy(down.at[0, :, pl.ds(first, sz.span)], out, sem.at[m])
         )
     for copy in copies:
         copy.start()
@@ -169,18 +181,29 @@
 
 
 def softmax_kernel(sz, table, *refs):
-    pieces, out = refs[: sz.seq], refs[sz.seq]
-    query, key = refs[sz.seq + 1 :]
+    pieces, (out, raise_picked, scale, query, key, raise_all) = refs[: sz.seq], refs[sz.seq :]
     here = lax.axis_index("seq")
     parts = sz.rows // sz.rows_half
     for k, piece in zip(sz.order, pieces):
         first = (here ^ k) * sz.rows
         for c in range(sz.group_size):
             unpack(sz, piece, query.at[c], c * parts, first, sz.rows)
-        unpack(sz, piece, key, sz.group_size * parts, first, sz.rows)
+        for owner in range(parts):
+            place = sz.seq * owner * sz.rows_half + (here ^ k) * sz.rows_half
+            unpack(sz, piece, key, sz.group_size * parts + owner, place, sz.rows_half)
+        size = sz.slots_here * sz.rank
+        unpack(sz, piece, raise_all, (sz.group_size + 1) * parts, k * size, size)
+    shape = scale.shape
+    request = request_column(sz, table, token_at(sz, lax.broadcasted_iota(jnp.int32, shape, 0)))
+    rank_here = jnp.ones(shape, jnp.int32)
+    for r in range(sz.requests):
+        rank_here = jnp.where(request == r, table[1, r], rank_here)
+        first = pl.multiple_of(table[3, r], sz.rank)
+        raise_picked[r * sz.rank : (r + 1) * sz.rank] = raise_all[pl.ds(first, sz.rank), :]
+    scale[...] = adapter_strength / rank_here.astype(f32)
     shape = (sz.tokens, sz.tokens)
     mine = lax.broadcasted_iota(jnp.int32, shape, 0)
-    theirs = lax.broadcasted_iota(jnp.int32, shape, 1)
+    theirs = token_at(sz, lax.broadcasted_iota(jnp.int32, shape, 1))
     live = (theirs <= mine) & (theirs > mine - WINDOW)
     live = live & (request_column(sz, table, mine) == request_column(sz, table, theirs))
     for c in range(sz.group_size):
@@ -189,7 +212,9 @@
         )
         scores = jnp.where(live, scores * query_scale, -1e30)
         weights = jnp.exp(scores - jnp.max(scores, axis=1, keepdims=True))
-        out[c] = (weights / jnp.sum(weights, axis=1, keepdims=True)).astype(bf16)
+        out[c * sz.tokens : (c + 1) * sz.tokens] = (
+            weights / jnp.sum(weights, axis=1, keepdims=True)
+        ).astype(bf16)
 
 
 def matrix_kernel(sz, base, base_other, out, sem):
@@ -217,92 +242,83 @@
         out[pl.ds(first, sz.rows_half), :] = piece[: sz.rows_half]
 
 
-def project_half(sz, table, matrix, rows, stacked, owner):
+def project_half(sz, table, matrix, rows, picked, owner):
     values = jnp.dot(rows[...], matrix[...], preferred_element_type=f32)
     low = lax.dot_general(
-        rows[...], stacked[...], (((1,), (1,)), ((), ())), preferred_element_type=f32
-    )
-    shape = (sz.seq * sz.rows_half, sz.rank)
-    row = lax.broadcasted_iota(jnp.int32, shape, 0)
-    position = row // sz.rows_half * sz.rows + owner * sz.rows_half + row % sz.rows_half
-    request = request_column(sz, table, position)
-    column = lax.broadcasted_iota(jnp.int32, shape, 1)
-    panel_here = jnp.full(shape, -1)
+        picked[...], rows[...], (((1,), (1,)), ((), ())), preferred_element_type=f32
+    )
+    shape = (sz.rank, sz.seq * sz.rows_half)
+    place = lax.broadcasted_iota(jnp.int32, shape, 1) + owner * shape[1]
+    request = request_column(sz, table, token_at(sz, place))
+    rank = lax.broadcasted_iota(jnp.int32, shape, 0)
+    reduced = jnp.zeros(shape, f32)
     for r in range(sz.requests):
-        panel_here = jnp.where((request == r) & (column < table[1, r]), table[2, r], panel_here)
-    reduced = jnp.zeros(shape, f32)
-    for p in range(stacked.shape[0] // sz.rank):
-        reduced = jnp.where(panel_here == p, low[:, p * sz.rank : (p + 1) * sz.rank], reduced)
-    return values.astype(bf16), reduced
+        live = (request == r) & (rank < table[1, r])
+        reduced = jnp.where(live, low[r * sz.rank : (r + 1) * sz.rank], reduced)
+    return values.astype(bf16), reduced.astype(bf16)
 
 
 def project_own_kernel(sz, table, matrix, own, *refs):
-    panels, (stacked, values, low) = refs[:-3], refs[-3:]
+    panels, (picked, values, low, stacked) = refs[:-4], refs[-4:]
     for p, panel in enumerate(panels):
         stacked[p * sz.rank : (p + 1) * sz.rank] = panel[...]
+    for r in range(sz.requests):
+        first = pl.multiple_of(table[2, r] * sz.rank, sz.rank)
+        picked[r * sz.rank : (r + 1) * sz.rank] = stacked[pl.ds(first, sz.rank), :]
     values[...], low[...] = project_half(
-        sz, table, matrix, own, stacked, lax.axis_index("owner")
-    )
-
-
-def project_other_kernel(sz, table, matrix, other, stacked, values_own, low_own, *refs):
-    outs, (product, reduced) = refs[: sz.seq], refs[sz.seq :]
+        sz, table, matrix, own, picked, lax.axis_index("owner")
+    )
+
+
+def project_other_kernel(sz, table, matrix, other, picked, values_own, low_own, *refs):
+    outs, values_other = refs[: sz.seq], refs[sz.seq]
     here, core = lax.axis_index("seq"), lax.axis_index("owner")
-    values_other, low_other = project_half(sz, table, matrix, other, stacked, 1 - core)
-    pairs = ((values_own[...], low_own[...], core), (values_other, low_other, 1 - core))
-    for values, low, owner in pairs:
-        for chip in range(sz.seq):
-            first = pl.multiple_of(chip * sz.rows + owner * sz.rows_half, sz.rows_half)
-            taken = slice(chip * sz.rows_half, (chip + 1) * sz.rows_half)
-            product[pl.ds(first, sz.rows_half), :] = values[taken]
-            reduced[pl.ds(first, sz.rows_half), :] = low[taken]
-    half = sz.tokens // 2
-    packed = jnp.concatenate([reduced[:half], reduced[half:]], axis=1).astype(bf16)
+    values_other[...], low_other = project_half(sz, table, matrix, other, picked, 1 - core)
+    count = sz.seq * sz.rows_half
     for k, out in enumerate(outs):
-        first = pl.multiple_of((here ^ k) * HEAD_SIZE, HEAD_SIZE)
-        out[: sz.tokens] = product[:, pl.ds(first, HEAD_SIZE)]
-        out[sz.tokens :] = packed
-
-
-def mix_kernel(sz, table, softmax, *refs):
-    pieces, refs = refs[: sz.seq], refs[sz.seq :]
+        columns = pl.ds(pl.multiple_of((here ^ k) * HEAD_SIZE, HEAD_SIZE), HEAD_SIZE)
+        for values, low, owner in (
+            (values_own, low_own[...], core),
+            (values_other, low_other, 1 - core),
+        ):
+            first = pl.multiple_of(owner * count, count)
+            out[pl.ds(first, count), :] = values[:, columns]
+            first = pl.multiple_of(sz.tokens + owner * sz.rank, sz.rank)
+            out[pl.ds(first, sz.rank), :] = low
+
+
+def mix_kernel(sz, table, softmax, raise_picked, scale, *refs):
     partials, refs = refs[: sz.seq], refs[sz.seq :]
-    outs, (wide, raise_all, raise_picked, mixed) = refs[: sz.seq], refs[sz.seq :]
+    outs, (wide, mixed) = refs[: sz.seq], refs[sz.seq :]
     here = lax.axis_index("seq")
-    parts = (sz.group_size + 1) * (sz.rows // sz.rows_half)
-    for k, piece in zip(sz.order, pieces):
-        size = sz.slots_here * sz.rank
-        unpack(sz, piece, raise_all, parts, k * size, size)
-    position = lax.broadcasted_iota(jnp.int32, (sz.tokens, sz.rank), 0)
-    request = request_column(sz, table, position)
-    position = lax.broadcasted_iota(jnp.int32, (sz.tokens, HEAD_SIZE), 0)
-    request_wide = request_column(sz, table, position)
-    rank_here = jnp.ones((sz.tokens, HEAD_SIZE), jnp.int32)
+    count = sz.seq * sz.rows_half
     low = sum(partial[sz.tokens :].astype(f32) for partial in partials)
-    low = jnp.concatenate([low[:, : sz.rank], low[:, sz.rank :]], axis=0)
-    for r in range(sz.requests):
-        rank_here = jnp.where(request_wide == r, table[1, r], rank_here)
-        own = slice(r * sz.rank, (r + 1) * sz.rank)
-        raise_picked[own] = raise_all[pl.ds(pl.multiple_of(table[3, r], sz.rank), sz.rank), :]
-        wide[:, own] = jnp.where(request == r, low, 0.0).astype(bf16)
-    scale = adapter_strength / rank_here.astype(f32)
-    raised = jnp.dot(wide[...], raise_picked[...], preferred_element_type=f32)
+    shape = (sz.rank, count)
+    for owner in range(2):
+        place = lax.broadcasted_iota(jnp.int32, shape, 1) + owner * count
+        request = request_column(sz, table, token_at(sz, place))
+        own = low[owner * sz.rank : (owner + 1) * sz.rank]
+        for r in range(sz.requests):
+            wide[r * sz.rank : (r + 1) * sz.rank, owner * count : (owner + 1) * count] = jnp.where(
+                request == r, own, 0.0
+            ).astype(bf16)
+    raised = lax.dot_general(
+        wide[...], raise_picked[...], (((0,), (0,)), ((), ())), preferred_element_type=f32
+    )
     base = sum(partial[: sz.tokens].astype(f32) for partial in partials)
-    values = (base + scale * raised).astype(bf16)
-    for c in range(sz.group_size):
-        mixed[:, c * HEAD_SIZE : (c + 1) * HEAD_SIZE] = jnp.dot(
-            softmax[c], values, preferred_element_type=f32
-        ).astype(bf16)
+    values = (base + scale[...] * raised).astype(bf16)
+    mixed[...] = jnp.dot(softmax[...], values, preferred_element_type=f32).astype(bf16)
     for k, out in enumerate(outs):
-        chip = here ^ k
-        out[...] = mixed[pl.ds(pl.multiple_of(chip * sz.rows, sz.rows), sz.rows), :]
+        for c in range(sz.group_size):
+            first = pl.multiple_of(c * sz.tokens + (here ^ k) * sz.rows, sz.rows)
+            out[:, c * HEAD_SIZE : (c + 1) * HEAD_SIZE] = mixed[pl.ds(first, sz.rows), :]
 
 
 def place_kernel(sz, *refs):
     pieces, out = refs[: sz.seq], refs[sz.seq]
     here = lax.axis_index("seq")
     wide = sz.group_size * HEAD_SIZE
-    for k, piece in zip(sz.order, pieces):
+    for k, piece in zip(sz.order_out, pieces):
         head = here ^ k
         out[:, pl.ds(pl.multiple_of(head * wide, wide), wide)] = piece[...]
 
@@ -316,7 +332,7 @@
 
     spread = (2 * sz.rows_half, sz.span)
 
-    def call(kernel, name, ins, outs, args, scratch=(), params=PARAMS):
+    def call(kernel, name, ins, outs, args, scratch=(), params=PARAMS, cost=None):
         return pl.pallas_call(
             functools.partial(kernel, sz),
             out_shape=[jax.ShapeDtypeStruct(shape, dtype) for shape, dtype, _ in outs],
@@ -324,6 +340,7 @@
             out_specs=[spec for _, _, spec in outs],
             scratch_shapes=list(scratch),
             compiler_params=params,
+            cost_estimate=cost,
             name=name,
         )(*args)
 
@@ -332,7 +349,7 @@
         "panels_out",
         [HBM],
         [((sz.rank, sz.span), bf16, VMEM)] * sz.side,
-        (jnp.swapaxes(down, 1, 2),),
+        (lax.dynamic_index_in_dim(jnp.swapaxes(down, 1, 2), lax.axis_index("groups"), 0, True),),
         (pltpu.SemaphoreType.DMA((sz.side,)),),
     )
     panels = []
@@ -368,6 +385,7 @@
         [((4, sz.requests), jnp.int32, SMEM), (spread, bf16, VMEM)],
         (lengths, adapters, ranks, slots, rows_out[0]),
         (pltpu.SemaphoreType.DMA,),
+        cost=pl.CostEstimate(flops=0, bytes_accessed=64 * 1024 * 1024, transcendentals=0),
     )
     (matrix,) = call(
         matrix_kernel,
@@ -379,10 +397,8 @@
     )
     rows_in = [held] + [swap(rows_out[k], "seq", k) for k in around]
 
-    panels[0], table, matrix, held = lax.optimization_barrier((panels[0], table, matrix, held))
-    rows_ready = rows_out[0]
-    for m in range(sz.side):
-        panels[m], rows_ready = lax.optimization_barrier((panels[m], rows_ready))
+    panels[0], table, matrix = lax.optimization_barrier((panels[0], table, matrix))
+    panels[1], held = lax.optimization_barrier((panels[1], held))
     rows_in[0] = held
     panels = panels + [swap(p, "groups", k) for k in range(1, sz.groups) for p in panels]
     panels = panels + [swap(p, "owner", 1) for p in panels]
@@ -396,52 +412,56 @@
         ordered(rows_in),
     )
     other = swap(own, "owner", 1)
-    (softmax,) = call(
+    softmax, raise_picked, scale = call(
         softmax_kernel,
         "softmax_rows",
         [SMEM] + [VMEM] * sz.seq,
-        [((sz.group_size, sz.tokens, sz.tokens), bf16, VMEM)],
+        [
+            ((sz.group_size * sz.tokens, sz.tokens), bf16, VMEM),
+            ((sz.requests * sz.rank, HEAD_SIZE), bf16, VMEM),
+            ((sz.tokens, HEAD_SIZE), f32, VMEM),
+        ],
         (table, *ordered(rows_in)),
         (
             pltpu.VMEM((sz.group_size, sz.tokens, HEAD_SIZE), bf16),
             pltpu.VMEM((sz.tokens, HEAD_SIZE), bf16),
+            pltpu.VMEM((sz.seq * sz.slots_here * sz.rank, HEAD_SIZE), bf16),
         ),
     )
 
-    partial_shape = (sz.tokens + sz.tokens // 2, HEAD_SIZE)
-    rows_half_all = sz.seq * sz.rows_half
-    stacked, values_own, low_own = call(
+    count = sz.seq * sz.rows_half
+    partial_shape = (sz.tokens + 2 * sz.rank, HEAD_SIZE)
+    picked, values_own, low_own = call(
         project_own_kernel,
         "project_own",
         [SMEM] + [VMEM] * (2 + len(panels)),
         [
-            ((len(panels) * sz.rank, sz.span), bf16, VMEM),
-            ((rows_half_all, half_columns), bf16, VMEM),
-            ((rows_half_all, sz.rank), f32, VMEM),
+            ((sz.requests * sz.rank, sz.span), bf16, VMEM),
+            ((count, half_columns), bf16, VMEM),
+            ((sz.rank, count), bf16, VMEM),
         ],
         (table, matrix, own, *panels),
+        (pltpu.VMEM((len(panels) * sz.rank, sz.span), bf16),),
     )
     partial_out = call(
         project_other_kernel,
         "project_other",
         [SMEM] + [VMEM] * 5,
         [(partial_shape, bf16, VMEM)] * sz.seq,
-        (table, matrix, other, stacked, values_own, low_own),
-        (pltpu.VMEM((sz.tokens, half_columns), bf16), pltpu.VMEM((sz.tokens, sz.rank), f32)),
+        (table, matrix, other, picked, values_own, low_own),
+        (pltpu.VMEM((count, half_columns), bf16),),
     )
     partial_in = [partial_out[0]] + [swap(partial_out[k], "seq", k) for k in around]
     wide = sz.group_size * HEAD_SIZE
     mixed = call(
         mix_kernel,
         "mix_values",
-        [SMEM] + [VMEM] * (1 + 2 * sz.seq),
+        [SMEM] + [VMEM] * (3 + sz.seq),
         [((sz.rows, wide), bf16, VMEM)] * sz.seq,
-        (table, softmax, *ordered(rows_in), *ordered(partial_in)),
+        (table, softmax, raise_picked, scale, *[partial_in[k] for k in sz.order_sum]),
         (
-            pltpu.VMEM((sz.tokens, sz.requests * sz.rank), bf16),
-            pltpu.VMEM((sz.seq * sz.slots_here * sz.rank, HEAD_SIZE), bf16),
-            pltpu.VMEM((sz.requests * sz.rank, HEAD_SIZE), bf16),
-            pltpu.VMEM((sz.tokens, wide), bf16),
+            pltpu.VMEM((sz.requests * sz.rank, sz.tokens), bf16),
+            pltpu.VMEM((sz.group_size * sz.tokens, HEAD_SIZE), bf16),
         ),
     )
     mixed_in = [mixed[0]] + [swap(mixed[k], "seq", k) for k in around]
@@ -450,7 +470,7 @@
         "place_heads",
         [VMEM] * sz.seq,
         [((sz.rows, sz.seq * wide), bf16, VMEM)],
-        ordered(mixed_in),
+        [mixed_in[k] for k in sz.order_out],
     )
     return result
 

time: 54.4 us -> 55.2 us (1.015)
  starting transfers between devices: 23 us -> 24.5 us
    ppermute x2, starting transfers between devices: 3.41 us -> 4.66 us  [by_heads(): panels.append(lax.ppermute(panels_out[m], ('seq', 'owner'), pairs))]
  transfers between devices with their start and end apart: 19 -> 19, of which waited for: 8 -> 9; matrix products, arithmetic and copies ran while one was open for 0% -> 0% of each run, Pallas kernels for 12% -> 13%
where the time goes in v4:
time: 55.2 us; the launch traced here: 55 us
  starting transfers between devices  24.5 us (44%)
  waiting for transfers between devices  18.8 us (34%)
  Pallas kernels  10 us (18%)
  local copies, waits for them, and re-layouts  1.57 us (3%)
    ppermute x17, starting transfers between devices, swap(): lax.ppermute(value, axis, [(i, i ^ mask) for i in range(lax.axis_size(axi...  19.8 us
    ppermute x17, waiting for transfers between devices, swap(): lax.ppermute(value, axis, [(i, i ^ mask) for i in range(lax.axis_size(axi...  18.8 us
    pallas_call x10, Pallas kernels, call(): pl.pallas_call(functools.partial(kernel, sz), out_shape=[jax.ShapeDtypeSt...  10 us
    ppermute x2, starting transfers between devices, by_heads(): panels.append(lax.ppermute(panels_out[m], ('seq', 'owner'), pairs))  4.66 us
    unnamed x16, local copies, waits for them, and re-layouts  1.54 us
  transfers between devices with their start and end apart: 19, of which 9 were waited for; matrix products, arithmetic and copies ran while one was open for 0% of the time, Pallas kernels for 13%

profile of v4, /device:TPU:0, one launch (start us, length us, event | category | flops | bytes accessed | tf_op | source)
XLA Modules:
  0.0 55.0 jit_solution(13021802219160446350)
XLA Ops:
  0.0 0.5 collective-permute-start.1
  0.6 0.6 %copy-done = bf16[1,2,2688,64]{2,3,1,0:T(8,128)(2,1)S(1)} copy-done((bf16[1,2,2688,64]{2,3,1,0:T(8,128)(2,1)S(1)}, bf16[1,2,2688,64]{2,3,1,0:T(8,128)(2,1)}, u32[]{:S(2)}) %copy-start) | copy-done | bytes 688152
  1.2 0.8 %panels_out.1 = (bf16[64,1408]{1,0:T(8,128)(2,1)}, bf16[64,1408]{1,0:T(8,128)(2,1)S(1)}) custom-call(bf16[1,64,2688]{2,1,0:T(8,128)(2,1)S(1)} %dynamic-slice_bitcast_fusion.down), custom_call_target="tpu_custom_call" | custom-call | tf_op jit(solution)/shard_map/panels_out/pallas_call | solution.py:336
  2.0 3.1 %collective-permute-start.2 = (bf16[64,1408]{1,0:T(8,128)(2,1)S(1)}, bf16[64,1408]{1,0:T(8,128)(2,1)S(1)}, u32[]{:S(2)}, u32[]{:S(2)}) collective-permute-start(bf16[64,1408]{1,0:T(8,128)(2,1)S(1)} %get-tuple-element.50), channel_id=1, source_target_pairs={{0,4},{1,12},{4,0},{5,8},{8,5},{9,13},{12,1},{13,9},{2,6},{3,14},{... | collective-permute-start | bytes 540680 | tf_op jit(solution)/shard_map/ppermute | solution.py:362
  5.1 1.6 %collective-permute-start = (bf16[64,1408]{1,0:T(8,128)(2,1)}, bf16[64,1408]{1,0:T(8,128)(2,1)S(1)}, u32[]{:S(2)}, u32[]{:S(2)}) collective-permute-start(bf16[64,1408]{1,0:T(8,128)(2,1)} %get-tuple-element.45), channel_id=1, source_target_pairs={{0,0},{1,8},{4,4},{5,12},{8,1},{9,9},{12,5},{13,13},{2,2},{3,10},{... | collective-permute-start | bytes 540680 | tf_op jit(solution)/shard_map/ppermute | solution.py:362
  6.6 2.2 %norm_rows.1 = (bf16[64,1408]{1,0:T(8,128)(2,1)}, bf16[64,1408]{1,0:T(8,128)(2,1)}, bf16[64,1408]{1,0:T(8,128)(2,1)}, bf16[64,1408]{1,0:T(8,128)(2,1)}) custom-call(bf16[64,5376]{1,0:T(8,128)(2,1)} %bitcast.12, f32[1,5376]{1,0:T(1,128)} %gain.1, bf16[64,1024]{1,0:T(8,128)(2,1)} %bitcast.13, bf16[64,512]{1,0:T(8,128)(2,1)} %bitcast.15, ...), custom_call_target="tpu_custom_call" | custom-call | tf_op jit(solution)/shard_map/norm_rows/pallas_call | solution.py:336
  8.8 0.1 collective-permute-start.3
  8.9 6.5 %collective-permute-start.4 = (bf16[64,1408]{1,0:T(8,128)(2,1)}, bf16[64,1408]{1,0:T(8,128)(2,1)S(1)}, u32[]{:S(2)}, u32[]{:S(2)}) collective-permute-start(bf16[64,1408]{1,0:T(8,128)(2,1)} %get-tuple-element.54), channel_id=1, source_target_pairs={{0,12},{4,8},{8,4},{12,0},{1,13},{5,9},{9,5},{13,1},{2,14},{6,10},... | collective-permute-start | bytes 540680 | tf_op jit(solution)/shard_map/ppermute | solution.py:31
  15.4 0.9 %copy-done.2 = bf16[64,1408]{1,0:T(8,128)(2,1)S(1)} copy-done((bf16[64,1408]{1,0:T(8,128)(2,1)S(1)}, bf16[64,1408]{1,0:T(8,128)(2,1)}, u32[]{:S(2)}) %copy-start.2) | copy-done | bytes 180248
  16.3 1.5 %table.1 = (s32[4,4]{1,0:T(4,128)S(1)}, bf16[64,1408]{1,0:T(8,128)(2,1)S(1)}) custom-call(s32[4]{0:T(128)S(1)} %copy-done.3, s32[4]{0:T(128)S(1)} %copy-done.4, s32[8]{0:T(128)S(1)} %copy-done.5, s32[8]{0:T(128)S(1)} %copy-done.6, bf16[64,1408]{1,0:T(8,128)(2,1)S(1)} %copy-done.2), custom_call_target="tpu_custom_call" | custom-call | bytes 67108864 | tf_op jit(solution)/shard_map/table/pallas_call | solution.py:336
  17.8 0.0 collective-permute-done.2.refs_1_
  17.8 1.6 %collective-permute-start.7 = (bf16[64,1408]{1,0:T(8,128)(2,1)S(1)}, bf16[64,1408]{1,0:T(8,128)(2,1)S(1)}, u32[]{:S(2)}, u32[]{:S(2)}) collective-permute-start(bf16[64,1408]{1,0:T(8,128)(2,1)S(1)} %collective-permute-done.2.refs_1_), channel_id=1, source_target_pairs={{0,16},{16,0},{1,17},{17,1},{2,18},{18,2},{3,19},{19,3},{4,20},{20... | collective-permute-start | bytes 540680 | tf_op jit(solution)/shard_map/ppermute | solution.py:31
  19.4 0.0 collective-permute-done.1.base_other
  19.4 0.2 matrix_rows.1.matrix
  19.6 0.0 collective-permute-done.refs_0_
  19.7 0.6 %collective-permute-start.6 = (bf16[64,1408]{1,0:T(8,128)(2,1)S(1)}, bf16[64,1408]{1,0:T(8,128)(2,1)S(1)}, u32[]{:S(2)}, u32[]{:S(2)}) collective-permute-start(bf16[64,1408]{1,0:T(8,128)(2,1)S(1)} %collective-permute-done.refs_0_), channel_id=1, source_target_pairs={{0,16},{16,0},{1,17},{17,1},{2,18},{18,2},{3,19},{19,3},{4,20},{20... | collective-permute-start | bytes 540680 | tf_op jit(solution)/shard_map/ppermute | solution.py:31
  20.2 0.0 collective-permute-start.5
  20.2 0.0 collective-permute-done.3.refs_3_
  20.2 0.7 %collective-permute-start.9 = (bf16[64,1408]{1,0:T(8,128)(2,1)S(1)}, bf16[64,1408]{1,0:T(8,128)(2,1)S(1)}, u32[]{:S(2)}, u32[]{:S(2)}) collective-permute-start(bf16[64,1408]{1,0:T(8,128)(2,1)S(1)} %collective-permute-done.2.refs_1_), channel_id=1, source_target_pairs={{0,1},{1,0},{2,3},{3,2},{4,5},{5,4},{6,7},{7,6},{8,9},{9,8},{10,11... | collective-permute-start | bytes 540680 | tf_op jit(solution)/shard_map/ppermute | solution.py:31
  20.9 3.9 %collective-permute-done.7.refs_3_ = bf16[64,1408]{1,0:T(8,128)(2,1)S(1)} collective-permute-done((bf16[64,1408]{1,0:T(8,128)(2,1)S(1)}, bf16[64,1408]{1,0:T(8,128)(2,1)S(1)}, u32[]{:S(2)}, u32[]{:S(2)}) %collective-permute-start.7) | collective-permute-done | bytes 180256 | tf_op jit(solution)/shard_map/ppermute | solution.py:31
  24.8 0.0 collective-permute-start.11
  24.8 0.0 collective-permute-done.4.refs_1_
  24.8 0.5 collective-permute-start.8
  25.3 1.4 %collective-permute-done.6.refs_2_ = bf16[64,1408]{1,0:T(8,128)(2,1)S(1)} collective-permute-done((bf16[64,1408]{1,0:T(8,128)(2,1)S(1)}, bf16[64,1408]{1,0:T(8,128)(2,1)S(1)}, u32[]{:S(2)}, u32[]{:S(2)}) %collective-permute-start.6) | collective-permute-done | bytes 180256 | tf_op jit(solution)/shard_map/ppermute | solution.py:31
  26.8 0.0 collective-permute-start.10
  26.8 4.9 %collective-permute-done.5.refs_2_ = bf16[64,1408]{1,0:T(8,128)(2,1)S(1)} collective-permute-done((bf16[64,1408]{1,0:T(8,128)(2,1)S(1)}, bf16[64,1408]{1,0:T(8,128)(2,1)S(1)}, u32[]{:S(2)}, u32[]{:S(2)}) %collective-permute-start.5) | collective-permute-done | bytes 180256 | tf_op jit(solution)/shard_map/ppermute | solution.py:31
  31.7 0.0 collective-permute-done.9.refs_5_
  31.7 0.0 collective-permute-done.11.refs_7_
  31.7 0.0 collective-permute-done.8.refs_4_
  31.7 0.0 collective-permute-done.10.refs_6_
  31.8 0.1 collective-permute-start.12
  31.8 1.3 %project_own.1 = (bf16[256,1408]{1,0:T(8,128)(2,1)S(1)}, bf16[128,512]{1,0:T(8,128)(2,1)S(1)}, bf16[64,128]{1,0:T(8,128)(2,1)S(1)}) custom-call(s32[4,4]{1,0:T(4,128)S(1)} %get-tuple-element.49.table, bf16[1408,512]{1,0:T(8,128)(2,1)S(1)} %matrix_rows.1.matrix, bf16[128,1408]{1,0:T(8,128)(2,1)S(1)} %gather_rows.1.own, ...), custom_call_target="tpu_custom_call" | custom-call | tf_op jit(solution)/shard_map/project_own/pallas_call | solution.py:336
  33.1 0.4 collective-permute-done.12.other
  33.5 1.2 %project_other.1 = (bf16[384,128]{1,0:T(8,128)(2,1)S(1)}, bf16[384,128]{1,0:T(8,128)(2,1)S(1)}, bf16[384,128]{1,0:T(8,128)(2,1)S(1)}, bf16[384,128]{1,0:T(8,128)(2,1)S(1)}) custom-call(s32[4,4]{1,0:T(4,128)S(1)} %get-tuple-element.49.table, bf16[1408,512]{1,0:T(8,128)(2,1)S(1)} %matrix_rows.1.matrix, bf16[128,1408]{1,0:T(8,128)(2,1)S(1)} %collective-permute-done.12.other, ...), custom_call_target="tpu_custom_call" | custom-call | tf_op jit(solution)/shard_map/project_other/pallas_call | solution.py:336
  34.7 0.1 collective-permute-start.13
  34.8 2.5 %collective-permute-start.14 = (bf16[384,128]{1,0:T(8,128)(2,1)S(1)}, bf16[384,128]{1,0:T(8,128)(2,1)S(1)}, u32[]{:S(2)}, u32[]{:S(2)}) collective-permute-start(bf16[384,128]{1,0:T(8,128)(2,1)S(1)} %get-tuple-element.79), channel_id=1, source_target_pairs={{0,4},{4,0},{8,12},{12,8},{1,5},{5,1},{9,13},{13,9},{2,6},{6,2},{1... | collective-permute-start | bytes 294920 | tf_op jit(solution)/shard_map/ppermute | solution.py:31
  37.2 1.9 %collective-permute-start.15 = (bf16[384,128]{1,0:T(8,128)(2,1)S(1)}, bf16[384,128]{1,0:T(8,128)(2,1)S(1)}, u32[]{:S(2)}, u32[]{:S(2)}) collective-permute-start(bf16[384,128]{1,0:T(8,128)(2,1)S(1)} %get-tuple-element.80), channel_id=1, source_target_pairs={{0,12},{4,8},{8,4},{12,0},{1,13},{5,9},{9,5},{13,1},{2,14},{6,10},... | collective-permute-start | bytes 294920 | tf_op jit(solution)/shard_map/ppermute | solution.py:31
  39.1 1.1 %softmax_rows.1 = (bf16[512,256]{1,0:T(8,128)(2,1)S(1)}, bf16[256,128]{1,0:T(8,128)(2,1)S(1)}, f32[256,128]{1,0:T(8,128)S(1)}) custom-call(s32[4,4]{1,0:T(4,128)S(1)} %get-tuple-element.49.table, bf16[64,1408]{1,0:T(8,128)(2,1)S(1)} %get-tuple-element.58.refs_0_, bf16[64,1408]{1,0:T(8,128)(2,1)S(1)} %collective-permute-done.4.refs_1_, ...), custom_call_target="tpu_custom_call" | custom-call | tf_op jit(solution)/shard_map/softmax_rows/pallas_call | solution.py:336
  40.3 3.8 %collective-permute-done.13.refs_1_ = bf16[384,128]{1,0:T(8,128)(2,1)S(1)} collective-permute-done((bf16[384,128]{1,0:T(8,128)(2,1)S(1)}, bf16[384,128]{1,0:T(8,128)(2,1)S(1)}, u32[]{:S(2)}, u32[]{:S(2)}) %collective-permute-start.13) | collective-permute-done | bytes 98336 | tf_op jit(solution)/shard_map/ppermute | solution.py:31
  44.1 0.2 collective-permute-done.14.refs_2_
  44.2 0.0 collective-permute-done.15.refs_3_
  44.2 1.1 %mix_values.1 = (bf16[64,256]{1,0:T(8,128)(2,1)S(1)}, bf16[64,256]{1,0:T(8,128)(2,1)S(1)}, bf16[64,256]{1,0:T(8,128)(2,1)S(1)}, bf16[64,256]{1,0:T(8,128)(2,1)S(1)}) custom-call(s32[4,4]{1,0:T(4,128)S(1)} %get-tuple-element.49.table, bf16[512,256]{1,0:T(8,128)(2,1)S(1)} %get-tuple-element.62.softmax, bf16[256,128]{1,0:T(8,128)(2,1)S(1)} %get-tuple-element.63.raise_picked, ...), custom_call_target="tpu_custom_call" | custom-call | tf_op jit(solution)/shard_map/mix_values/pallas_call | solution.py:336
  45.3 3.0 %collective-permute-start.16 = (bf16[64,256]{1,0:T(8,128)(2,1)S(1)}, bf16[64,256]{1,0:T(8,128)(2,1)S(1)}, u32[]{:S(2)}, u32[]{:S(2)}) collective-permute-start(bf16[64,256]{1,0:T(8,128)(2,1)S(1)} %get-tuple-element.82), channel_id=1, source_target_pairs={{0,8},{4,12},{8,0},{12,4},{1,9},{5,13},{9,1},{13,5},{2,10},{6,14},... | collective-permute-start | bytes 98312 | tf_op jit(solution)/shard_map/ppermute | solution.py:31
  48.3 1.9 %collective-permute-start.17 = (bf16[64,256]{1,0:T(8,128)(2,1)S(1)}, bf16[64,256]{1,0:T(8,128)(2,1)S(1)}, u32[]{:S(2)}, u32[]{:S(2)}) collective-permute-start(bf16[64,256]{1,0:T(8,128)(2,1)S(1)} %get-tuple-element.83), channel_id=1, source_target_pairs={{0,12},{4,8},{8,4},{12,0},{1,13},{5,9},{9,5},{13,1},{2,14},{6,10},... | collective-permute-start | bytes 98312 | tf_op jit(solution)/shard_map/ppermute | solution.py:31
  50.2 0.3 collective-permute-done.16.refs_1_
  50.5 3.6 %collective-permute-done.17.refs_2_ = bf16[64,256]{1,0:T(8,128)(2,1)S(1)} collective-permute-done((bf16[64,256]{1,0:T(8,128)(2,1)S(1)}, bf16[64,256]{1,0:T(8,128)(2,1)S(1)}, u32[]{:S(2)}, u32[]{:S(2)}) %collective-permute-start.17) | collective-permute-done | bytes 32800 | tf_op jit(solution)/shard_map/ppermute | solution.py:31
  54.0 0.3 collective-permute-done.18.refs_3_
  54.4 0.7 %place_heads.1 = bf16[64,1024]{1,0:T(8,128)(2,1)} custom-call(bf16[64,256]{1,0:T(8,128)(2,1)S(1)} %get-tuple-element.81.refs_0_, bf16[64,256]{1,0:T(8,128)(2,1)S(1)} %collective-permute-done.16.refs_1_, bf16[64,256]{1,0:T(8,128)(2,1)S(1)} %collective-permute-done.17.refs_2_, bf16[64,256]{1,0:T(8,128)(2,1)S(1)} %collective-permute-done.18.refs_3_), custom_call_target="tpu_custom_call" | custom-call | tf_op jit(solution)/shard_map/place_heads/pallas_call | solution.py:336
  (17 shorter events, 0.1 us)
Async XLA Ops:
  0.0 1.2 %copy-start = (bf16[1,2,2688,64]{2,3,1,0:T(8,128)(2,1)S(1)}, bf16[1,2,2688,64]{2,3,1,0:T(8,128)(2,1)}, u32[]{:S(2)}) copy-start(bf16[1,2,2688,64]{2,3,1,0:T(8,128)(2,1)} %param.16) | copy-start | bytes 2064388
  0.0 19.4 %copy-start.1 = (bf16[1,672,1024]{2,1,0:T(8,128)(2,1)S(1)}, bf16[1,672,1024]{2,1,0:T(8,128)(2,1)}, u32[]{:S(2)}) copy-start(bf16[1,672,1024]{2,1,0:T(8,128)(2,1)} %param.15) | copy-start | bytes 4128772
  0.0 15.4 %copy-start.6 = (s32[8]{0:T(128)S(1)}, s32[8]{0:T(128)}, u32[]{:S(2)}) copy-start(s32[8]{0:T(128)} %slots.1) | copy-start | bytes 100
  0.0 15.4 %copy-start.5 = (s32[8]{0:T(128)S(1)}, s32[8]{0:T(128)}, u32[]{:S(2)}) copy-start(s32[8]{0:T(128)} %ranks.1) | copy-start | bytes 100
  0.0 15.4 %copy-start.4 = (s32[4]{0:T(128)S(1)}, s32[4]{0:T(128)}, u32[]{:S(2)}) copy-start(s32[4]{0:T(128)} %adapters.1) | copy-start | bytes 52
  0.0 15.4 %copy-start.3 = (s32[4]{0:T(128)S(1)}, s32[4]{0:T(128)}, u32[]{:S(2)}) copy-start(s32[4]{0:T(128)} %lengths.1) | copy-start | bytes 52
  0.0 19.4 %collective-permute-start.1 = (bf16[672,1024]{1,0:T(8,128)(2,1)}, bf16[672,1024]{1,0:T(8,128)(2,1)S(1)}, u32[]{:S(2)}, u32[]{:S(2)}) collective-permute-start(bf16[672,1024]{1,0:T(8,128)(2,1)} %bitcast.10), channel_id=1, source_target_pairs={{0,1},{1,0},{2,3},{3,2},{4,5},{5,4},{6,7},{7,6},{8,9},{9,8},{10,11... | collective-permute-start | bytes 4128776 | tf_op jit(solution)/shard_map/ppermute | solution.py:31
  2.0 15.8 %collective-permute-start.2 = (bf16[64,1408]{1,0:T(8,128)(2,1)S(1)}, bf16[64,1408]{1,0:T(8,128)(2,1)S(1)}, u32[]{:S(2)}, u32[]{:S(2)}) collective-permute-start(bf16[64,1408]{1,0:T(8,128)(2,1)S(1)} %get-tuple-element.50), channel_id=1, source_target_pairs={{0,4},{1,12},{4,0},{5,8},{8,5},{9,13},{12,1},{13,9},{2,6},{3,14},{... | collective-permute-start | bytes 540680 | tf_op jit(solution)/shard_map/ppermute | solution.py:362
  5.1 14.6 %collective-permute-start = (bf16[64,1408]{1,0:T(8,128)(2,1)}, bf16[64,1408]{1,0:T(8,128)(2,1)S(1)}, u32[]{:S(2)}, u32[]{:S(2)}) collective-permute-start(bf16[64,1408]{1,0:T(8,128)(2,1)} %get-tuple-element.45), channel_id=1, source_target_pairs={{0,0},{1,8},{4,4},{5,12},{8,1},{9,9},{12,5},{13,13},{2,2},{3,10},{... | collective-permute-start | bytes 540680 | tf_op jit(solution)/shard_map/ppermute | solution.py:362
  8.8 11.4 %collective-permute-start.3 = (bf16[64,1408]{1,0:T(8,128)(2,1)}, bf16[64,1408]{1,0:T(8,128)(2,1)S(1)}, u32[]{:S(2)}, u32[]{:S(2)}) collective-permute-start(bf16[64,1408]{1,0:T(8,128)(2,1)} %get-tuple-element.53), channel_id=1, source_target_pairs={{0,4},{4,0},{8,12},{12,8},{1,5},{5,1},{9,13},{13,9},{2,6},{6,2},{1... | collective-permute-start | bytes 540680 | tf_op jit(solution)/shard_map/ppermute | solution.py:31
  8.9 15.9 %collective-permute-start.4 = (bf16[64,1408]{1,0:T(8,128)(2,1)}, bf16[64,1408]{1,0:T(8,128)(2,1)S(1)}, u32[]{:S(2)}, u32[]{:S(2)}) collective-permute-start(bf16[64,1408]{1,0:T(8,128)(2,1)} %get-tuple-element.54), channel_id=1, source_target_pairs={{0,12},{4,8},{8,4},{12,0},{1,13},{5,9},{9,5},{13,1},{2,14},{6,10},... | collective-permute-start | bytes 540680 | tf_op jit(solution)/shard_map/ppermute | solution.py:31
  15.4 0.9 %copy-start.2 = (bf16[64,1408]{1,0:T(8,128)(2,1)S(1)}, bf16[64,1408]{1,0:T(8,128)(2,1)}, u32[]{:S(2)}) copy-start(bf16[64,1408]{1,0:T(8,128)(2,1)} %get-tuple-element.47.piece) | copy-start | bytes 540676
  17.8 2.4 %copy-start.7 = (bf16[64,1408]{1,0:T(8,128)(2,1)S(1)}, bf16[64,1408]{1,0:T(8,128)(2,1)}, u32[]{:S(2)}) copy-start(bf16[64,1408]{1,0:T(8,128)(2,1)} %get-tuple-element.55) | copy-start | bytes 540676
  17.8 7.0 %collective-permute-start.7 = (bf16[64,1408]{1,0:T(8,128)(2,1)S(1)}, bf16[64,1408]{1,0:T(8,128)(2,1)S(1)}, u32[]{:S(2)}, u32[]{:S(2)}) collective-permute-start(bf16[64,1408]{1,0:T(8,128)(2,1)S(1)} %collective-permute-done.2.refs_1_), channel_id=1, source_target_pairs={{0,16},{16,0},{1,17},{17,1},{2,18},{18,2},{3,19},{19,3},{4,20},{20... | collective-permute-start | bytes 540680 | tf_op jit(solution)/shard_map/ppermute | solution.py:31
  19.7 7.1 %collective-permute-start.6 = (bf16[64,1408]{1,0:T(8,128)(2,1)S(1)}, bf16[64,1408]{1,0:T(8,128)(2,1)S(1)}, u32[]{:S(2)}, u32[]{:S(2)}) collective-permute-start(bf16[64,1408]{1,0:T(8,128)(2,1)S(1)} %collective-permute-done.refs_0_), channel_id=1, source_target_pairs={{0,16},{16,0},{1,17},{17,1},{2,18},{18,2},{3,19},{19,3},{4,20},{20... | collective-permute-start | bytes 540680 | tf_op jit(solution)/shard_map/ppermute | solution.py:31
  20.2 11.5 %collective-permute-start.5 = (bf16[64,1408]{1,0:T(8,128)(2,1)S(1)}, bf16[64,1408]{1,0:T(8,128)(2,1)S(1)}, u32[]{:S(2)}, u32[]{:S(2)}) collective-permute-start(bf16[64,1408]{1,0:T(8,128)(2,1)S(1)} %copy-done.7), channel_id=1, source_target_pairs={{0,8},{4,12},{8,0},{12,4},{1,9},{5,13},{9,1},{13,5},{2,10},{6,14},... | collective-permute-start | bytes 540680 | tf_op jit(solution)/shard_map/ppermute | solution.py:31
  20.2 11.5 %collective-permute-start.9 = (bf16[64,1408]{1,0:T(8,128)(2,1)S(1)}, bf16[64,1408]{1,0:T(8,128)(2,1)S(1)}, u32[]{:S(2)}, u32[]{:S(2)}) collective-permute-start(bf16[64,1408]{1,0:T(8,128)(2,1)S(1)} %collective-permute-done.2.refs_1_), channel_id=1, source_target_pairs={{0,1},{1,0},{2,3},{3,2},{4,5},{5,4},{6,7},{7,6},{8,9},{9,8},{10,11... | collective-permute-start | bytes 540680 | tf_op jit(solution)/shard_map/ppermute | solution.py:31
  24.8 6.9 %collective-permute-start.11 = (bf16[64,1408]{1,0:T(8,128)(2,1)S(1)}, bf16[64,1408]{1,0:T(8,128)(2,1)S(1)}, u32[]{:S(2)}, u32[]{:S(2)}) collective-permute-start(bf16[64,1408]{1,0:T(8,128)(2,1)S(1)} %collective-permute-done.7.refs_3_), channel_id=1, source_target_pairs={{0,1},{1,0},{2,3},{3,2},{4,5},{5,4},{6,7},{7,6},{8,9},{9,8},{10,11... | collective-permute-start | bytes 540680 | tf_op jit(solution)/shard_map/ppermute | solution.py:31
  24.8 6.9 %collective-permute-start.8 = (bf16[64,1408]{1,0:T(8,128)(2,1)S(1)}, bf16[64,1408]{1,0:T(8,128)(2,1)S(1)}, u32[]{:S(2)}, u32[]{:S(2)}) collective-permute-start(bf16[64,1408]{1,0:T(8,128)(2,1)S(1)} %collective-permute-done.refs_0_), channel_id=1, source_target_pairs={{0,1},{1,0},{2,3},{3,2},{4,5},{5,4},{6,7},{7,6},{8,9},{9,8},{10,11... | collective-permute-start | bytes 540680 | tf_op jit(solution)/shard_map/ppermute | solution.py:31
  26.8 5.0 %collective-permute-start.10 = (bf16[64,1408]{1,0:T(8,128)(2,1)S(1)}, bf16[64,1408]{1,0:T(8,128)(2,1)S(1)}, u32[]{:S(2)}, u32[]{:S(2)}) collective-permute-start(bf16[64,1408]{1,0:T(8,128)(2,1)S(1)} %collective-permute-done.6.refs_2_), channel_id=1, source_target_pairs={{0,1},{1,0},{2,3},{3,2},{4,5},{5,4},{6,7},{7,6},{8,9},{9,8},{10,11... | collective-permute-start | bytes 540680 | tf_op jit(solution)/shard_map/ppermute | solution.py:31
  31.8 1.7 %collective-permute-start.12 = (bf16[128,1408]{1,0:T(8,128)(2,1)S(1)}, bf16[128,1408]{1,0:T(8,128)(2,1)S(1)}, u32[]{:S(2)}, u32[]{:S(2)}) collective-permute-start(bf16[128,1408]{1,0:T(8,128)(2,1)S(1)} %gather_rows.1.own), channel_id=1, source_target_pairs={{0,1},{1,0},{2,3},{3,2},{4,5},{5,4},{6,7},{7,6},{8,9},{9,8},{10,11... | collective-permute-start | bytes 1081352 | tf_op jit(solution)/shard_map/ppermute | solution.py:31
  34.7 9.4 %collective-permute-start.13 = (bf16[384,128]{1,0:T(8,128)(2,1)S(1)}, bf16[384,128]{1,0:T(8,128)(2,1)S(1)}, u32[]{:S(2)}, u32[]{:S(2)}) collective-permute-start(bf16[384,128]{1,0:T(8,128)(2,1)S(1)} %get-tuple-element.78), channel_id=1, source_target_pairs={{0,8},{4,12},{8,0},{12,4},{1,9},{5,13},{9,1},{13,5},{2,10},{6,14},... | collective-permute-start | bytes 294920 | tf_op jit(solution)/shard_map/ppermute | solution.py:31
  34.8 9.5 %collective-permute-start.14 = (bf16[384,128]{1,0:T(8,128)(2,1)S(1)}, bf16[384,128]{1,0:T(8,128)(2,1)S(1)}, u32[]{:S(2)}, u32[]{:S(2)}) collective-permute-start(bf16[384,128]{1,0:T(8,128)(2,1)S(1)} %get-tuple-element.79), channel_id=1, source_target_pairs={{0,4},{4,0},{8,12},{12,8},{1,5},{5,1},{9,13},{13,9},{2,6},{6,2},{1... | collective-permute-start | bytes 294920 | tf_op jit(solution)/shard_map/ppermute | solution.py:31
  37.2 7.0 %collective-permute-start.15 = (bf16[384,128]{1,0:T(8,128)(2,1)S(1)}, bf16[384,128]{1,0:T(8,128)(2,1)S(1)}, u32[]{:S(2)}, u32[]{:S(2)}) collective-permute-start(bf16[384,128]{1,0:T(8,128)(2,1)S(1)} %get-tuple-element.80), channel_id=1, source_target_pairs={{0,12},{4,8},{8,4},{12,0},{1,13},{5,9},{9,5},{13,1},{2,14},{6,10},... | collective-permute-start | bytes 294920 | tf_op jit(solution)/shard_map/ppermute | solution.py:31
  45.3 5.1 %collective-permute-start.16 = (bf16[64,256]{1,0:T(8,128)(2,1)S(1)}, bf16[64,256]{1,0:T(8,128)(2,1)S(1)}, u32[]{:S(2)}, u32[]{:S(2)}) collective-permute-start(bf16[64,256]{1,0:T(8,128)(2,1)S(1)} %get-tuple-element.82), channel_id=1, source_target_pairs={{0,8},{4,12},{8,0},{12,4},{1,9},{5,13},{9,1},{13,5},{2,10},{6,14},... | collective-permute-start | bytes 98312 | tf_op jit(solution)/shard_map/ppermute | solution.py:31
  48.3 5.7 %collective-permute-start.17 = (bf16[64,256]{1,0:T(8,128)(2,1)S(1)}, bf16[64,256]{1,0:T(8,128)(2,1)S(1)}, u32[]{:S(2)}, u32[]{:S(2)}) collective-permute-start(bf16[64,256]{1,0:T(8,128)(2,1)S(1)} %get-tuple-element.83), channel_id=1, source_target_pairs={{0,12},{4,8},{8,4},{12,0},{1,13},{5,9},{9,5},{13,1},{2,14},{6,10},... | collective-permute-start | bytes 98312 | tf_op jit(solution)/shard_map/ppermute | solution.py:31
  50.2 4.2 %collective-permute-start.18 = (bf16[64,256]{1,0:T(8,128)(2,1)S(1)}, bf16[64,256]{1,0:T(8,128)(2,1)S(1)}, u32[]{:S(2)}, u32[]{:S(2)}) collective-permute-start(bf16[64,256]{1,0:T(8,128)(2,1)S(1)} %get-tuple-element.84), channel_id=1, source_target_pairs={{0,4},{4,0},{8,12},{12,8},{1,5},{5,1},{9,13},{13,9},{2,6},{6,2},{1... | collective-permute-start | bytes 98312 | tf_op jit(solution)/shard_map/ppermute | solution.py:31

commit v5 on v4

--- a/solution.py
+++ b/solution.py
@@ -48,9 +48,10 @@
         self.heads_here = up.shape[2] // HEAD_SIZE
         self.group_size = HEADS // KEY_VALUE_HEADS
         self.tokens = self.rows * self.seq
-        self.order = [0, 3, 2, 1]
-        self.order_sum = [0, 2, 1, 3]
-        self.order_out = [0, 2, 3, 1]
+        rest = list(range(1, self.seq))
+        self.order = [0] + rest[::-1]
+        self.order_rows = [0] + rest[:1] + rest[:0:-1]
+        self.order_sum = [0] + rest[1:2] + rest[:1] + rest[2:]
         tiles = [
             -(-((i * self.features) % LANES + self.features) // LANES) for i in range(self.side)
         ]
@@ -318,7 +319,7 @@
     pieces, out = refs[: sz.seq], refs[sz.seq]
     here = lax.axis_index("seq")
     wide = sz.group_size * HEAD_SIZE
-    for k, piece in zip(sz.order_out, pieces):
+    for k, piece in zip(sz.order, pieces):
         head = here ^ k
         out[:, pl.ds(pl.multiple_of(head * wide, wide), wide)] = piece[...]
 
@@ -402,8 +403,8 @@
     rows_in[0] = held
     panels = panels + [swap(p, "groups", k) for k in range(1, sz.groups) for p in panels]
     panels = panels + [swap(p, "owner", 1) for p in panels]
-    rows_ordered, panels = lax.optimization_barrier(([rows_in[k] for k in [0, 1, 3, 2]], panels))
-    rows_in = [rows_ordered[[0, 1, 3, 2].index(k)] for k in range(sz.seq)]
+    rows_ordered, panels = lax.optimization_barrier(([rows_in[k] for k in sz.order_rows], panels))
+    rows_in = [rows_ordered[sz.order_rows.index(k)] for k in range(sz.seq)]
     (own,) = call(
         gather_kernel,
         "gather_rows",
@@ -470,7 +471,7 @@
         "place_heads",
         [VMEM] * sz.seq,
         [((sz.rows, sz.seq * wide), bf16, VMEM)],
-        [mixed_in[k] for k in sz.order_out],
+        ordered(mixed_in),
     )
     return result
 

time: 55.2 us -> 54.1 us (0.980)
  waiting for transfers between devices: 18.8 us -> 18.1 us
    ppermute x17, waiting for transfers between devices: 18.8 us -> 18 us  [swap(): lax.ppermute(value, axis, [(i, i ^ mask) for i in range(lax.axis_size(axi...]
where the time goes in v5:
time: 54.1 us; the launch traced here: 53.9 us
  starting transfers between devices  24.1 us (45%)
  waiting for transfers between devices  18.1 us (33%)
  Pallas kernels  10 us (18%)
  local copies, waits for them, and re-layouts  1.57 us (3%)
    ppermute x17, starting transfers between devices, swap(): lax.ppermute(value, axis, [(i, i ^ mask) for i in range(lax.axis_size(axi...  19.4 us
    ppermute x17, waiting for transfers between devices, swap(): lax.ppermute(value, axis, [(i, i ^ mask) for i in range(lax.axis_size(axi...  18 us
    pallas_call x10, Pallas kernels, call(): pl.pallas_call(functools.partial(kernel, sz), out_shape=[jax.ShapeDtypeSt...  10 us
    ppermute x2, starting transfers between devices, by_heads(): panels.append(lax.ppermute(panels_out[m], ('seq', 'owner'), pairs))  4.66 us
    unnamed x16, local copies, waits for them, and re-layouts  1.54 us
  transfers between devices with their start and end apart: 19, of which 9 were waited for; matrix products, arithmetic and copies ran while one was open for 0% of the time, Pallas kernels for 13%

profile of v5, /device:TPU:0, one launch (start us, length us, event | category | flops | bytes accessed | tf_op | source)
XLA Modules:
  0.0 53.9 jit_solution(10248049305725167032)
XLA Ops:
  0.0 0.5 collective-permute-start.1
  0.6 0.6 %copy-done = bf16[1,2,2688,64]{2,3,1,0:T(8,128)(2,1)S(1)} copy-done((bf16[1,2,2688,64]{2,3,1,0:T(8,128)(2,1)S(1)}, bf16[1,2,2688,64]{2,3,1,0:T(8,128)(2,1)}, u32[]{:S(2)}) %copy-start) | copy-done | bytes 688152
  1.2 0.8 %panels_out.1 = (bf16[64,1408]{1,0:T(8,128)(2,1)}, bf16[64,1408]{1,0:T(8,128)(2,1)S(1)}) custom-call(bf16[1,64,2688]{2,1,0:T(8,128)(2,1)S(1)} %dynamic-slice_bitcast_fusion.down), custom_call_target="tpu_custom_call" | custom-call | tf_op jit(solution)/shard_map/panels_out/pallas_call | solution.py:337
  2.0 3.1 %collective-permute-start.2 = (bf16[64,1408]{1,0:T(8,128)(2,1)S(1)}, bf16[64,1408]{1,0:T(8,128)(2,1)S(1)}, u32[]{:S(2)}, u32[]{:S(2)}) collective-permute-start(bf16[64,1408]{1,0:T(8,128)(2,1)S(1)} %get-tuple-element.50), channel_id=1, source_target_pairs={{0,4},{1,12},{4,0},{5,8},{8,5},{9,13},{12,1},{13,9},{2,6},{3,14},{... | collective-permute-start | bytes 540680 | tf_op jit(solution)/shard_map/ppermute | solution.py:363
  5.1 1.6 %collective-permute-start = (bf16[64,1408]{1,0:T(8,128)(2,1)}, bf16[64,1408]{1,0:T(8,128)(2,1)S(1)}, u32[]{:S(2)}, u32[]{:S(2)}) collective-permute-start(bf16[64,1408]{1,0:T(8,128)(2,1)} %get-tuple-element.45), channel_id=1, source_target_pairs={{0,0},{1,8},{4,4},{5,12},{8,1},{9,9},{12,5},{13,13},{2,2},{3,10},{... | collective-permute-start | bytes 540680 | tf_op jit(solution)/shard_map/ppermute | solution.py:363
  6.6 2.2 %norm_rows.1 = (bf16[64,1408]{1,0:T(8,128)(2,1)}, bf16[64,1408]{1,0:T(8,128)(2,1)}, bf16[64,1408]{1,0:T(8,128)(2,1)}, bf16[64,1408]{1,0:T(8,128)(2,1)}) custom-call(bf16[64,5376]{1,0:T(8,128)(2,1)} %bitcast.12, f32[1,5376]{1,0:T(1,128)} %gain.1, bf16[64,1024]{1,0:T(8,128)(2,1)} %bitcast.13, bf16[64,512]{1,0:T(8,128)(2,1)} %bitcast.15, ...), custom_call_target="tpu_custom_call" | custom-call | tf_op jit(solution)/shard_map/norm_rows/pallas_call | solution.py:337
  8.8 0.1 collective-permute-start.3
  8.9 6.5 %collective-permute-start.4 = (bf16[64,1408]{1,0:T(8,128)(2,1)}, bf16[64,1408]{1,0:T(8,128)(2,1)S(1)}, u32[]{:S(2)}, u32[]{:S(2)}) collective-permute-start(bf16[64,1408]{1,0:T(8,128)(2,1)} %get-tuple-element.54), channel_id=1, source_target_pairs={{0,12},{4,8},{8,4},{12,0},{1,13},{5,9},{9,5},{13,1},{2,14},{6,10},... | collective-permute-start | bytes 540680 | tf_op jit(solution)/shard_map/ppermute | solution.py:31
  15.4 0.9 %copy-done.2 = bf16[64,1408]{1,0:T(8,128)(2,1)S(1)} copy-done((bf16[64,1408]{1,0:T(8,128)(2,1)S(1)}, bf16[64,1408]{1,0:T(8,128)(2,1)}, u32[]{:S(2)}) %copy-start.2) | copy-done | bytes 180248
  16.3 1.5 %table.1 = (s32[4,4]{1,0:T(4,128)S(1)}, bf16[64,1408]{1,0:T(8,128)(2,1)S(1)}) custom-call(s32[4]{0:T(128)S(1)} %copy-done.3, s32[4]{0:T(128)S(1)} %copy-done.4, s32[8]{0:T(128)S(1)} %copy-done.5, s32[8]{0:T(128)S(1)} %copy-done.6, bf16[64,1408]{1,0:T(8,128)(2,1)S(1)} %copy-done.2), custom_call_target="tpu_custom_call" | custom-call | bytes 67108864 | tf_op jit(solution)/shard_map/table/pallas_call | solution.py:337
  17.8 0.0 collective-permute-done.2.refs_1_
  17.8 1.6 %collective-permute-start.7 = (bf16[64,1408]{1,0:T(8,128)(2,1)S(1)}, bf16[64,1408]{1,0:T(8,128)(2,1)S(1)}, u32[]{:S(2)}, u32[]{:S(2)}) collective-permute-start(bf16[64,1408]{1,0:T(8,128)(2,1)S(1)} %collective-permute-done.2.refs_1_), channel_id=1, source_target_pairs={{0,16},{16,0},{1,17},{17,1},{2,18},{18,2},{3,19},{19,3},{4,20},{20... | collective-permute-start | bytes 540680 | tf_op jit(solution)/shard_map/ppermute | solution.py:31
  19.4 0.0 collective-permute-done.1.base_other
  19.4 0.2 matrix_rows.1.matrix
  19.6 0.0 collective-permute-done.refs_0_
  19.7 0.6 %collective-permute-start.6 = (bf16[64,1408]{1,0:T(8,128)(2,1)S(1)}, bf16[64,1408]{1,0:T(8,128)(2,1)S(1)}, u32[]{:S(2)}, u32[]{:S(2)}) collective-permute-start(bf16[64,1408]{1,0:T(8,128)(2,1)S(1)} %collective-permute-done.refs_0_), channel_id=1, source_target_pairs={{0,16},{16,0},{1,17},{17,1},{2,18},{18,2},{3,19},{19,3},{4,20},{20... | collective-permute-start | bytes 540680 | tf_op jit(solution)/shard_map/ppermute | solution.py:31
  20.2 0.0 collective-permute-start.5
  20.2 0.0 collective-permute-done.3.refs_3_
  20.2 0.7 %collective-permute-start.9 = (bf16[64,1408]{1,0:T(8,128)(2,1)S(1)}, bf16[64,1408]{1,0:T(8,128)(2,1)S(1)}, u32[]{:S(2)}, u32[]{:S(2)}) collective-permute-start(bf16[64,1408]{1,0:T(8,128)(2,1)S(1)} %collective-permute-done.2.refs_1_), channel_id=1, source_target_pairs={{0,1},{1,0},{2,3},{3,2},{4,5},{5,4},{6,7},{7,6},{8,9},{9,8},{10,11... | collective-permute-start | bytes 540680 | tf_op jit(solution)/shard_map/ppermute | solution.py:31
  20.9 3.9 %collective-permute-done.7.refs_3_ = bf16[64,1408]{1,0:T(8,128)(2,1)S(1)} collective-permute-done((bf16[64,1408]{1,0:T(8,128)(2,1)S(1)}, bf16[64,1408]{1,0:T(8,128)(2,1)S(1)}, u32[]{:S(2)}, u32[]{:S(2)}) %collective-permute-start.7) | collective-permute-done | bytes 180256 | tf_op jit(solution)/shard_map/ppermute | solution.py:31
  24.8 0.0 collective-permute-start.11
  24.8 0.0 collective-permute-done.4.refs_1_
  24.8 0.5 collective-permute-start.8
  25.3 1.4 %collective-permute-done.6.refs_2_ = bf16[64,1408]{1,0:T(8,128)(2,1)S(1)} collective-permute-done((bf16[64,1408]{1,0:T(8,128)(2,1)S(1)}, bf16[64,1408]{1,0:T(8,128)(2,1)S(1)}, u32[]{:S(2)}, u32[]{:S(2)}) %collective-permute-start.6) | collective-permute-done | bytes 180256 | tf_op jit(solution)/shard_map/ppermute | solution.py:31
  26.8 0.0 collective-permute-start.10
  26.8 4.9 %collective-permute-done.5.refs_2_ = bf16[64,1408]{1,0:T(8,128)(2,1)S(1)} collective-permute-done((bf16[64,1408]{1,0:T(8,128)(2,1)S(1)}, bf16[64,1408]{1,0:T(8,128)(2,1)S(1)}, u32[]{:S(2)}, u32[]{:S(2)}) %collective-permute-start.5) | collective-permute-done | bytes 180256 | tf_op jit(solution)/shard_map/ppermute | solution.py:31
  31.7 0.0 collective-permute-done.11.refs_7_
  31.7 0.0 collective-permute-done.8.refs_4_
  31.7 0.0 collective-permute-done.10.refs_6_
  31.8 0.1 collective-permute-start.12
  31.8 1.3 %project_own.1 = (bf16[256,1408]{1,0:T(8,128)(2,1)S(1)}, bf16[128,512]{1,0:T(8,128)(2,1)S(1)}, bf16[64,128]{1,0:T(8,128)(2,1)S(1)}) custom-call(s32[4,4]{1,0:T(4,128)S(1)} %get-tuple-element.49.table, bf16[1408,512]{1,0:T(8,128)(2,1)S(1)} %matrix_rows.1.matrix, bf16[128,1408]{1,0:T(8,128)(2,1)S(1)} %gather_rows.1.own, ...), custom_call_target="tpu_custom_call" | custom-call | tf_op jit(solution)/shard_map/project_own/pallas_call | solution.py:337
  33.1 0.4 collective-permute-done.12.other
  33.5 1.2 %project_other.1 = (bf16[384,128]{1,0:T(8,128)(2,1)S(1)}, bf16[384,128]{1,0:T(8,128)(2,1)S(1)}, bf16[384,128]{1,0:T(8,128)(2,1)S(1)}, bf16[384,128]{1,0:T(8,128)(2,1)S(1)}) custom-call(s32[4,4]{1,0:T(4,128)S(1)} %get-tuple-element.49.table, bf16[1408,512]{1,0:T(8,128)(2,1)S(1)} %matrix_rows.1.matrix, bf16[128,1408]{1,0:T(8,128)(2,1)S(1)} %collective-permute-done.12.other, ...), custom_call_target="tpu_custom_call" | custom-call | tf_op jit(solution)/shard_map/project_other/pallas_call | solution.py:337
  34.7 0.1 collective-permute-start.13
  34.8 2.5 %collective-permute-start.14 = (bf16[384,128]{1,0:T(8,128)(2,1)S(1)}, bf16[384,128]{1,0:T(8,128)(2,1)S(1)}, u32[]{:S(2)}, u32[]{:S(2)}) collective-permute-start(bf16[384,128]{1,0:T(8,128)(2,1)S(1)} %get-tuple-element.79), channel_id=1, source_target_pairs={{0,4},{4,0},{8,12},{12,8},{1,5},{5,1},{9,13},{13,9},{2,6},{6,2},{1... | collective-permute-start | bytes 294920 | tf_op jit(solution)/shard_map/ppermute | solution.py:31
  37.2 1.9 %collective-permute-start.15 = (bf16[384,128]{1,0:T(8,128)(2,1)S(1)}, bf16[384,128]{1,0:T(8,128)(2,1)S(1)}, u32[]{:S(2)}, u32[]{:S(2)}) collective-permute-start(bf16[384,128]{1,0:T(8,128)(2,1)S(1)} %get-tuple-element.80), channel_id=1, source_target_pairs={{0,12},{4,8},{8,4},{12,0},{1,13},{5,9},{9,5},{13,1},{2,14},{6,10},... | collective-permute-start | bytes 294920 | tf_op jit(solution)/shard_map/ppermute | solution.py:31
  39.1 1.1 %softmax_rows.1 = (bf16[512,256]{1,0:T(8,128)(2,1)S(1)}, bf16[256,128]{1,0:T(8,128)(2,1)S(1)}, f32[256,128]{1,0:T(8,128)S(1)}) custom-call(s32[4,4]{1,0:T(4,128)S(1)} %get-tuple-element.49.table, bf16[64,1408]{1,0:T(8,128)(2,1)S(1)} %get-tuple-element.58.refs_0_, bf16[64,1408]{1,0:T(8,128)(2,1)S(1)} %collective-permute-done.4.refs_1_, ...), custom_call_target="tpu_custom_call" | custom-call | tf_op jit(solution)/shard_map/softmax_rows/pallas_call | solution.py:337
  40.3 3.8 %collective-permute-done.13.refs_1_ = bf16[384,128]{1,0:T(8,128)(2,1)S(1)} collective-permute-done((bf16[384,128]{1,0:T(8,128)(2,1)S(1)}, bf16[384,128]{1,0:T(8,128)(2,1)S(1)}, u32[]{:S(2)}, u32[]{:S(2)}) %collective-permute-start.13) | collective-permute-done | bytes 98336 | tf_op jit(solution)/shard_map/ppermute | solution.py:31
  44.1 0.2 collective-permute-done.14.refs_2_
  44.2 0.0 collective-permute-done.15.refs_3_
  44.2 1.1 %mix_values.1 = (bf16[64,256]{1,0:T(8,128)(2,1)S(1)}, bf16[64,256]{1,0:T(8,128)(2,1)S(1)}, bf16[64,256]{1,0:T(8,128)(2,1)S(1)}, bf16[64,256]{1,0:T(8,128)(2,1)S(1)}) custom-call(s32[4,4]{1,0:T(4,128)S(1)} %get-tuple-element.49.table, bf16[512,256]{1,0:T(8,128)(2,1)S(1)} %get-tuple-element.62.softmax, bf16[256,128]{1,0:T(8,128)(2,1)S(1)} %get-tuple-element.63.raise_picked, ...), custom_call_target="tpu_custom_call" | custom-call | tf_op jit(solution)/shard_map/mix_values/pallas_call | solution.py:337
  45.3 2.0 %collective-permute-start.16 = (bf16[64,256]{1,0:T(8,128)(2,1)S(1)}, bf16[64,256]{1,0:T(8,128)(2,1)S(1)}, u32[]{:S(2)}, u32[]{:S(2)}) collective-permute-start(bf16[64,256]{1,0:T(8,128)(2,1)S(1)} %get-tuple-element.82), channel_id=1, source_target_pairs={{0,12},{4,8},{8,4},{12,0},{1,13},{5,9},{9,5},{13,1},{2,14},{6,10},... | collective-permute-start | bytes 98312 | tf_op jit(solution)/shard_map/ppermute | solution.py:31
  47.3 2.0 %collective-permute-start.17 = (bf16[64,256]{1,0:T(8,128)(2,1)S(1)}, bf16[64,256]{1,0:T(8,128)(2,1)S(1)}, u32[]{:S(2)}, u32[]{:S(2)}) collective-permute-start(bf16[64,256]{1,0:T(8,128)(2,1)S(1)} %get-tuple-element.83), channel_id=1, source_target_pairs={{0,8},{4,12},{8,0},{12,4},{1,9},{5,13},{9,1},{13,5},{2,10},{6,14},... | collective-permute-start | bytes 98312 | tf_op jit(solution)/shard_map/ppermute | solution.py:31
  49.3 0.5 collective-permute-start.18
  49.8 1.4 %collective-permute-done.16.refs_1_ = bf16[64,256]{1,0:T(8,128)(2,1)S(1)} collective-permute-done((bf16[64,256]{1,0:T(8,128)(2,1)S(1)}, bf16[64,256]{1,0:T(8,128)(2,1)S(1)}, u32[]{:S(2)}, u32[]{:S(2)}) %collective-permute-start.16) | collective-permute-done | bytes 32800 | tf_op jit(solution)/shard_map/ppermute | solution.py:31
  51.1 1.1 %collective-permute-done.17.refs_2_ = bf16[64,256]{1,0:T(8,128)(2,1)S(1)} collective-permute-done((bf16[64,256]{1,0:T(8,128)(2,1)S(1)}, bf16[64,256]{1,0:T(8,128)(2,1)S(1)}, u32[]{:S(2)}, u32[]{:S(2)}) %collective-permute-start.17) | collective-permute-done | bytes 32800 | tf_op jit(solution)/shard_map/ppermute | solution.py:31
  52.2 1.0 %collective-permute-done.18.refs_3_ = bf16[64,256]{1,0:T(8,128)(2,1)S(1)} collective-permute-done((bf16[64,256]{1,0:T(8,128)(2,1)S(1)}, bf16[64,256]{1,0:T(8,128)(2,1)S(1)}, u32[]{:S(2)}, u32[]{:S(2)}) %collective-permute-start.18) | collective-permute-done | bytes 32800 | tf_op jit(solution)/shard_map/ppermute | solution.py:31
  53.2 0.7 %place_heads.1 = bf16[64,1024]{1,0:T(8,128)(2,1)} custom-call(bf16[64,256]{1,0:T(8,128)(2,1)S(1)} %get-tuple-element.81.refs_0_, bf16[64,256]{1,0:T(8,128)(2,1)S(1)} %collective-permute-done.16.refs_1_, bf16[64,256]{1,0:T(8,128)(2,1)S(1)} %collective-permute-done.17.refs_2_, bf16[64,256]{1,0:T(8,128)(2,1)S(1)} %collective-permute-done.18.refs_3_), custom_call_target="tpu_custom_call" | custom-call | tf_op jit(solution)/shard_map/place_heads/pallas_call | solution.py:337
  (17 shorter events, 0.1 us)
Async XLA Ops:
  0.0 1.2 %copy-start = (bf16[1,2,2688,64]{2,3,1,0:T(8,128)(2,1)S(1)}, bf16[1,2,2688,64]{2,3,1,0:T(8,128)(2,1)}, u32[]{:S(2)}) copy-start(bf16[1,2,2688,64]{2,3,1,0:T(8,128)(2,1)} %param.16) | copy-start | bytes 2064388
  0.0 19.4 %copy-start.1 = (bf16[1,672,1024]{2,1,0:T(8,128)(2,1)S(1)}, bf16[1,672,1024]{2,1,0:T(8,128)(2,1)}, u32[]{:S(2)}) copy-start(bf16[1,672,1024]{2,1,0:T(8,128)(2,1)} %param.15) | copy-start | bytes 4128772
  0.0 15.4 %copy-start.6 = (s32[8]{0:T(128)S(1)}, s32[8]{0:T(128)}, u32[]{:S(2)}) copy-start(s32[8]{0:T(128)} %slots.1) | copy-start | bytes 100
  0.0 15.4 %copy-start.5 = (s32[8]{0:T(128)S(1)}, s32[8]{0:T(128)}, u32[]{:S(2)}) copy-start(s32[8]{0:T(128)} %ranks.1) | copy-start | bytes 100
  0.0 15.4 %copy-start.4 = (s32[4]{0:T(128)S(1)}, s32[4]{0:T(128)}, u32[]{:S(2)}) copy-start(s32[4]{0:T(128)} %adapters.1) | copy-start | bytes 52
  0.0 15.4 %copy-start.3 = (s32[4]{0:T(128)S(1)}, s32[4]{0:T(128)}, u32[]{:S(2)}) copy-start(s32[4]{0:T(128)} %lengths.1) | copy-start | bytes 52
  0.0 19.4 %collective-permute-start.1 = (bf16[672,1024]{1,0:T(8,128)(2,1)}, bf16[672,1024]{1,0:T(8,128)(2,1)S(1)}, u32[]{:S(2)}, u32[]{:S(2)}) collective-permute-start(bf16[672,1024]{1,0:T(8,128)(2,1)} %bitcast.10), channel_id=1, source_target_pairs={{0,1},{1,0},{2,3},{3,2},{4,5},{5,4},{6,7},{7,6},{8,9},{9,8},{10,11... | collective-permute-start | bytes 4128776 | tf_op jit(solution)/shard_map/ppermute | solution.py:31
  2.0 15.8 %collective-permute-start.2 = (bf16[64,1408]{1,0:T(8,128)(2,1)S(1)}, bf16[64,1408]{1,0:T(8,128)(2,1)S(1)}, u32[]{:S(2)}, u32[]{:S(2)}) collective-permute-start(bf16[64,1408]{1,0:T(8,128)(2,1)S(1)} %get-tuple-element.50), channel_id=1, source_target_pairs={{0,4},{1,12},{4,0},{5,8},{8,5},{9,13},{12,1},{13,9},{2,6},{3,14},{... | collective-permute-start | bytes 540680 | tf_op jit(solution)/shard_map/ppermute | solution.py:363
  5.1 14.6 %collective-permute-start = (bf16[64,1408]{1,0:T(8,128)(2,1)}, bf16[64,1408]{1,0:T(8,128)(2,1)S(1)}, u32[]{:S(2)}, u32[]{:S(2)}) collective-permute-start(bf16[64,1408]{1,0:T(8,128)(2,1)} %get-tuple-element.45), channel_id=1, source_target_pairs={{0,0},{1,8},{4,4},{5,12},{8,1},{9,9},{12,5},{13,13},{2,2},{3,10},{... | collective-permute-start | bytes 540680 | tf_op jit(solution)/shard_map/ppermute | solution.py:363
  8.8 11.4 %collective-permute-start.3 = (bf16[64,1408]{1,0:T(8,128)(2,1)}, bf16[64,1408]{1,0:T(8,128)(2,1)S(1)}, u32[]{:S(2)}, u32[]{:S(2)}) collective-permute-start(bf16[64,1408]{1,0:T(8,128)(2,1)} %get-tuple-element.53), channel_id=1, source_target_pairs={{0,4},{4,0},{8,12},{12,8},{1,5},{5,1},{9,13},{13,9},{2,6},{6,2},{1... | collective-permute-start | bytes 540680 | tf_op jit(solution)/shard_map/ppermute | solution.py:31
  8.9 15.9 %collective-permute-start.4 = (bf16[64,1408]{1,0:T(8,128)(2,1)}, bf16[64,1408]{1,0:T(8,128)(2,1)S(1)}, u32[]{:S(2)}, u32[]{:S(2)}) collective-permute-start(bf16[64,1408]{1,0:T(8,128)(2,1)} %get-tuple-element.54), channel_id=1, source_target_pairs={{0,12},{4,8},{8,4},{12,0},{1,13},{5,9},{9,5},{13,1},{2,14},{6,10},... | collective-permute-start | bytes 540680 | tf_op jit(solution)/shard_map/ppermute | solution.py:31
  15.4 0.9 %copy-start.2 = (bf16[64,1408]{1,0:T(8,128)(2,1)S(1)}, bf16[64,1408]{1,0:T(8,128)(2,1)}, u32[]{:S(2)}) copy-start(bf16[64,1408]{1,0:T(8,128)(2,1)} %get-tuple-element.47.piece) | copy-start | bytes 540676
  17.8 2.4 %copy-start.7 = (bf16[64,1408]{1,0:T(8,128)(2,1)S(1)}, bf16[64,1408]{1,0:T(8,128)(2,1)}, u32[]{:S(2)}) copy-start(bf16[64,1408]{1,0:T(8,128)(2,1)} %get-tuple-element.55) | copy-start | bytes 540676
  17.8 7.0 %collective-permute-start.7 = (bf16[64,1408]{1,0:T(8,128)(2,1)S(1)}, bf16[64,1408]{1,0:T(8,128)(2,1)S(1)}, u32[]{:S(2)}, u32[]{:S(2)}) collective-permute-start(bf16[64,1408]{1,0:T(8,128)(2,1)S(1)} %collective-permute-done.2.refs_1_), channel_id=1, source_target_pairs={{0,16},{16,0},{1,17},{17,1},{2,18},{18,2},{3,19},{19,3},{4,20},{20... | collective-permute-start | bytes 540680 | tf_op jit(solution)/shard_map/ppermute | solution.py:31
  19.7 7.1 %collective-permute-start.6 = (bf16[64,1408]{1,0:T(8,128)(2,1)S(1)}, bf16[64,1408]{1,0:T(8,128)(2,1)S(1)}, u32[]{:S(2)}, u32[]{:S(2)}) collective-permute-start(bf16[64,1408]{1,0:T(8,128)(2,1)S(1)} %collective-permute-done.refs_0_), channel_id=1, source_target_pairs={{0,16},{16,0},{1,17},{17,1},{2,18},{18,2},{3,19},{19,3},{4,20},{20... | collective-permute-start | bytes 540680 | tf_op jit(solution)/shard_map/ppermute | solution.py:31
  20.2 11.5 %collective-permute-start.5 = (bf16[64,1408]{1,0:T(8,128)(2,1)S(1)}, bf16[64,1408]{1,0:T(8,128)(2,1)S(1)}, u32[]{:S(2)}, u32[]{:S(2)}) collective-permute-start(bf16[64,1408]{1,0:T(8,128)(2,1)S(1)} %copy-done.7), channel_id=1, source_target_pairs={{0,8},{4,12},{8,0},{12,4},{1,9},{5,13},{9,1},{13,5},{2,10},{6,14},... | collective-permute-start | bytes 540680 | tf_op jit(solution)/shard_map/ppermute | solution.py:31
  20.2 11.5 %collective-permute-start.9 = (bf16[64,1408]{1,0:T(8,128)(2,1)S(1)}, bf16[64,1408]{1,0:T(8,128)(2,1)S(1)}, u32[]{:S(2)}, u32[]{:S(2)}) collective-permute-start(bf16[64,1408]{1,0:T(8,128)(2,1)S(1)} %collective-permute-done.2.refs_1_), channel_id=1, source_target_pairs={{0,1},{1,0},{2,3},{3,2},{4,5},{5,4},{6,7},{7,6},{8,9},{9,8},{10,11... | collective-permute-start | bytes 540680 | tf_op jit(solution)/shard_map/ppermute | solution.py:31
  24.8 6.9 %collective-permute-start.11 = (bf16[64,1408]{1,0:T(8,128)(2,1)S(1)}, bf16[64,1408]{1,0:T(8,128)(2,1)S(1)}, u32[]{:S(2)}, u32[]{:S(2)}) collective-permute-start(bf16[64,1408]{1,0:T(8,128)(2,1)S(1)} %collective-permute-done.7.refs_3_), channel_id=1, source_target_pairs={{0,1},{1,0},{2,3},{3,2},{4,5},{5,4},{6,7},{7,6},{8,9},{9,8},{10,11... | collective-permute-start | bytes 540680 | tf_op jit(solution)/shard_map/ppermute | solution.py:31
  24.8 6.9 %collective-permute-start.8 = (bf16[64,1408]{1,0:T(8,128)(2,1)S(1)}, bf16[64,1408]{1,0:T(8,128)(2,1)S(1)}, u32[]{:S(2)}, u32[]{:S(2)}) collective-permute-start(bf16[64,1408]{1,0:T(8,128)(2,1)S(1)} %collective-permute-done.refs_0_), channel_id=1, source_target_pairs={{0,1},{1,0},{2,3},{3,2},{4,5},{5,4},{6,7},{7,6},{8,9},{9,8},{10,11... | collective-permute-start | bytes 540680 | tf_op jit(solution)/shard_map/ppermute | solution.py:31
  26.8 5.0 %collective-permute-start.10 = (bf16[64,1408]{1,0:T(8,128)(2,1)S(1)}, bf16[64,1408]{1,0:T(8,128)(2,1)S(1)}, u32[]{:S(2)}, u32[]{:S(2)}) collective-permute-start(bf16[64,1408]{1,0:T(8,128)(2,1)S(1)} %collective-permute-done.6.refs_2_), channel_id=1, source_target_pairs={{0,1},{1,0},{2,3},{3,2},{4,5},{5,4},{6,7},{7,6},{8,9},{9,8},{10,11... | collective-permute-start | bytes 540680 | tf_op jit(solution)/shard_map/ppermute | solution.py:31
  31.8 1.7 %collective-permute-start.12 = (bf16[128,1408]{1,0:T(8,128)(2,1)S(1)}, bf16[128,1408]{1,0:T(8,128)(2,1)S(1)}, u32[]{:S(2)}, u32[]{:S(2)}) collective-permute-start(bf16[128,1408]{1,0:T(8,128)(2,1)S(1)} %gather_rows.1.own), channel_id=1, source_target_pairs={{0,1},{1,0},{2,3},{3,2},{4,5},{5,4},{6,7},{7,6},{8,9},{9,8},{10,11... | collective-permute-start | bytes 1081352 | tf_op jit(solution)/shard_map/ppermute | solution.py:31
  34.7 9.4 %collective-permute-start.13 = (bf16[384,128]{1,0:T(8,128)(2,1)S(1)}, bf16[384,128]{1,0:T(8,128)(2,1)S(1)}, u32[]{:S(2)}, u32[]{:S(2)}) collective-permute-start(bf16[384,128]{1,0:T(8,128)(2,1)S(1)} %get-tuple-element.78), channel_id=1, source_target_pairs={{0,8},{4,12},{8,0},{12,4},{1,9},{5,13},{9,1},{13,5},{2,10},{6,14},... | collective-permute-start | bytes 294920 | tf_op jit(solution)/shard_map/ppermute | solution.py:31
  34.8 9.5 %collective-permute-start.14 = (bf16[384,128]{1,0:T(8,128)(2,1)S(1)}, bf16[384,128]{1,0:T(8,128)(2,1)S(1)}, u32[]{:S(2)}, u32[]{:S(2)}) collective-permute-start(bf16[384,128]{1,0:T(8,128)(2,1)S(1)} %get-tuple-element.79), channel_id=1, source_target_pairs={{0,4},{4,0},{8,12},{12,8},{1,5},{5,1},{9,13},{13,9},{2,6},{6,2},{1... | collective-permute-start | bytes 294920 | tf_op jit(solution)/shard_map/ppermute | solution.py:31
  37.2 7.0 %collective-permute-start.15 = (bf16[384,128]{1,0:T(8,128)(2,1)S(1)}, bf16[384,128]{1,0:T(8,128)(2,1)S(1)}, u32[]{:S(2)}, u32[]{:S(2)}) collective-permute-start(bf16[384,128]{1,0:T(8,128)(2,1)S(1)} %get-tuple-element.80), channel_id=1, source_target_pairs={{0,12},{4,8},{8,4},{12,0},{1,13},{5,9},{9,5},{13,1},{2,14},{6,10},... | collective-permute-start | bytes 294920 | tf_op jit(solution)/shard_map/ppermute | solution.py:31
  45.3 5.8 %collective-permute-start.16 = (bf16[64,256]{1,0:T(8,128)(2,1)S(1)}, bf16[64,256]{1,0:T(8,128)(2,1)S(1)}, u32[]{:S(2)}, u32[]{:S(2)}) collective-permute-start(bf16[64,256]{1,0:T(8,128)(2,1)S(1)} %get-tuple-element.82), channel_id=1, source_target_pairs={{0,12},{4,8},{8,4},{12,0},{1,13},{5,9},{9,5},{13,1},{2,14},{6,10},... | collective-permute-start | bytes 98312 | tf_op jit(solution)/shard_map/ppermute | solution.py:31
  47.3 4.9 %collective-permute-start.17 = (bf16[64,256]{1,0:T(8,128)(2,1)S(1)}, bf16[64,256]{1,0:T(8,128)(2,1)S(1)}, u32[]{:S(2)}, u32[]{:S(2)}) collective-permute-start(bf16[64,256]{1,0:T(8,128)(2,1)S(1)} %get-tuple-element.83), channel_id=1, source_target_pairs={{0,8},{4,12},{8,0},{12,4},{1,9},{5,13},{9,1},{13,5},{2,10},{6,14},... | collective-permute-start | bytes 98312 | tf_op jit(solution)/shard_map/ppermute | solution.py:31
  49.3 3.9 %collective-permute-start.18 = (bf16[64,256]{1,0:T(8,128)(2,1)S(1)}, bf16[64,256]{1,0:T(8,128)(2,1)S(1)}, u32[]{:S(2)}, u32[]{:S(2)}) collective-permute-start(bf16[64,256]{1,0:T(8,128)(2,1)S(1)} %get-tuple-element.84), channel_id=1, source_target_pairs={{0,4},{4,0},{8,12},{12,8},{1,5},{5,1},{9,13},{13,9},{2,6},{6,2},{1... | collective-permute-start | bytes 98312 | tf_op jit(solution)/shard_map/ppermute | solution.py:31

commit v6 on v5

--- a/solution.py
+++ b/solution.py
@@ -120,12 +120,12 @@
 
 def panels_kernel(sz, down, *outs_and_sem):
     outs, sem = outs_and_sem[:-1], outs_and_sem[-1]
-    here = lax.axis_index("seq")
+    here, group = lax.axis_index("seq"), lax.axis_index("groups")
     copies = []
     for m, out in enumerate(outs):
         first = pl.multiple_of(sz.start_in_half((here % sz.side) ^ m), LANES)
         copies.append(
-            pltpu.make_async_copy(down.at[0, :, pl.ds(first, sz.span)], out, sem.at[m])
+            pltpu.make_async_copy(down.at[group, :, pl.ds(first, sz.span)], out, sem.at[m])
         )
     for copy in copies:
         copy.start()
@@ -350,7 +350,7 @@
         "panels_out",
         [HBM],
         [((sz.rank, sz.span), bf16, VMEM)] * sz.side,
-        (lax.dynamic_index_in_dim(jnp.swapaxes(down, 1, 2), lax.axis_index("groups"), 0, True),),
+        (jnp.swapaxes(down, 1, 2),),
         (pltpu.SemaphoreType.DMA((sz.side,)),),
     )
     panels = []

time: 54.1 us -> 53.4 us (0.987)
  starting transfers between devices: 24.1 us -> 23 us
  Pallas kernels: 10 us -> 9.36 us
  waiting for transfers between devices: 18.1 us -> 18.7 us
    ppermute x2, starting transfers between devices: 4.66 us -> 3.41 us  [by_heads(): panels.append(lax.ppermute(panels_out[m], ('seq', 'owner'), pairs))]
    pallas_call x10, Pallas kernels: 10 us -> 9.36 us  [call(): pl.pallas_call(functools.partial(kernel, sz), out_shape=[jax.ShapeDtypeSt...]
    ppermute x17, waiting for transfers between devices: 18 us -> 18.7 us  [swap(): lax.ppermute(value, axis, [(i, i ^ mask) for i in range(lax.axis_size(axi...]
  transfers between devices with their start and end apart: 19 -> 19, of which waited for: 9 -> 9; matrix products, arithmetic and copies ran while one was open for 0% -> 0% of each run, Pallas kernels for 13% -> 12%
where the time goes in v6:
time: 53.4 us; the launch traced here: 53.2 us
  starting transfers between devices  23 us (43%)
  waiting for transfers between devices  18.7 us (35%)
  Pallas kernels  9.36 us (18%)
  local copies, waits for them, and re-layouts  2.04 us (4%)
    ppermute x17, starting transfers between devices, swap(): lax.ppermute(value, axis, [(i, i ^ mask) for i in range(lax.axis_size(axi...  19.6 us
    ppermute x17, waiting for transfers between devices, swap(): lax.ppermute(value, axis, [(i, i ^ mask) for i in range(lax.axis_size(axi...  18.7 us
    pallas_call x10, Pallas kernels, call(): pl.pallas_call(functools.partial(kernel, sz), out_shape=[jax.ShapeDtypeSt...  9.36 us
    ppermute x2, starting transfers between devices, by_heads(): panels.append(lax.ppermute(panels_out[m], ('seq', 'owner'), pairs))  3.41 us
    unnamed x16, local copies, waits for them, and re-layouts  2.04 us
  transfers between devices with their start and end apart: 19, of which 9 were waited for; matrix products, arithmetic and copies ran while one was open for 0% of the time, Pallas kernels for 12%

profile of v6, /device:TPU:0, one launch (start us, length us, event | category | flops | bytes accessed | tf_op | source)
XLA Modules:
  0.0 53.2 jit_solution(8511048383701825895)
XLA Ops:
  0.0 0.5 collective-permute-start.1
  0.5 1.1 %copy-done.1 = bf16[1,2,2688,64]{2,3,1,0:T(8,128)(2,1)S(1)} copy-done((bf16[1,2,2688,64]{2,3,1,0:T(8,128)(2,1)S(1)}, bf16[1,2,2688,64]{2,3,1,0:T(8,128)(2,1)}, u32[]{:S(2)}) %copy-start.1) | copy-done | bytes 688152
  1.6 0.1 panels_out.1
  1.7 2.7 %collective-permute-start.2 = (bf16[64,1408]{1,0:T(8,128)(2,1)S(1)}, bf16[64,1408]{1,0:T(8,128)(2,1)S(1)}, u32[]{:S(2)}, u32[]{:S(2)}) collective-permute-start(bf16[64,1408]{1,0:T(8,128)(2,1)S(1)} %get-tuple-element.50), channel_id=1, source_target_pairs={{0,4},{1,12},{4,0},{5,8},{8,5},{9,13},{12,1},{13,9},{2,6},{3,14},{... | collective-permute-start | bytes 540680 | tf_op jit(solution)/shard_map/ppermute | solution.py:363
  4.4 0.7 %collective-permute-start = (bf16[64,1408]{1,0:T(8,128)(2,1)S(1)}, bf16[64,1408]{1,0:T(8,128)(2,1)S(1)}, u32[]{:S(2)}, u32[]{:S(2)}) collective-permute-start(bf16[64,1408]{1,0:T(8,128)(2,1)S(1)} %get-tuple-element.45), channel_id=1, source_target_pairs={{0,0},{1,8},{4,4},{5,12},{8,1},{9,9},{12,5},{13,13},{2,2},{3,10},{... | collective-permute-start | bytes 540680 | tf_op jit(solution)/shard_map/ppermute | solution.py:363
  5.1 2.2 %norm_rows.1 = (bf16[64,1408]{1,0:T(8,128)(2,1)}, bf16[64,1408]{1,0:T(8,128)(2,1)}, bf16[64,1408]{1,0:T(8,128)(2,1)}, bf16[64,1408]{1,0:T(8,128)(2,1)}) custom-call(bf16[64,5376]{1,0:T(8,128)(2,1)} %bitcast.12, f32[1,5376]{1,0:T(1,128)} %gain.1, bf16[64,1024]{1,0:T(8,128)(2,1)} %bitcast.13, bf16[64,512]{1,0:T(8,128)(2,1)} %bitcast.15, ...), custom_call_target="tpu_custom_call" | custom-call | tf_op jit(solution)/shard_map/norm_rows/pallas_call | solution.py:337
  7.3 0.1 collective-permute-start.3
  7.4 7.3 %collective-permute-start.4 = (bf16[64,1408]{1,0:T(8,128)(2,1)}, bf16[64,1408]{1,0:T(8,128)(2,1)S(1)}, u32[]{:S(2)}, u32[]{:S(2)}) collective-permute-start(bf16[64,1408]{1,0:T(8,128)(2,1)} %get-tuple-element.54), channel_id=1, source_target_pairs={{0,12},{4,8},{8,4},{12,0},{1,13},{5,9},{9,5},{13,1},{2,14},{6,10},... | collective-permute-start | bytes 540680 | tf_op jit(solution)/shard_map/ppermute | solution.py:31
  14.8 0.9 %copy-done.2 = bf16[64,1408]{1,0:T(8,128)(2,1)S(1)} copy-done((bf16[64,1408]{1,0:T(8,128)(2,1)S(1)}, bf16[64,1408]{1,0:T(8,128)(2,1)}, u32[]{:S(2)}) %copy-start.2) | copy-done | bytes 180248
  15.7 1.5 %table.1 = (s32[4,4]{1,0:T(4,128)S(1)}, bf16[64,1408]{1,0:T(8,128)(2,1)S(1)}) custom-call(s32[4]{0:T(128)S(1)} %copy-done.3, s32[4]{0:T(128)S(1)} %copy-done.4, s32[8]{0:T(128)S(1)} %copy-done.5, s32[8]{0:T(128)S(1)} %copy-done.6, bf16[64,1408]{1,0:T(8,128)(2,1)S(1)} %copy-done.2), custom_call_target="tpu_custom_call" | custom-call | bytes 67108864 | tf_op jit(solution)/shard_map/table/pallas_call | solution.py:337
  17.2 0.0 collective-permute-done.2.refs_1_
  17.2 1.6 %collective-permute-start.7 = (bf16[64,1408]{1,0:T(8,128)(2,1)S(1)}, bf16[64,1408]{1,0:T(8,128)(2,1)S(1)}, u32[]{:S(2)}, u32[]{:S(2)}) collective-permute-start(bf16[64,1408]{1,0:T(8,128)(2,1)S(1)} %collective-permute-done.2.refs_1_), channel_id=1, source_target_pairs={{0,16},{16,0},{1,17},{17,1},{2,18},{18,2},{3,19},{19,3},{4,20},{20... | collective-permute-start | bytes 540680 | tf_op jit(solution)/shard_map/ppermute | solution.py:31
  18.8 0.0 collective-permute-done.1.base_other
  18.8 0.2 matrix_rows.1.matrix
  19.0 0.0 collective-permute-done.refs_0_
  19.0 0.6 %collective-permute-start.6 = (bf16[64,1408]{1,0:T(8,128)(2,1)S(1)}, bf16[64,1408]{1,0:T(8,128)(2,1)S(1)}, u32[]{:S(2)}, u32[]{:S(2)}) collective-permute-start(bf16[64,1408]{1,0:T(8,128)(2,1)S(1)} %collective-permute-done.refs_0_), channel_id=1, source_target_pairs={{0,16},{16,0},{1,17},{17,1},{2,18},{18,2},{3,19},{19,3},{4,20},{20... | collective-permute-start | bytes 540680 | tf_op jit(solution)/shard_map/ppermute | solution.py:31
  19.6 0.0 collective-permute-start.5
  19.6 0.0 collective-permute-done.3.refs_3_
  19.6 0.1 collective-permute-start.9
  19.7 4.5 %collective-permute-done.7.refs_3_ = bf16[64,1408]{1,0:T(8,128)(2,1)S(1)} collective-permute-done((bf16[64,1408]{1,0:T(8,128)(2,1)S(1)}, bf16[64,1408]{1,0:T(8,128)(2,1)S(1)}, u32[]{:S(2)}, u32[]{:S(2)}) %collective-permute-start.7) | collective-permute-done | bytes 180256 | tf_op jit(solution)/shard_map/ppermute | solution.py:31
  24.2 0.0 collective-permute-start.11
  24.2 0.0 collective-permute-done.4.refs_1_
  24.2 0.5 collective-permute-start.8
  24.7 1.4 %collective-permute-done.6.refs_2_ = bf16[64,1408]{1,0:T(8,128)(2,1)S(1)} collective-permute-done((bf16[64,1408]{1,0:T(8,128)(2,1)S(1)}, bf16[64,1408]{1,0:T(8,128)(2,1)S(1)}, u32[]{:S(2)}, u32[]{:S(2)}) %collective-permute-start.6) | collective-permute-done | bytes 180256 | tf_op jit(solution)/shard_map/ppermute | solution.py:31
  26.1 0.0 collective-permute-start.10
  26.1 5.0 %collective-permute-done.5.refs_2_ = bf16[64,1408]{1,0:T(8,128)(2,1)S(1)} collective-permute-done((bf16[64,1408]{1,0:T(8,128)(2,1)S(1)}, bf16[64,1408]{1,0:T(8,128)(2,1)S(1)}, u32[]{:S(2)}, u32[]{:S(2)}) %collective-permute-start.5) | collective-permute-done | bytes 180256 | tf_op jit(solution)/shard_map/ppermute | solution.py:31
  31.1 0.0 collective-permute-done.9.refs_5_
  31.1 0.0 collective-permute-done.11.refs_7_
  31.1 0.0 collective-permute-done.10.refs_6_
  31.2 0.1 collective-permute-start.12
  31.2 1.3 %project_own.1 = (bf16[256,1408]{1,0:T(8,128)(2,1)S(1)}, bf16[128,512]{1,0:T(8,128)(2,1)S(1)}, bf16[64,128]{1,0:T(8,128)(2,1)S(1)}) custom-call(s32[4,4]{1,0:T(4,128)S(1)} %get-tuple-element.49.table, bf16[1408,512]{1,0:T(8,128)(2,1)S(1)} %matrix_rows.1.matrix, bf16[128,1408]{1,0:T(8,128)(2,1)S(1)} %gather_rows.1.own, ...), custom_call_target="tpu_custom_call" | custom-call | tf_op jit(solution)/shard_map/project_own/pallas_call | solution.py:337
  32.5 0.4 collective-permute-done.12.other
  32.9 1.2 %project_other.1 = (bf16[384,128]{1,0:T(8,128)(2,1)S(1)}, bf16[384,128]{1,0:T(8,128)(2,1)S(1)}, bf16[384,128]{1,0:T(8,128)(2,1)S(1)}, bf16[384,128]{1,0:T(8,128)(2,1)S(1)}) custom-call(s32[4,4]{1,0:T(4,128)S(1)} %get-tuple-element.49.table, bf16[1408,512]{1,0:T(8,128)(2,1)S(1)} %matrix_rows.1.matrix, bf16[128,1408]{1,0:T(8,128)(2,1)S(1)} %collective-permute-done.12.other, ...), custom_call_target="tpu_custom_call" | custom-call | tf_op jit(solution)/shard_map/project_other/pallas_call | solution.py:337
  34.1 0.1 collective-permute-start.13
  34.2 2.4 %collective-permute-start.14 = (bf16[384,128]{1,0:T(8,128)(2,1)S(1)}, bf16[384,128]{1,0:T(8,128)(2,1)S(1)}, u32[]{:S(2)}, u32[]{:S(2)}) collective-permute-start(bf16[384,128]{1,0:T(8,128)(2,1)S(1)} %get-tuple-element.79), channel_id=1, source_target_pairs={{0,4},{4,0},{8,12},{12,8},{1,5},{5,1},{9,13},{13,9},{2,6},{6,2},{1... | collective-permute-start | bytes 294920 | tf_op jit(solution)/shard_map/ppermute | solution.py:31
  36.6 1.9 %collective-permute-start.15 = (bf16[384,128]{1,0:T(8,128)(2,1)S(1)}, bf16[384,128]{1,0:T(8,128)(2,1)S(1)}, u32[]{:S(2)}, u32[]{:S(2)}) collective-permute-start(bf16[384,128]{1,0:T(8,128)(2,1)S(1)} %get-tuple-element.80), channel_id=1, source_target_pairs={{0,12},{4,8},{8,4},{12,0},{1,13},{5,9},{9,5},{13,1},{2,14},{6,10},... | collective-permute-start | bytes 294920 | tf_op jit(solution)/shard_map/ppermute | solution.py:31
  38.5 1.1 %softmax_rows.1 = (bf16[512,256]{1,0:T(8,128)(2,1)S(1)}, bf16[256,128]{1,0:T(8,128)(2,1)S(1)}, f32[256,128]{1,0:T(8,128)S(1)}) custom-call(s32[4,4]{1,0:T(4,128)S(1)} %get-tuple-element.49.table, bf16[64,1408]{1,0:T(8,128)(2,1)S(1)} %get-tuple-element.58.refs_0_, bf16[64,1408]{1,0:T(8,128)(2,1)S(1)} %collective-permute-done.4.refs_1_, ...), custom_call_target="tpu_custom_call" | custom-call | tf_op jit(solution)/shard_map/softmax_rows/pallas_call | solution.py:337
  39.7 3.8 %collective-permute-done.13.refs_1_ = bf16[384,128]{1,0:T(8,128)(2,1)S(1)} collective-permute-done((bf16[384,128]{1,0:T(8,128)(2,1)S(1)}, bf16[384,128]{1,0:T(8,128)(2,1)S(1)}, u32[]{:S(2)}, u32[]{:S(2)}) %collective-permute-start.13) | collective-permute-done | bytes 98336 | tf_op jit(solution)/shard_map/ppermute | solution.py:31
  43.4 0.2 collective-permute-done.14.refs_2_
  43.6 0.0 collective-permute-done.15.refs_3_
  43.6 1.1 %mix_values.1 = (bf16[64,256]{1,0:T(8,128)(2,1)S(1)}, bf16[64,256]{1,0:T(8,128)(2,1)S(1)}, bf16[64,256]{1,0:T(8,128)(2,1)S(1)}, bf16[64,256]{1,0:T(8,128)(2,1)S(1)}) custom-call(s32[4,4]{1,0:T(4,128)S(1)} %get-tuple-element.49.table, bf16[512,256]{1,0:T(8,128)(2,1)S(1)} %get-tuple-element.62.softmax, bf16[256,128]{1,0:T(8,128)(2,1)S(1)} %get-tuple-element.63.raise_picked, ...), custom_call_target="tpu_custom_call" | custom-call | tf_op jit(solution)/shard_map/mix_values/pallas_call | solution.py:337
  44.7 2.0 %collective-permute-start.16 = (bf16[64,256]{1,0:T(8,128)(2,1)S(1)}, bf16[64,256]{1,0:T(8,128)(2,1)S(1)}, u32[]{:S(2)}, u32[]{:S(2)}) collective-permute-start(bf16[64,256]{1,0:T(8,128)(2,1)S(1)} %get-tuple-element.82), channel_id=1, source_target_pairs={{0,12},{4,8},{8,4},{12,0},{1,13},{5,9},{9,5},{13,1},{2,14},{6,10},... | collective-permute-start | bytes 98312 | tf_op jit(solution)/shard_map/ppermute | solution.py:31
  46.7 1.9 %collective-permute-start.17 = (bf16[64,256]{1,0:T(8,128)(2,1)S(1)}, bf16[64,256]{1,0:T(8,128)(2,1)S(1)}, u32[]{:S(2)}, u32[]{:S(2)}) collective-permute-start(bf16[64,256]{1,0:T(8,128)(2,1)S(1)} %get-tuple-element.83), channel_id=1, source_target_pairs={{0,8},{4,12},{8,0},{12,4},{1,9},{5,13},{9,1},{13,5},{2,10},{6,14},... | collective-permute-start | bytes 98312 | tf_op jit(solution)/shard_map/ppermute | solution.py:31
  48.7 0.5 collective-permute-start.18
  49.1 1.4 %collective-permute-done.16.refs_1_ = bf16[64,256]{1,0:T(8,128)(2,1)S(1)} collective-permute-done((bf16[64,256]{1,0:T(8,128)(2,1)S(1)}, bf16[64,256]{1,0:T(8,128)(2,1)S(1)}, u32[]{:S(2)}, u32[]{:S(2)}) %collective-permute-start.16) | collective-permute-done | bytes 32800 | tf_op jit(solution)/shard_map/ppermute | solution.py:31
  50.5 1.1 %collective-permute-done.17.refs_2_ = bf16[64,256]{1,0:T(8,128)(2,1)S(1)} collective-permute-done((bf16[64,256]{1,0:T(8,128)(2,1)S(1)}, bf16[64,256]{1,0:T(8,128)(2,1)S(1)}, u32[]{:S(2)}, u32[]{:S(2)}) %collective-permute-start.17) | collective-permute-done | bytes 32800 | tf_op jit(solution)/shard_map/ppermute | solution.py:31
  51.6 1.0 %collective-permute-done.18.refs_3_ = bf16[64,256]{1,0:T(8,128)(2,1)S(1)} collective-permute-done((bf16[64,256]{1,0:T(8,128)(2,1)S(1)}, bf16[64,256]{1,0:T(8,128)(2,1)S(1)}, u32[]{:S(2)}, u32[]{:S(2)}) %collective-permute-start.18) | collective-permute-done | bytes 32800 | tf_op jit(solution)/shard_map/ppermute | solution.py:31
  52.6 0.7 %place_heads.1 = bf16[64,1024]{1,0:T(8,128)(2,1)} custom-call(bf16[64,256]{1,0:T(8,128)(2,1)S(1)} %get-tuple-element.81.refs_0_, bf16[64,256]{1,0:T(8,128)(2,1)S(1)} %collective-permute-done.16.refs_1_, bf16[64,256]{1,0:T(8,128)(2,1)S(1)} %collective-permute-done.17.refs_2_, bf16[64,256]{1,0:T(8,128)(2,1)S(1)} %collective-permute-done.18.refs_3_), custom_call_target="tpu_custom_call" | custom-call | tf_op jit(solution)/shard_map/place_heads/pallas_call | solution.py:337
  (16 shorter events, 0.1 us)
Async XLA Ops:
  0.0 18.8 %copy-start = (bf16[1,672,1024]{2,1,0:T(8,128)(2,1)S(1)}, bf16[1,672,1024]{2,1,0:T(8,128)(2,1)}, u32[]{:S(2)}) copy-start(bf16[1,672,1024]{2,1,0:T(8,128)(2,1)} %param.15) | copy-start | bytes 4128772
  0.0 18.8 %collective-permute-start.1 = (bf16[672,1024]{1,0:T(8,128)(2,1)}, bf16[672,1024]{1,0:T(8,128)(2,1)S(1)}, u32[]{:S(2)}, u32[]{:S(2)}) collective-permute-start(bf16[672,1024]{1,0:T(8,128)(2,1)} %bitcast.9), channel_id=1, source_target_pairs={{0,1},{1,0},{2,3},{3,2},{4,5},{5,4},{6,7},{7,6},{8,9},{9,8},{10,11... | collective-permute-start | bytes 4128776 | tf_op jit(solution)/shard_map/ppermute | solution.py:31
  0.5 1.1 %copy-start.1 = (bf16[1,2,2688,64]{2,3,1,0:T(8,128)(2,1)S(1)}, bf16[1,2,2688,64]{2,3,1,0:T(8,128)(2,1)}, u32[]{:S(2)}) copy-start(bf16[1,2,2688,64]{2,3,1,0:T(8,128)(2,1)} %param.16) | copy-start | bytes 2064388
  1.6 13.2 %copy-start.3 = (s32[4]{0:T(128)S(1)}, s32[4]{0:T(128)}, u32[]{:S(2)}) copy-start(s32[4]{0:T(128)} %lengths.1) | copy-start | bytes 52
  1.6 13.2 %copy-start.4 = (s32[4]{0:T(128)S(1)}, s32[4]{0:T(128)}, u32[]{:S(2)}) copy-start(s32[4]{0:T(128)} %adapters.1) | copy-start | bytes 52
  1.6 13.2 %copy-start.5 = (s32[8]{0:T(128)S(1)}, s32[8]{0:T(128)}, u32[]{:S(2)}) copy-start(s32[8]{0:T(128)} %ranks.1) | copy-start | bytes 100
  1.6 13.2 %copy-start.6 = (s32[8]{0:T(128)S(1)}, s32[8]{0:T(128)}, u32[]{:S(2)}) copy-start(s32[8]{0:T(128)} %slots.1) | copy-start | bytes 100
  1.7 15.5 %collective-permute-start.2 = (bf16[64,1408]{1,0:T(8,128)(2,1)S(1)}, bf16[64,1408]{1,0:T(8,128)(2,1)S(1)}, u32[]{:S(2)}, u32[]{:S(2)}) collective-permute-start(bf16[64,1408]{1,0:T(8,128)(2,1)S(1)} %get-tuple-element.50), channel_id=1, source_target_pairs={{0,4},{1,12},{4,0},{5,8},{8,5},{9,13},{12,1},{13,9},{2,6},{3,14},{... | collective-permute-start | bytes 540680 | tf_op jit(solution)/shard_map/ppermute | solution.py:363
  4.4 14.6 %collective-permute-start = (bf16[64,1408]{1,0:T(8,128)(2,1)S(1)}, bf16[64,1408]{1,0:T(8,128)(2,1)S(1)}, u32[]{:S(2)}, u32[]{:S(2)}) collective-permute-start(bf16[64,1408]{1,0:T(8,128)(2,1)S(1)} %get-tuple-element.45), channel_id=1, source_target_pairs={{0,0},{1,8},{4,4},{5,12},{8,1},{9,9},{12,5},{13,13},{2,2},{3,10},{... | collective-permute-start | bytes 540680 | tf_op jit(solution)/shard_map/ppermute | solution.py:363
  7.3 12.3 %collective-permute-start.3 = (bf16[64,1408]{1,0:T(8,128)(2,1)}, bf16[64,1408]{1,0:T(8,128)(2,1)S(1)}, u32[]{:S(2)}, u32[]{:S(2)}) collective-permute-start(bf16[64,1408]{1,0:T(8,128)(2,1)} %get-tuple-element.53), channel_id=1, source_target_pairs={{0,4},{4,0},{8,12},{12,8},{1,5},{5,1},{9,13},{13,9},{2,6},{6,2},{1... | collective-permute-start | bytes 540680 | tf_op jit(solution)/shard_map/ppermute | solution.py:31
  7.4 16.7 %collective-permute-start.4 = (bf16[64,1408]{1,0:T(8,128)(2,1)}, bf16[64,1408]{1,0:T(8,128)(2,1)S(1)}, u32[]{:S(2)}, u32[]{:S(2)}) collective-permute-start(bf16[64,1408]{1,0:T(8,128)(2,1)} %get-tuple-element.54), channel_id=1, source_target_pairs={{0,12},{4,8},{8,4},{12,0},{1,13},{5,9},{9,5},{13,1},{2,14},{6,10},... | collective-permute-start | bytes 540680 | tf_op jit(solution)/shard_map/ppermute | solution.py:31
  14.8 0.9 %copy-start.2 = (bf16[64,1408]{1,0:T(8,128)(2,1)S(1)}, bf16[64,1408]{1,0:T(8,128)(2,1)}, u32[]{:S(2)}) copy-start(bf16[64,1408]{1,0:T(8,128)(2,1)} %get-tuple-element.47.piece) | copy-start | bytes 540676
  17.2 2.4 %copy-start.7 = (bf16[64,1408]{1,0:T(8,128)(2,1)S(1)}, bf16[64,1408]{1,0:T(8,128)(2,1)}, u32[]{:S(2)}) copy-start(bf16[64,1408]{1,0:T(8,128)(2,1)} %get-tuple-element.55) | copy-start | bytes 540676
  17.2 7.0 %collective-permute-start.7 = (bf16[64,1408]{1,0:T(8,128)(2,1)S(1)}, bf16[64,1408]{1,0:T(8,128)(2,1)S(1)}, u32[]{:S(2)}, u32[]{:S(2)}) collective-permute-start(bf16[64,1408]{1,0:T(8,128)(2,1)S(1)} %collective-permute-done.2.refs_1_), channel_id=1, source_target_pairs={{0,16},{16,0},{1,17},{17,1},{2,18},{18,2},{3,19},{19,3},{4,20},{20... | collective-permute-start | bytes 540680 | tf_op jit(solution)/shard_map/ppermute | solution.py:31
  19.0 7.1 %collective-permute-start.6 = (bf16[64,1408]{1,0:T(8,128)(2,1)S(1)}, bf16[64,1408]{1,0:T(8,128)(2,1)S(1)}, u32[]{:S(2)}, u32[]{:S(2)}) collective-permute-start(bf16[64,1408]{1,0:T(8,128)(2,1)S(1)} %collective-permute-done.refs_0_), channel_id=1, source_target_pairs={{0,16},{16,0},{1,17},{17,1},{2,18},{18,2},{3,19},{19,3},{4,20},{20... | collective-permute-start | bytes 540680 | tf_op jit(solution)/shard_map/ppermute | solution.py:31
  19.6 11.5 %collective-permute-start.5 = (bf16[64,1408]{1,0:T(8,128)(2,1)S(1)}, bf16[64,1408]{1,0:T(8,128)(2,1)S(1)}, u32[]{:S(2)}, u32[]{:S(2)}) collective-permute-start(bf16[64,1408]{1,0:T(8,128)(2,1)S(1)} %copy-done.7), channel_id=1, source_target_pairs={{0,8},{4,12},{8,0},{12,4},{1,9},{5,13},{9,1},{13,5},{2,10},{6,14},... | collective-permute-start | bytes 540680 | tf_op jit(solution)/shard_map/ppermute | solution.py:31
  19.6 11.5 %collective-permute-start.9 = (bf16[64,1408]{1,0:T(8,128)(2,1)S(1)}, bf16[64,1408]{1,0:T(8,128)(2,1)S(1)}, u32[]{:S(2)}, u32[]{:S(2)}) collective-permute-start(bf16[64,1408]{1,0:T(8,128)(2,1)S(1)} %collective-permute-done.2.refs_1_), channel_id=1, source_target_pairs={{0,1},{1,0},{2,3},{3,2},{4,5},{5,4},{6,7},{7,6},{8,9},{9,8},{10,11... | collective-permute-start | bytes 540680 | tf_op jit(solution)/shard_map/ppermute | solution.py:31
  24.2 6.9 %collective-permute-start.11 = (bf16[64,1408]{1,0:T(8,128)(2,1)S(1)}, bf16[64,1408]{1,0:T(8,128)(2,1)S(1)}, u32[]{:S(2)}, u32[]{:S(2)}) collective-permute-start(bf16[64,1408]{1,0:T(8,128)(2,1)S(1)} %collective-permute-done.7.refs_3_), channel_id=1, source_target_pairs={{0,1},{1,0},{2,3},{3,2},{4,5},{5,4},{6,7},{7,6},{8,9},{9,8},{10,11... | collective-permute-start | bytes 540680 | tf_op jit(solution)/shard_map/ppermute | solution.py:31
  24.2 6.9 %collective-permute-start.8 = (bf16[64,1408]{1,0:T(8,128)(2,1)S(1)}, bf16[64,1408]{1,0:T(8,128)(2,1)S(1)}, u32[]{:S(2)}, u32[]{:S(2)}) collective-permute-start(bf16[64,1408]{1,0:T(8,128)(2,1)S(1)} %collective-permute-done.refs_0_), channel_id=1, source_target_pairs={{0,1},{1,0},{2,3},{3,2},{4,5},{5,4},{6,7},{7,6},{8,9},{9,8},{10,11... | collective-permute-start | bytes 540680 | tf_op jit(solution)/shard_map/ppermute | solution.py:31
  26.1 5.0 %collective-permute-start.10 = (bf16[64,1408]{1,0:T(8,128)(2,1)S(1)}, bf16[64,1408]{1,0:T(8,128)(2,1)S(1)}, u32[]{:S(2)}, u32[]{:S(2)}) collective-permute-start(bf16[64,1408]{1,0:T(8,128)(2,1)S(1)} %collective-permute-done.6.refs_2_), channel_id=1, source_target_pairs={{0,1},{1,0},{2,3},{3,2},{4,5},{5,4},{6,7},{7,6},{8,9},{9,8},{10,11... | collective-permute-start | bytes 540680 | tf_op jit(solution)/shard_map/ppermute | solution.py:31
  31.2 1.7 %collective-permute-start.12 = (bf16[128,1408]{1,0:T(8,128)(2,1)S(1)}, bf16[128,1408]{1,0:T(8,128)(2,1)S(1)}, u32[]{:S(2)}, u32[]{:S(2)}) collective-permute-start(bf16[128,1408]{1,0:T(8,128)(2,1)S(1)} %gather_rows.1.own), channel_id=1, source_target_pairs={{0,1},{1,0},{2,3},{3,2},{4,5},{5,4},{6,7},{7,6},{8,9},{9,8},{10,11... | collective-permute-start | bytes 1081352 | tf_op jit(solution)/shard_map/ppermute | solution.py:31
  34.1 9.4 %collective-permute-start.13 = (bf16[384,128]{1,0:T(8,128)(2,1)S(1)}, bf16[384,128]{1,0:T(8,128)(2,1)S(1)}, u32[]{:S(2)}, u32[]{:S(2)}) collective-permute-start(bf16[384,128]{1,0:T(8,128)(2,1)S(1)} %get-tuple-element.78), channel_id=1, source_target_pairs={{0,8},{4,12},{8,0},{12,4},{1,9},{5,13},{9,1},{13,5},{2,10},{6,14},... | collective-permute-start | bytes 294920 | tf_op jit(solution)/shard_map/ppermute | solution.py:31
  34.2 9.5 %collective-permute-start.14 = (bf16[384,128]{1,0:T(8,128)(2,1)S(1)}, bf16[384,128]{1,0:T(8,128)(2,1)S(1)}, u32[]{:S(2)}, u32[]{:S(2)}) collective-permute-start(bf16[384,128]{1,0:T(8,128)(2,1)S(1)} %get-tuple-element.79), channel_id=1, source_target_pairs={{0,4},{4,0},{8,12},{12,8},{1,5},{5,1},{9,13},{13,9},{2,6},{6,2},{1... | collective-permute-start | bytes 294920 | tf_op jit(solution)/shard_map/ppermute | solution.py:31
  36.6 7.0 %collective-permute-start.15 = (bf16[384,128]{1,0:T(8,128)(2,1)S(1)}, bf16[384,128]{1,0:T(8,128)(2,1)S(1)}, u32[]{:S(2)}, u32[]{:S(2)}) collective-permute-start(bf16[384,128]{1,0:T(8,128)(2,1)S(1)} %get-tuple-element.80), channel_id=1, source_target_pairs={{0,12},{4,8},{8,4},{12,0},{1,13},{5,9},{9,5},{13,1},{2,14},{6,10},... | collective-permute-start | bytes 294920 | tf_op jit(solution)/shard_map/ppermute | solution.py:31
  44.7 5.8 %collective-permute-start.16 = (bf16[64,256]{1,0:T(8,128)(2,1)S(1)}, bf16[64,256]{1,0:T(8,128)(2,1)S(1)}, u32[]{:S(2)}, u32[]{:S(2)}) collective-permute-start(bf16[64,256]{1,0:T(8,128)(2,1)S(1)} %get-tuple-element.82), channel_id=1, source_target_pairs={{0,12},{4,8},{8,4},{12,0},{1,13},{5,9},{9,5},{13,1},{2,14},{6,10},... | collective-permute-start | bytes 98312 | tf_op jit(solution)/shard_map/ppermute | solution.py:31
  46.7 4.9 %collective-permute-start.17 = (bf16[64,256]{1,0:T(8,128)(2,1)S(1)}, bf16[64,256]{1,0:T(8,128)(2,1)S(1)}, u32[]{:S(2)}, u32[]{:S(2)}) collective-permute-start(bf16[64,256]{1,0:T(8,128)(2,1)S(1)} %get-tuple-element.83), channel_id=1, source_target_pairs={{0,8},{4,12},{8,0},{12,4},{1,9},{5,13},{9,1},{13,5},{2,10},{6,14},... | collective-permute-start | bytes 98312 | tf_op jit(solution)/shard_map/ppermute | solution.py:31
  48.7 3.9 %collective-permute-start.18 = (bf16[64,256]{1,0:T(8,128)(2,1)S(1)}, bf16[64,256]{1,0:T(8,128)(2,1)S(1)}, u32[]{:S(2)}, u32[]{:S(2)}) collective-permute-start(bf16[64,256]{1,0:T(8,128)(2,1)S(1)} %get-tuple-element.84), channel_id=1, source_target_pairs={{0,4},{4,0},{8,12},{12,8},{1,5},{5,1},{9,13},{13,9},{2,6},{6,2},{1... | collective-permute-start | bytes 98312 | tf_op jit(solution)/shard_map/ppermute | solution.py:31

commit v7 on v6

--- a/solution.py
+++ b/solution.py
@@ -225,11 +225,10 @@
     spare = sz.span - sz.features
     out[0:spare] = jnp.zeros((spare, wide), bf16)
     out[sz.span - spare :] = jnp.zeros((spare, wide), bf16)
-    columns = pl.ds(pl.multiple_of(core * wide, wide), wide)
     copies = []
     for j, (ref, owner) in enumerate(((base, core), (base_other, 1 - core))):
         place = pl.ds(pl.multiple_of(skip + owner * depth, 16), depth)
-        copies.append(pltpu.make_async_copy(ref.at[:, columns], out.at[place], sem.at[j]))
+        copies.append(pltpu.make_async_copy(ref, out.at[place], sem.at[j]))
         copies[-1].start()
     for copy in copies:
         copy.wait()
@@ -243,71 +242,66 @@
         out[pl.ds(first, sz.rows_half), :] = piece[: sz.rows_half]
 
 
-def project_half(sz, table, matrix, rows, picked, owner):
-    values = jnp.dot(rows[...], matrix[...], preferred_element_type=f32)
+def project_kernel(sz, table, matrix, own, *refs):
+    panels, refs = refs[: 2 * sz.groups * sz.side], refs[2 * sz.groups * sz.side :]
+    outs, (picked, stacked, values) = refs[: sz.seq], refs[sz.seq :]
+    here, core = lax.axis_index("seq"), lax.axis_index("owner")
+    for p, panel in enumerate(panels):
+        stacked[p * sz.rank : (p + 1) * sz.rank] = panel[...]
+    for r in range(sz.requests):
+        first = pl.multiple_of(table[2, r] * sz.rank, sz.rank)
+        picked[r * sz.rank : (r + 1) * sz.rank] = stacked[pl.ds(first, sz.rank), :]
+    values[...] = jnp.dot(own[...], matrix[...], preferred_element_type=f32).astype(bf16)
     low = lax.dot_general(
-        picked[...], rows[...], (((1,), (1,)), ((), ())), preferred_element_type=f32
-    )
-    shape = (sz.rank, sz.seq * sz.rows_half)
-    place = lax.broadcasted_iota(jnp.int32, shape, 1) + owner * shape[1]
+        picked[...], own[...], (((1,), (1,)), ((), ())), preferred_element_type=f32
+    )
+    count = sz.seq * sz.rows_half
+    shape = (sz.rank, count)
+    place = lax.broadcasted_iota(jnp.int32, shape, 1) + core * count
     request = request_column(sz, table, token_at(sz, place))
     rank = lax.broadcasted_iota(jnp.int32, shape, 0)
     reduced = jnp.zeros(shape, f32)
     for r in range(sz.requests):
         live = (request == r) & (rank < table[1, r])
         reduced = jnp.where(live, low[r * sz.rank : (r + 1) * sz.rank], reduced)
-    return values.astype(bf16), reduced.astype(bf16)
-
-
-def project_own_kernel(sz, table, matrix, own, *refs):
-    panels, (picked, values, low, stacked) = refs[:-4], refs[-4:]
-    for p, panel in enumerate(panels):
-        stacked[p * sz.rank : (p + 1) * sz.rank] = panel[...]
-    for r in range(sz.requests):
-        first = pl.multiple_of(table[2, r] * sz.rank, sz.rank)
-        picked[r * sz.rank : (r + 1) * sz.rank] = stacked[pl.ds(first, sz.rank), :]
-    values[...], low[...] = project_half(
-        sz, table, matrix, own, picked, lax.axis_index("owner")
-    )
-
-
-def project_other_kernel(sz, table, matrix, other, picked, values_own, low_own, *refs):
-    outs, values_other = refs[: sz.seq], refs[sz.seq]
+    reduced = reduced.astype(bf16)
+    for k, out in enumerate(outs):
+        for half in range(2):
+            first = pl.multiple_of((half * sz.heads_here + (here ^ k)) * HEAD_SIZE, HEAD_SIZE)
+            out[half * count : (half + 1) * count] = values[:, pl.ds(first, HEAD_SIZE)]
+        out[2 * count :] = reduced
+
+
+def add_kernel(sz, *refs):
+    pieces, (kept, sent) = refs[: sz.seq], refs[sz.seq :]
+    core = lax.axis_index("owner")
+    count = sz.seq * sz.rows_half
+    for out, head in ((kept, core), (sent, 1 - core)):
+        place = pl.ds(pl.multiple_of(head * count, count), count)
+        out[:count] = sum(piece[place, :].astype(f32) for piece in pieces)
+    low = sum(piece[2 * count :].astype(f32) for piece in pieces)
+    kept[count:] = low
+    sent[count:] = low
+
+
+def mix_kernel(sz, table, softmax, raise_picked, scale, kept, received, *refs):
+    outs, (wide, base, mixed) = refs[: sz.seq], refs[sz.seq :]
     here, core = lax.axis_index("seq"), lax.axis_index("owner")
-    values_other[...], low_other = project_half(sz, table, matrix, other, picked, 1 - core)
     count = sz.seq * sz.rows_half
-    for k, out in enumerate(outs):
-        columns = pl.ds(pl.multiple_of((here ^ k) * HEAD_SIZE, HEAD_SIZE), HEAD_SIZE)
-        for values, low, owner in (
-            (values_own, low_own[...], core),
-            (values_other, low_other, 1 - core),
-        ):
-            first = pl.multiple_of(owner * count, count)
-            out[pl.ds(first, count), :] = values[:, columns]
-            first = pl.multiple_of(sz.tokens + owner * sz.rank, sz.rank)
-            out[pl.ds(first, sz.rank), :] = low
-
-
-def mix_kernel(sz, table, softmax, raise_picked, scale, *refs):
-    partials, refs = refs[: sz.seq], refs[sz.seq :]
-    outs, (wide, mixed) = refs[: sz.seq], refs[sz.seq :]
-    here = lax.axis_index("seq")
-    count = sz.seq * sz.rows_half
-    low = sum(partial[sz.tokens :].astype(f32) for partial in partials)
     shape = (sz.rank, count)
-    for owner in range(2):
-        place = lax.broadcasted_iota(jnp.int32, shape, 1) + owner * count
+    for ref, owner in ((kept, core), (received, 1 - core)):
+        first = pl.multiple_of(owner * count, count)
+        base[pl.ds(first, count), :] = ref[:count]
+        place = lax.broadcasted_iota(jnp.int32, shape, 1) + first
         request = request_column(sz, table, token_at(sz, place))
-        own = low[owner * sz.rank : (owner + 1) * sz.rank]
         for r in range(sz.requests):
-            wide[r * sz.rank : (r + 1) * sz.rank, owner * count : (owner + 1) * count] = jnp.where(
-                request == r, own, 0.0
+            wide[r * sz.rank : (r + 1) * sz.rank, pl.ds(first, count)] = jnp.where(
+                request == r, ref[count:], 0.0
             ).astype(bf16)
     raised = lax.dot_general(
         wide[...], raise_picked[...], (((0,), (0,)), ((), ())), preferred_element_type=f32
     )
-    base = sum(partial[: sz.tokens].astype(f32) for partial in partials)
-    values = (base + scale[...] * raised).astype(bf16)
+    values = (base[...] + scale[...] * raised).astype(bf16)
     mixed[...] = jnp.dot(softmax[...], values, preferred_element_type=f32).astype(bf16)
     for k, out in enumerate(outs):
         for c in range(sz.group_size):
@@ -326,7 +320,6 @@
 
 def by_heads(sz, x, queries, keys, gain, base, down, up, lengths, adapters, ranks, slots):
     around = range(1, sz.seq)
-    half_columns = base.shape[1] // 2
 
     def ordered(values):
         return [values[k] for k in sz.order]
@@ -392,7 +385,7 @@
         matrix_kernel,
         "matrix_rows",
         [HBM, ANY],
-        [((sz.span, half_columns), bf16, VMEM)],
+        [((sz.span, base.shape[1]), bf16, VMEM)],
         (base, swap(base, "owner", 1)),
         (pltpu.SemaphoreType.DMA((2,)),),
     )
@@ -412,7 +405,6 @@
         [((sz.seq * sz.rows_half, sz.span), bf16, VMEM)],
         ordered(rows_in),
     )
-    other = swap(own, "owner", 1)
     softmax, raise_picked, scale = call(
         softmax_kernel,
         "softmax_rows",
@@ -431,37 +423,36 @@
     )
 
     count = sz.seq * sz.rows_half
-    partial_shape = (sz.tokens + 2 * sz.rank, HEAD_SIZE)
-    picked, values_own, low_own = call(
-        project_own_kernel,
-        "project_own",
+    partial_out = call(
+        project_kernel,
+        "project",
         [SMEM] + [VMEM] * (2 + len(panels)),
-        [
-            ((sz.requests * sz.rank, sz.span), bf16, VMEM),
-            ((count, half_columns), bf16, VMEM),
-            ((sz.rank, count), bf16, VMEM),
-        ],
+        [((2 * count + sz.rank, HEAD_SIZE), bf16, VMEM)] * sz.seq,
         (table, matrix, own, *panels),
-        (pltpu.VMEM((len(panels) * sz.rank, sz.span), bf16),),
-    )
-    partial_out = call(
-        project_other_kernel,
-        "project_other",
-        [SMEM] + [VMEM] * 5,
-        [(partial_shape, bf16, VMEM)] * sz.seq,
-        (table, matrix, other, picked, values_own, low_own),
-        (pltpu.VMEM((count, half_columns), bf16),),
+        (
+            pltpu.VMEM((sz.requests * sz.rank, sz.span), bf16),
+            pltpu.VMEM((len(panels) * sz.rank, sz.span), bf16),
+            pltpu.VMEM((count, base.shape[1]), bf16),
+        ),
     )
     partial_in = [partial_out[0]] + [swap(partial_out[k], "seq", k) for k in around]
+    kept, sent = call(
+        add_kernel,
+        "add_partials",
+        [VMEM] * sz.seq,
+        [((count + sz.rank, HEAD_SIZE), f32, VMEM)] * 2,
+        [partial_in[k] for k in sz.order_sum],
+    )
     wide = sz.group_size * HEAD_SIZE
     mixed = call(
         mix_kernel,
         "mix_values",
-        [SMEM] + [VMEM] * (3 + sz.seq),
+        [SMEM] + [VMEM] * 5,
         [((sz.rows, wide), bf16, VMEM)] * sz.seq,
-        (table, softmax, raise_picked, scale, *[partial_in[k] for k in sz.order_sum]),
+        (table, softmax, raise_picked, scale, kept, swap(sent, "owner", 1)),
         (
             pltpu.VMEM((sz.requests * sz.rank, sz.tokens), bf16),
+            pltpu.VMEM((sz.tokens, HEAD_SIZE), f32),
             pltpu.VMEM((sz.group_size * sz.tokens, HEAD_SIZE), bf16),
         ),
     )

time: 53.4 us -> 52 us (0.974)
  waiting for transfers between devices: 18.7 us -> 17.9 us
  Pallas kernels: 9.36 us -> 8.68 us
    ppermute x17, waiting for transfers between devices: 18.7 us -> 17.9 us  [swap(): lax.ppermute(value, axis, [(i, i ^ mask) for i in range(lax.axis_size(axi...]
    pallas_call x10, Pallas kernels: 9.36 us -> 8.68 us  [call(): pl.pallas_call(functools.partial(kernel, sz), out_shape=[jax.ShapeDtypeSt...]
  transfers between devices with their start and end apart: 19 -> 19, of which waited for: 9 -> 9; matrix products, arithmetic and copies ran while one was open for 0% -> 0% of each run, Pallas kernels for 12% -> 10%
where the time goes in v7:
time: 52 us; the launch traced here: 51.8 us
  starting transfers between devices  23 us (44%)
  waiting for transfers between devices  17.9 us (34%)
  Pallas kernels  8.68 us (17%)
  local copies, waits for them, and re-layouts  2.04 us (4%)
    ppermute x17, starting transfers between devices, swap(): lax.ppermute(value, axis, [(i, i ^ mask) for i in range(lax.axis_size(axi...  19.6 us
    ppermute x17, waiting for transfers between devices, swap(): lax.ppermute(value, axis, [(i, i ^ mask) for i in range(lax.axis_size(axi...  17.9 us
    pallas_call x10, Pallas kernels, call(): pl.pallas_call(functools.partial(kernel, sz), out_shape=[jax.ShapeDtypeSt...  8.68 us
    ppermute x2, starting transfers between devices, by_heads(): panels.append(lax.ppermute(panels_out[m], ('seq', 'owner'), pairs))  3.41 us
    unnamed x16, local copies, waits for them, and re-layouts  2.04 us
  transfers between devices with their start and end apart: 19, of which 9 were waited for; matrix products, arithmetic and copies ran while one was open for 0% of the time, Pallas kernels for 10%

profile of v7, /device:TPU:0, one launch (start us, length us, event | category | flops | bytes accessed | tf_op | source)
XLA Modules:
  0.0 51.8 jit_solution(15475251031912423697)
XLA Ops:
  0.0 0.5 collective-permute-start.1
  0.5 1.1 %copy-done.1 = bf16[1,2,2688,64]{2,3,1,0:T(8,128)(2,1)S(1)} copy-done((bf16[1,2,2688,64]{2,3,1,0:T(8,128)(2,1)S(1)}, bf16[1,2,2688,64]{2,3,1,0:T(8,128)(2,1)}, u32[]{:S(2)}) %copy-start.1) | copy-done | bytes 688152
  1.6 0.1 panels_out.1
  1.7 2.7 %collective-permute-start.2 = (bf16[64,1408]{1,0:T(8,128)(2,1)S(1)}, bf16[64,1408]{1,0:T(8,128)(2,1)S(1)}, u32[]{:S(2)}, u32[]{:S(2)}) collective-permute-start(bf16[64,1408]{1,0:T(8,128)(2,1)S(1)} %get-tuple-element.49), channel_id=1, source_target_pairs={{0,4},{1,12},{4,0},{5,8},{8,5},{9,13},{12,1},{13,9},{2,6},{3,14},{... | collective-permute-start | bytes 540680 | tf_op jit(solution)/shard_map/ppermute | solution.py:356
  4.4 0.7 %collective-permute-start = (bf16[64,1408]{1,0:T(8,128)(2,1)S(1)}, bf16[64,1408]{1,0:T(8,128)(2,1)S(1)}, u32[]{:S(2)}, u32[]{:S(2)}) collective-permute-start(bf16[64,1408]{1,0:T(8,128)(2,1)S(1)} %get-tuple-element.44), channel_id=1, source_target_pairs={{0,0},{1,8},{4,4},{5,12},{8,1},{9,9},{12,5},{13,13},{2,2},{3,10},{... | collective-permute-start | bytes 540680 | tf_op jit(solution)/shard_map/ppermute | solution.py:356
  5.1 2.2 %norm_rows.1 = (bf16[64,1408]{1,0:T(8,128)(2,1)}, bf16[64,1408]{1,0:T(8,128)(2,1)}, bf16[64,1408]{1,0:T(8,128)(2,1)}, bf16[64,1408]{1,0:T(8,128)(2,1)}) custom-call(bf16[64,5376]{1,0:T(8,128)(2,1)} %bitcast.12, f32[1,5376]{1,0:T(1,128)} %gain.1, bf16[64,1024]{1,0:T(8,128)(2,1)} %bitcast.13, bf16[64,512]{1,0:T(8,128)(2,1)} %bitcast.15, ...), custom_call_target="tpu_custom_call" | custom-call | tf_op jit(solution)/shard_map/norm_rows/pallas_call | solution.py:330
  7.3 0.1 collective-permute-start.3
  7.4 7.3 %collective-permute-start.4 = (bf16[64,1408]{1,0:T(8,128)(2,1)}, bf16[64,1408]{1,0:T(8,128)(2,1)S(1)}, u32[]{:S(2)}, u32[]{:S(2)}) collective-permute-start(bf16[64,1408]{1,0:T(8,128)(2,1)} %get-tuple-element.53), channel_id=1, source_target_pairs={{0,12},{4,8},{8,4},{12,0},{1,13},{5,9},{9,5},{13,1},{2,14},{6,10},... | collective-permute-start | bytes 540680 | tf_op jit(solution)/shard_map/ppermute | solution.py:31
  14.8 0.9 %copy-done.2 = bf16[64,1408]{1,0:T(8,128)(2,1)S(1)} copy-done((bf16[64,1408]{1,0:T(8,128)(2,1)S(1)}, bf16[64,1408]{1,0:T(8,128)(2,1)}, u32[]{:S(2)}) %copy-start.2) | copy-done | bytes 180248
  15.7 1.5 %table.1 = (s32[4,4]{1,0:T(4,128)S(1)}, bf16[64,1408]{1,0:T(8,128)(2,1)S(1)}) custom-call(s32[4]{0:T(128)S(1)} %copy-done.3, s32[4]{0:T(128)S(1)} %copy-done.4, s32[8]{0:T(128)S(1)} %copy-done.5, s32[8]{0:T(128)S(1)} %copy-done.6, bf16[64,1408]{1,0:T(8,128)(2,1)S(1)} %copy-done.2), custom_call_target="tpu_custom_call" | custom-call | bytes 67108864 | tf_op jit(solution)/shard_map/table/pallas_call | solution.py:330
  17.2 0.0 collective-permute-done.2.refs_1_
  17.2 1.6 %collective-permute-start.7 = (bf16[64,1408]{1,0:T(8,128)(2,1)S(1)}, bf16[64,1408]{1,0:T(8,128)(2,1)S(1)}, u32[]{:S(2)}, u32[]{:S(2)}) collective-permute-start(bf16[64,1408]{1,0:T(8,128)(2,1)S(1)} %collective-permute-done.2.refs_1_), channel_id=1, source_target_pairs={{0,16},{16,0},{1,17},{17,1},{2,18},{18,2},{3,19},{19,3},{4,20},{20... | collective-permute-start | bytes 540680 | tf_op jit(solution)/shard_map/ppermute | solution.py:31
  18.8 0.0 collective-permute-done.1.base_other
  18.8 0.4 matrix_rows.1.matrix
  19.2 0.0 collective-permute-done.refs_0_
  19.2 0.6 %collective-permute-start.6 = (bf16[64,1408]{1,0:T(8,128)(2,1)S(1)}, bf16[64,1408]{1,0:T(8,128)(2,1)S(1)}, u32[]{:S(2)}, u32[]{:S(2)}) collective-permute-start(bf16[64,1408]{1,0:T(8,128)(2,1)S(1)} %collective-permute-done.refs_0_), channel_id=1, source_target_pairs={{0,16},{16,0},{1,17},{17,1},{2,18},{18,2},{3,19},{19,3},{4,20},{20... | collective-permute-start | bytes 540680 | tf_op jit(solution)/shard_map/ppermute | solution.py:31
  19.8 0.0 collective-permute-start.5
  19.8 0.0 collective-permute-done.3.refs_3_
  19.8 0.1 collective-permute-start.9
  19.9 4.3 %collective-permute-done.7.refs_3_ = bf16[64,1408]{1,0:T(8,128)(2,1)S(1)} collective-permute-done((bf16[64,1408]{1,0:T(8,128)(2,1)S(1)}, bf16[64,1408]{1,0:T(8,128)(2,1)S(1)}, u32[]{:S(2)}, u32[]{:S(2)}) %collective-permute-start.7) | collective-permute-done | bytes 180256 | tf_op jit(solution)/shard_map/ppermute | solution.py:31
  24.2 0.0 collective-permute-start.11
  24.2 0.0 collective-permute-done.4.refs_1_
  24.2 0.5 collective-permute-start.8
  24.7 1.4 %collective-permute-done.6.refs_2_ = bf16[64,1408]{1,0:T(8,128)(2,1)S(1)} collective-permute-done((bf16[64,1408]{1,0:T(8,128)(2,1)S(1)}, bf16[64,1408]{1,0:T(8,128)(2,1)S(1)}, u32[]{:S(2)}, u32[]{:S(2)}) %collective-permute-start.6) | collective-permute-done | bytes 180256 | tf_op jit(solution)/shard_map/ppermute | solution.py:31
  26.1 0.0 collective-permute-start.10
  26.1 5.0 %collective-permute-done.5.refs_2_ = bf16[64,1408]{1,0:T(8,128)(2,1)S(1)} collective-permute-done((bf16[64,1408]{1,0:T(8,128)(2,1)S(1)}, bf16[64,1408]{1,0:T(8,128)(2,1)S(1)}, u32[]{:S(2)}, u32[]{:S(2)}) %collective-permute-start.5) | collective-permute-done | bytes 180256 | tf_op jit(solution)/shard_map/ppermute | solution.py:31
  31.1 0.0 collective-permute-done.9.refs_5_
  31.1 0.0 collective-permute-done.11.refs_7_
  31.1 0.0 collective-permute-done.8.refs_4_
  31.1 0.0 collective-permute-done.10.refs_6_
  31.2 1.5 %project.1 = (bf16[320,128]{1,0:T(8,128)(2,1)S(1)}, bf16[320,128]{1,0:T(8,128)(2,1)S(1)}, bf16[320,128]{1,0:T(8,128)(2,1)S(1)}, bf16[320,128]{1,0:T(8,128)(2,1)S(1)}) custom-call(s32[4,4]{1,0:T(4,128)S(1)} %get-tuple-element.48.table, bf16[1408,1024]{1,0:T(8,128)(2,1)S(1)} %matrix_rows.1.matrix, bf16[128,1408]{1,0:T(8,128)(2,1)S(1)} %gather_rows.1.own, ...), custom_call_target="tpu_custom_call" | custom-call | tf_op jit(solution)/shard_map/project/pallas_call | solution.py:330
  32.7 0.1 collective-permute-start.12
  32.7 2.4 %collective-permute-start.13 = (bf16[320,128]{1,0:T(8,128)(2,1)S(1)}, bf16[320,128]{1,0:T(8,128)(2,1)S(1)}, u32[]{:S(2)}, u32[]{:S(2)}) collective-permute-start(bf16[320,128]{1,0:T(8,128)(2,1)S(1)} %get-tuple-element.75), channel_id=1, source_target_pairs={{0,4},{4,0},{8,12},{12,8},{1,5},{5,1},{9,13},{13,9},{2,6},{6,2},{1... | collective-permute-start | bytes 245768 | tf_op jit(solution)/shard_map/ppermute | solution.py:31
  35.2 2.0 %collective-permute-start.14 = (bf16[320,128]{1,0:T(8,128)(2,1)S(1)}, bf16[320,128]{1,0:T(8,128)(2,1)S(1)}, u32[]{:S(2)}, u32[]{:S(2)}) collective-permute-start(bf16[320,128]{1,0:T(8,128)(2,1)S(1)} %get-tuple-element.76), channel_id=1, source_target_pairs={{0,12},{4,8},{8,4},{12,0},{1,13},{5,9},{9,5},{13,1},{2,14},{6,10},... | collective-permute-start | bytes 245768 | tf_op jit(solution)/shard_map/ppermute | solution.py:31
  37.1 2.7 %collective-permute-done.12.refs_1_ = bf16[320,128]{1,0:T(8,128)(2,1)S(1)} collective-permute-done((bf16[320,128]{1,0:T(8,128)(2,1)S(1)}, bf16[320,128]{1,0:T(8,128)(2,1)S(1)}, u32[]{:S(2)}, u32[]{:S(2)}) %collective-permute-start.12) | collective-permute-done | bytes 81952 | tf_op jit(solution)/shard_map/ppermute | solution.py:31
  39.8 0.0 collective-permute-done.13.refs_2_
  39.8 1.7 %collective-permute-done.14.refs_3_ = bf16[320,128]{1,0:T(8,128)(2,1)S(1)} collective-permute-done((bf16[320,128]{1,0:T(8,128)(2,1)S(1)}, bf16[320,128]{1,0:T(8,128)(2,1)S(1)}, u32[]{:S(2)}, u32[]{:S(2)}) %collective-permute-start.14) | collective-permute-done | bytes 81952 | tf_op jit(solution)/shard_map/ppermute | solution.py:31
  41.5 0.1 collective-permute-start.15
  41.6 1.1 %softmax_rows.1 = (bf16[512,256]{1,0:T(8,128)(2,1)S(1)}, bf16[256,128]{1,0:T(8,128)(2,1)S(1)}, f32[256,128]{1,0:T(8,128)S(1)}) custom-call(s32[4,4]{1,0:T(4,128)S(1)} %get-tuple-element.48.table, bf16[64,1408]{1,0:T(8,128)(2,1)S(1)} %get-tuple-element.57.refs_0_, bf16[64,1408]{1,0:T(8,128)(2,1)S(1)} %collective-permute-done.4.refs_1_, ...), custom_call_target="tpu_custom_call" | custom-call | tf_op jit(solution)/shard_map/softmax_rows/pallas_call | solution.py:330
  42.7 0.1 collective-permute-done.15.received
  42.9 1.1 %mix_values.1 = (bf16[64,256]{1,0:T(8,128)(2,1)S(1)}, bf16[64,256]{1,0:T(8,128)(2,1)S(1)}, bf16[64,256]{1,0:T(8,128)(2,1)S(1)}, bf16[64,256]{1,0:T(8,128)(2,1)S(1)}) custom-call(s32[4,4]{1,0:T(4,128)S(1)} %get-tuple-element.48.table, bf16[512,256]{1,0:T(8,128)(2,1)S(1)} %get-tuple-element.61.softmax, bf16[256,128]{1,0:T(8,128)(2,1)S(1)} %get-tuple-element.62.raise_picked, ...), custom_call_target="tpu_custom_call" | custom-call | tf_op jit(solution)/shard_map/mix_values/pallas_call | solution.py:330
  44.0 2.1 %collective-permute-start.16 = (bf16[64,256]{1,0:T(8,128)(2,1)S(1)}, bf16[64,256]{1,0:T(8,128)(2,1)S(1)}, u32[]{:S(2)}, u32[]{:S(2)}) collective-permute-start(bf16[64,256]{1,0:T(8,128)(2,1)S(1)} %get-tuple-element.80), channel_id=1, source_target_pairs={{0,12},{4,8},{8,4},{12,0},{1,13},{5,9},{9,5},{13,1},{2,14},{6,10},... | collective-permute-start | bytes 98312 | tf_op jit(solution)/shard_map/ppermute | solution.py:31
  46.1 0.6 %collective-permute-start.17 = (bf16[64,256]{1,0:T(8,128)(2,1)S(1)}, bf16[64,256]{1,0:T(8,128)(2,1)S(1)}, u32[]{:S(2)}, u32[]{:S(2)}) collective-permute-start(bf16[64,256]{1,0:T(8,128)(2,1)S(1)} %get-tuple-element.81), channel_id=1, source_target_pairs={{0,8},{4,12},{8,0},{12,4},{1,9},{5,13},{9,1},{13,5},{2,10},{6,14},... | collective-permute-start | bytes 98312 | tf_op jit(solution)/shard_map/ppermute | solution.py:31
  46.7 1.8 %collective-permute-start.18 = (bf16[64,256]{1,0:T(8,128)(2,1)S(1)}, bf16[64,256]{1,0:T(8,128)(2,1)S(1)}, u32[]{:S(2)}, u32[]{:S(2)}) collective-permute-start(bf16[64,256]{1,0:T(8,128)(2,1)S(1)} %get-tuple-element.82), channel_id=1, source_target_pairs={{0,4},{4,0},{8,12},{12,8},{1,5},{5,1},{9,13},{13,9},{2,6},{6,2},{1... | collective-permute-start | bytes 98312 | tf_op jit(solution)/shard_map/ppermute | solution.py:31
  48.5 1.4 %collective-permute-done.16.refs_1_ = bf16[64,256]{1,0:T(8,128)(2,1)S(1)} collective-permute-done((bf16[64,256]{1,0:T(8,128)(2,1)S(1)}, bf16[64,256]{1,0:T(8,128)(2,1)S(1)}, u32[]{:S(2)}, u32[]{:S(2)}) %collective-permute-start.16) | collective-permute-done | bytes 32800 | tf_op jit(solution)/shard_map/ppermute | solution.py:31
  49.9 1.1 %collective-permute-done.17.refs_2_ = bf16[64,256]{1,0:T(8,128)(2,1)S(1)} collective-permute-done((bf16[64,256]{1,0:T(8,128)(2,1)S(1)}, bf16[64,256]{1,0:T(8,128)(2,1)S(1)}, u32[]{:S(2)}, u32[]{:S(2)}) %collective-permute-start.17) | collective-permute-done | bytes 32800 | tf_op jit(solution)/shard_map/ppermute | solution.py:31
  51.0 0.2 collective-permute-done.18.refs_3_
  51.2 0.7 %place_heads.1 = bf16[64,1024]{1,0:T(8,128)(2,1)} custom-call(bf16[64,256]{1,0:T(8,128)(2,1)S(1)} %get-tuple-element.79.refs_0_, bf16[64,256]{1,0:T(8,128)(2,1)S(1)} %collective-permute-done.16.refs_1_, bf16[64,256]{1,0:T(8,128)(2,1)S(1)} %collective-permute-done.17.refs_2_, bf16[64,256]{1,0:T(8,128)(2,1)S(1)} %collective-permute-done.18.refs_3_), custom_call_target="tpu_custom_call" | custom-call | tf_op jit(solution)/shard_map/place_heads/pallas_call | solution.py:330
  (16 shorter events, 0.1 us)
Async XLA Ops:
  0.0 18.8 %copy-start = (bf16[1,672,1024]{2,1,0:T(8,128)(2,1)S(1)}, bf16[1,672,1024]{2,1,0:T(8,128)(2,1)}, u32[]{:S(2)}) copy-start(bf16[1,672,1024]{2,1,0:T(8,128)(2,1)} %param.15) | copy-start | bytes 4128772
  0.0 18.8 %collective-permute-start.1 = (bf16[672,1024]{1,0:T(8,128)(2,1)}, bf16[672,1024]{1,0:T(8,128)(2,1)S(1)}, u32[]{:S(2)}, u32[]{:S(2)}) collective-permute-start(bf16[672,1024]{1,0:T(8,128)(2,1)} %bitcast.9), channel_id=1, source_target_pairs={{0,1},{1,0},{2,3},{3,2},{4,5},{5,4},{6,7},{7,6},{8,9},{9,8},{10,11... | collective-permute-start | bytes 4128776 | tf_op jit(solution)/shard_map/ppermute | solution.py:31
  0.5 1.1 %copy-start.1 = (bf16[1,2,2688,64]{2,3,1,0:T(8,128)(2,1)S(1)}, bf16[1,2,2688,64]{2,3,1,0:T(8,128)(2,1)}, u32[]{:S(2)}) copy-start(bf16[1,2,2688,64]{2,3,1,0:T(8,128)(2,1)} %param.16) | copy-start | bytes 2064388
  1.6 13.2 %copy-start.3 = (s32[4]{0:T(128)S(1)}, s32[4]{0:T(128)}, u32[]{:S(2)}) copy-start(s32[4]{0:T(128)} %lengths.1) | copy-start | bytes 52
  1.6 13.2 %copy-start.4 = (s32[4]{0:T(128)S(1)}, s32[4]{0:T(128)}, u32[]{:S(2)}) copy-start(s32[4]{0:T(128)} %adapters.1) | copy-start | bytes 52
  1.6 13.2 %copy-start.5 = (s32[8]{0:T(128)S(1)}, s32[8]{0:T(128)}, u32[]{:S(2)}) copy-start(s32[8]{0:T(128)} %ranks.1) | copy-start | bytes 100
  1.6 13.2 %copy-start.6 = (s32[8]{0:T(128)S(1)}, s32[8]{0:T(128)}, u32[]{:S(2)}) copy-start(s32[8]{0:T(128)} %slots.1) | copy-start | bytes 100
  1.7 15.5 %collective-permute-start.2 = (bf16[64,1408]{1,0:T(8,128)(2,1)S(1)}, bf16[64,1408]{1,0:T(8,128)(2,1)S(1)}, u32[]{:S(2)}, u32[]{:S(2)}) collective-permute-start(bf16[64,1408]{1,0:T(8,128)(2,1)S(1)} %get-tuple-element.49), channel_id=1, source_target_pairs={{0,4},{1,12},{4,0},{5,8},{8,5},{9,13},{12,1},{13,9},{2,6},{3,14},{... | collective-permute-start | bytes 540680 | tf_op jit(solution)/shard_map/ppermute | solution.py:356
  4.4 14.8 %collective-permute-start = (bf16[64,1408]{1,0:T(8,128)(2,1)S(1)}, bf16[64,1408]{1,0:T(8,128)(2,1)S(1)}, u32[]{:S(2)}, u32[]{:S(2)}) collective-permute-start(bf16[64,1408]{1,0:T(8,128)(2,1)S(1)} %get-tuple-element.44), channel_id=1, source_target_pairs={{0,0},{1,8},{4,4},{5,12},{8,1},{9,9},{12,5},{13,13},{2,2},{3,10},{... | collective-permute-start | bytes 540680 | tf_op jit(solution)/shard_map/ppermute | solution.py:356
  7.3 12.4 %collective-permute-start.3 = (bf16[64,1408]{1,0:T(8,128)(2,1)}, bf16[64,1408]{1,0:T(8,128)(2,1)S(1)}, u32[]{:S(2)}, u32[]{:S(2)}) collective-permute-start(bf16[64,1408]{1,0:T(8,128)(2,1)} %get-tuple-element.52), channel_id=1, source_target_pairs={{0,4},{4,0},{8,12},{12,8},{1,5},{5,1},{9,13},{13,9},{2,6},{6,2},{1... | collective-permute-start | bytes 540680 | tf_op jit(solution)/shard_map/ppermute | solution.py:31
  7.4 16.7 %collective-permute-start.4 = (bf16[64,1408]{1,0:T(8,128)(2,1)}, bf16[64,1408]{1,0:T(8,128)(2,1)S(1)}, u32[]{:S(2)}, u32[]{:S(2)}) collective-permute-start(bf16[64,1408]{1,0:T(8,128)(2,1)} %get-tuple-element.53), channel_id=1, source_target_pairs={{0,12},{4,8},{8,4},{12,0},{1,13},{5,9},{9,5},{13,1},{2,14},{6,10},... | collective-permute-start | bytes 540680 | tf_op jit(solution)/shard_map/ppermute | solution.py:31
  14.8 0.9 %copy-start.2 = (bf16[64,1408]{1,0:T(8,128)(2,1)S(1)}, bf16[64,1408]{1,0:T(8,128)(2,1)}, u32[]{:S(2)}) copy-start(bf16[64,1408]{1,0:T(8,128)(2,1)} %get-tuple-element.46.piece) | copy-start | bytes 540676
  17.2 2.6 %copy-start.7 = (bf16[64,1408]{1,0:T(8,128)(2,1)S(1)}, bf16[64,1408]{1,0:T(8,128)(2,1)}, u32[]{:S(2)}) copy-start(bf16[64,1408]{1,0:T(8,128)(2,1)} %get-tuple-element.54) | copy-start | bytes 540676
  17.2 7.0 %collective-permute-start.7 = (bf16[64,1408]{1,0:T(8,128)(2,1)S(1)}, bf16[64,1408]{1,0:T(8,128)(2,1)S(1)}, u32[]{:S(2)}, u32[]{:S(2)}) collective-permute-start(bf16[64,1408]{1,0:T(8,128)(2,1)S(1)} %collective-permute-done.2.refs_1_), channel_id=1, source_target_pairs={{0,16},{16,0},{1,17},{17,1},{2,18},{18,2},{3,19},{19,3},{4,20},{20... | collective-permute-start | bytes 540680 | tf_op jit(solution)/shard_map/ppermute | solution.py:31
  19.2 6.9 %collective-permute-start.6 = (bf16[64,1408]{1,0:T(8,128)(2,1)S(1)}, bf16[64,1408]{1,0:T(8,128)(2,1)S(1)}, u32[]{:S(2)}, u32[]{:S(2)}) collective-permute-start(bf16[64,1408]{1,0:T(8,128)(2,1)S(1)} %collective-permute-done.refs_0_), channel_id=1, source_target_pairs={{0,16},{16,0},{1,17},{17,1},{2,18},{18,2},{3,19},{19,3},{4,20},{20... | collective-permute-start | bytes 540680 | tf_op jit(solution)/shard_map/ppermute | solution.py:31
  19.8 11.3 %collective-permute-start.5 = (bf16[64,1408]{1,0:T(8,128)(2,1)S(1)}, bf16[64,1408]{1,0:T(8,128)(2,1)S(1)}, u32[]{:S(2)}, u32[]{:S(2)}) collective-permute-start(bf16[64,1408]{1,0:T(8,128)(2,1)S(1)} %copy-done.7), channel_id=1, source_target_pairs={{0,8},{4,12},{8,0},{12,4},{1,9},{5,13},{9,1},{13,5},{2,10},{6,14},... | collective-permute-start | bytes 540680 | tf_op jit(solution)/shard_map/ppermute | solution.py:31
  19.8 11.3 %collective-permute-start.9 = (bf16[64,1408]{1,0:T(8,128)(2,1)S(1)}, bf16[64,1408]{1,0:T(8,128)(2,1)S(1)}, u32[]{:S(2)}, u32[]{:S(2)}) collective-permute-start(bf16[64,1408]{1,0:T(8,128)(2,1)S(1)} %collective-permute-done.2.refs_1_), channel_id=1, source_target_pairs={{0,1},{1,0},{2,3},{3,2},{4,5},{5,4},{6,7},{7,6},{8,9},{9,8},{10,11... | collective-permute-start | bytes 540680 | tf_op jit(solution)/shard_map/ppermute | solution.py:31
  24.2 6.9 %collective-permute-start.11 = (bf16[64,1408]{1,0:T(8,128)(2,1)S(1)}, bf16[64,1408]{1,0:T(8,128)(2,1)S(1)}, u32[]{:S(2)}, u32[]{:S(2)}) collective-permute-start(bf16[64,1408]{1,0:T(8,128)(2,1)S(1)} %collective-permute-done.7.refs_3_), channel_id=1, source_target_pairs={{0,1},{1,0},{2,3},{3,2},{4,5},{5,4},{6,7},{7,6},{8,9},{9,8},{10,11... | collective-permute-start | bytes 540680 | tf_op jit(solution)/shard_map/ppermute | solution.py:31
  24.2 6.9 %collective-permute-start.8 = (bf16[64,1408]{1,0:T(8,128)(2,1)S(1)}, bf16[64,1408]{1,0:T(8,128)(2,1)S(1)}, u32[]{:S(2)}, u32[]{:S(2)}) collective-permute-start(bf16[64,1408]{1,0:T(8,128)(2,1)S(1)} %collective-permute-done.refs_0_), channel_id=1, source_target_pairs={{0,1},{1,0},{2,3},{3,2},{4,5},{5,4},{6,7},{7,6},{8,9},{9,8},{10,11... | collective-permute-start | bytes 540680 | tf_op jit(solution)/shard_map/ppermute | solution.py:31
  26.1 5.0 %collective-permute-start.10 = (bf16[64,1408]{1,0:T(8,128)(2,1)S(1)}, bf16[64,1408]{1,0:T(8,128)(2,1)S(1)}, u32[]{:S(2)}, u32[]{:S(2)}) collective-permute-start(bf16[64,1408]{1,0:T(8,128)(2,1)S(1)} %collective-permute-done.6.refs_2_), channel_id=1, source_target_pairs={{0,1},{1,0},{2,3},{3,2},{4,5},{5,4},{6,7},{7,6},{8,9},{9,8},{10,11... | collective-permute-start | bytes 540680 | tf_op jit(solution)/shard_map/ppermute | solution.py:31
  32.7 7.1 %collective-permute-start.12 = (bf16[320,128]{1,0:T(8,128)(2,1)S(1)}, bf16[320,128]{1,0:T(8,128)(2,1)S(1)}, u32[]{:S(2)}, u32[]{:S(2)}) collective-permute-start(bf16[320,128]{1,0:T(8,128)(2,1)S(1)} %get-tuple-element.74), channel_id=1, source_target_pairs={{0,8},{4,12},{8,0},{12,4},{1,9},{5,13},{9,1},{13,5},{2,10},{6,14},... | collective-permute-start | bytes 245768 | tf_op jit(solution)/shard_map/ppermute | solution.py:31
  32.7 7.1 %collective-permute-start.13 = (bf16[320,128]{1,0:T(8,128)(2,1)S(1)}, bf16[320,128]{1,0:T(8,128)(2,1)S(1)}, u32[]{:S(2)}, u32[]{:S(2)}) collective-permute-start(bf16[320,128]{1,0:T(8,128)(2,1)S(1)} %get-tuple-element.75), channel_id=1, source_target_pairs={{0,4},{4,0},{8,12},{12,8},{1,5},{5,1},{9,13},{13,9},{2,6},{6,2},{1... | collective-permute-start | bytes 245768 | tf_op jit(solution)/shard_map/ppermute | solution.py:31
  35.2 6.3 %collective-permute-start.14 = (bf16[320,128]{1,0:T(8,128)(2,1)S(1)}, bf16[320,128]{1,0:T(8,128)(2,1)S(1)}, u32[]{:S(2)}, u32[]{:S(2)}) collective-permute-start(bf16[320,128]{1,0:T(8,128)(2,1)S(1)} %get-tuple-element.76), channel_id=1, source_target_pairs={{0,12},{4,8},{8,4},{12,0},{1,13},{5,9},{9,5},{13,1},{2,14},{6,10},... | collective-permute-start | bytes 245768 | tf_op jit(solution)/shard_map/ppermute | solution.py:31
  41.5 1.4 %collective-permute-start.15 = (f32[192,128]{1,0:T(8,128)S(1)}, f32[192,128]{1,0:T(8,128)S(1)}, u32[]{:S(2)}, u32[]{:S(2)}) collective-permute-start(f32[192,128]{1,0:T(8,128)S(1)} %get-tuple-element.78), channel_id=1, source_target_pairs={{0,1},{1,0},{2,3},{3,2},{4,5},{5,4},{6,7},{7,6},{8,9},{9,8},{10,11... | collective-permute-start | bytes 294920 | tf_op jit(solution)/shard_map/ppermute | solution.py:31
  44.0 5.9 %collective-permute-start.16 = (bf16[64,256]{1,0:T(8,128)(2,1)S(1)}, bf16[64,256]{1,0:T(8,128)(2,1)S(1)}, u32[]{:S(2)}, u32[]{:S(2)}) collective-permute-start(bf16[64,256]{1,0:T(8,128)(2,1)S(1)} %get-tuple-element.80), channel_id=1, source_target_pairs={{0,12},{4,8},{8,4},{12,0},{1,13},{5,9},{9,5},{13,1},{2,14},{6,10},... | collective-permute-start | bytes 98312 | tf_op jit(solution)/shard_map/ppermute | solution.py:31
  46.1 4.9 %collective-permute-start.17 = (bf16[64,256]{1,0:T(8,128)(2,1)S(1)}, bf16[64,256]{1,0:T(8,128)(2,1)S(1)}, u32[]{:S(2)}, u32[]{:S(2)}) collective-permute-start(bf16[64,256]{1,0:T(8,128)(2,1)S(1)} %get-tuple-element.81), channel_id=1, source_target_pairs={{0,8},{4,12},{8,0},{12,4},{1,9},{5,13},{9,1},{13,5},{2,10},{6,14},... | collective-permute-start | bytes 98312 | tf_op jit(solution)/shard_map/ppermute | solution.py:31
  46.7 4.5 %collective-permute-start.18 = (bf16[64,256]{1,0:T(8,128)(2,1)S(1)}, bf16[64,256]{1,0:T(8,128)(2,1)S(1)}, u32[]{:S(2)}, u32[]{:S(2)}) collective-permute-start(bf16[64,256]{1,0:T(8,128)(2,1)S(1)} %get-tuple-element.82), channel_id=1, source_target_pairs={{0,4},{4,0},{8,12},{12,8},{1,5},{5,1},{9,13},{13,9},{2,6},{6,2},{1... | collective-permute-start | bytes 98312 | tf_op jit(solution)/shard_map/ppermute | solution.py:31

commit v8 on v7

--- a/solution.py
+++ b/solution.py
@@ -61,6 +61,7 @@
     def fits(self):
         return (
             lax.axis_size("owner") == 2
+            and self.seq >= 4
             and self.seq & (self.seq - 1) == 0
             and self.groups & (self.groups - 1) == 0
             and self.half % LANES == 0
@@ -234,18 +235,14 @@
         copy.wait()
 
 
-def gather_kernel(sz, *refs):
-    pieces, out = refs[: sz.seq], refs[sz.seq]
-    here = lax.axis_index("seq")
+def project_kernel(sz, table, matrix, *refs):
+    pieces, refs = refs[: sz.seq], refs[sz.seq :]
+    panels, refs = refs[: 2 * sz.groups * sz.side], refs[2 * sz.groups * sz.side :]
+    outs, (own, picked, stacked, values) = refs[: sz.seq], refs[sz.seq :]
+    here, core = lax.axis_index("seq"), lax.axis_index("owner")
     for k, piece in zip(sz.order, pieces):
         first = pl.multiple_of((here ^ k) * sz.rows_half, sz.rows_half)
-        out[pl.ds(first, sz.rows_half), :] = piece[: sz.rows_half]
-
-
-def project_kernel(sz, table, matrix, own, *refs):
-    panels, refs = refs[: 2 * sz.groups * sz.side], refs[2 * sz.groups * sz.side :]
-    outs, (picked, stacked, values) = refs[: sz.seq], refs[sz.seq :]
-    here, core = lax.axis_index("seq"), lax.axis_index("owner")
+        own[pl.ds(first, sz.rows_half), :] = piece[: sz.rows_half]
     for p, panel in enumerate(panels):
         stacked[p * sz.rank : (p + 1) * sz.rank] = panel[...]
     for r in range(sz.requests):
@@ -326,7 +323,7 @@
 
     spread = (2 * sz.rows_half, sz.span)
 
-    def call(kernel, name, ins, outs, args, scratch=(), params=PARAMS, cost=None):
+    def call(kernel, name, ins, outs, args, scratch=(), params=PARAMS):
         return pl.pallas_call(
             functools.partial(kernel, sz),
             out_shape=[jax.ShapeDtypeStruct(shape, dtype) for shape, dtype, _ in outs],
@@ -334,7 +331,6 @@
             out_specs=[spec for _, _, spec in outs],
             scratch_shapes=list(scratch),
             compiler_params=params,
-            cost_estimate=cost,
             name=name,
         )(*args)
 
@@ -379,7 +375,6 @@
         [((4, sz.requests), jnp.int32, SMEM), (spread, bf16, VMEM)],
         (lengths, adapters, ranks, slots, rows_out[0]),
         (pltpu.SemaphoreType.DMA,),
-        cost=pl.CostEstimate(flops=0, bytes_accessed=64 * 1024 * 1024, transcendentals=0),
     )
     (matrix,) = call(
         matrix_kernel,
@@ -398,13 +393,6 @@
     panels = panels + [swap(p, "owner", 1) for p in panels]
     rows_ordered, panels = lax.optimization_barrier(([rows_in[k] for k in sz.order_rows], panels))
     rows_in = [rows_ordered[sz.order_rows.index(k)] for k in range(sz.seq)]
-    (own,) = call(
-        gather_kernel,
-        "gather_rows",
-        [VMEM] * sz.seq,
-        [((sz.seq * sz.rows_half, sz.span), bf16, VMEM)],
-        ordered(rows_in),
-    )
     softmax, raise_picked, scale = call(
         softmax_kernel,
         "softmax_rows",
@@ -426,10 +414,11 @@
     partial_out = call(
         project_kernel,
         "project",
-        [SMEM] + [VMEM] * (2 + len(panels)),
+        [SMEM] + [VMEM] * (1 + sz.seq + len(panels)),
         [((2 * count + sz.rank, HEAD_SIZE), bf16, VMEM)] * sz.seq,
-        (table, matrix, own, *panels),
+        (table, matrix, *ordered(rows_in), *panels),
         (
+            pltpu.VMEM((count, sz.span), bf16),
             pltpu.VMEM((sz.requests * sz.rank, sz.span), bf16),
             pltpu.VMEM((len(panels) * sz.rank, sz.span), bf16),
             pltpu.VMEM((count, base.shape[1]), bf16),

time: 52 us -> 52 us (level)
    pallas_call x10 -> x9, Pallas kernels: 8.68 us -> 8.7 us  [call(): pl.pallas_call(functools.partial(kernel, sz), out_shape=[jax.ShapeDtypeSt...]
where the time goes in v8:
time: 52 us; the launch traced here: 51.9 us
  starting transfers between devices  23 us (44%)
  waiting for transfers between devices  17.9 us (34%)
  Pallas kernels  8.7 us (17%)
  local copies, waits for them, and re-layouts  2.04 us (4%)
    ppermute x17, starting transfers between devices, swap(): lax.ppermute(value, axis, [(i, i ^ mask) for i in range(lax.axis_size(axi...  19.6 us
    ppermute x17, waiting for transfers between devices, swap(): lax.ppermute(value, axis, [(i, i ^ mask) for i in range(lax.axis_size(axi...  17.9 us
    pallas_call x9, Pallas kernels, call(): pl.pallas_call(functools.partial(kernel, sz), out_shape=[jax.ShapeDtypeSt...  8.7 us
    ppermute x2, starting transfers between devices, by_heads(): panels.append(lax.ppermute(panels_out[m], ('seq', 'owner'), pairs))  3.41 us
    unnamed x16, local copies, waits for them, and re-layouts  2.04 us
  transfers between devices with their start and end apart: 19, of which 9 were waited for; matrix products, arithmetic and copies ran while one was open for 0% of the time, Pallas kernels for 10%

profile of v8, /device:TPU:0, one launch (start us, length us, event | category | flops | bytes accessed | tf_op | source)
XLA Modules:
  0.0 51.9 jit_solution(3446880654807314882)
XLA Ops:
  0.0 0.5 collective-permute-start.1
  0.5 1.1 %copy-done.1 = bf16[1,2,2688,64]{2,3,1,0:T(8,128)(2,1)S(1)} copy-done((bf16[1,2,2688,64]{2,3,1,0:T(8,128)(2,1)S(1)}, bf16[1,2,2688,64]{2,3,1,0:T(8,128)(2,1)}, u32[]{:S(2)}) %copy-start.1) | copy-done | bytes 688152
  1.6 0.1 panels_out.1
  1.7 2.7 %collective-permute-start.2 = (bf16[64,1408]{1,0:T(8,128)(2,1)S(1)}, bf16[64,1408]{1,0:T(8,128)(2,1)S(1)}, u32[]{:S(2)}, u32[]{:S(2)}) collective-permute-start(bf16[64,1408]{1,0:T(8,128)(2,1)S(1)} %get-tuple-element.49), channel_id=1, source_target_pairs={{0,4},{1,12},{4,0},{5,8},{8,5},{9,13},{12,1},{13,9},{2,6},{3,14},{... | collective-permute-start | bytes 540680 | tf_op jit(solution)/shard_map/ppermute | solution.py:352
  4.4 0.7 %collective-permute-start = (bf16[64,1408]{1,0:T(8,128)(2,1)S(1)}, bf16[64,1408]{1,0:T(8,128)(2,1)S(1)}, u32[]{:S(2)}, u32[]{:S(2)}) collective-permute-start(bf16[64,1408]{1,0:T(8,128)(2,1)S(1)} %get-tuple-element.44), channel_id=1, source_target_pairs={{0,0},{1,8},{4,4},{5,12},{8,1},{9,9},{12,5},{13,13},{2,2},{3,10},{... | collective-permute-start | bytes 540680 | tf_op jit(solution)/shard_map/ppermute | solution.py:352
  5.1 2.2 %norm_rows.1 = (bf16[64,1408]{1,0:T(8,128)(2,1)}, bf16[64,1408]{1,0:T(8,128)(2,1)}, bf16[64,1408]{1,0:T(8,128)(2,1)}, bf16[64,1408]{1,0:T(8,128)(2,1)}) custom-call(bf16[64,5376]{1,0:T(8,128)(2,1)} %bitcast.12, f32[1,5376]{1,0:T(1,128)} %gain.1, bf16[64,1024]{1,0:T(8,128)(2,1)} %bitcast.13, bf16[64,512]{1,0:T(8,128)(2,1)} %bitcast.15, ...), custom_call_target="tpu_custom_call" | custom-call | tf_op jit(solution)/shard_map/norm_rows/pallas_call | solution.py:327
  7.3 0.1 collective-permute-start.3
  7.4 7.3 %collective-permute-start.4 = (bf16[64,1408]{1,0:T(8,128)(2,1)}, bf16[64,1408]{1,0:T(8,128)(2,1)S(1)}, u32[]{:S(2)}, u32[]{:S(2)}) collective-permute-start(bf16[64,1408]{1,0:T(8,128)(2,1)} %get-tuple-element.53), channel_id=1, source_target_pairs={{0,12},{4,8},{8,4},{12,0},{1,13},{5,9},{9,5},{13,1},{2,14},{6,10},... | collective-permute-start | bytes 540680 | tf_op jit(solution)/shard_map/ppermute | solution.py:31
  14.8 0.9 %copy-done.2 = bf16[64,1408]{1,0:T(8,128)(2,1)S(1)} copy-done((bf16[64,1408]{1,0:T(8,128)(2,1)S(1)}, bf16[64,1408]{1,0:T(8,128)(2,1)}, u32[]{:S(2)}) %copy-start.2) | copy-done | bytes 180248
  15.7 1.5 %table.1 = (s32[4,4]{1,0:T(4,128)S(1)}, bf16[64,1408]{1,0:T(8,128)(2,1)S(1)}) custom-call(s32[4]{0:T(128)S(1)} %copy-done.3, s32[4]{0:T(128)S(1)} %copy-done.4, s32[8]{0:T(128)S(1)} %copy-done.5, s32[8]{0:T(128)S(1)} %copy-done.6, bf16[64,1408]{1,0:T(8,128)(2,1)S(1)} %copy-done.2), custom_call_target="tpu_custom_call" | custom-call | tf_op jit(solution)/shard_map/table/pallas_call | solution.py:327
  17.2 0.0 collective-permute-done.2.refs_5_
  17.2 1.6 %collective-permute-start.7 = (bf16[64,1408]{1,0:T(8,128)(2,1)S(1)}, bf16[64,1408]{1,0:T(8,128)(2,1)S(1)}, u32[]{:S(2)}, u32[]{:S(2)}) collective-permute-start(bf16[64,1408]{1,0:T(8,128)(2,1)S(1)} %collective-permute-done.2.refs_5_), channel_id=1, source_target_pairs={{0,16},{16,0},{1,17},{17,1},{2,18},{18,2},{3,19},{19,3},{4,20},{20... | collective-permute-start | bytes 540680 | tf_op jit(solution)/shard_map/ppermute | solution.py:31
  18.8 0.0 collective-permute-done.1.base_other
  18.8 0.4 matrix_rows.1.matrix
  19.2 0.0 collective-permute-done.refs_4_
  19.2 0.6 %collective-permute-start.6 = (bf16[64,1408]{1,0:T(8,128)(2,1)S(1)}, bf16[64,1408]{1,0:T(8,128)(2,1)S(1)}, u32[]{:S(2)}, u32[]{:S(2)}) collective-permute-start(bf16[64,1408]{1,0:T(8,128)(2,1)S(1)} %collective-permute-done.refs_4_), channel_id=1, source_target_pairs={{0,16},{16,0},{1,17},{17,1},{2,18},{18,2},{3,19},{19,3},{4,20},{20... | collective-permute-start | bytes 540680 | tf_op jit(solution)/shard_map/ppermute | solution.py:31
  19.8 0.0 collective-permute-start.5
  19.8 0.0 collective-permute-done.3.refs_3_
  19.8 0.1 collective-permute-start.9
  19.9 4.3 %collective-permute-done.7.refs_7_ = bf16[64,1408]{1,0:T(8,128)(2,1)S(1)} collective-permute-done((bf16[64,1408]{1,0:T(8,128)(2,1)S(1)}, bf16[64,1408]{1,0:T(8,128)(2,1)S(1)}, u32[]{:S(2)}, u32[]{:S(2)}) %collective-permute-start.7) | collective-permute-done | bytes 180256 | tf_op jit(solution)/shard_map/ppermute | solution.py:31
  24.2 0.0 collective-permute-start.11
  24.2 0.0 collective-permute-done.4.refs_1_
  24.2 0.5 collective-permute-start.8
  24.7 1.4 %collective-permute-done.6.refs_6_ = bf16[64,1408]{1,0:T(8,128)(2,1)S(1)} collective-permute-done((bf16[64,1408]{1,0:T(8,128)(2,1)S(1)}, bf16[64,1408]{1,0:T(8,128)(2,1)S(1)}, u32[]{:S(2)}, u32[]{:S(2)}) %collective-permute-start.6) | collective-permute-done | bytes 180256 | tf_op jit(solution)/shard_map/ppermute | solution.py:31
  26.1 0.0 collective-permute-start.10
  26.1 5.0 %collective-permute-done.5.refs_2_ = bf16[64,1408]{1,0:T(8,128)(2,1)S(1)} collective-permute-done((bf16[64,1408]{1,0:T(8,128)(2,1)S(1)}, bf16[64,1408]{1,0:T(8,128)(2,1)S(1)}, u32[]{:S(2)}, u32[]{:S(2)}) %collective-permute-start.5) | collective-permute-done | bytes 180256 | tf_op jit(solution)/shard_map/ppermute | solution.py:31
  31.1 0.0 collective-permute-done.9.refs_9_
  31.1 0.0 collective-permute-done.11.refs_11_
  31.1 0.0 collective-permute-done.8.refs_8_
  31.1 0.0 collective-permute-done.10.refs_10_
  31.1 1.5 %project.1 = (bf16[320,128]{1,0:T(8,128)(2,1)S(1)}, bf16[320,128]{1,0:T(8,128)(2,1)S(1)}, bf16[320,128]{1,0:T(8,128)(2,1)S(1)}, bf16[320,128]{1,0:T(8,128)(2,1)S(1)}) custom-call(s32[4,4]{1,0:T(4,128)S(1)} %get-tuple-element.48.table, bf16[1408,1024]{1,0:T(8,128)(2,1)S(1)} %matrix_rows.1.matrix, bf16[64,1408]{1,0:T(8,128)(2,1)S(1)} %get-tuple-element.57.refs_0_, ...), custom_call_target="tpu_custom_call" | custom-call | tf_op jit(solution)/shard_map/project/pallas_call | solution.py:327
  32.7 0.1 collective-permute-start.12
  32.8 2.4 %collective-permute-start.13 = (bf16[320,128]{1,0:T(8,128)(2,1)S(1)}, bf16[320,128]{1,0:T(8,128)(2,1)S(1)}, u32[]{:S(2)}, u32[]{:S(2)}) collective-permute-start(bf16[320,128]{1,0:T(8,128)(2,1)S(1)} %get-tuple-element.75), channel_id=1, source_target_pairs={{0,4},{4,0},{8,12},{12,8},{1,5},{5,1},{9,13},{13,9},{2,6},{6,2},{1... | collective-permute-start | bytes 245768 | tf_op jit(solution)/shard_map/ppermute | solution.py:31
  35.2 2.0 %collective-permute-start.14 = (bf16[320,128]{1,0:T(8,128)(2,1)S(1)}, bf16[320,128]{1,0:T(8,128)(2,1)S(1)}, u32[]{:S(2)}, u32[]{:S(2)}) collective-permute-start(bf16[320,128]{1,0:T(8,128)(2,1)S(1)} %get-tuple-element.76), channel_id=1, source_target_pairs={{0,12},{4,8},{8,4},{12,0},{1,13},{5,9},{9,5},{13,1},{2,14},{6,10},... | collective-permute-start | bytes 245768 | tf_op jit(solution)/shard_map/ppermute | solution.py:31
  37.1 2.7 %collective-permute-done.12.refs_1_ = bf16[320,128]{1,0:T(8,128)(2,1)S(1)} collective-permute-done((bf16[320,128]{1,0:T(8,128)(2,1)S(1)}, bf16[320,128]{1,0:T(8,128)(2,1)S(1)}, u32[]{:S(2)}, u32[]{:S(2)}) %collective-permute-start.12) | collective-permute-done | bytes 81952 | tf_op jit(solution)/shard_map/ppermute | solution.py:31
  39.8 0.0 collective-permute-done.13.refs_2_
  39.8 1.7 %collective-permute-done.14.refs_3_ = bf16[320,128]{1,0:T(8,128)(2,1)S(1)} collective-permute-done((bf16[320,128]{1,0:T(8,128)(2,1)S(1)}, bf16[320,128]{1,0:T(8,128)(2,1)S(1)}, u32[]{:S(2)}, u32[]{:S(2)}) %collective-permute-start.14) | collective-permute-done | bytes 81952 | tf_op jit(solution)/shard_map/ppermute | solution.py:31
  41.6 0.1 collective-permute-start.15
  41.6 1.1 %softmax_rows.1 = (bf16[512,256]{1,0:T(8,128)(2,1)S(1)}, bf16[256,128]{1,0:T(8,128)(2,1)S(1)}, f32[256,128]{1,0:T(8,128)S(1)}) custom-call(s32[4,4]{1,0:T(4,128)S(1)} %get-tuple-element.48.table, bf16[64,1408]{1,0:T(8,128)(2,1)S(1)} %get-tuple-element.57.refs_0_, bf16[64,1408]{1,0:T(8,128)(2,1)S(1)} %collective-permute-done.4.refs_1_, ...), custom_call_target="tpu_custom_call" | custom-call | tf_op jit(solution)/shard_map/softmax_rows/pallas_call | solution.py:327
  42.8 0.1 collective-permute-done.15.received
  42.9 1.1 %mix_values.1 = (bf16[64,256]{1,0:T(8,128)(2,1)S(1)}, bf16[64,256]{1,0:T(8,128)(2,1)S(1)}, bf16[64,256]{1,0:T(8,128)(2,1)S(1)}, bf16[64,256]{1,0:T(8,128)(2,1)S(1)}) custom-call(s32[4,4]{1,0:T(4,128)S(1)} %get-tuple-element.48.table, bf16[512,256]{1,0:T(8,128)(2,1)S(1)} %get-tuple-element.61.softmax, bf16[256,128]{1,0:T(8,128)(2,1)S(1)} %get-tuple-element.62.raise_picked, ...), custom_call_target="tpu_custom_call" | custom-call | tf_op jit(solution)/shard_map/mix_values/pallas_call | solution.py:327
  44.0 2.0 %collective-permute-start.16 = (bf16[64,256]{1,0:T(8,128)(2,1)S(1)}, bf16[64,256]{1,0:T(8,128)(2,1)S(1)}, u32[]{:S(2)}, u32[]{:S(2)}) collective-permute-start(bf16[64,256]{1,0:T(8,128)(2,1)S(1)} %get-tuple-element.80), channel_id=1, source_target_pairs={{0,12},{4,8},{8,4},{12,0},{1,13},{5,9},{9,5},{13,1},{2,14},{6,10},... | collective-permute-start | bytes 98312 | tf_op jit(solution)/shard_map/ppermute | solution.py:31
  46.1 0.6 %collective-permute-start.17 = (bf16[64,256]{1,0:T(8,128)(2,1)S(1)}, bf16[64,256]{1,0:T(8,128)(2,1)S(1)}, u32[]{:S(2)}, u32[]{:S(2)}) collective-permute-start(bf16[64,256]{1,0:T(8,128)(2,1)S(1)} %get-tuple-element.81), channel_id=1, source_target_pairs={{0,8},{4,12},{8,0},{12,4},{1,9},{5,13},{9,1},{13,5},{2,10},{6,14},... | collective-permute-start | bytes 98312 | tf_op jit(solution)/shard_map/ppermute | solution.py:31
  46.6 1.9 %collective-permute-start.18 = (bf16[64,256]{1,0:T(8,128)(2,1)S(1)}, bf16[64,256]{1,0:T(8,128)(2,1)S(1)}, u32[]{:S(2)}, u32[]{:S(2)}) collective-permute-start(bf16[64,256]{1,0:T(8,128)(2,1)S(1)} %get-tuple-element.82), channel_id=1, source_target_pairs={{0,4},{4,0},{8,12},{12,8},{1,5},{5,1},{9,13},{13,9},{2,6},{6,2},{1... | collective-permute-start | bytes 98312 | tf_op jit(solution)/shard_map/ppermute | solution.py:31
  48.5 1.4 %collective-permute-done.16.refs_1_ = bf16[64,256]{1,0:T(8,128)(2,1)S(1)} collective-permute-done((bf16[64,256]{1,0:T(8,128)(2,1)S(1)}, bf16[64,256]{1,0:T(8,128)(2,1)S(1)}, u32[]{:S(2)}, u32[]{:S(2)}) %collective-permute-start.16) | collective-permute-done | bytes 32800 | tf_op jit(solution)/shard_map/ppermute | solution.py:31
  50.0 1.1 %collective-permute-done.17.refs_2_ = bf16[64,256]{1,0:T(8,128)(2,1)S(1)} collective-permute-done((bf16[64,256]{1,0:T(8,128)(2,1)S(1)}, bf16[64,256]{1,0:T(8,128)(2,1)S(1)}, u32[]{:S(2)}, u32[]{:S(2)}) %collective-permute-start.17) | collective-permute-done | bytes 32800 | tf_op jit(solution)/shard_map/ppermute | solution.py:31
  51.0 0.1 collective-permute-done.18.refs_3_
  51.2 0.7 %place_heads.1 = bf16[64,1024]{1,0:T(8,128)(2,1)} custom-call(bf16[64,256]{1,0:T(8,128)(2,1)S(1)} %get-tuple-element.79.refs_0_, bf16[64,256]{1,0:T(8,128)(2,1)S(1)} %collective-permute-done.16.refs_1_, bf16[64,256]{1,0:T(8,128)(2,1)S(1)} %collective-permute-done.17.refs_2_, bf16[64,256]{1,0:T(8,128)(2,1)S(1)} %collective-permute-done.18.refs_3_), custom_call_target="tpu_custom_call" | custom-call | tf_op jit(solution)/shard_map/place_heads/pallas_call | solution.py:327
  (15 shorter events, 0.1 us)
Async XLA Ops:
  0.0 18.8 %copy-start = (bf16[1,672,1024]{2,1,0:T(8,128)(2,1)S(1)}, bf16[1,672,1024]{2,1,0:T(8,128)(2,1)}, u32[]{:S(2)}) copy-start(bf16[1,672,1024]{2,1,0:T(8,128)(2,1)} %param.15) | copy-start | bytes 4128772
  0.0 18.8 %collective-permute-start.1 = (bf16[672,1024]{1,0:T(8,128)(2,1)}, bf16[672,1024]{1,0:T(8,128)(2,1)S(1)}, u32[]{:S(2)}, u32[]{:S(2)}) collective-permute-start(bf16[672,1024]{1,0:T(8,128)(2,1)} %bitcast.9), channel_id=1, source_target_pairs={{0,1},{1,0},{2,3},{3,2},{4,5},{5,4},{6,7},{7,6},{8,9},{9,8},{10,11... | collective-permute-start | bytes 4128776 | tf_op jit(solution)/shard_map/ppermute | solution.py:31
  0.5 1.1 %copy-start.1 = (bf16[1,2,2688,64]{2,3,1,0:T(8,128)(2,1)S(1)}, bf16[1,2,2688,64]{2,3,1,0:T(8,128)(2,1)}, u32[]{:S(2)}) copy-start(bf16[1,2,2688,64]{2,3,1,0:T(8,128)(2,1)} %param.16) | copy-start | bytes 2064388
  1.6 13.2 %copy-start.3 = (s32[4]{0:T(128)S(1)}, s32[4]{0:T(128)}, u32[]{:S(2)}) copy-start(s32[4]{0:T(128)} %lengths.1) | copy-start | bytes 52
  1.6 13.2 %copy-start.4 = (s32[4]{0:T(128)S(1)}, s32[4]{0:T(128)}, u32[]{:S(2)}) copy-start(s32[4]{0:T(128)} %adapters.1) | copy-start | bytes 52
  1.6 13.2 %copy-start.5 = (s32[8]{0:T(128)S(1)}, s32[8]{0:T(128)}, u32[]{:S(2)}) copy-start(s32[8]{0:T(128)} %ranks.1) | copy-start | bytes 100
  1.6 13.2 %copy-start.6 = (s32[8]{0:T(128)S(1)}, s32[8]{0:T(128)}, u32[]{:S(2)}) copy-start(s32[8]{0:T(128)} %slots.1) | copy-start | bytes 100
  1.7 15.5 %collective-permute-start.2 = (bf16[64,1408]{1,0:T(8,128)(2,1)S(1)}, bf16[64,1408]{1,0:T(8,128)(2,1)S(1)}, u32[]{:S(2)}, u32[]{:S(2)}) collective-permute-start(bf16[64,1408]{1,0:T(8,128)(2,1)S(1)} %get-tuple-element.49), channel_id=1, source_target_pairs={{0,4},{1,12},{4,0},{5,8},{8,5},{9,13},{12,1},{13,9},{2,6},{3,14},{... | collective-permute-start | bytes 540680 | tf_op jit(solution)/shard_map/ppermute | solution.py:352
  4.4 14.8 %collective-permute-start = (bf16[64,1408]{1,0:T(8,128)(2,1)S(1)}, bf16[64,1408]{1,0:T(8,128)(2,1)S(1)}, u32[]{:S(2)}, u32[]{:S(2)}) collective-permute-start(bf16[64,1408]{1,0:T(8,128)(2,1)S(1)} %get-tuple-element.44), channel_id=1, source_target_pairs={{0,0},{1,8},{4,4},{5,12},{8,1},{9,9},{12,5},{13,13},{2,2},{3,10},{... | collective-permute-start | bytes 540680 | tf_op jit(solution)/shard_map/ppermute | solution.py:352
  7.3 12.4 %collective-permute-start.3 = (bf16[64,1408]{1,0:T(8,128)(2,1)}, bf16[64,1408]{1,0:T(8,128)(2,1)S(1)}, u32[]{:S(2)}, u32[]{:S(2)}) collective-permute-start(bf16[64,1408]{1,0:T(8,128)(2,1)} %get-tuple-element.52), channel_id=1, source_target_pairs={{0,4},{4,0},{8,12},{12,8},{1,5},{5,1},{9,13},{13,9},{2,6},{6,2},{1... | collective-permute-start | bytes 540680 | tf_op jit(solution)/shard_map/ppermute | solution.py:31
  7.4 16.7 %collective-permute-start.4 = (bf16[64,1408]{1,0:T(8,128)(2,1)}, bf16[64,1408]{1,0:T(8,128)(2,1)S(1)}, u32[]{:S(2)}, u32[]{:S(2)}) collective-permute-start(bf16[64,1408]{1,0:T(8,128)(2,1)} %get-tuple-element.53), channel_id=1, source_target_pairs={{0,12},{4,8},{8,4},{12,0},{1,13},{5,9},{9,5},{13,1},{2,14},{6,10},... | collective-permute-start | bytes 540680 | tf_op jit(solution)/shard_map/ppermute | solution.py:31
  14.8 0.9 %copy-start.2 = (bf16[64,1408]{1,0:T(8,128)(2,1)S(1)}, bf16[64,1408]{1,0:T(8,128)(2,1)}, u32[]{:S(2)}) copy-start(bf16[64,1408]{1,0:T(8,128)(2,1)} %get-tuple-element.46.piece) | copy-start | bytes 540676
  17.2 2.6 %copy-start.7 = (bf16[64,1408]{1,0:T(8,128)(2,1)S(1)}, bf16[64,1408]{1,0:T(8,128)(2,1)}, u32[]{:S(2)}) copy-start(bf16[64,1408]{1,0:T(8,128)(2,1)} %get-tuple-element.54) | copy-start | bytes 540676
  17.2 7.0 %collective-permute-start.7 = (bf16[64,1408]{1,0:T(8,128)(2,1)S(1)}, bf16[64,1408]{1,0:T(8,128)(2,1)S(1)}, u32[]{:S(2)}, u32[]{:S(2)}) collective-permute-start(bf16[64,1408]{1,0:T(8,128)(2,1)S(1)} %collective-permute-done.2.refs_5_), channel_id=1, source_target_pairs={{0,16},{16,0},{1,17},{17,1},{2,18},{18,2},{3,19},{19,3},{4,20},{20... | collective-permute-start | bytes 540680 | tf_op jit(solution)/shard_map/ppermute | solution.py:31
  19.2 6.9 %collective-permute-start.6 = (bf16[64,1408]{1,0:T(8,128)(2,1)S(1)}, bf16[64,1408]{1,0:T(8,128)(2,1)S(1)}, u32[]{:S(2)}, u32[]{:S(2)}) collective-permute-start(bf16[64,1408]{1,0:T(8,128)(2,1)S(1)} %collective-permute-done.refs_4_), channel_id=1, source_target_pairs={{0,16},{16,0},{1,17},{17,1},{2,18},{18,2},{3,19},{19,3},{4,20},{20... | collective-permute-start | bytes 540680 | tf_op jit(solution)/shard_map/ppermute | solution.py:31
  19.8 11.3 %collective-permute-start.5 = (bf16[64,1408]{1,0:T(8,128)(2,1)S(1)}, bf16[64,1408]{1,0:T(8,128)(2,1)S(1)}, u32[]{:S(2)}, u32[]{:S(2)}) collective-permute-start(bf16[64,1408]{1,0:T(8,128)(2,1)S(1)} %copy-done.7), channel_id=1, source_target_pairs={{0,8},{4,12},{8,0},{12,4},{1,9},{5,13},{9,1},{13,5},{2,10},{6,14},... | collective-permute-start | bytes 540680 | tf_op jit(solution)/shard_map/ppermute | solution.py:31
  19.8 11.3 %collective-permute-start.9 = (bf16[64,1408]{1,0:T(8,128)(2,1)S(1)}, bf16[64,1408]{1,0:T(8,128)(2,1)S(1)}, u32[]{:S(2)}, u32[]{:S(2)}) collective-permute-start(bf16[64,1408]{1,0:T(8,128)(2,1)S(1)} %collective-permute-done.2.refs_5_), channel_id=1, source_target_pairs={{0,1},{1,0},{2,3},{3,2},{4,5},{5,4},{6,7},{7,6},{8,9},{9,8},{10,11... | collective-permute-start | bytes 540680 | tf_op jit(solution)/shard_map/ppermute | solution.py:31
  24.2 6.9 %collective-permute-start.11 = (bf16[64,1408]{1,0:T(8,128)(2,1)S(1)}, bf16[64,1408]{1,0:T(8,128)(2,1)S(1)}, u32[]{:S(2)}, u32[]{:S(2)}) collective-permute-start(bf16[64,1408]{1,0:T(8,128)(2,1)S(1)} %collective-permute-done.7.refs_7_), channel_id=1, source_target_pairs={{0,1},{1,0},{2,3},{3,2},{4,5},{5,4},{6,7},{7,6},{8,9},{9,8},{10,11... | collective-permute-start | bytes 540680 | tf_op jit(solution)/shard_map/ppermute | solution.py:31
  24.2 6.9 %collective-permute-start.8 = (bf16[64,1408]{1,0:T(8,128)(2,1)S(1)}, bf16[64,1408]{1,0:T(8,128)(2,1)S(1)}, u32[]{:S(2)}, u32[]{:S(2)}) collective-permute-start(bf16[64,1408]{1,0:T(8,128)(2,1)S(1)} %collective-permute-done.refs_4_), channel_id=1, source_target_pairs={{0,1},{1,0},{2,3},{3,2},{4,5},{5,4},{6,7},{7,6},{8,9},{9,8},{10,11... | collective-permute-start | bytes 540680 | tf_op jit(solution)/shard_map/ppermute | solution.py:31
  26.1 5.0 %collective-permute-start.10 = (bf16[64,1408]{1,0:T(8,128)(2,1)S(1)}, bf16[64,1408]{1,0:T(8,128)(2,1)S(1)}, u32[]{:S(2)}, u32[]{:S(2)}) collective-permute-start(bf16[64,1408]{1,0:T(8,128)(2,1)S(1)} %collective-permute-done.6.refs_6_), channel_id=1, source_target_pairs={{0,1},{1,0},{2,3},{3,2},{4,5},{5,4},{6,7},{7,6},{8,9},{9,8},{10,11... | collective-permute-start | bytes 540680 | tf_op jit(solution)/shard_map/ppermute | solution.py:31
  32.7 7.2 %collective-permute-start.12 = (bf16[320,128]{1,0:T(8,128)(2,1)S(1)}, bf16[320,128]{1,0:T(8,128)(2,1)S(1)}, u32[]{:S(2)}, u32[]{:S(2)}) collective-permute-start(bf16[320,128]{1,0:T(8,128)(2,1)S(1)} %get-tuple-element.74), channel_id=1, source_target_pairs={{0,8},{4,12},{8,0},{12,4},{1,9},{5,13},{9,1},{13,5},{2,10},{6,14},... | collective-permute-start | bytes 245768 | tf_op jit(solution)/shard_map/ppermute | solution.py:31
  32.8 7.1 %collective-permute-start.13 = (bf16[320,128]{1,0:T(8,128)(2,1)S(1)}, bf16[320,128]{1,0:T(8,128)(2,1)S(1)}, u32[]{:S(2)}, u32[]{:S(2)}) collective-permute-start(bf16[320,128]{1,0:T(8,128)(2,1)S(1)} %get-tuple-element.75), channel_id=1, source_target_pairs={{0,4},{4,0},{8,12},{12,8},{1,5},{5,1},{9,13},{13,9},{2,6},{6,2},{1... | collective-permute-start | bytes 245768 | tf_op jit(solution)/shard_map/ppermute | solution.py:31
  35.2 6.3 %collective-permute-start.14 = (bf16[320,128]{1,0:T(8,128)(2,1)S(1)}, bf16[320,128]{1,0:T(8,128)(2,1)S(1)}, u32[]{:S(2)}, u32[]{:S(2)}) collective-permute-start(bf16[320,128]{1,0:T(8,128)(2,1)S(1)} %get-tuple-element.76), channel_id=1, source_target_pairs={{0,12},{4,8},{8,4},{12,0},{1,13},{5,9},{9,5},{13,1},{2,14},{6,10},... | collective-permute-start | bytes 245768 | tf_op jit(solution)/shard_map/ppermute | solution.py:31
  41.6 1.4 %collective-permute-start.15 = (f32[192,128]{1,0:T(8,128)S(1)}, f32[192,128]{1,0:T(8,128)S(1)}, u32[]{:S(2)}, u32[]{:S(2)}) collective-permute-start(f32[192,128]{1,0:T(8,128)S(1)} %get-tuple-element.78), channel_id=1, source_target_pairs={{0,1},{1,0},{2,3},{3,2},{4,5},{5,4},{6,7},{7,6},{8,9},{9,8},{10,11... | collective-permute-start | bytes 294920 | tf_op jit(solution)/shard_map/ppermute | solution.py:31
  44.0 5.9 %collective-permute-start.16 = (bf16[64,256]{1,0:T(8,128)(2,1)S(1)}, bf16[64,256]{1,0:T(8,128)(2,1)S(1)}, u32[]{:S(2)}, u32[]{:S(2)}) collective-permute-start(bf16[64,256]{1,0:T(8,128)(2,1)S(1)} %get-tuple-element.80), channel_id=1, source_target_pairs={{0,12},{4,8},{8,4},{12,0},{1,13},{5,9},{9,5},{13,1},{2,14},{6,10},... | collective-permute-start | bytes 98312 | tf_op jit(solution)/shard_map/ppermute | solution.py:31
  46.1 4.9 %collective-permute-start.17 = (bf16[64,256]{1,0:T(8,128)(2,1)S(1)}, bf16[64,256]{1,0:T(8,128)(2,1)S(1)}, u32[]{:S(2)}, u32[]{:S(2)}) collective-permute-start(bf16[64,256]{1,0:T(8,128)(2,1)S(1)} %get-tuple-element.81), channel_id=1, source_target_pairs={{0,8},{4,12},{8,0},{12,4},{1,9},{5,13},{9,1},{13,5},{2,10},{6,14},... | collective-permute-start | bytes 98312 | tf_op jit(solution)/shard_map/ppermute | solution.py:31
  46.6 4.5 %collective-permute-start.18 = (bf16[64,256]{1,0:T(8,128)(2,1)S(1)}, bf16[64,256]{1,0:T(8,128)(2,1)S(1)}, u32[]{:S(2)}, u32[]{:S(2)}) collective-permute-start(bf16[64,256]{1,0:T(8,128)(2,1)S(1)} %get-tuple-element.82), channel_id=1, source_target_pairs={{0,4},{4,0},{8,12},{12,8},{1,5},{5,1},{9,13},{13,9},{2,6},{6,2},{1... | collective-permute-start | bytes 98312 | tf_op jit(solution)/shard_map/ppermute | solution.py:31

commit v9 on v8

--- a/solution.py
+++ b/solution.py
@@ -23,6 +23,7 @@
 HBM = pl.BlockSpec(memory_space=pltpu.HBM)
 PARAMS = pltpu.CompilerParams(vmem_limit_bytes=16 * 1024 * 1024)
 FIRST = pltpu.CompilerParams(vmem_limit_bytes=60 * 1024 * 1024)
+SLOT = pltpu.CompilerParams(vmem_limit_bytes=107 * 512 * 1024)
 bf16 = jnp.bfloat16
 f32 = jnp.float32
 
@@ -341,6 +342,7 @@
         [((sz.rank, sz.span), bf16, VMEM)] * sz.side,
         (jnp.swapaxes(down, 1, 2),),
         (pltpu.SemaphoreType.DMA((sz.side,)),),
+        SLOT,
     )
     panels = []
     for m in range(sz.side):

time: 52 us -> 51.9 us (level)
  local copies, waits for them, and re-layouts: 2.04 us -> 0.94 us
  Pallas kernels: 8.7 us -> 9.61 us
    unnamed x16 -> x14, local copies, waits for them, and re-layouts: 2.04 us -> 0.94 us
    pallas_call x9, Pallas kernels: 8.7 us -> 9.61 us  [call(): pl.pallas_call(functools.partial(kernel, sz), out_shape=[jax.ShapeDtypeSt...]
  transfers between devices with their start and end apart: 19 -> 19, of which waited for: 9 -> 9; matrix products, arithmetic and copies ran while one was open for 0% -> 0% of each run, Pallas kernels for 10% -> 12%
where the time goes in v9:
time: 51.9 us; the launch traced here: 51.7 us
  starting transfers between devices  23.1 us (45%)
  waiting for transfers between devices  17.9 us (34%)
  Pallas kernels  9.61 us (19%)
  local copies, waits for them, and re-layouts  0.94 us (2%)
    ppermute x17, starting transfers between devices, swap(): lax.ppermute(value, axis, [(i, i ^ mask) for i in range(lax.axis_size(axi...  19.7 us
    ppermute x17, waiting for transfers between devices, swap(): lax.ppermute(value, axis, [(i, i ^ mask) for i in range(lax.axis_size(axi...  17.9 us
    pallas_call x9, Pallas kernels, call(): pl.pallas_call(functools.partial(kernel, sz), out_shape=[jax.ShapeDtypeSt...  9.61 us
    ppermute x2, starting transfers between devices, by_heads(): panels.append(lax.ppermute(panels_out[m], ('seq', 'owner'), pairs))  3.42 us
  transfers between devices with their start and end apart: 19, of which 9 were waited for; matrix products, arithmetic and copies ran while one was open for 0% of the time, Pallas kernels for 12%

profile of v9, /device:TPU:0, one launch (start us, length us, event | category | flops | bytes accessed | tf_op | source)
XLA Modules:
  0.0 51.7 jit_solution(3649945042668309375)
XLA Ops:
  0.0 0.5 %collective-permute-start.1 = (bf16[672,1024]{1,0:T(8,128)(2,1)}, bf16[672,1024]{1,0:T(8,128)(2,1)S(1)}, u32[]{:S(2)}, u32[]{:S(2)}) collective-permute-start(bf16[672,1024]{1,0:T(8,128)(2,1)} %bitcast.9), channel_id=1, source_target_pairs={{0,1},{1,0},{2,3},{3,2},{4,5},{5,4},{6,7},{7,6},{8,9},{9,8},{10,11... | collective-permute-start | bytes 4128776 | tf_op jit(solution)/shard_map/ppermute | solution.py:32
  0.5 1.0 %panels_out.1 = (bf16[64,1408]{1,0:T(8,128)(2,1)S(1)}, bf16[64,1408]{1,0:T(8,128)(2,1)S(1)}) custom-call(bf16[2,64,2688]{2,1,0:T(8,128)(2,1)} %bitcast.12), custom_call_target="tpu_custom_call" | custom-call | tf_op jit(solution)/shard_map/panels_out/pallas_call | solution.py:328
  1.6 2.8 %collective-permute-start.2 = (bf16[64,1408]{1,0:T(8,128)(2,1)S(1)}, bf16[64,1408]{1,0:T(8,128)(2,1)S(1)}, u32[]{:S(2)}, u32[]{:S(2)}) collective-permute-start(bf16[64,1408]{1,0:T(8,128)(2,1)S(1)} %get-tuple-element.49), channel_id=1, source_target_pairs={{0,4},{1,12},{4,0},{5,8},{8,5},{9,13},{12,1},{13,9},{2,6},{3,14},{... | collective-permute-start | bytes 540680 | tf_op jit(solution)/shard_map/ppermute | solution.py:354
  4.3 0.7 %collective-permute-start = (bf16[64,1408]{1,0:T(8,128)(2,1)S(1)}, bf16[64,1408]{1,0:T(8,128)(2,1)S(1)}, u32[]{:S(2)}, u32[]{:S(2)}) collective-permute-start(bf16[64,1408]{1,0:T(8,128)(2,1)S(1)} %get-tuple-element.44), channel_id=1, source_target_pairs={{0,0},{1,8},{4,4},{5,12},{8,1},{9,9},{12,5},{13,13},{2,2},{3,10},{... | collective-permute-start | bytes 540680 | tf_op jit(solution)/shard_map/ppermute | solution.py:354
  5.0 2.2 %norm_rows.1 = (bf16[64,1408]{1,0:T(8,128)(2,1)}, bf16[64,1408]{1,0:T(8,128)(2,1)}, bf16[64,1408]{1,0:T(8,128)(2,1)}, bf16[64,1408]{1,0:T(8,128)(2,1)}) custom-call(bf16[64,5376]{1,0:T(8,128)(2,1)} %bitcast.11, f32[1,5376]{1,0:T(1,128)} %gain.1, bf16[64,1024]{1,0:T(8,128)(2,1)} %bitcast.13, bf16[64,512]{1,0:T(8,128)(2,1)} %bitcast.15, ...), custom_call_target="tpu_custom_call" | custom-call | tf_op jit(solution)/shard_map/norm_rows/pallas_call | solution.py:328
  7.3 0.1 collective-permute-start.3
  7.3 7.3 %collective-permute-start.4 = (bf16[64,1408]{1,0:T(8,128)(2,1)}, bf16[64,1408]{1,0:T(8,128)(2,1)S(1)}, u32[]{:S(2)}, u32[]{:S(2)}) collective-permute-start(bf16[64,1408]{1,0:T(8,128)(2,1)} %get-tuple-element.53), channel_id=1, source_target_pairs={{0,12},{4,8},{8,4},{12,0},{1,13},{5,9},{9,5},{13,1},{2,14},{6,10},... | collective-permute-start | bytes 540680 | tf_op jit(solution)/shard_map/ppermute | solution.py:32
  14.7 0.0 copy-done.2
  14.7 0.9 %copy-done.1 = bf16[64,1408]{1,0:T(8,128)(2,1)S(1)} copy-done((bf16[64,1408]{1,0:T(8,128)(2,1)S(1)}, bf16[64,1408]{1,0:T(8,128)(2,1)}, u32[]{:S(2)}) %copy-start.1) | copy-done | bytes 180248
  15.6 1.5 %table.1 = (s32[4,4]{1,0:T(4,128)S(1)}, bf16[64,1408]{1,0:T(8,128)(2,1)S(1)}) custom-call(s32[4]{0:T(128)S(1)} %copy-done.2, s32[4]{0:T(128)S(1)} %copy-done.3, s32[8]{0:T(128)S(1)} %copy-done.4, s32[8]{0:T(128)S(1)} %copy-done.5, bf16[64,1408]{1,0:T(8,128)(2,1)S(1)} %copy-done.1), custom_call_target="tpu_custom_call" | custom-call | tf_op jit(solution)/shard_map/table/pallas_call | solution.py:328
  17.1 0.0 collective-permute-done.2.refs_5_
  17.1 1.6 %collective-permute-start.7 = (bf16[64,1408]{1,0:T(8,128)(2,1)S(1)}, bf16[64,1408]{1,0:T(8,128)(2,1)S(1)}, u32[]{:S(2)}, u32[]{:S(2)}) collective-permute-start(bf16[64,1408]{1,0:T(8,128)(2,1)S(1)} %collective-permute-done.2.refs_5_), channel_id=1, source_target_pairs={{0,16},{16,0},{1,17},{17,1},{2,18},{18,2},{3,19},{19,3},{4,20},{20... | collective-permute-start | bytes 540680 | tf_op jit(solution)/shard_map/ppermute | solution.py:32
  18.7 0.0 collective-permute-done.1.base_other
  18.7 0.4 matrix_rows.1.matrix
  19.1 0.0 collective-permute-done.refs_4_
  19.1 0.6 %collective-permute-start.6 = (bf16[64,1408]{1,0:T(8,128)(2,1)S(1)}, bf16[64,1408]{1,0:T(8,128)(2,1)S(1)}, u32[]{:S(2)}, u32[]{:S(2)}) collective-permute-start(bf16[64,1408]{1,0:T(8,128)(2,1)S(1)} %collective-permute-done.refs_4_), channel_id=1, source_target_pairs={{0,16},{16,0},{1,17},{17,1},{2,18},{18,2},{3,19},{19,3},{4,20},{20... | collective-permute-start | bytes 540680 | tf_op jit(solution)/shard_map/ppermute | solution.py:32
  19.7 0.0 collective-permute-start.5
  19.7 0.0 collective-permute-done.3.refs_3_
  19.7 0.1 collective-permute-start.9
  19.8 4.3 %collective-permute-done.7.refs_7_ = bf16[64,1408]{1,0:T(8,128)(2,1)S(1)} collective-permute-done((bf16[64,1408]{1,0:T(8,128)(2,1)S(1)}, bf16[64,1408]{1,0:T(8,128)(2,1)S(1)}, u32[]{:S(2)}, u32[]{:S(2)}) %collective-permute-start.7) | collective-permute-done | bytes 180256 | tf_op jit(solution)/shard_map/ppermute | solution.py:32
  24.1 0.0 collective-permute-start.11
  24.1 0.0 collective-permute-done.4.refs_1_
  24.1 0.5 collective-permute-start.8
  24.6 1.4 %collective-permute-done.6.refs_6_ = bf16[64,1408]{1,0:T(8,128)(2,1)S(1)} collective-permute-done((bf16[64,1408]{1,0:T(8,128)(2,1)S(1)}, bf16[64,1408]{1,0:T(8,128)(2,1)S(1)}, u32[]{:S(2)}, u32[]{:S(2)}) %collective-permute-start.6) | collective-permute-done | bytes 180256 | tf_op jit(solution)/shard_map/ppermute | solution.py:32
  26.0 0.0 collective-permute-start.10
  26.0 5.0 %collective-permute-done.5.refs_2_ = bf16[64,1408]{1,0:T(8,128)(2,1)S(1)} collective-permute-done((bf16[64,1408]{1,0:T(8,128)(2,1)S(1)}, bf16[64,1408]{1,0:T(8,128)(2,1)S(1)}, u32[]{:S(2)}, u32[]{:S(2)}) %collective-permute-start.5) | collective-permute-done | bytes 180256 | tf_op jit(solution)/shard_map/ppermute | solution.py:32
  31.0 0.0 collective-permute-done.9.refs_9_
  31.0 0.0 collective-permute-done.11.refs_11_
  31.0 0.0 collective-permute-done.8.refs_8_
  31.0 0.0 collective-permute-done.10.refs_10_
  31.0 1.5 %project.1 = (bf16[320,128]{1,0:T(8,128)(2,1)S(1)}, bf16[320,128]{1,0:T(8,128)(2,1)S(1)}, bf16[320,128]{1,0:T(8,128)(2,1)S(1)}, bf16[320,128]{1,0:T(8,128)(2,1)S(1)}) custom-call(s32[4,4]{1,0:T(4,128)S(1)} %get-tuple-element.48.table, bf16[1408,1024]{1,0:T(8,128)(2,1)S(1)} %matrix_rows.1.matrix, bf16[64,1408]{1,0:T(8,128)(2,1)S(1)} %get-tuple-element.57.refs_0_, ...), custom_call_target="tpu_custom_call" | custom-call | tf_op jit(solution)/shard_map/project/pallas_call | solution.py:328
  32.6 0.1 collective-permute-start.12
  32.7 2.4 %collective-permute-start.13 = (bf16[320,128]{1,0:T(8,128)(2,1)S(1)}, bf16[320,128]{1,0:T(8,128)(2,1)S(1)}, u32[]{:S(2)}, u32[]{:S(2)}) collective-permute-start(bf16[320,128]{1,0:T(8,128)(2,1)S(1)} %get-tuple-element.75), channel_id=1, source_target_pairs={{0,4},{4,0},{8,12},{12,8},{1,5},{5,1},{9,13},{13,9},{2,6},{6,2},{1... | collective-permute-start | bytes 245768 | tf_op jit(solution)/shard_map/ppermute | solution.py:32
  35.1 1.9 %collective-permute-start.14 = (bf16[320,128]{1,0:T(8,128)(2,1)S(1)}, bf16[320,128]{1,0:T(8,128)(2,1)S(1)}, u32[]{:S(2)}, u32[]{:S(2)}) collective-permute-start(bf16[320,128]{1,0:T(8,128)(2,1)S(1)} %get-tuple-element.76), channel_id=1, source_target_pairs={{0,12},{4,8},{8,4},{12,0},{1,13},{5,9},{9,5},{13,1},{2,14},{6,10},... | collective-permute-start | bytes 245768 | tf_op jit(solution)/shard_map/ppermute | solution.py:32
  37.0 2.7 %collective-permute-done.12.refs_1_ = bf16[320,128]{1,0:T(8,128)(2,1)S(1)} collective-permute-done((bf16[320,128]{1,0:T(8,128)(2,1)S(1)}, bf16[320,128]{1,0:T(8,128)(2,1)S(1)}, u32[]{:S(2)}, u32[]{:S(2)}) %collective-permute-start.12) | collective-permute-done | bytes 81952 | tf_op jit(solution)/shard_map/ppermute | solution.py:32
  39.7 0.0 collective-permute-done.13.refs_2_
  39.7 1.7 %collective-permute-done.14.refs_3_ = bf16[320,128]{1,0:T(8,128)(2,1)S(1)} collective-permute-done((bf16[320,128]{1,0:T(8,128)(2,1)S(1)}, bf16[320,128]{1,0:T(8,128)(2,1)S(1)}, u32[]{:S(2)}, u32[]{:S(2)}) %collective-permute-start.14) | collective-permute-done | bytes 81952 | tf_op jit(solution)/shard_map/ppermute | solution.py:32
  41.4 0.1 collective-permute-start.15
  41.5 1.1 %softmax_rows.1 = (bf16[512,256]{1,0:T(8,128)(2,1)S(1)}, bf16[256,128]{1,0:T(8,128)(2,1)S(1)}, f32[256,128]{1,0:T(8,128)S(1)}) custom-call(s32[4,4]{1,0:T(4,128)S(1)} %get-tuple-element.48.table, bf16[64,1408]{1,0:T(8,128)(2,1)S(1)} %get-tuple-element.57.refs_0_, bf16[64,1408]{1,0:T(8,128)(2,1)S(1)} %collective-permute-done.4.refs_1_, ...), custom_call_target="tpu_custom_call" | custom-call | tf_op jit(solution)/shard_map/softmax_rows/pallas_call | solution.py:328
  42.6 0.2 collective-permute-done.15.received
  42.8 1.1 %mix_values.1 = (bf16[64,256]{1,0:T(8,128)(2,1)S(1)}, bf16[64,256]{1,0:T(8,128)(2,1)S(1)}, bf16[64,256]{1,0:T(8,128)(2,1)S(1)}, bf16[64,256]{1,0:T(8,128)(2,1)S(1)}) custom-call(s32[4,4]{1,0:T(4,128)S(1)} %get-tuple-element.48.table, bf16[512,256]{1,0:T(8,128)(2,1)S(1)} %get-tuple-element.61.softmax, bf16[256,128]{1,0:T(8,128)(2,1)S(1)} %get-tuple-element.62.raise_picked, ...), custom_call_target="tpu_custom_call" | custom-call | tf_op jit(solution)/shard_map/mix_values/pallas_call | solution.py:328
  43.9 2.1 %collective-permute-start.16 = (bf16[64,256]{1,0:T(8,128)(2,1)S(1)}, bf16[64,256]{1,0:T(8,128)(2,1)S(1)}, u32[]{:S(2)}, u32[]{:S(2)}) collective-permute-start(bf16[64,256]{1,0:T(8,128)(2,1)S(1)} %get-tuple-element.80), channel_id=1, source_target_pairs={{0,12},{4,8},{8,4},{12,0},{1,13},{5,9},{9,5},{13,1},{2,14},{6,10},... | collective-permute-start | bytes 98312 | tf_op jit(solution)/shard_map/ppermute | solution.py:32
  46.0 0.6 %collective-permute-start.17 = (bf16[64,256]{1,0:T(8,128)(2,1)S(1)}, bf16[64,256]{1,0:T(8,128)(2,1)S(1)}, u32[]{:S(2)}, u32[]{:S(2)}) collective-permute-start(bf16[64,256]{1,0:T(8,128)(2,1)S(1)} %get-tuple-element.81), channel_id=1, source_target_pairs={{0,8},{4,12},{8,0},{12,4},{1,9},{5,13},{9,1},{13,5},{2,10},{6,14},... | collective-permute-start | bytes 98312 | tf_op jit(solution)/shard_map/ppermute | solution.py:32
  46.5 1.8 %collective-permute-start.18 = (bf16[64,256]{1,0:T(8,128)(2,1)S(1)}, bf16[64,256]{1,0:T(8,128)(2,1)S(1)}, u32[]{:S(2)}, u32[]{:S(2)}) collective-permute-start(bf16[64,256]{1,0:T(8,128)(2,1)S(1)} %get-tuple-element.82), channel_id=1, source_target_pairs={{0,4},{4,0},{8,12},{12,8},{1,5},{5,1},{9,13},{13,9},{2,6},{6,2},{1... | collective-permute-start | bytes 98312 | tf_op jit(solution)/shard_map/ppermute | solution.py:32
  48.4 1.4 %collective-permute-done.16.refs_1_ = bf16[64,256]{1,0:T(8,128)(2,1)S(1)} collective-permute-done((bf16[64,256]{1,0:T(8,128)(2,1)S(1)}, bf16[64,256]{1,0:T(8,128)(2,1)S(1)}, u32[]{:S(2)}, u32[]{:S(2)}) %collective-permute-start.16) | collective-permute-done | bytes 32800 | tf_op jit(solution)/shard_map/ppermute | solution.py:32
  49.8 1.1 %collective-permute-done.17.refs_2_ = bf16[64,256]{1,0:T(8,128)(2,1)S(1)} collective-permute-done((bf16[64,256]{1,0:T(8,128)(2,1)S(1)}, bf16[64,256]{1,0:T(8,128)(2,1)S(1)}, u32[]{:S(2)}, u32[]{:S(2)}) %collective-permute-start.17) | collective-permute-done | bytes 32800 | tf_op jit(solution)/shard_map/ppermute | solution.py:32
  50.9 0.2 collective-permute-done.18.refs_3_
  51.0 0.7 %place_heads.1 = bf16[64,1024]{1,0:T(8,128)(2,1)} custom-call(bf16[64,256]{1,0:T(8,128)(2,1)S(1)} %get-tuple-element.79.refs_0_, bf16[64,256]{1,0:T(8,128)(2,1)S(1)} %collective-permute-done.16.refs_1_, bf16[64,256]{1,0:T(8,128)(2,1)S(1)} %collective-permute-done.17.refs_2_, bf16[64,256]{1,0:T(8,128)(2,1)S(1)} %collective-permute-done.18.refs_3_), custom_call_target="tpu_custom_call" | custom-call | tf_op jit(solution)/shard_map/place_heads/pallas_call | solution.py:328
  (13 shorter events, 0.1 us)
Async XLA Ops:
  0.0 18.7 %copy-start = (bf16[1,672,1024]{2,1,0:T(8,128)(2,1)S(1)}, bf16[1,672,1024]{2,1,0:T(8,128)(2,1)}, u32[]{:S(2)}) copy-start(bf16[1,672,1024]{2,1,0:T(8,128)(2,1)} %param.15) | copy-start | bytes 4128772
  0.0 14.7 %copy-start.2 = (s32[4]{0:T(128)S(1)}, s32[4]{0:T(128)}, u32[]{:S(2)}) copy-start(s32[4]{0:T(128)} %lengths.1) | copy-start | bytes 52
  0.0 14.7 %copy-start.3 = (s32[4]{0:T(128)S(1)}, s32[4]{0:T(128)}, u32[]{:S(2)}) copy-start(s32[4]{0:T(128)} %adapters.1) | copy-start | bytes 52
  0.0 14.7 %copy-start.4 = (s32[8]{0:T(128)S(1)}, s32[8]{0:T(128)}, u32[]{:S(2)}) copy-start(s32[8]{0:T(128)} %ranks.1) | copy-start | bytes 100
  0.0 14.7 %copy-start.5 = (s32[8]{0:T(128)S(1)}, s32[8]{0:T(128)}, u32[]{:S(2)}) copy-start(s32[8]{0:T(128)} %slots.1) | copy-start | bytes 100
  0.0 18.7 %collective-permute-start.1 = (bf16[672,1024]{1,0:T(8,128)(2,1)}, bf16[672,1024]{1,0:T(8,128)(2,1)S(1)}, u32[]{:S(2)}, u32[]{:S(2)}) collective-permute-start(bf16[672,1024]{1,0:T(8,128)(2,1)} %bitcast.9), channel_id=1, source_target_pairs={{0,1},{1,0},{2,3},{3,2},{4,5},{5,4},{6,7},{7,6},{8,9},{9,8},{10,11... | collective-permute-start | bytes 4128776 | tf_op jit(solution)/shard_map/ppermute | solution.py:32
  1.6 15.5 %collective-permute-start.2 = (bf16[64,1408]{1,0:T(8,128)(2,1)S(1)}, bf16[64,1408]{1,0:T(8,128)(2,1)S(1)}, u32[]{:S(2)}, u32[]{:S(2)}) collective-permute-start(bf16[64,1408]{1,0:T(8,128)(2,1)S(1)} %get-tuple-element.49), channel_id=1, source_target_pairs={{0,4},{1,12},{4,0},{5,8},{8,5},{9,13},{12,1},{13,9},{2,6},{3,14},{... | collective-permute-start | bytes 540680 | tf_op jit(solution)/shard_map/ppermute | solution.py:354
  4.3 14.8 %collective-permute-start = (bf16[64,1408]{1,0:T(8,128)(2,1)S(1)}, bf16[64,1408]{1,0:T(8,128)(2,1)S(1)}, u32[]{:S(2)}, u32[]{:S(2)}) collective-permute-start(bf16[64,1408]{1,0:T(8,128)(2,1)S(1)} %get-tuple-element.44), channel_id=1, source_target_pairs={{0,0},{1,8},{4,4},{5,12},{8,1},{9,9},{12,5},{13,13},{2,2},{3,10},{... | collective-permute-start | bytes 540680 | tf_op jit(solution)/shard_map/ppermute | solution.py:354
  7.3 12.4 %collective-permute-start.3 = (bf16[64,1408]{1,0:T(8,128)(2,1)}, bf16[64,1408]{1,0:T(8,128)(2,1)S(1)}, u32[]{:S(2)}, u32[]{:S(2)}) collective-permute-start(bf16[64,1408]{1,0:T(8,128)(2,1)} %get-tuple-element.52), channel_id=1, source_target_pairs={{0,4},{4,0},{8,12},{12,8},{1,5},{5,1},{9,13},{13,9},{2,6},{6,2},{1... | collective-permute-start | bytes 540680 | tf_op jit(solution)/shard_map/ppermute | solution.py:32
  7.3 16.7 %collective-permute-start.4 = (bf16[64,1408]{1,0:T(8,128)(2,1)}, bf16[64,1408]{1,0:T(8,128)(2,1)S(1)}, u32[]{:S(2)}, u32[]{:S(2)}) collective-permute-start(bf16[64,1408]{1,0:T(8,128)(2,1)} %get-tuple-element.53), channel_id=1, source_target_pairs={{0,12},{4,8},{8,4},{12,0},{1,13},{5,9},{9,5},{13,1},{2,14},{6,10},... | collective-permute-start | bytes 540680 | tf_op jit(solution)/shard_map/ppermute | solution.py:32
  14.7 0.9 %copy-start.1 = (bf16[64,1408]{1,0:T(8,128)(2,1)S(1)}, bf16[64,1408]{1,0:T(8,128)(2,1)}, u32[]{:S(2)}) copy-start(bf16[64,1408]{1,0:T(8,128)(2,1)} %get-tuple-element.46.piece) | copy-start | bytes 540676
  17.1 2.6 %copy-start.6 = (bf16[64,1408]{1,0:T(8,128)(2,1)S(1)}, bf16[64,1408]{1,0:T(8,128)(2,1)}, u32[]{:S(2)}) copy-start(bf16[64,1408]{1,0:T(8,128)(2,1)} %get-tuple-element.54) | copy-start | bytes 540676
  17.1 7.0 %collective-permute-start.7 = (bf16[64,1408]{1,0:T(8,128)(2,1)S(1)}, bf16[64,1408]{1,0:T(8,128)(2,1)S(1)}, u32[]{:S(2)}, u32[]{:S(2)}) collective-permute-start(bf16[64,1408]{1,0:T(8,128)(2,1)S(1)} %collective-permute-done.2.refs_5_), channel_id=1, source_target_pairs={{0,16},{16,0},{1,17},{17,1},{2,18},{18,2},{3,19},{19,3},{4,20},{20... | collective-permute-start | bytes 540680 | tf_op jit(solution)/shard_map/ppermute | solution.py:32
  19.1 6.9 %collective-permute-start.6 = (bf16[64,1408]{1,0:T(8,128)(2,1)S(1)}, bf16[64,1408]{1,0:T(8,128)(2,1)S(1)}, u32[]{:S(2)}, u32[]{:S(2)}) collective-permute-start(bf16[64,1408]{1,0:T(8,128)(2,1)S(1)} %collective-permute-done.refs_4_), channel_id=1, source_target_pairs={{0,16},{16,0},{1,17},{17,1},{2,18},{18,2},{3,19},{19,3},{4,20},{20... | collective-permute-start | bytes 540680 | tf_op jit(solution)/shard_map/ppermute | solution.py:32
  19.7 11.3 %collective-permute-start.5 = (bf16[64,1408]{1,0:T(8,128)(2,1)S(1)}, bf16[64,1408]{1,0:T(8,128)(2,1)S(1)}, u32[]{:S(2)}, u32[]{:S(2)}) collective-permute-start(bf16[64,1408]{1,0:T(8,128)(2,1)S(1)} %copy-done.6), channel_id=1, source_target_pairs={{0,8},{4,12},{8,0},{12,4},{1,9},{5,13},{9,1},{13,5},{2,10},{6,14},... | collective-permute-start | bytes 540680 | tf_op jit(solution)/shard_map/ppermute | solution.py:32
  19.7 11.3 %collective-permute-start.9 = (bf16[64,1408]{1,0:T(8,128)(2,1)S(1)}, bf16[64,1408]{1,0:T(8,128)(2,1)S(1)}, u32[]{:S(2)}, u32[]{:S(2)}) collective-permute-start(bf16[64,1408]{1,0:T(8,128)(2,1)S(1)} %collective-permute-done.2.refs_5_), channel_id=1, source_target_pairs={{0,1},{1,0},{2,3},{3,2},{4,5},{5,4},{6,7},{7,6},{8,9},{9,8},{10,11... | collective-permute-start | bytes 540680 | tf_op jit(solution)/shard_map/ppermute | solution.py:32
  24.1 6.9 %collective-permute-start.11 = (bf16[64,1408]{1,0:T(8,128)(2,1)S(1)}, bf16[64,1408]{1,0:T(8,128)(2,1)S(1)}, u32[]{:S(2)}, u32[]{:S(2)}) collective-permute-start(bf16[64,1408]{1,0:T(8,128)(2,1)S(1)} %collective-permute-done.7.refs_7_), channel_id=1, source_target_pairs={{0,1},{1,0},{2,3},{3,2},{4,5},{5,4},{6,7},{7,6},{8,9},{9,8},{10,11... | collective-permute-start | bytes 540680 | tf_op jit(solution)/shard_map/ppermute | solution.py:32
  24.1 6.9 %collective-permute-start.8 = (bf16[64,1408]{1,0:T(8,128)(2,1)S(1)}, bf16[64,1408]{1,0:T(8,128)(2,1)S(1)}, u32[]{:S(2)}, u32[]{:S(2)}) collective-permute-start(bf16[64,1408]{1,0:T(8,128)(2,1)S(1)} %collective-permute-done.refs_4_), channel_id=1, source_target_pairs={{0,1},{1,0},{2,3},{3,2},{4,5},{5,4},{6,7},{7,6},{8,9},{9,8},{10,11... | collective-permute-start | bytes 540680 | tf_op jit(solution)/shard_map/ppermute | solution.py:32
  26.0 5.0 %collective-permute-start.10 = (bf16[64,1408]{1,0:T(8,128)(2,1)S(1)}, bf16[64,1408]{1,0:T(8,128)(2,1)S(1)}, u32[]{:S(2)}, u32[]{:S(2)}) collective-permute-start(bf16[64,1408]{1,0:T(8,128)(2,1)S(1)} %collective-permute-done.6.refs_6_), channel_id=1, source_target_pairs={{0,1},{1,0},{2,3},{3,2},{4,5},{5,4},{6,7},{7,6},{8,9},{9,8},{10,11... | collective-permute-start | bytes 540680 | tf_op jit(solution)/shard_map/ppermute | solution.py:32
  32.6 7.1 %collective-permute-start.12 = (bf16[320,128]{1,0:T(8,128)(2,1)S(1)}, bf16[320,128]{1,0:T(8,128)(2,1)S(1)}, u32[]{:S(2)}, u32[]{:S(2)}) collective-permute-start(bf16[320,128]{1,0:T(8,128)(2,1)S(1)} %get-tuple-element.74), channel_id=1, source_target_pairs={{0,8},{4,12},{8,0},{12,4},{1,9},{5,13},{9,1},{13,5},{2,10},{6,14},... | collective-permute-start | bytes 245768 | tf_op jit(solution)/shard_map/ppermute | solution.py:32
  32.7 7.1 %collective-permute-start.13 = (bf16[320,128]{1,0:T(8,128)(2,1)S(1)}, bf16[320,128]{1,0:T(8,128)(2,1)S(1)}, u32[]{:S(2)}, u32[]{:S(2)}) collective-permute-start(bf16[320,128]{1,0:T(8,128)(2,1)S(1)} %get-tuple-element.75), channel_id=1, source_target_pairs={{0,4},{4,0},{8,12},{12,8},{1,5},{5,1},{9,13},{13,9},{2,6},{6,2},{1... | collective-permute-start | bytes 245768 | tf_op jit(solution)/shard_map/ppermute | solution.py:32
  35.1 6.3 %collective-permute-start.14 = (bf16[320,128]{1,0:T(8,128)(2,1)S(1)}, bf16[320,128]{1,0:T(8,128)(2,1)S(1)}, u32[]{:S(2)}, u32[]{:S(2)}) collective-permute-start(bf16[320,128]{1,0:T(8,128)(2,1)S(1)} %get-tuple-element.76), channel_id=1, source_target_pairs={{0,12},{4,8},{8,4},{12,0},{1,13},{5,9},{9,5},{13,1},{2,14},{6,10},... | collective-permute-start | bytes 245768 | tf_op jit(solution)/shard_map/ppermute | solution.py:32
  41.4 1.4 %collective-permute-start.15 = (f32[192,128]{1,0:T(8,128)S(1)}, f32[192,128]{1,0:T(8,128)S(1)}, u32[]{:S(2)}, u32[]{:S(2)}) collective-permute-start(f32[192,128]{1,0:T(8,128)S(1)} %get-tuple-element.78), channel_id=1, source_target_pairs={{0,1},{1,0},{2,3},{3,2},{4,5},{5,4},{6,7},{7,6},{8,9},{9,8},{10,11... | collective-permute-start | bytes 294920 | tf_op jit(solution)/shard_map/ppermute | solution.py:32
  43.9 5.9 %collective-permute-start.16 = (bf16[64,256]{1,0:T(8,128)(2,1)S(1)}, bf16[64,256]{1,0:T(8,128)(2,1)S(1)}, u32[]{:S(2)}, u32[]{:S(2)}) collective-permute-start(bf16[64,256]{1,0:T(8,128)(2,1)S(1)} %get-tuple-element.80), channel_id=1, source_target_pairs={{0,12},{4,8},{8,4},{12,0},{1,13},{5,9},{9,5},{13,1},{2,14},{6,10},... | collective-permute-start | bytes 98312 | tf_op jit(solution)/shard_map/ppermute | solution.py:32
  46.0 4.9 %collective-permute-start.17 = (bf16[64,256]{1,0:T(8,128)(2,1)S(1)}, bf16[64,256]{1,0:T(8,128)(2,1)S(1)}, u32[]{:S(2)}, u32[]{:S(2)}) collective-permute-start(bf16[64,256]{1,0:T(8,128)(2,1)S(1)} %get-tuple-element.81), channel_id=1, source_target_pairs={{0,8},{4,12},{8,0},{12,4},{1,9},{5,13},{9,1},{13,5},{2,10},{6,14},... | collective-permute-start | bytes 98312 | tf_op jit(solution)/shard_map/ppermute | solution.py:32
  46.5 4.5 %collective-permute-start.18 = (bf16[64,256]{1,0:T(8,128)(2,1)S(1)}, bf16[64,256]{1,0:T(8,128)(2,1)S(1)}, u32[]{:S(2)}, u32[]{:S(2)}) collective-permute-start(bf16[64,256]{1,0:T(8,128)(2,1)S(1)} %get-tuple-element.82), channel_id=1, source_target_pairs={{0,4},{4,0},{8,12},{12,8},{1,5},{5,1},{9,13},{13,9},{2,6},{6,2},{1... | collective-permute-start | bytes 98312 | tf_op jit(solution)/shard_map/ppermute | solution.py:32

commit v10 on v8

--- a/solution.py
+++ b/solution.py
@@ -51,7 +51,7 @@
         rest = list(range(1, self.seq))
         self.order = [0] + rest[::-1]
         self.order_rows = [0] + rest[:1] + rest[:0:-1]
-        self.order_sum = [0] + rest[1:2] + rest[:1] + rest[2:]
+        self.order_sum = [0] + rest[-1:] + rest[:-1]
         tiles = [
             -(-((i * self.features) % LANES + self.features) // LANES) for i in range(self.side)
         ]

time: 52 us -> 52.1 us (level)
  transfers between devices with their start and end apart: 19 -> 19, of which waited for: 9 -> 8; matrix products, arithmetic and copies ran while one was open for 0% -> 0% of each run, Pallas kernels for 10% -> 10%
where the time goes in v10:
time: 52.1 us; the launch traced here: 51.9 us
  starting transfers between devices  23 us (44%)
  waiting for transfers between devices  18 us (35%)
  Pallas kernels  8.7 us (17%)
  local copies, waits for them, and re-layouts  2.04 us (4%)
    ppermute x17, starting transfers between devices, swap(): lax.ppermute(value, axis, [(i, i ^ mask) for i in range(lax.axis_size(axi...  19.6 us
    ppermute x17, waiting for transfers between devices, swap(): lax.ppermute(value, axis, [(i, i ^ mask) for i in range(lax.axis_size(axi...  18 us
    pallas_call x9, Pallas kernels, call(): pl.pallas_call(functools.partial(kernel, sz), out_shape=[jax.ShapeDtypeSt...  8.7 us
    ppermute x2, starting transfers between devices, by_heads(): panels.append(lax.ppermute(panels_out[m], ('seq', 'owner'), pairs))  3.41 us
    unnamed x16, local copies, waits for them, and re-layouts  2.04 us
  transfers between devices with their start and end apart: 19, of which 8 were waited for; matrix products, arithmetic and copies ran while one was open for 0% of the time, Pallas kernels for 10%

profile of v10, /device:TPU:0, one launch (start us, length us, event | category | flops | bytes accessed | tf_op | source)
XLA Modules:
  0.0 51.9 jit_solution(7257185459542930036)
XLA Ops:
  0.0 0.5 collective-permute-start.1
  0.5 1.1 %copy-done.1 = bf16[1,2,2688,64]{2,3,1,0:T(8,128)(2,1)S(1)} copy-done((bf16[1,2,2688,64]{2,3,1,0:T(8,128)(2,1)S(1)}, bf16[1,2,2688,64]{2,3,1,0:T(8,128)(2,1)}, u32[]{:S(2)}) %copy-start.1) | copy-done | bytes 688152
  1.6 0.1 panels_out.1
  1.7 2.7 %collective-permute-start.2 = (bf16[64,1408]{1,0:T(8,128)(2,1)S(1)}, bf16[64,1408]{1,0:T(8,128)(2,1)S(1)}, u32[]{:S(2)}, u32[]{:S(2)}) collective-permute-start(bf16[64,1408]{1,0:T(8,128)(2,1)S(1)} %get-tuple-element.49), channel_id=1, source_target_pairs={{0,4},{1,12},{4,0},{5,8},{8,5},{9,13},{12,1},{13,9},{2,6},{3,14},{... | collective-permute-start | bytes 540680 | tf_op jit(solution)/shard_map/ppermute | solution.py:352
  4.4 0.7 %collective-permute-start = (bf16[64,1408]{1,0:T(8,128)(2,1)S(1)}, bf16[64,1408]{1,0:T(8,128)(2,1)S(1)}, u32[]{:S(2)}, u32[]{:S(2)}) collective-permute-start(bf16[64,1408]{1,0:T(8,128)(2,1)S(1)} %get-tuple-element.44), channel_id=1, source_target_pairs={{0,0},{1,8},{4,4},{5,12},{8,1},{9,9},{12,5},{13,13},{2,2},{3,10},{... | collective-permute-start | bytes 540680 | tf_op jit(solution)/shard_map/ppermute | solution.py:352
  5.1 2.2 %norm_rows.1 = (bf16[64,1408]{1,0:T(8,128)(2,1)}, bf16[64,1408]{1,0:T(8,128)(2,1)}, bf16[64,1408]{1,0:T(8,128)(2,1)}, bf16[64,1408]{1,0:T(8,128)(2,1)}) custom-call(bf16[64,5376]{1,0:T(8,128)(2,1)} %bitcast.12, f32[1,5376]{1,0:T(1,128)} %gain.1, bf16[64,1024]{1,0:T(8,128)(2,1)} %bitcast.13, bf16[64,512]{1,0:T(8,128)(2,1)} %bitcast.15, ...), custom_call_target="tpu_custom_call" | custom-call | tf_op jit(solution)/shard_map/norm_rows/pallas_call | solution.py:327
  7.3 0.1 collective-permute-start.3
  7.4 7.3 %collective-permute-start.4 = (bf16[64,1408]{1,0:T(8,128)(2,1)}, bf16[64,1408]{1,0:T(8,128)(2,1)S(1)}, u32[]{:S(2)}, u32[]{:S(2)}) collective-permute-start(bf16[64,1408]{1,0:T(8,128)(2,1)} %get-tuple-element.53), channel_id=1, source_target_pairs={{0,12},{4,8},{8,4},{12,0},{1,13},{5,9},{9,5},{13,1},{2,14},{6,10},... | collective-permute-start | bytes 540680 | tf_op jit(solution)/shard_map/ppermute | solution.py:31
  14.8 0.9 %copy-done.2 = bf16[64,1408]{1,0:T(8,128)(2,1)S(1)} copy-done((bf16[64,1408]{1,0:T(8,128)(2,1)S(1)}, bf16[64,1408]{1,0:T(8,128)(2,1)}, u32[]{:S(2)}) %copy-start.2) | copy-done | bytes 180248
  15.7 1.5 %table.1 = (s32[4,4]{1,0:T(4,128)S(1)}, bf16[64,1408]{1,0:T(8,128)(2,1)S(1)}) custom-call(s32[4]{0:T(128)S(1)} %copy-done.3, s32[4]{0:T(128)S(1)} %copy-done.4, s32[8]{0:T(128)S(1)} %copy-done.5, s32[8]{0:T(128)S(1)} %copy-done.6, bf16[64,1408]{1,0:T(8,128)(2,1)S(1)} %copy-done.2), custom_call_target="tpu_custom_call" | custom-call | tf_op jit(solution)/shard_map/table/pallas_call | solution.py:327
  17.2 0.0 collective-permute-done.2.refs_5_
  17.2 1.6 %collective-permute-start.7 = (bf16[64,1408]{1,0:T(8,128)(2,1)S(1)}, bf16[64,1408]{1,0:T(8,128)(2,1)S(1)}, u32[]{:S(2)}, u32[]{:S(2)}) collective-permute-start(bf16[64,1408]{1,0:T(8,128)(2,1)S(1)} %collective-permute-done.2.refs_5_), channel_id=1, source_target_pairs={{0,16},{16,0},{1,17},{17,1},{2,18},{18,2},{3,19},{19,3},{4,20},{20... | collective-permute-start | bytes 540680 | tf_op jit(solution)/shard_map/ppermute | solution.py:31
  18.8 0.0 collective-permute-done.1.base_other
  18.8 0.4 matrix_rows.1.matrix
  19.2 0.0 collective-permute-done.refs_4_
  19.2 0.6 %collective-permute-start.6 = (bf16[64,1408]{1,0:T(8,128)(2,1)S(1)}, bf16[64,1408]{1,0:T(8,128)(2,1)S(1)}, u32[]{:S(2)}, u32[]{:S(2)}) collective-permute-start(bf16[64,1408]{1,0:T(8,128)(2,1)S(1)} %collective-permute-done.refs_4_), channel_id=1, source_target_pairs={{0,16},{16,0},{1,17},{17,1},{2,18},{18,2},{3,19},{19,3},{4,20},{20... | collective-permute-start | bytes 540680 | tf_op jit(solution)/shard_map/ppermute | solution.py:31
  19.8 0.0 collective-permute-start.5
  19.8 0.0 collective-permute-done.3.refs_3_
  19.8 0.1 collective-permute-start.9
  19.9 4.3 %collective-permute-done.7.refs_7_ = bf16[64,1408]{1,0:T(8,128)(2,1)S(1)} collective-permute-done((bf16[64,1408]{1,0:T(8,128)(2,1)S(1)}, bf16[64,1408]{1,0:T(8,128)(2,1)S(1)}, u32[]{:S(2)}, u32[]{:S(2)}) %collective-permute-start.7) | collective-permute-done | bytes 180256 | tf_op jit(solution)/shard_map/ppermute | solution.py:31
  24.2 0.0 collective-permute-start.11
  24.2 0.0 collective-permute-done.4.refs_1_
  24.2 0.5 collective-permute-start.8
  24.7 1.4 %collective-permute-done.6.refs_6_ = bf16[64,1408]{1,0:T(8,128)(2,1)S(1)} collective-permute-done((bf16[64,1408]{1,0:T(8,128)(2,1)S(1)}, bf16[64,1408]{1,0:T(8,128)(2,1)S(1)}, u32[]{:S(2)}, u32[]{:S(2)}) %collective-permute-start.6) | collective-permute-done | bytes 180256 | tf_op jit(solution)/shard_map/ppermute | solution.py:31
  26.1 0.0 collective-permute-start.10
  26.1 5.0 %collective-permute-done.5.refs_2_ = bf16[64,1408]{1,0:T(8,128)(2,1)S(1)} collective-permute-done((bf16[64,1408]{1,0:T(8,128)(2,1)S(1)}, bf16[64,1408]{1,0:T(8,128)(2,1)S(1)}, u32[]{:S(2)}, u32[]{:S(2)}) %collective-permute-start.5) | collective-permute-done | bytes 180256 | tf_op jit(solution)/shard_map/ppermute | solution.py:31
  31.1 0.0 collective-permute-done.9.refs_9_
  31.1 0.0 collective-permute-done.11.refs_11_
  31.1 0.0 collective-permute-done.8.refs_8_
  31.1 0.0 collective-permute-done.10.refs_10_
  31.1 1.5 %project.1 = (bf16[320,128]{1,0:T(8,128)(2,1)S(1)}, bf16[320,128]{1,0:T(8,128)(2,1)S(1)}, bf16[320,128]{1,0:T(8,128)(2,1)S(1)}, bf16[320,128]{1,0:T(8,128)(2,1)S(1)}) custom-call(s32[4,4]{1,0:T(4,128)S(1)} %get-tuple-element.48.table, bf16[1408,1024]{1,0:T(8,128)(2,1)S(1)} %matrix_rows.1.matrix, bf16[64,1408]{1,0:T(8,128)(2,1)S(1)} %get-tuple-element.57.refs_0_, ...), custom_call_target="tpu_custom_call" | custom-call | tf_op jit(solution)/shard_map/project/pallas_call | solution.py:327
  32.7 1.9 %collective-permute-start.12 = (bf16[320,128]{1,0:T(8,128)(2,1)S(1)}, bf16[320,128]{1,0:T(8,128)(2,1)S(1)}, u32[]{:S(2)}, u32[]{:S(2)}) collective-permute-start(bf16[320,128]{1,0:T(8,128)(2,1)S(1)} %get-tuple-element.74), channel_id=1, source_target_pairs={{0,12},{4,8},{8,4},{12,0},{1,13},{5,9},{9,5},{13,1},{2,14},{6,10},... | collective-permute-start | bytes 245768 | tf_op jit(solution)/shard_map/ppermute | solution.py:31
  34.6 0.0 collective-permute-start.13
  34.6 2.5 %collective-permute-start.14 = (bf16[320,128]{1,0:T(8,128)(2,1)S(1)}, bf16[320,128]{1,0:T(8,128)(2,1)S(1)}, u32[]{:S(2)}, u32[]{:S(2)}) collective-permute-start(bf16[320,128]{1,0:T(8,128)(2,1)S(1)} %get-tuple-element.76), channel_id=1, source_target_pairs={{0,8},{4,12},{8,0},{12,4},{1,9},{5,13},{9,1},{13,5},{2,10},{6,14},... | collective-permute-start | bytes 245768 | tf_op jit(solution)/shard_map/ppermute | solution.py:31
  37.1 2.7 %collective-permute-done.12.refs_1_ = bf16[320,128]{1,0:T(8,128)(2,1)S(1)} collective-permute-done((bf16[320,128]{1,0:T(8,128)(2,1)S(1)}, bf16[320,128]{1,0:T(8,128)(2,1)S(1)}, u32[]{:S(2)}, u32[]{:S(2)}) %collective-permute-start.12) | collective-permute-done | bytes 81952 | tf_op jit(solution)/shard_map/ppermute | solution.py:31
  39.9 1.8 %collective-permute-done.13.refs_2_ = bf16[320,128]{1,0:T(8,128)(2,1)S(1)} collective-permute-done((bf16[320,128]{1,0:T(8,128)(2,1)S(1)}, bf16[320,128]{1,0:T(8,128)(2,1)S(1)}, u32[]{:S(2)}, u32[]{:S(2)}) %collective-permute-start.13) | collective-permute-done | bytes 81952 | tf_op jit(solution)/shard_map/ppermute | solution.py:31
  41.7 0.0 collective-permute-done.14.refs_3_
  41.7 0.1 collective-permute-start.15
  41.8 1.1 %softmax_rows.1 = (bf16[512,256]{1,0:T(8,128)(2,1)S(1)}, bf16[256,128]{1,0:T(8,128)(2,1)S(1)}, f32[256,128]{1,0:T(8,128)S(1)}) custom-call(s32[4,4]{1,0:T(4,128)S(1)} %get-tuple-element.48.table, bf16[64,1408]{1,0:T(8,128)(2,1)S(1)} %get-tuple-element.57.refs_0_, bf16[64,1408]{1,0:T(8,128)(2,1)S(1)} %collective-permute-done.4.refs_1_, ...), custom_call_target="tpu_custom_call" | custom-call | tf_op jit(solution)/shard_map/softmax_rows/pallas_call | solution.py:327
  43.0 0.1 collective-permute-done.15.received
  43.1 1.1 %mix_values.1 = (bf16[64,256]{1,0:T(8,128)(2,1)S(1)}, bf16[64,256]{1,0:T(8,128)(2,1)S(1)}, bf16[64,256]{1,0:T(8,128)(2,1)S(1)}, bf16[64,256]{1,0:T(8,128)(2,1)S(1)}) custom-call(s32[4,4]{1,0:T(4,128)S(1)} %get-tuple-element.48.table, bf16[512,256]{1,0:T(8,128)(2,1)S(1)} %get-tuple-element.61.softmax, bf16[256,128]{1,0:T(8,128)(2,1)S(1)} %get-tuple-element.62.raise_picked, ...), custom_call_target="tpu_custom_call" | custom-call | tf_op jit(solution)/shard_map/mix_values/pallas_call | solution.py:327
  44.2 1.9 %collective-permute-start.16 = (bf16[64,256]{1,0:T(8,128)(2,1)S(1)}, bf16[64,256]{1,0:T(8,128)(2,1)S(1)}, u32[]{:S(2)}, u32[]{:S(2)}) collective-permute-start(bf16[64,256]{1,0:T(8,128)(2,1)S(1)} %get-tuple-element.80), channel_id=1, source_target_pairs={{0,12},{4,8},{8,4},{12,0},{1,13},{5,9},{9,5},{13,1},{2,14},{6,10},... | collective-permute-start | bytes 98312 | tf_op jit(solution)/shard_map/ppermute | solution.py:31
  46.1 0.3 collective-permute-start.17
  46.4 2.2 %collective-permute-start.18 = (bf16[64,256]{1,0:T(8,128)(2,1)S(1)}, bf16[64,256]{1,0:T(8,128)(2,1)S(1)}, u32[]{:S(2)}, u32[]{:S(2)}) collective-permute-start(bf16[64,256]{1,0:T(8,128)(2,1)S(1)} %get-tuple-element.82), channel_id=1, source_target_pairs={{0,4},{4,0},{8,12},{12,8},{1,5},{5,1},{9,13},{13,9},{2,6},{6,2},{1... | collective-permute-start | bytes 98312 | tf_op jit(solution)/shard_map/ppermute | solution.py:31
  48.7 1.4 %collective-permute-done.16.refs_1_ = bf16[64,256]{1,0:T(8,128)(2,1)S(1)} collective-permute-done((bf16[64,256]{1,0:T(8,128)(2,1)S(1)}, bf16[64,256]{1,0:T(8,128)(2,1)S(1)}, u32[]{:S(2)}, u32[]{:S(2)}) %collective-permute-start.16) | collective-permute-done | bytes 32800 | tf_op jit(solution)/shard_map/ppermute | solution.py:31
  50.1 1.1 %collective-permute-done.17.refs_2_ = bf16[64,256]{1,0:T(8,128)(2,1)S(1)} collective-permute-done((bf16[64,256]{1,0:T(8,128)(2,1)S(1)}, bf16[64,256]{1,0:T(8,128)(2,1)S(1)}, u32[]{:S(2)}, u32[]{:S(2)}) %collective-permute-start.17) | collective-permute-done | bytes 32800 | tf_op jit(solution)/shard_map/ppermute | solution.py:31
  51.2 0.0 collective-permute-done.18.refs_3_
  51.2 0.7 %place_heads.1 = bf16[64,1024]{1,0:T(8,128)(2,1)} custom-call(bf16[64,256]{1,0:T(8,128)(2,1)S(1)} %get-tuple-element.79.refs_0_, bf16[64,256]{1,0:T(8,128)(2,1)S(1)} %collective-permute-done.16.refs_1_, bf16[64,256]{1,0:T(8,128)(2,1)S(1)} %collective-permute-done.17.refs_2_, bf16[64,256]{1,0:T(8,128)(2,1)S(1)} %collective-permute-done.18.refs_3_), custom_call_target="tpu_custom_call" | custom-call | tf_op jit(solution)/shard_map/place_heads/pallas_call | solution.py:327
  (15 shorter events, 0.1 us)
Async XLA Ops:
  0.0 18.8 %copy-start = (bf16[1,672,1024]{2,1,0:T(8,128)(2,1)S(1)}, bf16[1,672,1024]{2,1,0:T(8,128)(2,1)}, u32[]{:S(2)}) copy-start(bf16[1,672,1024]{2,1,0:T(8,128)(2,1)} %param.15) | copy-start | bytes 4128772
  0.0 18.8 %collective-permute-start.1 = (bf16[672,1024]{1,0:T(8,128)(2,1)}, bf16[672,1024]{1,0:T(8,128)(2,1)S(1)}, u32[]{:S(2)}, u32[]{:S(2)}) collective-permute-start(bf16[672,1024]{1,0:T(8,128)(2,1)} %bitcast.9), channel_id=1, source_target_pairs={{0,1},{1,0},{2,3},{3,2},{4,5},{5,4},{6,7},{7,6},{8,9},{9,8},{10,11... | collective-permute-start | bytes 4128776 | tf_op jit(solution)/shard_map/ppermute | solution.py:31
  0.5 1.1 %copy-start.1 = (bf16[1,2,2688,64]{2,3,1,0:T(8,128)(2,1)S(1)}, bf16[1,2,2688,64]{2,3,1,0:T(8,128)(2,1)}, u32[]{:S(2)}) copy-start(bf16[1,2,2688,64]{2,3,1,0:T(8,128)(2,1)} %param.16) | copy-start | bytes 2064388
  1.6 13.2 %copy-start.3 = (s32[4]{0:T(128)S(1)}, s32[4]{0:T(128)}, u32[]{:S(2)}) copy-start(s32[4]{0:T(128)} %lengths.1) | copy-start | bytes 52
  1.6 13.2 %copy-start.4 = (s32[4]{0:T(128)S(1)}, s32[4]{0:T(128)}, u32[]{:S(2)}) copy-start(s32[4]{0:T(128)} %adapters.1) | copy-start | bytes 52
  1.6 13.2 %copy-start.5 = (s32[8]{0:T(128)S(1)}, s32[8]{0:T(128)}, u32[]{:S(2)}) copy-start(s32[8]{0:T(128)} %ranks.1) | copy-start | bytes 100
  1.6 13.2 %copy-start.6 = (s32[8]{0:T(128)S(1)}, s32[8]{0:T(128)}, u32[]{:S(2)}) copy-start(s32[8]{0:T(128)} %slots.1) | copy-start | bytes 100
  1.7 15.5 %collective-permute-start.2 = (bf16[64,1408]{1,0:T(8,128)(2,1)S(1)}, bf16[64,1408]{1,0:T(8,128)(2,1)S(1)}, u32[]{:S(2)}, u32[]{:S(2)}) collective-permute-start(bf16[64,1408]{1,0:T(8,128)(2,1)S(1)} %get-tuple-element.49), channel_id=1, source_target_pairs={{0,4},{1,12},{4,0},{5,8},{8,5},{9,13},{12,1},{13,9},{2,6},{3,14},{... | collective-permute-start | bytes 540680 | tf_op jit(solution)/shard_map/ppermute | solution.py:352
  4.4 14.8 %collective-permute-start = (bf16[64,1408]{1,0:T(8,128)(2,1)S(1)}, bf16[64,1408]{1,0:T(8,128)(2,1)S(1)}, u32[]{:S(2)}, u32[]{:S(2)}) collective-permute-start(bf16[64,1408]{1,0:T(8,128)(2,1)S(1)} %get-tuple-element.44), channel_id=1, source_target_pairs={{0,0},{1,8},{4,4},{5,12},{8,1},{9,9},{12,5},{13,13},{2,2},{3,10},{... | collective-permute-start | bytes 540680 | tf_op jit(solution)/shard_map/ppermute | solution.py:352
  7.3 12.4 %collective-permute-start.3 = (bf16[64,1408]{1,0:T(8,128)(2,1)}, bf16[64,1408]{1,0:T(8,128)(2,1)S(1)}, u32[]{:S(2)}, u32[]{:S(2)}) collective-permute-start(bf16[64,1408]{1,0:T(8,128)(2,1)} %get-tuple-element.52), channel_id=1, source_target_pairs={{0,4},{4,0},{8,12},{12,8},{1,5},{5,1},{9,13},{13,9},{2,6},{6,2},{1... | collective-permute-start | bytes 540680 | tf_op jit(solution)/shard_map/ppermute | solution.py:31
  7.4 16.7 %collective-permute-start.4 = (bf16[64,1408]{1,0:T(8,128)(2,1)}, bf16[64,1408]{1,0:T(8,128)(2,1)S(1)}, u32[]{:S(2)}, u32[]{:S(2)}) collective-permute-start(bf16[64,1408]{1,0:T(8,128)(2,1)} %get-tuple-element.53), channel_id=1, source_target_pairs={{0,12},{4,8},{8,4},{12,0},{1,13},{5,9},{9,5},{13,1},{2,14},{6,10},... | collective-permute-start | bytes 540680 | tf_op jit(solution)/shard_map/ppermute | solution.py:31
  14.8 0.9 %copy-start.2 = (bf16[64,1408]{1,0:T(8,128)(2,1)S(1)}, bf16[64,1408]{1,0:T(8,128)(2,1)}, u32[]{:S(2)}) copy-start(bf16[64,1408]{1,0:T(8,128)(2,1)} %get-tuple-element.46.piece) | copy-start | bytes 540676
  17.2 2.6 %copy-start.7 = (bf16[64,1408]{1,0:T(8,128)(2,1)S(1)}, bf16[64,1408]{1,0:T(8,128)(2,1)}, u32[]{:S(2)}) copy-start(bf16[64,1408]{1,0:T(8,128)(2,1)} %get-tuple-element.54) | copy-start | bytes 540676
  17.2 7.0 %collective-permute-start.7 = (bf16[64,1408]{1,0:T(8,128)(2,1)S(1)}, bf16[64,1408]{1,0:T(8,128)(2,1)S(1)}, u32[]{:S(2)}, u32[]{:S(2)}) collective-permute-start(bf16[64,1408]{1,0:T(8,128)(2,1)S(1)} %collective-permute-done.2.refs_5_), channel_id=1, source_target_pairs={{0,16},{16,0},{1,17},{17,1},{2,18},{18,2},{3,19},{19,3},{4,20},{20... | collective-permute-start | bytes 540680 | tf_op jit(solution)/shard_map/ppermute | solution.py:31
  19.2 6.9 %collective-permute-start.6 = (bf16[64,1408]{1,0:T(8,128)(2,1)S(1)}, bf16[64,1408]{1,0:T(8,128)(2,1)S(1)}, u32[]{:S(2)}, u32[]{:S(2)}) collective-permute-start(bf16[64,1408]{1,0:T(8,128)(2,1)S(1)} %collective-permute-done.refs_4_), channel_id=1, source_target_pairs={{0,16},{16,0},{1,17},{17,1},{2,18},{18,2},{3,19},{19,3},{4,20},{20... | collective-permute-start | bytes 540680 | tf_op jit(solution)/shard_map/ppermute | solution.py:31
  19.8 11.3 %collective-permute-start.5 = (bf16[64,1408]{1,0:T(8,128)(2,1)S(1)}, bf16[64,1408]{1,0:T(8,128)(2,1)S(1)}, u32[]{:S(2)}, u32[]{:S(2)}) collective-permute-start(bf16[64,1408]{1,0:T(8,128)(2,1)S(1)} %copy-done.7), channel_id=1, source_target_pairs={{0,8},{4,12},{8,0},{12,4},{1,9},{5,13},{9,1},{13,5},{2,10},{6,14},... | collective-permute-start | bytes 540680 | tf_op jit(solution)/shard_map/ppermute | solution.py:31
  19.8 11.3 %collective-permute-start.9 = (bf16[64,1408]{1,0:T(8,128)(2,1)S(1)}, bf16[64,1408]{1,0:T(8,128)(2,1)S(1)}, u32[]{:S(2)}, u32[]{:S(2)}) collective-permute-start(bf16[64,1408]{1,0:T(8,128)(2,1)S(1)} %collective-permute-done.2.refs_5_), channel_id=1, source_target_pairs={{0,1},{1,0},{2,3},{3,2},{4,5},{5,4},{6,7},{7,6},{8,9},{9,8},{10,11... | collective-permute-start | bytes 540680 | tf_op jit(solution)/shard_map/ppermute | solution.py:31
  24.2 6.9 %collective-permute-start.11 = (bf16[64,1408]{1,0:T(8,128)(2,1)S(1)}, bf16[64,1408]{1,0:T(8,128)(2,1)S(1)}, u32[]{:S(2)}, u32[]{:S(2)}) collective-permute-start(bf16[64,1408]{1,0:T(8,128)(2,1)S(1)} %collective-permute-done.7.refs_7_), channel_id=1, source_target_pairs={{0,1},{1,0},{2,3},{3,2},{4,5},{5,4},{6,7},{7,6},{8,9},{9,8},{10,11... | collective-permute-start | bytes 540680 | tf_op jit(solution)/shard_map/ppermute | solution.py:31
  24.2 6.9 %collective-permute-start.8 = (bf16[64,1408]{1,0:T(8,128)(2,1)S(1)}, bf16[64,1408]{1,0:T(8,128)(2,1)S(1)}, u32[]{:S(2)}, u32[]{:S(2)}) collective-permute-start(bf16[64,1408]{1,0:T(8,128)(2,1)S(1)} %collective-permute-done.refs_4_), channel_id=1, source_target_pairs={{0,1},{1,0},{2,3},{3,2},{4,5},{5,4},{6,7},{7,6},{8,9},{9,8},{10,11... | collective-permute-start | bytes 540680 | tf_op jit(solution)/shard_map/ppermute | solution.py:31
  26.1 5.0 %collective-permute-start.10 = (bf16[64,1408]{1,0:T(8,128)(2,1)S(1)}, bf16[64,1408]{1,0:T(8,128)(2,1)S(1)}, u32[]{:S(2)}, u32[]{:S(2)}) collective-permute-start(bf16[64,1408]{1,0:T(8,128)(2,1)S(1)} %collective-permute-done.6.refs_6_), channel_id=1, source_target_pairs={{0,1},{1,0},{2,3},{3,2},{4,5},{5,4},{6,7},{7,6},{8,9},{9,8},{10,11... | collective-permute-start | bytes 540680 | tf_op jit(solution)/shard_map/ppermute | solution.py:31
  32.7 7.2 %collective-permute-start.12 = (bf16[320,128]{1,0:T(8,128)(2,1)S(1)}, bf16[320,128]{1,0:T(8,128)(2,1)S(1)}, u32[]{:S(2)}, u32[]{:S(2)}) collective-permute-start(bf16[320,128]{1,0:T(8,128)(2,1)S(1)} %get-tuple-element.74), channel_id=1, source_target_pairs={{0,12},{4,8},{8,4},{12,0},{1,13},{5,9},{9,5},{13,1},{2,14},{6,10},... | collective-permute-start | bytes 245768 | tf_op jit(solution)/shard_map/ppermute | solution.py:31
  34.6 7.1 %collective-permute-start.13 = (bf16[320,128]{1,0:T(8,128)(2,1)S(1)}, bf16[320,128]{1,0:T(8,128)(2,1)S(1)}, u32[]{:S(2)}, u32[]{:S(2)}) collective-permute-start(bf16[320,128]{1,0:T(8,128)(2,1)S(1)} %get-tuple-element.75), channel_id=1, source_target_pairs={{0,4},{4,0},{8,12},{12,8},{1,5},{5,1},{9,13},{13,9},{2,6},{6,2},{1... | collective-permute-start | bytes 245768 | tf_op jit(solution)/shard_map/ppermute | solution.py:31
  34.6 7.1 %collective-permute-start.14 = (bf16[320,128]{1,0:T(8,128)(2,1)S(1)}, bf16[320,128]{1,0:T(8,128)(2,1)S(1)}, u32[]{:S(2)}, u32[]{:S(2)}) collective-permute-start(bf16[320,128]{1,0:T(8,128)(2,1)S(1)} %get-tuple-element.76), channel_id=1, source_target_pairs={{0,8},{4,12},{8,0},{12,4},{1,9},{5,13},{9,1},{13,5},{2,10},{6,14},... | collective-permute-start | bytes 245768 | tf_op jit(solution)/shard_map/ppermute | solution.py:31
  41.7 1.4 %collective-permute-start.15 = (f32[192,128]{1,0:T(8,128)S(1)}, f32[192,128]{1,0:T(8,128)S(1)}, u32[]{:S(2)}, u32[]{:S(2)}) collective-permute-start(f32[192,128]{1,0:T(8,128)S(1)} %get-tuple-element.78), channel_id=1, source_target_pairs={{0,1},{1,0},{2,3},{3,2},{4,5},{5,4},{6,7},{7,6},{8,9},{9,8},{10,11... | collective-permute-start | bytes 294920 | tf_op jit(solution)/shard_map/ppermute | solution.py:31
  44.2 5.9 %collective-permute-start.16 = (bf16[64,256]{1,0:T(8,128)(2,1)S(1)}, bf16[64,256]{1,0:T(8,128)(2,1)S(1)}, u32[]{:S(2)}, u32[]{:S(2)}) collective-permute-start(bf16[64,256]{1,0:T(8,128)(2,1)S(1)} %get-tuple-element.80), channel_id=1, source_target_pairs={{0,12},{4,8},{8,4},{12,0},{1,13},{5,9},{9,5},{13,1},{2,14},{6,10},... | collective-permute-start | bytes 98312 | tf_op jit(solution)/shard_map/ppermute | solution.py:31
  46.1 5.1 %collective-permute-start.17 = (bf16[64,256]{1,0:T(8,128)(2,1)S(1)}, bf16[64,256]{1,0:T(8,128)(2,1)S(1)}, u32[]{:S(2)}, u32[]{:S(2)}) collective-permute-start(bf16[64,256]{1,0:T(8,128)(2,1)S(1)} %get-tuple-element.81), channel_id=1, source_target_pairs={{0,8},{4,12},{8,0},{12,4},{1,9},{5,13},{9,1},{13,5},{2,10},{6,14},... | collective-permute-start | bytes 98312 | tf_op jit(solution)/shard_map/ppermute | solution.py:31
  46.4 4.8 %collective-permute-start.18 = (bf16[64,256]{1,0:T(8,128)(2,1)S(1)}, bf16[64,256]{1,0:T(8,128)(2,1)S(1)}, u32[]{:S(2)}, u32[]{:S(2)}) collective-permute-start(bf16[64,256]{1,0:T(8,128)(2,1)S(1)} %get-tuple-element.82), channel_id=1, source_target_pairs={{0,4},{4,0},{8,12},{12,8},{1,5},{5,1},{9,13},{13,9},{2,6},{6,2},{1... | collective-permute-start | bytes 98312 | tf_op jit(solution)/shard_map/ppermute | solution.py:31
